TPU v7x, 32 devices: a whole 2x2x4 slice. The times are simulated.
32 devices in a mesh: gx: 2 (over x), gy: 4 (over y, core), gz: 4 (over z).
Axes of the slice: x: 2, y: 2, z: 4, core: 2. Of those that a mesh axis runs over, the one named last changes fastest.
Arguments:
- facies: int32 [64, 32, 512], P('gz', 'gx', 'gy'), may hold values from 0 to 15
- perm_table: float32 [3, 16], replicated, may hold values from 0.0003 to 3, as said below
- line_breaks: int32 [63], replicated, may hold values 0 or 1
Outputs:
- pressure: float32 [3, 64, 32, 512], P(None, 'gz', 'gx', 'gy')
- residual: float32 [3, 64, 32, 512], P(None, 'gz', 'gx', 'gy')
Inputs may be any that keep to these rules, and one draw needn't show every extreme that they name: `perm_table`: positive coefficients.
All inputs are finite; a program needn't handle non-finite values.
Results may differ from a plain program's by a relative error of at most 0.0003.
Values sent between devices are 32-bit elements; how exact they have to be, the bound alone decides.
No kernel may reach another device: no remote copies, remote signals or barrier semaphores. Data moves between devices by JAX's collectives and lax.ppermute only.
A program may use at most 64 MiB of HBM per device.

v0:
```python
import jax
import jax.numpy as jnp
from jax import lax
from jax.sharding import PartitionSpec as P


def with_halo(x, sides, width):
    for axis, dim in sides:
        size, length = (lax.axis_size(axis), x.shape[dim])
        up = [(i, (i + 1) % size) for i in range(size - 1)]
        down = [(j, i) for i, j in up]
        last = lax.slice_in_dim(x, length - width, length, axis=dim)
        leading = lax.slice_in_dim(x, 0, width, axis=dim)
        before = lax.ppermute(last, axis, up)
        after = lax.ppermute(leading, axis, down)
        x = jnp.concatenate([before, x, after], axis=dim)
    return x


def from_behind(block, axis, distance):
    devices = range(lax.axis_size(axis))
    route = [(i - distance, i) for i in devices if i - distance in devices]
    return lax.ppermute(block, axis, route)


def six_sides(padded):
    return (
        padded[..., :-2, 1:-1, 1:-1],
        padded[..., 2:, 1:-1, 1:-1],
        padded[..., 1:-1, :-2, 1:-1],
        padded[..., 1:-1, 2:, 1:-1],
        padded[..., 1:-1, 1:-1, :-2],
        padded[..., 1:-1, 1:-1, 2:],
    )


def face_pair(centre, beside):
    inside = beside > 0.0
    harmonic = 2.0 * centre * beside / (centre + beside)
    return (
        jnp.where(inside, harmonic, 2.0 * centre),
        jnp.where(inside, harmonic, centre),
        jnp.where(inside, harmonic, 0.0),
    )


def assemble(perm, padded):
    z_sides = six_sides(padded[2])
    x_sides = six_sides(padded[0])
    y_sides = six_sides(padded[1])
    z_low = face_pair(perm[2], z_sides[0])
    z_high = face_pair(perm[2], z_sides[1])
    x_low = face_pair(perm[0], x_sides[2])
    x_high = face_pair(perm[0], x_sides[3])
    y_low = face_pair(perm[1], y_sides[4])
    y_high = face_pair(perm[1], y_sides[5])
    taus = (z_low[0], z_high[0], x_low[0], x_high[0], y_low[0], y_high[0])
    source = jnp.stack([x_high[1] - x_low[1], y_high[1] - y_low[1], z_high[1] - z_low[1]])
    centre_sum = taus[0] + taus[1] + taus[2] + taus[3] + taus[4] + taus[5]
    return (taus, source, centre_sum, z_low[2], z_high[2])


def explicit_terms(taus, sides, break_low, break_high):
    return (
        taus[2] * sides[2]
        + taus[3] * sides[3]
        + taus[4] * sides[4]
        + taus[5] * sides[5]
        + taus[0] * break_low * sides[0]
        + taus[1] * break_high * sides[1]
    )


def residual_of(taus, sides, source, centre_sum, field):
    total = (
        taus[0] * sides[0]
        + taus[1] * sides[1]
        + taus[2] * sides[2]
        + taus[3] * sides[3]
        + taus[4] * sides[4]
        + taus[5] * sides[5]
    )
    return source - centre_sum * field + total


def table_lookup(facies, perm_table):
    perm = jnp.zeros((3,) + facies.shape, jnp.float32)
    for label in range(perm_table.shape[1]):
        perm = jnp.where((facies == label)[None], perm_table[:, label][:, None, None, None], perm)
    return perm


def widened(field):
    return with_halo(field, (("gx", 2), ("gy", 3), ("gz", 1)), 1)


def shift_rows(values, stride, fill, axis):
    count = values.shape[axis]
    step = abs(stride)
    filler = jnp.full_like(lax.slice_in_dim(values, 0, step, axis=axis), fill)
    if stride > 0:
        return jnp.concatenate([filler, lax.slice_in_dim(values, 0, count - step, axis=axis)], axis)
    return jnp.concatenate([lax.slice_in_dim(values, step, count, axis=axis), filler], axis)


def interior_solve(sub_diag, main_diag, super_diag, columns):
    stride = 1
    count = main_diag.shape[0]
    while stride < count:
        sub_low = shift_rows(sub_diag, stride, 0.0, 0)
        super_low = shift_rows(super_diag, stride, 0.0, 0)
        main_low = shift_rows(main_diag, stride, 1.0, 0)
        column_low = shift_rows(columns, stride, 0.0, 1)
        sub_high = shift_rows(sub_diag, -stride, 0.0, 0)
        super_high = shift_rows(super_diag, -stride, 0.0, 0)
        main_high = shift_rows(main_diag, -stride, 1.0, 0)
        column_high = shift_rows(columns, -stride, 0.0, 1)
        left = sub_diag / main_low
        right = super_diag / main_high
        main_diag = main_diag - left * super_low - right * sub_high
        columns = columns - left[None] * column_low - right[None] * column_high
        sub_diag = -left * sub_low
        super_diag = -right * super_high
        stride *= 2
    return columns / main_diag[None]


def block_product(left, right):
    return jnp.stack(
        [
            left[0] * right[0] + left[1] * right[2],
            left[0] * right[1] + left[1] * right[3],
            left[2] * right[0] + left[3] * right[2],
            left[2] * right[1] + left[3] * right[3],
        ]
    )


def block_inverse(block):
    determinant = block[0] * block[3] - block[1] * block[2]
    return jnp.stack([block[3], -block[1], -block[2], block[0]]) / determinant


def block_apply(block, pair):
    return jnp.stack(
        [
            block[0][None] * pair[0] + block[1][None] * pair[1],
            block[2][None] * pair[0] + block[3][None] * pair[1],
        ]
    )


def cyclic_reduce(blocks, pair):
    sub_block, mid_block, sup_block = blocks
    count = lax.axis_size("gz")
    position = lax.axis_index("gz")
    solid = jnp.ones_like(mid_block[0])
    empty = jnp.zeros_like(mid_block[0])
    unit = jnp.stack([solid, empty, empty, solid])
    stride = 1
    while stride < count:
        below = from_behind((sub_block, mid_block, sup_block, pair), "gz", stride)
        above = from_behind((sub_block, mid_block, sup_block, pair), "gz", -stride)
        mid_below = jnp.where(position >= stride, below[1], unit)
        mid_above = jnp.where(position + stride < count, above[1], unit)
        left_factor = -block_product(sub_block, block_inverse(mid_below))
        right_factor = -block_product(sup_block, block_inverse(mid_above))
        mid_block = (
            mid_block + block_product(left_factor, below[2]) + block_product(right_factor, above[0])
        )
        pair = pair + block_apply(left_factor, below[3]) + block_apply(right_factor, above[3])
        sub_block = block_product(left_factor, below[0])
        sup_block = block_product(right_factor, above[2])
        stride *= 2
    return block_apply(block_inverse(mid_block), pair)


def per_device(facies, perm_table, line_breaks):
    depth = facies.shape[0]
    inner = depth - 2
    perm = table_lookup(facies, perm_table)
    padded = with_halo(perm, (("gx", 2), ("gy", 3), ("gz", 1)), 1)
    taus, source, centre_sum, link_low, link_high = assemble(perm, padded)
    extended = jnp.concatenate(
        [jnp.zeros((1,), jnp.int32), line_breaks, jnp.zeros((1,), jnp.int32)]
    ).astype(jnp.float32)
    window = lax.dynamic_slice_in_dim(extended, lax.axis_index("gz") * depth, depth + 1)
    break_low = window[:depth][:, None, None]
    break_high = window[1:][:, None, None]
    sub_diag = -link_low * (1.0 - break_low)
    super_diag = -link_high * (1.0 - break_high)
    single_row = jnp.zeros_like(sub_diag[1:2])
    blank = jnp.zeros((inner - 1,) + sub_diag.shape[1:], jnp.float32)
    inner_sub = jnp.concatenate([single_row, sub_diag[2 : depth - 1]])
    inner_super = jnp.concatenate([super_diag[1 : depth - 2], single_row])
    inner_main = centre_sum[1 : depth - 1]
    push_low = jnp.concatenate([-sub_diag[1:2], blank])
    push_high = jnp.concatenate([blank, -super_diag[depth - 2 : depth - 1]])
    columns = jnp.concatenate([source[:, 1 : depth - 1], push_low[None], push_high[None]])
    solved = interior_solve(inner_sub, inner_main, inner_super, columns)
    inner_first = solved[:3]
    weight_low = solved[3]
    weight_high = solved[4]
    lower_u = sub_diag[0]
    centre_u = centre_sum[0] + super_diag[0] * weight_low[0]
    upper_u = super_diag[0] * weight_high[0]
    lower_v = sub_diag[depth - 1] * weight_low[inner - 1]
    centre_v = centre_sum[depth - 1] + sub_diag[depth - 1] * weight_high[inner - 1]
    upper_v = super_diag[depth - 1]

    def reduced_source(right, interior):
        return jnp.stack(
            [
                right[:, 0] - super_diag[0][None] * interior[:, 0],
                right[:, depth - 1] - sub_diag[depth - 1][None] * interior[:, inner - 1],
            ]
        )

    def rebuild(interior, ends):
        middle = (
            interior + weight_low[None] * ends[0][:, None] + weight_high[None] * ends[1][:, None]
        )
        return jnp.concatenate([ends[0][:, None], middle, ends[1][:, None]], axis=1)

    nothing = jnp.zeros_like(lower_u)
    blocks = (
        jnp.stack([nothing, lower_u, nothing, nothing]),
        jnp.stack([centre_u, upper_u, lower_v, centre_v]),
        jnp.stack([nothing, nothing, upper_v, nothing]),
    )

    def solve_reduced(pair):
        return cyclic_reduce(blocks, pair)

    first = rebuild(inner_first, solve_reduced(reduced_source(source, inner_first)))
    right = source + explicit_terms(taus, six_sides(widened(first)), break_low, break_high)
    inner_second = interior_solve(inner_sub, inner_main, inner_super, right[:, 1 : depth - 1])
    second = rebuild(inner_second, solve_reduced(reduced_source(right, inner_second)))
    residual = residual_of(taus, six_sides(widened(second)), source, centre_sum, second)
    return (second, residual)


def solution(mesh):
    return jax.shard_map(
        per_device,
        mesh=mesh,
        in_specs=(P("gz", "gx", "gy"), P(), P()),
        out_specs=(P(None, "gz", "gx", "gy"), P(None, "gz", "gx", "gy")),
        check_vma=False,
    )
```

profile of v0, /device:TPU:14, one launch (start us, length us, event | category | flops | bytes accessed | tf_op | source)
XLA Modules:
  0.0 165.4 jit_solution(15934409779143316895)
XLA Ops:
  0.6 1.7 %slice_reduce_fusion.15 = (f32[3]{0:T(128)S(1)}, f32[3]{0:T(128)S(1)}, f32[3]{0:T(128)S(1)}, f32[3]{0:T(128)S(1)}, f32[3]{0:T(128)S(1)}, /*index=5*/f32[3]{0:T(1...) fusion(f32[3,16]{1,0:T(4,128)} %param.4), kind=kLoop, calls=%fused_computation.403 | loop fusion | bytes 384 | tf_op jit(solution)/shard_map/slice | solution.py:89
  4.5 2.4 %collective-permute-start.1 = (f32[3,16,1,128]{3,1,2,0:T(8,128)S(1)}, f32[3,16,1,128]{3,1,2,0:T(8,128)S(1)}, u32[]{:S(2)}, u32[]{:S(2)}) collective-permute-start(f32[3,16,1,128]{3,1,2,0:T(8,128)S(1)} %get-tuple-element.127), channel_id=1, source_target_pairs={{16,0},{17,1},{18,2},{19,3},{20,4},{21,5},{22,6},{23,7},{24,8},{25... | collective-permute-start | bytes 73736 | tf_op jit(solution)/shard_map/ppermute | solution.py:15
  8.5 4.2 %collective-permute-done = f32[3,16,1,128]{3,1,2,0:T(8,128)S(1)} collective-permute-done((f32[3,16,1,128]{3,1,2,0:T(8,128)S(1)}, f32[3,16,1,128]{3,1,2,0:T(8,128)S(1)}, u32[]{:S(2)}, u32[]{:S(2)}) %collective-permute-start) | collective-permute-done | bytes 24608 | tf_op jit(solution)/shard_map/ppermute | solution.py:14
  13.3 1.9 %collective-permute-start.3 = (f32[3,16,18,1]{2,1,3,0:T(8,128)S(1)}, f32[3,16,18,1]{2,1,3,0:T(8,128)S(1)}, u32[]{:S(2)}, u32[]{:S(2)}) collective-permute-start(f32[3,16,18,1]{2,1,3,0:T(8,128)S(1)} %copy.372), channel_id=1, source_target_pairs={{4,0},{8,4},{12,8},{5,1},{9,5},{13,9},{6,2},{10,6},{14,10},{7,3},{... | collective-permute-start | bytes 10376 | tf_op jit(solution)/shard_map/ppermute | solution.py:15
  15.7 2.4 %collective-permute-start.2 = (f32[3,16,18,1]{2,1,3,0:T(8,128)S(1)}, f32[3,16,18,1]{2,1,3,0:T(8,128)S(1)}, u32[]{:S(2)}, u32[]{:S(2)}) collective-permute-start(f32[3,16,18,1]{2,1,3,0:T(8,128)S(1)} %copy.371), channel_id=1, source_target_pairs={{0,4},{4,8},{8,12},{1,5},{5,9},{9,13},{2,6},{6,10},{10,14},{3,7},{... | collective-permute-start | bytes 10376 | tf_op jit(solution)/shard_map/ppermute | solution.py:14
  18.6 2.2 %collective-permute-done.2 = f32[3,16,18,1]{2,1,3,0:T(8,128)S(1)} collective-permute-done((f32[3,16,18,1]{2,1,3,0:T(8,128)S(1)}, f32[3,16,18,1]{2,1,3,0:T(8,128)S(1)}, u32[]{:S(2)}, u32[]{:S(2)}) %collective-permute-start.2) | collective-permute-done | bytes 3488 | tf_op jit(solution)/shard_map/ppermute | solution.py:14
  21.7 3.5 %collective-permute-start.4 = (f32[3,1,18,130]{3,1,2,0:T(1,128)S(1)}, f32[3,1,18,130]{3,1,2,0:T(1,128)S(1)}, u32[]{:S(2)}, u32[]{:S(2)}) collective-permute-start(f32[3,1,18,130]{3,1,2,0:T(1,128)S(1)} %get-tuple-element.80), channel_id=1, source_target_pairs={{0,1},{1,2},{2,3},{4,5},{5,6},{6,7},{8,9},{9,10},{10,11},{12,13},{... | collective-permute-start | bytes 84248 | tf_op jit(solution)/shard_map/ppermute | solution.py:14
  25.3 2.3 %collective-permute-start.5 = (f32[3,1,18,130]{3,1,2,0:T(1,128)S(1)}, f32[3,1,18,130]{3,1,2,0:T(1,128)S(1)}, u32[]{:S(2)}, u32[]{:S(2)}) collective-permute-start(f32[3,1,18,130]{3,1,2,0:T(1,128)S(1)} %get-tuple-element.79), channel_id=1, source_target_pairs={{1,0},{2,1},{3,2},{5,4},{6,5},{7,6},{9,8},{10,9},{11,10},{13,12},{... | collective-permute-start | bytes 84248 | tf_op jit(solution)/shard_map/ppermute | solution.py:15
  28.3 3.0 %collective-permute-done.5 = f32[3,1,18,130]{3,1,2,0:T(1,128)S(1)} collective-permute-done((f32[3,1,18,130]{3,1,2,0:T(1,128)S(1)}, f32[3,1,18,130]{3,1,2,0:T(1,128)S(1)}, u32[]{:S(2)}, u32[]{:S(2)}) %collective-permute-start.5) | collective-permute-done | bytes 28112 | tf_op jit(solution)/shard_map/ppermute | solution.py:15
  35.8 2.4 %collective-permute-start.8 = (f32[4,16,128]{2,1,0:T(8,128)S(1)}, f32[4,16,128]{2,1,0:T(8,128)S(1)}, u32[]{:S(2)}, u32[]{:S(2)}) collective-permute-start(f32[4,16,128]{2,1,0:T(8,128)S(1)} %pad_maximum_fusion.55), channel_id=1, source_target_pairs={{1,0},{2,1},{3,2},{5,4},{6,5},{7,6},{9,8},{10,9},{11,10},{13,12},{... | collective-permute-start | bytes 98312 | tf_op jit(solution)/shard_map/ppermute | solution.py:23
  38.2 3.5 %collective-permute-start.6 = (f32[4,16,128]{2,1,0:T(8,128)S(1)}, f32[4,16,128]{2,1,0:T(8,128)S(1)}, u32[]{:S(2)}, u32[]{:S(2)}) collective-permute-start(f32[4,16,128]{2,1,0:T(8,128)S(1)} %pad_maximum_fusion.55), channel_id=1, source_target_pairs={{0,1},{1,2},{2,3},{4,5},{5,6},{6,7},{8,9},{9,10},{10,11},{12,13},{... | collective-permute-start | bytes 98312 | tf_op jit(solution)/shard_map/ppermute | solution.py:23
  41.8 2.2 %collective-permute-done.6 = f32[4,16,128]{2,1,0:T(8,128)S(1)} collective-permute-done((f32[4,16,128]{2,1,0:T(8,128)S(1)}, f32[4,16,128]{2,1,0:T(8,128)S(1)}, u32[]{:S(2)}, u32[]{:S(2)}) %collective-permute-start.6) | collective-permute-done | bytes 32800 | tf_op jit(solution)/shard_map/ppermute | solution.py:23
  44.1 1.9 %collective-permute-start.9 = (f32[4,16,128]{2,1,0:T(8,128)S(1)}, f32[4,16,128]{2,1,0:T(8,128)S(1)}, u32[]{:S(2)}, u32[]{:S(2)}) collective-permute-start(f32[4,16,128]{2,1,0:T(8,128)S(1)} %get-tuple-element.277), channel_id=1, source_target_pairs={{1,0},{2,1},{3,2},{5,4},{6,5},{7,6},{9,8},{10,9},{11,10},{13,12},{... | collective-permute-start | bytes 98312 | tf_op jit(solution)/shard_map/ppermute | solution.py:23
  46.0 3.9 %collective-permute-start.10 = (f32[4,16,128]{2,1,0:T(8,128)S(1)}, f32[4,16,128]{2,1,0:T(8,128)S(1)}, u32[]{:S(2)}, u32[]{:S(2)}) collective-permute-start(f32[4,16,128]{2,1,0:T(8,128)S(1)} %get-tuple-element.277), channel_id=1, source_target_pairs={{0,1},{1,2},{2,3},{4,5},{5,6},{6,7},{8,9},{9,10},{10,11},{12,13},{... | collective-permute-start | bytes 98312 | tf_op jit(solution)/shard_map/ppermute | solution.py:23
  49.9 3.5 %collective-permute-start.7 = (f32[4,16,128]{2,1,0:T(8,128)S(1)}, f32[4,16,128]{2,1,0:T(8,128)S(1)}, u32[]{:S(2)}, u32[]{:S(2)}) collective-permute-start(f32[4,16,128]{2,1,0:T(8,128)S(1)} %get-tuple-element.278), channel_id=1, source_target_pairs={{0,1},{1,2},{2,3},{4,5},{5,6},{6,7},{8,9},{9,10},{10,11},{12,13},{... | collective-permute-start | bytes 98312 | tf_op jit(solution)/shard_map/ppermute | solution.py:23
  53.5 2.2 %collective-permute-done.7 = f32[4,16,128]{2,1,0:T(8,128)S(1)} collective-permute-done((f32[4,16,128]{2,1,0:T(8,128)S(1)}, f32[4,16,128]{2,1,0:T(8,128)S(1)}, u32[]{:S(2)}, u32[]{:S(2)}) %collective-permute-start.7) | collective-permute-done | bytes 32800 | tf_op jit(solution)/shard_map/ppermute | solution.py:23
  57.1 5.4 %collective-permute-start.11 = (f32[4,16,128]{2,1,0:T(8,128)S(1)}, f32[4,16,128]{2,1,0:T(8,128)S(1)}, u32[]{:S(2)}, u32[]{:S(2)}) collective-permute-start(f32[4,16,128]{2,1,0:T(8,128)S(1)} %fusion.62), channel_id=1, source_target_pairs={{0,2},{1,3},{4,6},{5,7},{8,10},{9,11},{12,14},{13,15},{16,18},{17,... | collective-permute-start | bytes 98312 | tf_op jit(solution)/shard_map/ppermute | solution.py:23
  62.6 1.9 %collective-permute-start.16 = (f32[2,3,16,128]{3,2,1,0:T(8,128)S(1)}, f32[2,3,16,128]{3,2,1,0:T(8,128)S(1)}, u32[]{:S(2)}, u32[]{:S(2)}) collective-permute-start(f32[2,3,16,128]{3,2,1,0:T(8,128)S(1)} %pad_maximum_fusion.53), channel_id=1, source_target_pairs={{0,1},{1,2},{2,3},{4,5},{5,6},{6,7},{8,9},{9,10},{10,11},{12,13},{... | collective-permute-start | bytes 147464 | tf_op jit(solution)/shard_map/ppermute | solution.py:23
  64.5 3.9 %collective-permute-start.17 = (f32[2,3,16,128]{3,2,1,0:T(8,128)S(1)}, f32[2,3,16,128]{3,2,1,0:T(8,128)S(1)}, u32[]{:S(2)}, u32[]{:S(2)}) collective-permute-start(f32[2,3,16,128]{3,2,1,0:T(8,128)S(1)} %pad_maximum_fusion.53), channel_id=1, source_target_pairs={{1,0},{2,1},{3,2},{5,4},{6,5},{7,6},{9,8},{10,9},{11,10},{13,12},{... | collective-permute-start | bytes 147464 | tf_op jit(solution)/shard_map/ppermute | solution.py:23
  68.5 1.9 %collective-permute-start.12 = (f32[4,16,128]{2,1,0:T(8,128)S(1)}, f32[4,16,128]{2,1,0:T(8,128)S(1)}, u32[]{:S(2)}, u32[]{:S(2)}) collective-permute-start(f32[4,16,128]{2,1,0:T(8,128)S(1)} %get-tuple-element.278), channel_id=1, source_target_pairs={{1,0},{2,1},{3,2},{5,4},{6,5},{7,6},{9,8},{10,9},{11,10},{13,12},{... | collective-permute-start | bytes 98312 | tf_op jit(solution)/shard_map/ppermute | solution.py:23
  70.6 3.9 %collective-permute-done.12 = f32[4,16,128]{2,1,0:T(8,128)S(1)} collective-permute-done((f32[4,16,128]{2,1,0:T(8,128)S(1)}, f32[4,16,128]{2,1,0:T(8,128)S(1)}, u32[]{:S(2)}, u32[]{:S(2)}) %collective-permute-start.12) | collective-permute-done | bytes 32800 | tf_op jit(solution)/shard_map/ppermute | solution.py:23
  74.7 1.3 collective-permute-start.18
  76.0 1.3 collective-permute-start.19
  77.3 5.4 %collective-permute-start.13 = (f32[4,16,128]{2,1,0:T(8,128)S(1)}, f32[4,16,128]{2,1,0:T(8,128)S(1)}, u32[]{:S(2)}, u32[]{:S(2)}) collective-permute-start(f32[4,16,128]{2,1,0:T(8,128)S(1)} %pad_maximum_fusion.58), channel_id=1, source_target_pairs={{0,2},{1,3},{4,6},{5,7},{8,10},{9,11},{12,14},{13,15},{16,18},{17,... | collective-permute-start | bytes 98312 | tf_op jit(solution)/shard_map/ppermute | solution.py:23
  82.8 1.3 collective-permute-start.15
  84.4 5.1 %collective-permute-done.15 = f32[4,16,128]{2,1,0:T(8,128)S(1)} collective-permute-done((f32[4,16,128]{2,1,0:T(8,128)S(1)}, f32[4,16,128]{2,1,0:T(8,128)S(1)}, u32[]{:S(2)}, u32[]{:S(2)}) %collective-permute-start.15) | collective-permute-done | bytes 32800 | tf_op jit(solution)/shard_map/ppermute | solution.py:23
  90.4 1.6 collective-permute-start.21
  94.1 3.7 %collective-permute-done.20 = f32[3,16,1,128]{3,1,2,0:T(8,128)S(1)} collective-permute-done((f32[3,16,1,128]{3,1,2,0:T(8,128)S(1)}, f32[3,16,1,128]{3,1,2,0:T(8,128)S(1)}, u32[]{:S(2)}, u32[]{:S(2)}) %collective-permute-start.20) | collective-permute-done | bytes 24608 | tf_op jit(solution)/shard_map/ppermute | solution.py:14
  98.5 1.9 %collective-permute-start.23 = (f32[3,16,18,1]{2,1,3,0:T(8,128)S(1)}, f32[3,16,18,1]{2,1,3,0:T(8,128)S(1)}, u32[]{:S(2)}, u32[]{:S(2)}) collective-permute-start(f32[3,16,18,1]{2,1,3,0:T(8,128)S(1)} %copy.343), channel_id=1, source_target_pairs={{4,0},{8,4},{12,8},{5,1},{9,5},{13,9},{6,2},{10,6},{14,10},{7,3},{... | collective-permute-start | bytes 10376 | tf_op jit(solution)/shard_map/ppermute | solution.py:15
  100.8 2.4 %collective-permute-start.22 = (f32[3,16,18,1]{2,1,3,0:T(8,128)S(1)}, f32[3,16,18,1]{2,1,3,0:T(8,128)}, u32[]{:S(2)}, u32[]{:S(2)}) collective-permute-start(f32[3,16,18,1]{2,1,3,0:T(8,128)S(1)} %copy.340), channel_id=1, source_target_pairs={{0,4},{4,8},{8,12},{1,5},{5,9},{9,13},{2,6},{6,10},{10,14},{3,7},{... | collective-permute-start | bytes 10376 | tf_op jit(solution)/shard_map/ppermute | solution.py:14
  103.7 2.3 %collective-permute-done.22 = f32[3,16,18,1]{2,1,3,0:T(8,128)} collective-permute-done((f32[3,16,18,1]{2,1,3,0:T(8,128)S(1)}, f32[3,16,18,1]{2,1,3,0:T(8,128)}, u32[]{:S(2)}, u32[]{:S(2)}) %collective-permute-start.22) | collective-permute-done | bytes 3488 | tf_op jit(solution)/shard_map/ppermute | solution.py:14
  108.1 2.2 %collective-permute-start.24 = (f32[3,1,18,130]{3,2,0,1:T(8,128)S(1)}, f32[3,1,18,130]{3,2,0,1:T(8,128)S(1)}, u32[]{:S(2)}, u32[]{:S(2)}) collective-permute-start(f32[3,1,18,130]{3,2,0,1:T(8,128)S(1)} %get-tuple-element.72), channel_id=1, source_target_pairs={{0,1},{1,2},{2,3},{4,5},{5,6},{6,7},{8,9},{9,10},{10,11},{12,13},{... | collective-permute-start | bytes 84248 | tf_op jit(solution)/shard_map/ppermute | solution.py:14
  110.3 3.9 %collective-permute-start.25 = (f32[3,1,18,130]{3,2,0,1:T(8,128)S(1)}, f32[3,1,18,130]{3,2,0,1:T(8,128)S(1)}, u32[]{:S(2)}, u32[]{:S(2)}) collective-permute-start(f32[3,1,18,130]{3,2,0,1:T(8,128)S(1)} %get-tuple-element.73), channel_id=1, source_target_pairs={{1,0},{2,1},{3,2},{5,4},{6,5},{7,6},{9,8},{10,9},{11,10},{13,12},{... | collective-permute-start | bytes 84248 | tf_op jit(solution)/shard_map/ppermute | solution.py:15
  114.7 1.8 %collective-permute-done.25 = f32[3,1,18,130]{3,2,0,1:T(8,128)S(1)} collective-permute-done((f32[3,1,18,130]{3,2,0,1:T(8,128)S(1)}, f32[3,1,18,130]{3,2,0,1:T(8,128)S(1)}, u32[]{:S(2)}, u32[]{:S(2)}) %collective-permute-start.25) | collective-permute-done | bytes 28112 | tf_op jit(solution)/shard_map/ppermute | solution.py:15
  120.0 1.9 %collective-permute-start.26 = (f32[2,3,16,128]{3,2,1,0:T(8,128)S(1)}, f32[2,3,16,128]{3,2,1,0:T(8,128)S(1)}, u32[]{:S(2)}, u32[]{:S(2)}) collective-permute-start(f32[2,3,16,128]{3,2,1,0:T(8,128)S(1)} %pad_maximum_fusion.54), channel_id=1, source_target_pairs={{0,1},{1,2},{2,3},{4,5},{5,6},{6,7},{8,9},{9,10},{10,11},{12,13},{... | collective-permute-start | bytes 147464 | tf_op jit(solution)/shard_map/ppermute | solution.py:23
  122.0 3.9 %collective-permute-start.27 = (f32[2,3,16,128]{3,2,1,0:T(8,128)S(1)}, f32[2,3,16,128]{3,2,1,0:T(8,128)S(1)}, u32[]{:S(2)}, u32[]{:S(2)}) collective-permute-start(f32[2,3,16,128]{3,2,1,0:T(8,128)S(1)} %pad_maximum_fusion.54), channel_id=1, source_target_pairs={{1,0},{2,1},{3,2},{5,4},{6,5},{7,6},{9,8},{10,9},{11,10},{13,12},{... | collective-permute-start | bytes 147464 | tf_op jit(solution)/shard_map/ppermute | solution.py:23
  126.1 1.9 %collective-permute-done.27 = f32[2,3,16,128]{3,2,1,0:T(8,128)S(1)} collective-permute-done((f32[2,3,16,128]{3,2,1,0:T(8,128)S(1)}, f32[2,3,16,128]{3,2,1,0:T(8,128)S(1)}, u32[]{:S(2)}, u32[]{:S(2)}) %collective-permute-start.27) | collective-permute-done | bytes 49184 | tf_op jit(solution)/shard_map/ppermute | solution.py:23
  128.0 1.3 collective-permute-start.28
  129.3 1.3 collective-permute-start.29
  131.1 5.1 %collective-permute-done.29 = f32[2,3,16,128]{3,2,1,0:T(8,128)S(1)} collective-permute-done((f32[2,3,16,128]{3,2,1,0:T(8,128)S(1)}, f32[2,3,16,128]{3,2,1,0:T(8,128)S(1)}, u32[]{:S(2)}, u32[]{:S(2)}) %collective-permute-start.29) | collective-permute-done | bytes 49184 | tf_op jit(solution)/shard_map/ppermute | solution.py:23
  136.6 1.6 collective-permute-start.31
  139.8 4.2 %collective-permute-done.30 = f32[3,16,1,128]{3,1,2,0:T(8,128)S(1)} collective-permute-done((f32[3,16,1,128]{3,1,2,0:T(8,128)S(1)}, f32[3,16,1,128]{3,1,2,0:T(8,128)S(1)}, u32[]{:S(2)}, u32[]{:S(2)}) %collective-permute-start.30) | collective-permute-done | bytes 24608 | tf_op jit(solution)/shard_map/ppermute | solution.py:14
  144.7 1.9 %collective-permute-start.33 = (f32[3,16,18,1]{2,1,3,0:T(8,128)S(1)}, f32[3,16,18,1]{2,1,3,0:T(8,128)S(1)}, u32[]{:S(2)}, u32[]{:S(2)}) collective-permute-start(f32[3,16,18,1]{2,1,3,0:T(8,128)S(1)} %copy.360), channel_id=1, source_target_pairs={{4,0},{8,4},{12,8},{5,1},{9,5},{13,9},{6,2},{10,6},{14,10},{7,3},{... | collective-permute-start | bytes 10376 | tf_op jit(solution)/shard_map/ppermute | solution.py:15
  147.0 2.5 %collective-permute-start.32 = (f32[3,16,18,1]{2,1,3,0:T(8,128)S(1)}, f32[3,16,18,1]{2,1,3,0:T(8,128)S(1)}, u32[]{:S(2)}, u32[]{:S(2)}) collective-permute-start(f32[3,16,18,1]{2,1,3,0:T(8,128)S(1)} %copy.359), channel_id=1, source_target_pairs={{0,4},{4,8},{8,12},{1,5},{5,9},{9,13},{2,6},{6,10},{10,14},{3,7},{... | collective-permute-start | bytes 10376 | tf_op jit(solution)/shard_map/ppermute | solution.py:14
  149.9 2.3 %collective-permute-done.32 = f32[3,16,18,1]{2,1,3,0:T(8,128)S(1)} collective-permute-done((f32[3,16,18,1]{2,1,3,0:T(8,128)S(1)}, f32[3,16,18,1]{2,1,3,0:T(8,128)S(1)}, u32[]{:S(2)}, u32[]{:S(2)}) %collective-permute-start.32) | collective-permute-done | bytes 3488 | tf_op jit(solution)/shard_map/ppermute | solution.py:14
  153.3 4.1 %collective-permute-start.35 = (f32[3,1,18,130]{3,1,2,0:T(1,128)S(1)}, f32[3,1,18,130]{3,1,2,0:T(1,128)S(1)}, u32[]{:S(2)}, u32[]{:S(2)}) collective-permute-start(f32[3,1,18,130]{3,1,2,0:T(1,128)S(1)} %get-tuple-element.75), channel_id=1, source_target_pairs={{1,0},{2,1},{3,2},{5,4},{6,5},{7,6},{9,8},{10,9},{11,10},{13,12},{... | collective-permute-start | bytes 84248 | tf_op jit(solution)/shard_map/ppermute | solution.py:15
  157.4 1.9 %collective-permute-start.34 = (f32[3,1,18,130]{3,1,2,0:T(1,128)S(1)}, f32[3,1,18,130]{3,1,2,0:T(1,128)S(1)}, u32[]{:S(2)}, u32[]{:S(2)}) collective-permute-start(f32[3,1,18,130]{3,1,2,0:T(1,128)S(1)} %get-tuple-element.74), channel_id=1, source_target_pairs={{0,1},{1,2},{2,3},{4,5},{5,6},{6,7},{8,9},{9,10},{10,11},{12,13},{... | collective-permute-start | bytes 84248 | tf_op jit(solution)/shard_map/ppermute | solution.py:14
  160.6 2.9 %collective-permute-done.34 = f32[3,1,18,130]{3,1,2,0:T(1,128)S(1)} collective-permute-done((f32[3,1,18,130]{3,1,2,0:T(1,128)S(1)}, f32[3,1,18,130]{3,1,2,0:T(1,128)S(1)}, u32[]{:S(2)}, u32[]{:S(2)}) %collective-permute-start.34) | collective-permute-done | bytes 28112 | tf_op jit(solution)/shard_map/ppermute | solution.py:14
  (353 shorter events, 30.8 us)
Async XLA Ops:
  4.5 3.9 %collective-permute-start.1 = (f32[3,16,1,128]{3,1,2,0:T(8,128)S(1)}, f32[3,16,1,128]{3,1,2,0:T(8,128)S(1)}, u32[]{:S(2)}, u32[]{:S(2)}) collective-permute-start(f32[3,16,1,128]{3,1,2,0:T(8,128)S(1)} %get-tuple-element.127), channel_id=1, source_target_pairs={{16,0},{17,1},{18,2},{19,3},{20,4},{21,5},{22,6},{23,7},{24,8},{25... | collective-permute-start | bytes 73736 | tf_op jit(solution)/shard_map/ppermute | solution.py:15
  7.0 5.7 %collective-permute-start = (f32[3,16,1,128]{3,1,2,0:T(8,128)S(1)}, f32[3,16,1,128]{3,1,2,0:T(8,128)S(1)}, u32[]{:S(2)}, u32[]{:S(2)}) collective-permute-start(f32[3,16,1,128]{3,1,2,0:T(8,128)S(1)} %get-tuple-element.126), channel_id=1, source_target_pairs={{0,16},{1,17},{2,18},{3,19},{4,20},{5,21},{6,22},{7,23},{8,24},{9,... | collective-permute-start | bytes 73736 | tf_op jit(solution)/shard_map/ppermute | solution.py:14
  13.3 4.9 %collective-permute-start.3 = (f32[3,16,18,1]{2,1,3,0:T(8,128)S(1)}, f32[3,16,18,1]{2,1,3,0:T(8,128)S(1)}, u32[]{:S(2)}, u32[]{:S(2)}) collective-permute-start(f32[3,16,18,1]{2,1,3,0:T(8,128)S(1)} %copy.372), channel_id=1, source_target_pairs={{4,0},{8,4},{12,8},{5,1},{9,5},{13,9},{6,2},{10,6},{14,10},{7,3},{... | collective-permute-start | bytes 10376 | tf_op jit(solution)/shard_map/ppermute | solution.py:15
  15.7 5.1 %collective-permute-start.2 = (f32[3,16,18,1]{2,1,3,0:T(8,128)S(1)}, f32[3,16,18,1]{2,1,3,0:T(8,128)S(1)}, u32[]{:S(2)}, u32[]{:S(2)}) collective-permute-start(f32[3,16,18,1]{2,1,3,0:T(8,128)S(1)} %copy.371), channel_id=1, source_target_pairs={{0,4},{4,8},{8,12},{1,5},{5,9},{9,13},{2,6},{6,10},{10,14},{3,7},{... | collective-permute-start | bytes 10376 | tf_op jit(solution)/shard_map/ppermute | solution.py:14
  21.7 6.0 %collective-permute-start.4 = (f32[3,1,18,130]{3,1,2,0:T(1,128)S(1)}, f32[3,1,18,130]{3,1,2,0:T(1,128)S(1)}, u32[]{:S(2)}, u32[]{:S(2)}) collective-permute-start(f32[3,1,18,130]{3,1,2,0:T(1,128)S(1)} %get-tuple-element.80), channel_id=1, source_target_pairs={{0,1},{1,2},{2,3},{4,5},{5,6},{6,7},{8,9},{9,10},{10,11},{12,13},{... | collective-permute-start | bytes 84248 | tf_op jit(solution)/shard_map/ppermute | solution.py:14
  25.3 6.0 %collective-permute-start.5 = (f32[3,1,18,130]{3,1,2,0:T(1,128)S(1)}, f32[3,1,18,130]{3,1,2,0:T(1,128)S(1)}, u32[]{:S(2)}, u32[]{:S(2)}) collective-permute-start(f32[3,1,18,130]{3,1,2,0:T(1,128)S(1)} %get-tuple-element.79), channel_id=1, source_target_pairs={{1,0},{2,1},{3,2},{5,4},{6,5},{7,6},{9,8},{10,9},{11,10},{13,12},{... | collective-permute-start | bytes 84248 | tf_op jit(solution)/shard_map/ppermute | solution.py:15
  33.5 69.7 %copy-start = (f32[16,16,128]{2,1,0:T(8,128)}, f32[16,16,128]{2,1,0:T(8,128)S(1)}, u32[]{:S(2)}) copy-start(f32[16,16,128]{2,1,0:T(8,128)S(1)} %get-tuple-element.289) | copy-start | bytes 393220
  35.8 34.7 %copy-start.53 = (f32[16,128]{1,0:T(8,128)}, f32[16,128]{1,0:T(8,128)S(1)}, u32[]{:S(2)}) copy-start(f32[16,128]{1,0:T(8,128)S(1)} %get-tuple-element.141) | copy-start | bytes 24580
  35.8 6.0 %collective-permute-start.8 = (f32[4,16,128]{2,1,0:T(8,128)S(1)}, f32[4,16,128]{2,1,0:T(8,128)S(1)}, u32[]{:S(2)}, u32[]{:S(2)}) collective-permute-start(f32[4,16,128]{2,1,0:T(8,128)S(1)} %pad_maximum_fusion.55), channel_id=1, source_target_pairs={{1,0},{2,1},{3,2},{5,4},{6,5},{7,6},{9,8},{10,9},{11,10},{13,12},{... | collective-permute-start | bytes 98312 | tf_op jit(solution)/shard_map/ppermute | solution.py:23
  38.2 5.8 %collective-permute-start.6 = (f32[4,16,128]{2,1,0:T(8,128)S(1)}, f32[4,16,128]{2,1,0:T(8,128)S(1)}, u32[]{:S(2)}, u32[]{:S(2)}) collective-permute-start(f32[4,16,128]{2,1,0:T(8,128)S(1)} %pad_maximum_fusion.55), channel_id=1, source_target_pairs={{0,1},{1,2},{2,3},{4,5},{5,6},{6,7},{8,9},{9,10},{10,11},{12,13},{... | collective-permute-start | bytes 98312 | tf_op jit(solution)/shard_map/ppermute | solution.py:23
  41.7 48.6 %copy-start.8 = (f32[14,16,128]{2,1,0:T(8,128)}, f32[14,16,128]{2,1,0:T(8,128)S(1)}, u32[]{:S(2)}) copy-start(f32[14,16,128]{2,1,0:T(8,128)S(1)} %get-tuple-element.91) | copy-start | bytes 344068
  44.0 26.5 %copy-start.31 = (f32[16,128]{1,0:T(8,128)}, f32[16,128]{1,0:T(8,128)S(1)}, u32[]{:S(2)}) copy-start(f32[16,128]{1,0:T(8,128)S(1)} %get-tuple-element.143) | copy-start | bytes 24580
  44.1 11.7 %collective-permute-start.9 = (f32[4,16,128]{2,1,0:T(8,128)S(1)}, f32[4,16,128]{2,1,0:T(8,128)S(1)}, u32[]{:S(2)}, u32[]{:S(2)}) collective-permute-start(f32[4,16,128]{2,1,0:T(8,128)S(1)} %get-tuple-element.277), channel_id=1, source_target_pairs={{1,0},{2,1},{3,2},{5,4},{6,5},{7,6},{9,8},{10,9},{11,10},{13,12},{... | collective-permute-start | bytes 98312 | tf_op jit(solution)/shard_map/ppermute | solution.py:23
  46.0 24.4 %collective-permute-start.10 = (f32[4,16,128]{2,1,0:T(8,128)S(1)}, f32[4,16,128]{2,1,0:T(8,128)S(1)}, u32[]{:S(2)}, u32[]{:S(2)}) collective-permute-start(f32[4,16,128]{2,1,0:T(8,128)S(1)} %get-tuple-element.277), channel_id=1, source_target_pairs={{0,1},{1,2},{2,3},{4,5},{5,6},{6,7},{8,9},{9,10},{10,11},{12,13},{... | collective-permute-start | bytes 98312 | tf_op jit(solution)/shard_map/ppermute | solution.py:23
  49.9 5.8 %collective-permute-start.7 = (f32[4,16,128]{2,1,0:T(8,128)S(1)}, f32[4,16,128]{2,1,0:T(8,128)S(1)}, u32[]{:S(2)}, u32[]{:S(2)}) collective-permute-start(f32[4,16,128]{2,1,0:T(8,128)S(1)} %get-tuple-element.278), channel_id=1, source_target_pairs={{0,1},{1,2},{2,3},{4,5},{5,6},{6,7},{8,9},{9,10},{10,11},{12,13},{... | collective-permute-start | bytes 98312 | tf_op jit(solution)/shard_map/ppermute | solution.py:23
  55.8 33.8 %copy-start.49 = (f32[16,128]{1,0:T(8,128)}, f32[16,128]{1,0:T(8,128)S(1)}, u32[]{:S(2)}) copy-start(f32[16,128]{1,0:T(8,128)S(1)} %get-tuple-element.261) | copy-start | bytes 24580
  55.8 12.6 %collective-permute-start.14 = (f32[4,16,128]{2,1,0:T(8,128)S(1)}, f32[4,16,128]{2,1,0:T(8,128)S(1)}, u32[]{:S(2)}, u32[]{:S(2)}) collective-permute-start(f32[4,16,128]{2,1,0:T(8,128)S(1)} %fusion.62), channel_id=1, source_target_pairs={{2,0},{3,1},{6,4},{7,5},{10,8},{11,9},{14,12},{15,13},{18,16},{19,... | collective-permute-start | bytes 98312 | tf_op jit(solution)/shard_map/ppermute | solution.py:23
  57.1 13.3 %collective-permute-start.11 = (f32[4,16,128]{2,1,0:T(8,128)S(1)}, f32[4,16,128]{2,1,0:T(8,128)S(1)}, u32[]{:S(2)}, u32[]{:S(2)}) collective-permute-start(f32[4,16,128]{2,1,0:T(8,128)S(1)} %fusion.62), channel_id=1, source_target_pairs={{0,2},{1,3},{4,6},{5,7},{8,10},{9,11},{12,14},{13,15},{16,18},{17,... | collective-permute-start | bytes 98312 | tf_op jit(solution)/shard_map/ppermute | solution.py:23
  62.6 7.9 %collective-permute-start.16 = (f32[2,3,16,128]{3,2,1,0:T(8,128)S(1)}, f32[2,3,16,128]{3,2,1,0:T(8,128)S(1)}, u32[]{:S(2)}, u32[]{:S(2)}) collective-permute-start(f32[2,3,16,128]{3,2,1,0:T(8,128)S(1)} %pad_maximum_fusion.53), channel_id=1, source_target_pairs={{0,1},{1,2},{2,3},{4,5},{5,6},{6,7},{8,9},{9,10},{10,11},{12,13},{... | collective-permute-start | bytes 147464 | tf_op jit(solution)/shard_map/ppermute | solution.py:23
  64.5 10.1 %collective-permute-start.17 = (f32[2,3,16,128]{3,2,1,0:T(8,128)S(1)}, f32[2,3,16,128]{3,2,1,0:T(8,128)S(1)}, u32[]{:S(2)}, u32[]{:S(2)}) collective-permute-start(f32[2,3,16,128]{3,2,1,0:T(8,128)S(1)} %pad_maximum_fusion.53), channel_id=1, source_target_pairs={{1,0},{2,1},{3,2},{5,4},{6,5},{7,6},{9,8},{10,9},{11,10},{13,12},{... | collective-permute-start | bytes 147464 | tf_op jit(solution)/shard_map/ppermute | solution.py:23
  68.5 6.1 %collective-permute-start.12 = (f32[4,16,128]{2,1,0:T(8,128)S(1)}, f32[4,16,128]{2,1,0:T(8,128)S(1)}, u32[]{:S(2)}, u32[]{:S(2)}) collective-permute-start(f32[4,16,128]{2,1,0:T(8,128)S(1)} %get-tuple-element.278), channel_id=1, source_target_pairs={{1,0},{2,1},{3,2},{5,4},{6,5},{7,6},{9,8},{10,9},{11,10},{13,12},{... | collective-permute-start | bytes 98312 | tf_op jit(solution)/shard_map/ppermute | solution.py:23
  70.5 19.2 %copy-start.37 = (f32[16,128]{1,0:T(8,128)}, f32[16,128]{1,0:T(8,128)S(1)}, u32[]{:S(2)}) copy-start(f32[16,128]{1,0:T(8,128)S(1)} %get-tuple-element.255) | copy-start | bytes 24580
  74.7 15.0 %collective-permute-start.18 = (f32[2,3,16,128]{3,2,1,0:T(8,128)S(1)}, f32[2,3,16,128]{3,2,1,0:T(8,128)S(1)}, u32[]{:S(2)}, u32[]{:S(2)}) collective-permute-start(f32[2,3,16,128]{3,2,1,0:T(8,128)S(1)} %fusion.58), channel_id=1, source_target_pairs={{0,2},{1,3},{4,6},{5,7},{8,10},{9,11},{12,14},{13,15},{16,18},{17,... | collective-permute-start | bytes 147464 | tf_op jit(solution)/shard_map/ppermute | solution.py:23
  76.0 13.7 %collective-permute-start.19 = (f32[2,3,16,128]{3,2,1,0:T(8,128)S(1)}, f32[2,3,16,128]{3,2,1,0:T(8,128)S(1)}, u32[]{:S(2)}, u32[]{:S(2)}) collective-permute-start(f32[2,3,16,128]{3,2,1,0:T(8,128)S(1)} %fusion.58), channel_id=1, source_target_pairs={{2,0},{3,1},{6,4},{7,5},{10,8},{11,9},{14,12},{15,13},{18,16},{19,... | collective-permute-start | bytes 147464 | tf_op jit(solution)/shard_map/ppermute | solution.py:23
  77.3 7.0 %collective-permute-start.13 = (f32[4,16,128]{2,1,0:T(8,128)S(1)}, f32[4,16,128]{2,1,0:T(8,128)S(1)}, u32[]{:S(2)}, u32[]{:S(2)}) collective-permute-start(f32[4,16,128]{2,1,0:T(8,128)S(1)} %pad_maximum_fusion.58), channel_id=1, source_target_pairs={{0,2},{1,3},{4,6},{5,7},{8,10},{9,11},{12,14},{13,15},{16,18},{17,... | collective-permute-start | bytes 98312 | tf_op jit(solution)/shard_map/ppermute | solution.py:23
  82.8 6.7 %collective-permute-start.15 = (f32[4,16,128]{2,1,0:T(8,128)S(1)}, f32[4,16,128]{2,1,0:T(8,128)S(1)}, u32[]{:S(2)}, u32[]{:S(2)}) collective-permute-start(f32[4,16,128]{2,1,0:T(8,128)S(1)} %pad_maximum_fusion.59), channel_id=1, source_target_pairs={{2,0},{3,1},{6,4},{7,5},{10,8},{11,9},{14,12},{15,13},{18,16},{19,... | collective-permute-start | bytes 98312 | tf_op jit(solution)/shard_map/ppermute | solution.py:23
  90.4 3.6 %collective-permute-start.21 = (f32[3,16,1,128]{3,1,2,0:T(8,128)S(1)}, f32[3,16,1,128]{3,1,2,0:T(8,128)S(1)}, u32[]{:S(2)}, u32[]{:S(2)}) collective-permute-start(f32[3,16,1,128]{3,1,2,0:T(8,128)S(1)} %copy.335), channel_id=1, source_target_pairs={{16,0},{17,1},{18,2},{19,3},{20,4},{21,5},{22,6},{23,7},{24,8},{25... | collective-permute-start | bytes 73736 | tf_op jit(solution)/shard_map/ppermute | solution.py:15
  92.0 5.7 %collective-permute-start.20 = (f32[3,16,1,128]{3,1,2,0:T(8,128)S(1)}, f32[3,16,1,128]{3,1,2,0:T(8,128)S(1)}, u32[]{:S(2)}, u32[]{:S(2)}) collective-permute-start(f32[3,16,1,128]{3,1,2,0:T(8,128)S(1)} %copy.332), channel_id=1, source_target_pairs={{0,16},{1,17},{2,18},{3,19},{4,20},{5,21},{6,22},{7,23},{8,24},{9,... | collective-permute-start | bytes 73736 | tf_op jit(solution)/shard_map/ppermute | solution.py:14
  98.5 4.8 %collective-permute-start.23 = (f32[3,16,18,1]{2,1,3,0:T(8,128)S(1)}, f32[3,16,18,1]{2,1,3,0:T(8,128)S(1)}, u32[]{:S(2)}, u32[]{:S(2)}) collective-permute-start(f32[3,16,18,1]{2,1,3,0:T(8,128)S(1)} %copy.343), channel_id=1, source_target_pairs={{4,0},{8,4},{12,8},{5,1},{9,5},{13,9},{6,2},{10,6},{14,10},{7,3},{... | collective-permute-start | bytes 10376 | tf_op jit(solution)/shard_map/ppermute | solution.py:15
  100.8 5.2 %collective-permute-start.22 = (f32[3,16,18,1]{2,1,3,0:T(8,128)S(1)}, f32[3,16,18,1]{2,1,3,0:T(8,128)}, u32[]{:S(2)}, u32[]{:S(2)}) collective-permute-start(f32[3,16,18,1]{2,1,3,0:T(8,128)S(1)} %copy.340), channel_id=1, source_target_pairs={{0,4},{4,8},{8,12},{1,5},{5,9},{9,13},{2,6},{6,10},{10,14},{3,7},{... | collective-permute-start | bytes 10376 | tf_op jit(solution)/shard_map/ppermute | solution.py:14
  108.1 6.6 %collective-permute-start.24 = (f32[3,1,18,130]{3,2,0,1:T(8,128)S(1)}, f32[3,1,18,130]{3,2,0,1:T(8,128)S(1)}, u32[]{:S(2)}, u32[]{:S(2)}) collective-permute-start(f32[3,1,18,130]{3,2,0,1:T(8,128)S(1)} %get-tuple-element.72), channel_id=1, source_target_pairs={{0,1},{1,2},{2,3},{4,5},{5,6},{6,7},{8,9},{9,10},{10,11},{12,13},{... | collective-permute-start | bytes 84248 | tf_op jit(solution)/shard_map/ppermute | solution.py:14
  110.3 6.2 %collective-permute-start.25 = (f32[3,1,18,130]{3,2,0,1:T(8,128)S(1)}, f32[3,1,18,130]{3,2,0,1:T(8,128)S(1)}, u32[]{:S(2)}, u32[]{:S(2)}) collective-permute-start(f32[3,1,18,130]{3,2,0,1:T(8,128)S(1)} %get-tuple-element.73), channel_id=1, source_target_pairs={{1,0},{2,1},{3,2},{5,4},{6,5},{7,6},{9,8},{10,9},{11,10},{13,12},{... | collective-permute-start | bytes 84248 | tf_op jit(solution)/shard_map/ppermute | solution.py:15
  119.2 17.0 %copy-start.48 = (f32[16,128]{1,0:T(8,128)S(1)}, f32[16,128]{1,0:T(8,128)}, u32[]{:S(2)}) copy-start(f32[16,128]{1,0:T(8,128)} %copy-done.47) | copy-start | bytes 24580
  119.2 17.0 %copy-start.62 = (f32[16,128]{1,0:T(8,128)S(1)}, f32[16,128]{1,0:T(8,128)}, u32[]{:S(2)}) copy-start(f32[16,128]{1,0:T(8,128)} %copy-done.61) | copy-start | bytes 24580
  119.3 17.0 %copy-start.23 = (f32[16,128]{1,0:T(8,128)S(1)}, f32[16,128]{1,0:T(8,128)}, u32[]{:S(2)}) copy-start(f32[16,128]{1,0:T(8,128)} %copy-done.22) | copy-start | bytes 24580
  119.3 17.0 %copy-start.25 = (f32[16,128]{1,0:T(8,128)S(1)}, f32[16,128]{1,0:T(8,128)}, u32[]{:S(2)}) copy-start(f32[16,128]{1,0:T(8,128)} %copy-done.24) | copy-start | bytes 24580
  119.3 17.0 %copy-start.27 = (f32[16,128]{1,0:T(8,128)S(1)}, f32[16,128]{1,0:T(8,128)}, u32[]{:S(2)}) copy-start(f32[16,128]{1,0:T(8,128)} %copy-done.26) | copy-start | bytes 24580
  119.3 17.0 %copy-start.29 = (f32[16,128]{1,0:T(8,128)S(1)}, f32[16,128]{1,0:T(8,128)}, u32[]{:S(2)}) copy-start(f32[16,128]{1,0:T(8,128)} %copy-done.28) | copy-start | bytes 24580
  120.0 6.0 %collective-permute-start.26 = (f32[2,3,16,128]{3,2,1,0:T(8,128)S(1)}, f32[2,3,16,128]{3,2,1,0:T(8,128)S(1)}, u32[]{:S(2)}, u32[]{:S(2)}) collective-permute-start(f32[2,3,16,128]{3,2,1,0:T(8,128)S(1)} %pad_maximum_fusion.54), channel_id=1, source_target_pairs={{0,1},{1,2},{2,3},{4,5},{5,6},{6,7},{8,9},{9,10},{10,11},{12,13},{... | collective-permute-start | bytes 147464 | tf_op jit(solution)/shard_map/ppermute | solution.py:23
  122.0 6.0 %collective-permute-start.27 = (f32[2,3,16,128]{3,2,1,0:T(8,128)S(1)}, f32[2,3,16,128]{3,2,1,0:T(8,128)S(1)}, u32[]{:S(2)}, u32[]{:S(2)}) collective-permute-start(f32[2,3,16,128]{3,2,1,0:T(8,128)S(1)} %pad_maximum_fusion.54), channel_id=1, source_target_pairs={{1,0},{2,1},{3,2},{5,4},{6,5},{7,6},{9,8},{10,9},{11,10},{13,12},{... | collective-permute-start | bytes 147464 | tf_op jit(solution)/shard_map/ppermute | solution.py:23
  128.0 3.0 %collective-permute-start.28 = (f32[2,3,16,128]{3,2,1,0:T(8,128)S(1)}, f32[2,3,16,128]{3,2,1,0:T(8,128)S(1)}, u32[]{:S(2)}, u32[]{:S(2)}) collective-permute-start(f32[2,3,16,128]{3,2,1,0:T(8,128)S(1)} %fusion.60), channel_id=1, source_target_pairs={{0,2},{1,3},{4,6},{5,7},{8,10},{9,11},{12,14},{13,15},{16,18},{17,... | collective-permute-start | bytes 147464 | tf_op jit(solution)/shard_map/ppermute | solution.py:23
  129.3 6.9 %collective-permute-start.29 = (f32[2,3,16,128]{3,2,1,0:T(8,128)S(1)}, f32[2,3,16,128]{3,2,1,0:T(8,128)S(1)}, u32[]{:S(2)}, u32[]{:S(2)}) collective-permute-start(f32[2,3,16,128]{3,2,1,0:T(8,128)S(1)} %fusion.60), channel_id=1, source_target_pairs={{2,0},{3,1},{6,4},{7,5},{10,8},{11,9},{14,12},{15,13},{18,16},{19,... | collective-permute-start | bytes 147464 | tf_op jit(solution)/shard_map/ppermute | solution.py:23
  136.6 3.1 %collective-permute-start.31 = (f32[3,16,1,128]{3,1,2,0:T(8,128)S(1)}, f32[3,16,1,128]{3,1,2,0:T(8,128)S(1)}, u32[]{:S(2)}, u32[]{:S(2)}) collective-permute-start(f32[3,16,1,128]{3,1,2,0:T(8,128)S(1)} %get-tuple-element.114), channel_id=1, source_target_pairs={{16,0},{17,1},{18,2},{19,3},{20,4},{21,5},{22,6},{23,7},{24,8},{25... | collective-permute-start | bytes 73736 | tf_op jit(solution)/shard_map/ppermute | solution.py:15
  138.3 5.7 %collective-permute-start.30 = (f32[3,16,1,128]{3,1,2,0:T(8,128)S(1)}, f32[3,16,1,128]{3,1,2,0:T(8,128)S(1)}, u32[]{:S(2)}, u32[]{:S(2)}) collective-permute-start(f32[3,16,1,128]{3,1,2,0:T(8,128)S(1)} %get-tuple-element.113), channel_id=1, source_target_pairs={{0,16},{1,17},{2,18},{3,19},{4,20},{5,21},{6,22},{7,23},{8,24},{9,... | collective-permute-start | bytes 73736 | tf_op jit(solution)/shard_map/ppermute | solution.py:14
  144.7 4.9 %collective-permute-start.33 = (f32[3,16,18,1]{2,1,3,0:T(8,128)S(1)}, f32[3,16,18,1]{2,1,3,0:T(8,128)S(1)}, u32[]{:S(2)}, u32[]{:S(2)}) collective-permute-start(f32[3,16,18,1]{2,1,3,0:T(8,128)S(1)} %copy.360), channel_id=1, source_target_pairs={{4,0},{8,4},{12,8},{5,1},{9,5},{13,9},{6,2},{10,6},{14,10},{7,3},{... | collective-permute-start | bytes 10376 | tf_op jit(solution)/shard_map/ppermute | solution.py:15
  147.0 5.3 %collective-permute-start.32 = (f32[3,16,18,1]{2,1,3,0:T(8,128)S(1)}, f32[3,16,18,1]{2,1,3,0:T(8,128)S(1)}, u32[]{:S(2)}, u32[]{:S(2)}) collective-permute-start(f32[3,16,18,1]{2,1,3,0:T(8,128)S(1)} %copy.359), channel_id=1, source_target_pairs={{0,4},{4,8},{8,12},{1,5},{5,9},{9,13},{2,6},{6,10},{10,14},{3,7},{... | collective-permute-start | bytes 10376 | tf_op jit(solution)/shard_map/ppermute | solution.py:14
  153.3 7.3 %collective-permute-start.35 = (f32[3,1,18,130]{3,1,2,0:T(1,128)S(1)}, f32[3,1,18,130]{3,1,2,0:T(1,128)S(1)}, u32[]{:S(2)}, u32[]{:S(2)}) collective-permute-start(f32[3,1,18,130]{3,1,2,0:T(1,128)S(1)} %get-tuple-element.75), channel_id=1, source_target_pairs={{1,0},{2,1},{3,2},{5,4},{6,5},{7,6},{9,8},{10,9},{11,10},{13,12},{... | collective-permute-start | bytes 84248 | tf_op jit(solution)/shard_map/ppermute | solution.py:15
  157.4 6.0 %collective-permute-start.34 = (f32[3,1,18,130]{3,1,2,0:T(1,128)S(1)}, f32[3,1,18,130]{3,1,2,0:T(1,128)S(1)}, u32[]{:S(2)}, u32[]{:S(2)}) collective-permute-start(f32[3,1,18,130]{3,1,2,0:T(1,128)S(1)} %get-tuple-element.74), channel_id=1, source_target_pairs={{0,1},{1,2},{2,3},{4,5},{5,6},{6,7},{8,9},{9,10},{10,11},{12,13},{... | collective-permute-start | bytes 84248 | tf_op jit(solution)/shard_map/ppermute | solution.py:14
  (56 other events, 394.7 us)
where the time goes:
time: 167 us; the launch traced here: 165 us
  starting transfers between devices  87.9 us (53%)
  waiting for transfers between devices  48.5 us (29%)
  local copies, waits for them, and re-layouts  14.9 us (9%)
  other arithmetic  11.1 us (7%)
  between operations  2.99 us (2%)
    ppermute x18, starting transfers between devices, from_behind(): return lax.ppermute(block, axis, route)  47.4 us
    ppermute x9, waiting for transfers between devices, with_halo(): before = lax.ppermute(last, axis, up)  22 us
    ppermute x9, starting transfers between devices, with_halo(): after = lax.ppermute(leading, axis, down)  21.8 us
    ppermute x18, waiting for transfers between devices, from_behind(): return lax.ppermute(block, axis, route)  21.3 us
    ppermute x9, starting transfers between devices, with_halo(): before = lax.ppermute(last, axis, up)  18.7 us
    unnamed x148, local copies, waits for them, and re-layouts  5.39 us
    ppermute x9, waiting for transfers between devices, with_halo(): after = lax.ppermute(leading, axis, down)  5.2 us
  transfers between devices with their start and end apart: 36, of which 21 were waited for; matrix products, arithmetic and copies ran while one was open for 4% of the time, Pallas kernels for 0%

commit v1 on v0

v1 whole, which is shorter than its diff:
```python
import functools

import jax
import jax.numpy as jnp
from jax import lax
from jax.experimental import pallas as pl
from jax.experimental.pallas import tpu as pltpu
from jax.sharding import PartitionSpec as P


WIDE = 3
FIRST_COUNT = 11
SECOND_COUNT = 6


def moved(values, amount, axis):
    size = values.shape[axis]
    amount = amount % size
    if amount == 0:
        return values
    return pltpu.roll(values, amount, axis)


def flag(condition):
    return condition.astype(jnp.float32)


def pack_kernel(facies_ref, strip_ref, *row_refs):
    nz, nx, ny = facies_ref.shape
    lane = lax.broadcasted_iota(jnp.int32, (nx, ny), 1)
    strip = jnp.zeros((nx, ny), jnp.int32)
    for z in range(nz):
        strip = jnp.where(lane // 8 == z, moved(facies_ref[z], 8 * z + WIDE, 1), strip)
    strip_ref[...] = strip
    for z in range(nz):
        leading = facies_ref[z, 0:WIDE, :]
        last = facies_ref[z, nx - WIDE : nx, :]
        spot = slice(z * WIDE, (z + 1) * WIDE)
        if len(row_refs) == 1:
            row_refs[0][spot, :] = jnp.where(lax.axis_index("gx") == 0, last, leading)
        else:
            row_refs[0][spot, :] = leading
            row_refs[1][spot, :] = last


def face(a, b):
    product = a * b
    total = a + b
    harmonic = 2.0 * product / total
    inside = product > 0.0
    link = jnp.where(inside, harmonic, 0.0)
    flow = jnp.where(inside, harmonic, total)
    tau = jnp.where(inside, harmonic, 2.0 * total)
    return link, flow, tau


def message_rows(nx, count, halo):
    side_rows = -(-count * 2 * halo // 8) * 8
    return count * nx + nx + 8 + side_rows


def write_message(ref, slabs, nx, ny, halo):
    count = len(slabs)
    row = lax.broadcasted_iota(jnp.int32, (8, ny), 0)
    lane = lax.broadcasted_iota(jnp.int32, (nx + 8, ny), 1)
    per_tile = 8 // (2 * halo)
    strip = jnp.zeros((nx + 8, ny), jnp.float32)
    tile = jnp.zeros((8, ny), jnp.float32)
    base = count * nx + nx + 8
    for q, slab in enumerate(slabs):
        ref[q * nx : (q + 1) * nx, :] = slab[:nx, :ny]
        strip = jnp.where(lane // (2 * halo) == q, moved(slab[:, ny:], 2 * halo * q + halo, 1), strip)
        part = q % per_tile
        tile = jnp.where(
            row // (2 * halo) == part, moved(slab[nx:, :ny], 2 * halo * part + halo, 0), tile
        )
        if part == per_tile - 1 or q == count - 1:
            start = base + (q // per_tile) * 8
            ref[start : start + 8, :] = tile
    ref[count * nx : count * nx + nx + 8, :] = strip


def read_message(ref, q, count, nx, ny, halo):
    per_tile = 8 // (2 * halo)
    part = q % per_tile
    start = count * nx + nx + 8 + (q // per_tile) * 8
    tile = moved(ref[start : start + 8, :], -(2 * halo * part + halo), 0)
    strip = moved(ref[count * nx : count * nx + nx + 8, :], -(2 * halo * q + halo), 1)
    main = jnp.concatenate([ref[q * nx : (q + 1) * nx, :], tile], axis=0)
    return jnp.concatenate([main, strip], axis=1)


def cut_after(breaks_ref, layer):
    spot = jnp.clip(layer, 0, breaks_ref.shape[0] - 1)
    return breaks_ref[spot].astype(jnp.float32)


def eliminate_kernel(
    table_ref, breaks_ref, facies_ref, row_low, row_high, y_low, y_high,
    low_low, low_high, high_low, high_high,
    message_ref, lx_ref, ly_ref, lz_ref, source_ref, centre_ref, d_ref, e_ref, inverse_ref,
    side_ref,
):
    nz, nx, ny = facies_ref.shape
    labels = table_ref.shape[1]
    outside = labels
    at_x, at_y, at_z = lax.axis_index("gx"), lax.axis_index("gy"), lax.axis_index("gz")
    has_x_low, has_x_high = at_x > 0, at_x < lax.axis_size("gx") - 1
    has_y_low, has_y_high = at_y > 0, at_y < lax.axis_size("gy") - 1

    lane8 = lax.broadcasted_iota(jnp.int32, (8, ny), 1)
    row8 = lax.broadcasted_iota(jnp.int32, (8, ny), 0)
    tables = []
    for q in range(3):
        table = jnp.zeros((8, ny), jnp.float32)
        for label in range(labels):
            table = jnp.where(lane8 == label, table_ref[q, label], table)
        tables.append(table)

    side_ref[...] = jnp.full(side_ref.shape, outside, jnp.int32)
    for z in range(nz):
        spot = slice(z * WIDE, (z + 1) * WIDE)
        side_ref[z, 0:WIDE, :] = jnp.where(has_x_high, row_high[spot, :], outside)
        side_ref[z, 8 - WIDE : 8, :] = jnp.where(has_x_low, row_low[spot, :], outside)

    def corner(high_ref, low_ref):
        high = jnp.where(has_x_high, high_ref[0:8, :], outside)
        low = jnp.where(has_x_low, low_ref[nx - 8 : nx, :], outside)
        middle = jnp.where(row8 >= 8 - WIDE, low, outside)
        return jnp.where(row8 < WIDE, high, middle)

    before = jnp.concatenate([y_low[...], corner(low_high, low_low)], axis=0)
    after = jnp.concatenate([y_high[...], corner(high_high, high_low)], axis=0)
    lane = lax.broadcasted_iota(jnp.int32, (nx + 8, ny), 1)
    strip = jnp.where(
        lane % 8 < WIDE,
        jnp.where(has_y_low, before, outside),
        jnp.where(has_y_high, after, outside),
    )
    near = (lane < WIDE) | (lane >= ny - WIDE)

    def lookup(table, index):
        rows = []
        for r in range(0, nx + 8, 8):
            columns = []
            for c in range(0, 2 * ny, ny):
                columns.append(
                    jnp.take_along_axis(table, index[r : r + 8, c : c + ny], axis=1)
                )
            rows.append(jnp.concatenate(columns, axis=1))
        return jnp.concatenate(rows, axis=0)

    def coefficients(z):
        body = jnp.concatenate([facies_ref[z], side_ref[z]], axis=0)
        beside = jnp.where(near, moved(strip, -(8 * z + WIDE), 1), outside)
        label = jnp.concatenate([body, beside], axis=1)
        return [lookup(table, label) for table in tables]

    def open_after(z):
        return 1.0 - cut_after(breaks_ref, at_z * nz + z)

    kz_now = kz_first = None
    link_below = None
    tau_below = flow_below = None
    state = None
    next_k = coefficients(0)
    for z in range(nz):
        kx, ky, kz = next_k
        link_x, flow_x, tau_x = face(kx, moved(kx, -1, 0))
        link_y, flow_y, tau_y = face(ky, moved(ky, -1, 1))
        lx_ref[z] = link_x
        ly_ref[z] = link_y
        centre = tau_x + moved(tau_x, 1, 0) + (tau_y + moved(tau_y, 1, 1))
        sources = [flow_x - moved(flow_x, 1, 0), flow_y - moved(flow_y, 1, 1)]
        source_z = jnp.zeros_like(centre)
        if z > 0:
            centre = centre + link_below
            source_z = source_z - link_below
        else:
            kz_first = kz
        if z < nz - 1:
            next_k = coefficients(z + 1)
            link_z = face(kz, next_k[2])[0]
            lz_ref[z] = link_z
            centre = centre + link_z
            source_z = source_z + link_z
        centre = jnp.where(kz > 0.0, centre, 1.0)
        sources.append(source_z)
        for f in range(3):
            source_ref[f, z] = sources[f]
        centre_ref[z] = centre
        if z == 0:
            s_uu = centre
            g_u = list(sources)
            coupling = link_z * open_after(0)
        elif z < nz - 1:
            if z == 1:
                pivot = centre
                forward = list(sources)
                numerator = coupling
            else:
                pivot = centre - coupling * ratio
                forward = [sources[f] + coupling * value[f] for f in range(3)]
                numerator = coupling * spike
            inverse = 1.0 / pivot
            value = [forward[f] * inverse for f in range(3)]
            spike = numerator * inverse
            s_uu = s_uu - numerator * spike
            g_u = [g_u[f] + spike * forward[f] for f in range(3)]
            coupling = link_z * open_after(z)
            ratio = coupling * inverse
            inverse_ref[z] = inverse
            e_ref[z] = spike
            for f in range(3):
                d_ref[f, z] = value[f]
        else:
            s_vv = centre - coupling * ratio
            s_uv = -coupling * spike
            g_v = [sources[f] + coupling * value[f] for f in range(3)]
        link_below = link_z
    write_message(
        message_ref, [s_uu, s_uv, s_vv, kz_first, kz] + g_u + g_v, nx, ny, 2
    )


def stencil(f_slab, link_x, link_y):
    return (
        link_x * moved(f_slab, -1, 0)
        + moved(link_x * f_slab, 1, 0)
        + (link_y * moved(f_slab, -1, 1) + moved(link_y * f_slab, 1, 1))
    )


def middle_kernel(
    count, breaks_ref, *refs
):
    blocks = refs[:count]
    lx_ref, ly_ref, lz_ref, source_ref, d_ref, e_ref, inverse_ref = refs[count : count + 7]
    message_ref, d2_ref, factor_ref, end_ref, first_ref = refs[count + 7 :]
    nz = lx_ref.shape[0]
    nx, ny = lx_ref.shape[1] - 8, lx_ref.shape[2] // 2
    at_z = lax.axis_index("gz")

    def quantity(block, q):
        return read_message(blocks[block], q, FIRST_COUNT, nx, ny, 2)

    def triple(block, q):
        return [quantity(block, q + f) for f in range(3)]

    def open_after(layer):
        return 1.0 - cut_after(breaks_ref, layer)

    slots = []

    def keep(values):
        factor_ref[len(slots)] = values
        slots.append(None)

    def chain(below):
        near, far, sign = (8, 5, 1.0) if below else (5, 8, -1.0)
        near_s, far_s = (2, 0) if below else (0, 2)
        near_k, far_k = (4, 3) if below else (3, 4)
        carry = None
        for step in range(count - 1, 0, -1):
            block = step if below else count - step
            if carry is None:
                own_k = quantity(block, far_k)
                tau, flow = 2.0 * own_k, own_k
                pivot = quantity(block, far_s) + tau
                right = triple(block, far)
            else:
                pivot = quantity(block, far_s) + tau - coupling * carry[0]
                right = [a + carry[0] * b for a, b in zip(triple(block, far), carry[1])]
            right[2] = right[2] - sign * flow
            s_uv = quantity(block, 1)
            factor = s_uv / pivot
            keep(factor)
            if below:
                exists = at_z >= step
                layer = (at_z - step + 1) * nz - 1
            else:
                exists = at_z + step < count
                layer = (at_z + step) * nz - 1
            k_here = quantity(block, near_k) * flag(exists)
            k_next = quantity((step - 1 if below else (count - step + 1) % count), far_k)
            link, flow, tau = face(k_here, k_next)
            coupling = link * open_after(layer)
            next_pivot = quantity(block, near_s) + tau - s_uv * factor
            next_right = [a - factor * b for a, b in zip(triple(block, near), right)]
            next_right[2] = next_right[2] + sign * flow
            inverse = 1.0 / next_pivot
            carry = (coupling * inverse, next_right)
            keep(carry[0])
        held = inverse * flag(exists)
        keep(held)
        return carry, coupling, held, link, flow, tau

    carry_b, coupling_b, held_b, link_b, flow_b, tau_b = chain(True)
    carry_a, coupling_a, held_a, link_a, flow_a, tau_a = chain(False)
    pivot_u = quantity(0, 0) + tau_b - coupling_b * carry_b[0]
    right_u = [a + carry_b[0] * b for a, b in zip(triple(0, 5), carry_b[1])]
    right_u[2] = right_u[2] - flow_b
    pivot_v = quantity(0, 2) + tau_a - coupling_a * carry_a[0]
    right_v = [a + carry_a[0] * b for a, b in zip(triple(0, 8), carry_a[1])]
    right_v[2] = right_v[2] + flow_a
    s_uv = quantity(0, 1)
    inverse_u = 1.0 / pivot_u
    factor = s_uv * inverse_u
    inverse_v = 1.0 / (pivot_v - s_uv * factor)
    keep(inverse_u)
    keep(factor)
    keep(inverse_v)
    end_ref[0] = link_b
    end_ref[1] = link_a
    end_ref[2] = tau_b
    end_ref[3] = tau_a
    end_ref[4] = flow_b
    end_ref[5] = flow_a

    for f in range(3):
        last = (right_v[f] - factor * right_u[f]) * inverse_v
        first_u = right_u[f] * inverse_u - factor * last
        first_ref[f, 0] = carry_b[1][f] * held_b + carry_b[0] * first_u
        first_ref[f, nz + 1] = carry_a[1][f] * held_a + carry_a[0] * last
        first_ref[f, 1] = first_u
        first_ref[f, nz] = last
    for z in range(nz - 2, 0, -1):
        ratio = lz_ref[z] * open_after(at_z * nz + z) * inverse_ref[z]
        spike = e_ref[z]
        for f in range(3):
            first_ref[f, z + 1] = (
                d_ref[f, z] + spike * first_ref[f, 1] + ratio * first_ref[f, z + 2]
            )

    for z in range(nz):
        link_x, link_y = lx_ref[z], ly_ref[z]
        link_low = link_b if z == 0 else lz_ref[z - 1]
        link_high = link_a if z == nz - 1 else lz_ref[z]
        cut_low = link_low * cut_after(breaks_ref, at_z * nz + z - 1)
        cut_high = link_high * cut_after(breaks_ref, at_z * nz + z)
        right = []
        for f in range(3):
            origin = source_ref[f, z]
            if f == 2 and z == 0:
                origin = origin - flow_b
            if f == 2 and z == nz - 1:
                origin = origin + flow_a
            right.append(
                origin
                + stencil(first_ref[f, z + 1], link_x, link_y)
                + (cut_low * first_ref[f, z] + cut_high * first_ref[f, z + 2])
            )
        if z == 0:
            g_u = list(right)
        else:
            if z == 1:
                forward = right
            else:
                forward = [right[f] + coupling * value[f] for f in range(3)]
            if z < nz - 1:
                inverse, spike = inverse_ref[z], e_ref[z]
                value = [forward[f] * inverse for f in range(3)]
                g_u = [g_u[f] + spike * forward[f] for f in range(3)]
                for f in range(3):
                    d2_ref[f, z] = value[f]
                coupling = lz_ref[z] * open_after(at_z * nz + z)
    write_message(message_ref, g_u + forward, nx, ny, 1)


def final_kernel(count, breaks_ref, *refs):
    blocks = refs[:count]
    lx_ref, ly_ref, lz_ref, source_ref, centre_ref, d2_ref, e_ref, inverse_ref = refs[count : count + 8]
    factor_ref, end_ref, pressure_ref, residual_ref, second_ref = refs[count + 8 :]
    nz = lx_ref.shape[0]
    nx, ny = lx_ref.shape[1] - 8, lx_ref.shape[2] // 2
    at_z = lax.axis_index("gz")

    def triple(block, q):
        return [read_message(blocks[block], q + f, SECOND_COUNT, nx, ny, 1) for f in range(3)]

    slots = []

    def kept():
        slots.append(None)
        return factor_ref[len(slots) - 1]

    def chain(below):
        near, far = (3, 0) if below else (0, 3)
        carry = None
        for step in range(count - 1, 0, -1):
            block = step if below else count - step
            right = triple(block, far)
            if carry is not None:
                right = [a + carry[0] * b for a, b in zip(right, carry[1])]
            factor = kept()
            next_right = [a - factor * b for a, b in zip(triple(block, near), right)]
            carry = (kept(), next_right)
        return carry, kept()

    carry_b, held_b = chain(True)
    carry_a, held_a = chain(False)
    inverse_u, factor, inverse_v = kept(), kept(), kept()
    right_u = [a + carry_b[0] * b for a, b in zip(triple(0, 0), carry_b[1])]
    right_v = [a + carry_a[0] * b for a, b in zip(triple(0, 3), carry_a[1])]
    for f in range(3):
        last = (right_v[f] - factor * right_u[f]) * inverse_v
        first_u = right_u[f] * inverse_u - factor * last
        second_ref[f, 0] = carry_b[1][f] * held_b + carry_b[0] * first_u
        second_ref[f, nz + 1] = carry_a[1][f] * held_a + carry_a[0] * last
        second_ref[f, 1] = first_u
        second_ref[f, nz] = last
    for z in range(nz - 2, 0, -1):
        ratio = lz_ref[z] * (1.0 - cut_after(breaks_ref, at_z * nz + z)) * inverse_ref[z]
        spike = e_ref[z]
        for f in range(3):
            second_ref[f, z + 1] = (
                d2_ref[f, z] + spike * second_ref[f, 1] + ratio * second_ref[f, z + 2]
            )
    own = (slice(0, nx), slice(0, ny))
    for z in range(nz):
        link_x, link_y = lx_ref[z], ly_ref[z]
        link_low = end_ref[0] if z == 0 else lz_ref[z - 1]
        link_high = end_ref[1] if z == nz - 1 else lz_ref[z]
        centre = centre_ref[z]
        if z == 0:
            centre = centre + end_ref[2]
        if z == nz - 1:
            centre = centre + end_ref[3]
        for f in range(3):
            origin = source_ref[f, z]
            if f == 2 and z == 0:
                origin = origin - end_ref[4]
            if f == 2 and z == nz - 1:
                origin = origin + end_ref[5]
            here = second_ref[f, z + 1]
            total = (
                stencil(here, link_x, link_y)
                + (link_low * second_ref[f, z] + link_high * second_ref[f, z + 2])
            )
            pressure_ref[f, z] = here[own]
            residual_ref[f, z] = (origin - centre * here + total)[own]


def kernel_call(kernel, outputs, smem, operands, scratch=()):
    specs = [pl.BlockSpec(memory_space=pltpu.SMEM)] * smem
    specs += [pl.BlockSpec(memory_space=pltpu.VMEM)] * (len(operands) - smem)
    return pl.pallas_call(
        kernel,
        out_shape=[jax.ShapeDtypeStruct(s, t) for s, t in outputs],
        in_specs=specs,
        out_specs=[pl.BlockSpec(memory_space=pltpu.VMEM)] * len(outputs),
        scratch_shapes=list(scratch),
        compiler_params=pltpu.CompilerParams(vmem_limit_bytes=24 * 2**20),
    )(*operands)


def ring(values, axis, distance):
    size = lax.axis_size(axis)
    return lax.ppermute(values, axis, [(i, (i + distance) % size) for i in range(size)])


def diagonal(values, x_distance, y_distance):
    nx, ny = lax.axis_size("gx"), lax.axis_size("gy")
    route = []
    for i in range(nx):
        for j in range(ny):
            target = ((i + x_distance) % nx) * ny + (j + y_distance) % ny
            route.append((i * ny + j, target))
    return lax.ppermute(values, ("gx", "gy"), route)


def per_device(facies, perm_table, line_breaks):
    nz, nx, ny = facies.shape
    gx, gz = lax.axis_size("gx"), lax.axis_size("gz")
    i32, f32 = jnp.int32, jnp.float32
    rows = ((nz * WIDE, ny), i32)
    two = gx == 2
    packed = kernel_call(pack_kernel, [((nx, ny), i32)] + [rows] * (1 if two else 2), 0, [facies])
    strip = packed[0]
    y_low, y_high = ring(strip, "gy", 1), ring(strip, "gy", -1)
    if two:
        row_low = row_high = ring(packed[1], "gx", 1)
        low_low = low_high = diagonal(strip, 1, 1)
        high_low = high_high = diagonal(strip, 1, -1)
    else:
        row_low, row_high = ring(packed[2], "gx", 1), ring(packed[1], "gx", -1)
        low_low, low_high = diagonal(strip, 1, 1), diagonal(strip, -1, 1)
        high_low, high_high = diagonal(strip, 1, -1), diagonal(strip, -1, -1)

    slab = (nx + 8, 2 * ny)
    one, three = ((nz,) + slab, f32), ((3, nz) + slab, f32)
    message, lx, ly, lz, source, centre, d, e, inverse = kernel_call(
        eliminate_kernel,
        [((message_rows(nx, FIRST_COUNT, 2), ny), f32), one, one, one, three, one, three, one, one],
        2,
        [perm_table, line_breaks, facies, row_low, row_high, y_low, y_high,
         low_low, low_high, high_low, high_high],
        [pltpu.VMEM((nz, 8, ny), i32)],
    )
    gathered = [message] + [ring(message, "gz", step) for step in range(1, gz)]
    factors = 2 * (2 * (gz - 1) + 1) + 3
    message, d2, factor, ends = kernel_call(
        functools.partial(middle_kernel, gz),
        [((message_rows(nx, SECOND_COUNT, 1), ny), f32), three, ((factors,) + slab, f32), ((6,) + slab, f32)],
        1,
        [line_breaks] + gathered + [lx, ly, lz, source, d, e, inverse],
        [pltpu.VMEM((3, nz + 2) + slab, f32)],
    )
    gathered = [message] + [ring(message, "gz", step) for step in range(1, gz)]
    out = ((3, nz, nx, ny), f32)
    pressure, residual = kernel_call(
        functools.partial(final_kernel, gz),
        [out, out],
        1,
        [line_breaks] + gathered + [lx, ly, lz, source, centre, d2, e, inverse, factor, ends],
        [pltpu.VMEM((3, nz + 2) + slab, f32)],
    )
    return pressure, residual


def solution(mesh):
    return jax.shard_map(
        per_device,
        mesh=mesh,
        in_specs=(P("gz", "gx", "gy"), P(), P()),
        out_specs=(P(None, "gz", "gx", "gy"), P(None, "gz", "gx", "gy")),
        check_vma=False,
    )
```

time: 167 us -> 43.9 us (0.26)
  the two profiles are of different devices: /device:TPU:14 before, /device:TPU:0 now
where the time goes in v1:
time: 43.9 us; the launch traced here: 43.7 us
  waiting for transfers between devices  17 us (39%)
  starting transfers between devices  15.1 us (34%)
  Pallas kernels  8.1 us (18%)
  local copies, waits for them, and re-layouts  2.89 us (7%)
  between operations  0.66 us (2%)
    ppermute x9, waiting for transfers between devices, ring(): lax.ppermute(values, axis, [(i, (i + distance) % size) for i in range(siz...  15.7 us
    ppermute x9, starting transfers between devices, ring(): lax.ppermute(values, axis, [(i, (i + distance) % size) for i in range(siz...  13.3 us
    pallas_call x4, Pallas kernels, kernel_call(): pl.pallas_call(kernel, out_shape=[jax.ShapeDtypeStruct(s, t) for s, t in...  8.1 us
    unnamed x8, local copies, waits for them, and re-layouts  2.89 us
    ppermute x2, starting transfers between devices, diagonal(): return lax.ppermute(values, ('gx', 'gy'), route)  1.75 us
    ppermute x2, waiting for transfers between devices, diagonal(): return lax.ppermute(values, ('gx', 'gy'), route)  1.3 us
  transfers between devices with their start and end apart: 11, of which 7 were waited for; matrix products, arithmetic and copies ran while one was open for 0% of the time, Pallas kernels for 0%

profile of v1, /device:TPU:0, one launch (start us, length us, event | category | flops | bytes accessed | tf_op | source)
XLA Modules:
  0.0 43.7 jit_solution(14485358035033906638)
XLA Ops:
  0.6 0.0 copy-start
  0.6 0.9 %copy-done = s32[16,16,128]{2,1,0:T(8,128)S(1)} copy-done((s32[16,16,128]{2,1,0:T(8,128)S(1)}, s32[16,16,128]{2,1,0:T(8,128)}, u32[]{:S(2)}) %copy-start) | copy-done | bytes 131096
  1.5 0.1 shard_map.50
  1.6 3.0 %collective-permute-start = (s32[48,128]{1,0:T(8,128)S(1)}, s32[48,128]{1,0:T(8,128)S(1)}, u32[]{:S(2)}, u32[]{:S(2)}) collective-permute-start(s32[48,128]{1,0:T(8,128)S(1)} %get-tuple-element.17), channel_id=1, source_target_pairs={{0,16},{16,0},{1,17},{17,1},{2,18},{18,2},{3,19},{19,3},{4,20},{20... | collective-permute-start | bytes 73736 | tf_op jit(solution)/shard_map/ppermute | solution.py:459
  4.6 0.7 %collective-permute-start.4 = (s32[16,128]{1,0:T(8,128)S(1)}, s32[16,128]{1,0:T(8,128)S(1)}, u32[]{:S(2)}, u32[]{:S(2)}) collective-permute-start(s32[16,128]{1,0:T(8,128)S(1)} %get-tuple-element.18), channel_id=1, source_target_pairs={{0,28},{4,16},{8,20},{12,24},{16,12},{20,0},{24,4},{28,8},{1,29},{... | collective-permute-start | bytes 24584 | tf_op jit(solution)/shard_map/ppermute | solution.py:469
  5.3 1.1 %collective-permute-start.3 = (s32[16,128]{1,0:T(8,128)S(1)}, s32[16,128]{1,0:T(8,128)S(1)}, u32[]{:S(2)}, u32[]{:S(2)}) collective-permute-start(s32[16,128]{1,0:T(8,128)S(1)} %get-tuple-element.18), channel_id=1, source_target_pairs={{0,20},{4,24},{8,28},{12,16},{16,4},{20,8},{24,12},{28,0},{1,21},{... | collective-permute-start | bytes 24584 | tf_op jit(solution)/shard_map/ppermute | solution.py:469
  6.4 1.6 %collective-permute-start.2 = (s32[16,128]{1,0:T(8,128)S(1)}, s32[16,128]{1,0:T(8,128)S(1)}, u32[]{:S(2)}, u32[]{:S(2)}) collective-permute-start(s32[16,128]{1,0:T(8,128)S(1)} %get-tuple-element.18), channel_id=1, source_target_pairs={{0,12},{4,0},{8,4},{12,8},{1,13},{5,1},{9,5},{13,9},{2,14},{6,2},{... | collective-permute-start | bytes 24584 | tf_op jit(solution)/shard_map/ppermute | solution.py:459
  8.0 0.0 collective-permute-start.1
  8.0 0.0 collective-permute-done.4.high_low.high_high
  8.0 1.3 %collective-permute-done.3.low_low.low_high = s32[16,128]{1,0:T(8,128)S(1)} collective-permute-done((s32[16,128]{1,0:T(8,128)S(1)}, s32[16,128]{1,0:T(8,128)S(1)}, u32[]{:S(2)}, u32[]{:S(2)}) %collective-permute-start.3) | collective-permute-done | bytes 8224 | tf_op jit(solution)/shard_map/ppermute | solution.py:469
  9.3 0.1 collective-permute-done.2.y_high
  9.3 1.7 %collective-permute-done.1.y_low = s32[16,128]{1,0:T(8,128)S(1)} collective-permute-done((s32[16,128]{1,0:T(8,128)S(1)}, s32[16,128]{1,0:T(8,128)S(1)}, u32[]{:S(2)}, u32[]{:S(2)}) %collective-permute-start.1) | collective-permute-done | bytes 8224 | tf_op jit(solution)/shard_map/ppermute | solution.py:459
  11.0 0.0 collective-permute-done.row_low.row_high
  11.0 0.0 copy-start.1
  11.0 0.7 %copy-done.1 = s32[63]{0:T(128)S(1)} copy-done((s32[63]{0:T(128)S(1)}, s32[63]{0:T(128)}, u32[]{:S(2)}) %copy-start.1) | copy-done | bytes 276
  11.7 0.0 copy-start.3
  11.7 0.7 %copy-done.3 = f32[3,16]{1,0:T(4,128)S(1)} copy-done((f32[3,16]{1,0:T(4,128)S(1)}, f32[3,16]{1,0:T(4,128)}, u32[]{:S(2)}) %copy-start.3) | copy-done | bytes 216
  12.4 3.8 %shard_map.51 = (f32[248,128]{1,0:T(8,128)S(1)}, f32[16,24,256]{2,1,0:T(8,128)S(1)}, f32[16,24,256]{2,1,0:T(8,128)S(1)}, f32[16,24,256]{2,1,0:T(8,128)S(1)}, f32...) custom-call(f32[3,16]{1,0:T(4,128)S(1)} %copy-done.3, ...), custom_call_target="tpu_custom_call" | custom-call | tf_op jit(solution)/shard_map/pallas_call | solution.py:447
  16.1 3.6 %collective-permute-start.7 = (f32[248,128]{1,0:T(8,128)S(1)}, f32[248,128]{1,0:T(8,128)S(1)}, u32[]{:S(2)}, u32[]{:S(2)}) collective-permute-start(f32[248,128]{1,0:T(8,128)S(1)} %get-tuple-element.19.refs_0_), channel_id=1, source_target_pairs={{0,3},{1,0},{2,1},{3,2},{4,7},{5,4},{6,5},{7,6},{8,11},{9,8},{10,9... | collective-permute-start | bytes 380936 | tf_op jit(solution)/shard_map/ppermute | solution.py:459
  19.8 0.0 collective-permute-start.6
  19.8 1.0 %collective-permute-start.5 = (f32[248,128]{1,0:T(8,128)S(1)}, f32[248,128]{1,0:T(8,128)S(1)}, u32[]{:S(2)}, u32[]{:S(2)}) collective-permute-start(f32[248,128]{1,0:T(8,128)S(1)} %get-tuple-element.19.refs_0_), channel_id=1, source_target_pairs={{0,1},{1,2},{2,3},{3,0},{4,5},{5,6},{6,7},{7,4},{8,9},{9,10},{10,1... | collective-permute-start | bytes 380936 | tf_op jit(solution)/shard_map/ppermute | solution.py:459
  20.8 2.9 %collective-permute-done.7.refs_3_ = f32[248,128]{1,0:T(8,128)S(1)} collective-permute-done((f32[248,128]{1,0:T(8,128)S(1)}, f32[248,128]{1,0:T(8,128)S(1)}, u32[]{:S(2)}, u32[]{:S(2)}) %collective-permute-start.7) | collective-permute-done | bytes 127008 | tf_op jit(solution)/shard_map/ppermute | solution.py:459
  23.7 6.6 %collective-permute-done.6.refs_2_ = f32[248,128]{1,0:T(8,128)S(1)} collective-permute-done((f32[248,128]{1,0:T(8,128)S(1)}, f32[248,128]{1,0:T(8,128)S(1)}, u32[]{:S(2)}, u32[]{:S(2)}) %collective-permute-start.6) | collective-permute-done | bytes 127008 | tf_op jit(solution)/shard_map/ppermute | solution.py:459
  30.3 0.0 collective-permute-done.5.refs_1_
  30.3 0.0 copy-start.2
  30.3 0.7 %copy-done.2 = s32[63]{0:T(128)S(1)} copy-done((s32[63]{0:T(128)S(1)}, s32[63]{0:T(128)}, u32[]{:S(2)}) %copy-start.2) | copy-done | bytes 276
  30.9 2.3 %shard_map.52 = (f32[136,128]{1,0:T(8,128)S(1)}, f32[3,16,24,256]{3,2,1,0:T(8,128)S(1)}, f32[17,24,256]{2,1,0:T(8,128)S(1)}, f32[6,24,256]{2,1,0:T(8,128)S(1)}) custom-call(s32[63]{0:T(128)S(1)} %copy-done.2, f32[248,128]{1,0:T(8,128)S(1)} %get-tuple-element.19.refs_0_, f32[248,128]{1,0:T(8,128)S(1)} %collective-permute-done.5.refs_1_, ...), custom_call_target="tpu_custom_call" | custom-call | tf_op jit(solution)/shard_map/pallas_call | solution.py:447
  33.2 1.1 %collective-permute-start.10 = (f32[136,128]{1,0:T(8,128)S(1)}, f32[136,128]{1,0:T(8,128)S(1)}, u32[]{:S(2)}, u32[]{:S(2)}) collective-permute-start(f32[136,128]{1,0:T(8,128)S(1)} %get-tuple-element.27.refs_0_), channel_id=1, source_target_pairs={{0,3},{1,0},{2,1},{3,2},{4,7},{5,4},{6,5},{7,6},{8,11},{9,8},{10,9... | collective-permute-start | bytes 208904 | tf_op jit(solution)/shard_map/ppermute | solution.py:459
  34.4 1.0 %collective-permute-start.9 = (f32[136,128]{1,0:T(8,128)S(1)}, f32[136,128]{1,0:T(8,128)S(1)}, u32[]{:S(2)}, u32[]{:S(2)}) collective-permute-start(f32[136,128]{1,0:T(8,128)S(1)} %get-tuple-element.27.refs_0_), channel_id=1, source_target_pairs={{0,2},{1,3},{2,0},{3,1},{4,6},{5,7},{6,4},{7,5},{8,10},{9,11},{10,... | collective-permute-start | bytes 208904 | tf_op jit(solution)/shard_map/ppermute | solution.py:459
  35.4 1.9 %collective-permute-start.8 = (f32[136,128]{1,0:T(8,128)S(1)}, f32[136,128]{1,0:T(8,128)S(1)}, u32[]{:S(2)}, u32[]{:S(2)}) collective-permute-start(f32[136,128]{1,0:T(8,128)S(1)} %get-tuple-element.27.refs_0_), channel_id=1, source_target_pairs={{0,1},{1,2},{2,3},{3,0},{4,5},{5,6},{6,7},{7,4},{8,9},{9,10},{10,1... | collective-permute-start | bytes 208904 | tf_op jit(solution)/shard_map/ppermute | solution.py:459
  37.3 0.3 collective-permute-done.10.refs_3_
  37.6 4.1 %collective-permute-done.9.refs_2_ = f32[136,128]{1,0:T(8,128)S(1)} collective-permute-done((f32[136,128]{1,0:T(8,128)S(1)}, f32[136,128]{1,0:T(8,128)S(1)}, u32[]{:S(2)}, u32[]{:S(2)}) %collective-permute-start.9) | collective-permute-done | bytes 69664 | tf_op jit(solution)/shard_map/ppermute | solution.py:459
  41.7 0.0 collective-permute-done.8.refs_1_
  41.7 2.0 %shard_map.53 = (f32[3,16,16,128]{3,2,1,0:T(8,128)}, f32[3,16,16,128]{3,2,1,0:T(8,128)}) custom-call(s32[63]{0:T(128)S(1)} %copy-done.2, f32[136,128]{1,0:T(8,128)S(1)} %get-tuple-element.27.refs_0_, f32[136,128]{1,0:T(8,128)S(1)} %collective-permute-done.8.refs_1_, f32[136,128]{1,0:T(8,128)S(1)} %collective-permute-done.9.refs_2_, ...), custom_call_target="tpu_custom_call" | custom-call | tf_op jit(solution)/shard_map/pallas_call | solution.py:447
Async XLA Ops:
  0.6 0.9 %copy-start = (s32[16,16,128]{2,1,0:T(8,128)S(1)}, s32[16,16,128]{2,1,0:T(8,128)}, u32[]{:S(2)}) copy-start(s32[16,16,128]{2,1,0:T(8,128)} %facies_ref.3) | copy-start | bytes 393220
  1.6 9.4 %collective-permute-start = (s32[48,128]{1,0:T(8,128)S(1)}, s32[48,128]{1,0:T(8,128)S(1)}, u32[]{:S(2)}, u32[]{:S(2)}) collective-permute-start(s32[48,128]{1,0:T(8,128)S(1)} %get-tuple-element.17), channel_id=1, source_target_pairs={{0,16},{16,0},{1,17},{17,1},{2,18},{18,2},{3,19},{19,3},{4,20},{20... | collective-permute-start | bytes 73736 | tf_op jit(solution)/shard_map/ppermute | solution.py:459
  4.6 3.3 %collective-permute-start.4 = (s32[16,128]{1,0:T(8,128)S(1)}, s32[16,128]{1,0:T(8,128)S(1)}, u32[]{:S(2)}, u32[]{:S(2)}) collective-permute-start(s32[16,128]{1,0:T(8,128)S(1)} %get-tuple-element.18), channel_id=1, source_target_pairs={{0,28},{4,16},{8,20},{12,24},{16,12},{20,0},{24,4},{28,8},{1,29},{... | collective-permute-start | bytes 24584 | tf_op jit(solution)/shard_map/ppermute | solution.py:469
  5.3 4.0 %collective-permute-start.3 = (s32[16,128]{1,0:T(8,128)S(1)}, s32[16,128]{1,0:T(8,128)S(1)}, u32[]{:S(2)}, u32[]{:S(2)}) collective-permute-start(s32[16,128]{1,0:T(8,128)S(1)} %get-tuple-element.18), channel_id=1, source_target_pairs={{0,20},{4,24},{8,28},{12,16},{16,4},{20,8},{24,12},{28,0},{1,21},{... | collective-permute-start | bytes 24584 | tf_op jit(solution)/shard_map/ppermute | solution.py:469
  6.4 2.9 %collective-permute-start.2 = (s32[16,128]{1,0:T(8,128)S(1)}, s32[16,128]{1,0:T(8,128)S(1)}, u32[]{:S(2)}, u32[]{:S(2)}) collective-permute-start(s32[16,128]{1,0:T(8,128)S(1)} %get-tuple-element.18), channel_id=1, source_target_pairs={{0,12},{4,0},{8,4},{12,8},{1,13},{5,1},{9,5},{13,9},{2,14},{6,2},{... | collective-permute-start | bytes 24584 | tf_op jit(solution)/shard_map/ppermute | solution.py:459
  8.0 3.1 %collective-permute-start.1 = (s32[16,128]{1,0:T(8,128)S(1)}, s32[16,128]{1,0:T(8,128)S(1)}, u32[]{:S(2)}, u32[]{:S(2)}) collective-permute-start(s32[16,128]{1,0:T(8,128)S(1)} %get-tuple-element.18), channel_id=1, source_target_pairs={{0,4},{4,8},{8,12},{12,0},{1,5},{5,9},{9,13},{13,1},{2,6},{6,10},{... | collective-permute-start | bytes 24584 | tf_op jit(solution)/shard_map/ppermute | solution.py:459
  11.0 0.7 %copy-start.1 = (s32[63]{0:T(128)S(1)}, s32[63]{0:T(128)}, u32[]{:S(2)}) copy-start(s32[63]{0:T(128)} %breaks_ref.5) | copy-start | bytes 760
  11.7 0.7 %copy-start.3 = (f32[3,16]{1,0:T(4,128)S(1)}, f32[3,16]{1,0:T(4,128)}, u32[]{:S(2)}) copy-start(f32[3,16]{1,0:T(4,128)} %table_ref.1) | copy-start | bytes 580
  16.1 7.5 %collective-permute-start.7 = (f32[248,128]{1,0:T(8,128)S(1)}, f32[248,128]{1,0:T(8,128)S(1)}, u32[]{:S(2)}, u32[]{:S(2)}) collective-permute-start(f32[248,128]{1,0:T(8,128)S(1)} %get-tuple-element.19.refs_0_), channel_id=1, source_target_pairs={{0,3},{1,0},{2,1},{3,2},{4,7},{5,4},{6,5},{7,6},{8,11},{9,8},{10,9... | collective-permute-start | bytes 380936 | tf_op jit(solution)/shard_map/ppermute | solution.py:459
  19.8 10.5 %collective-permute-start.6 = (f32[248,128]{1,0:T(8,128)S(1)}, f32[248,128]{1,0:T(8,128)S(1)}, u32[]{:S(2)}, u32[]{:S(2)}) collective-permute-start(f32[248,128]{1,0:T(8,128)S(1)} %get-tuple-element.19.refs_0_), channel_id=1, source_target_pairs={{0,2},{1,3},{2,0},{3,1},{4,6},{5,7},{6,4},{7,5},{8,10},{9,11},{10,... | collective-permute-start | bytes 380936 | tf_op jit(solution)/shard_map/ppermute | solution.py:459
  19.8 10.5 %collective-permute-start.5 = (f32[248,128]{1,0:T(8,128)S(1)}, f32[248,128]{1,0:T(8,128)S(1)}, u32[]{:S(2)}, u32[]{:S(2)}) collective-permute-start(f32[248,128]{1,0:T(8,128)S(1)} %get-tuple-element.19.refs_0_), channel_id=1, source_target_pairs={{0,1},{1,2},{2,3},{3,0},{4,5},{5,6},{6,7},{7,4},{8,9},{9,10},{10,1... | collective-permute-start | bytes 380936 | tf_op jit(solution)/shard_map/ppermute | solution.py:459
  30.3 0.7 %copy-start.2 = (s32[63]{0:T(128)S(1)}, s32[63]{0:T(128)}, u32[]{:S(2)}) copy-start(s32[63]{0:T(128)} %breaks_ref.5) | copy-start | bytes 760
  33.2 4.4 %collective-permute-start.10 = (f32[136,128]{1,0:T(8,128)S(1)}, f32[136,128]{1,0:T(8,128)S(1)}, u32[]{:S(2)}, u32[]{:S(2)}) collective-permute-start(f32[136,128]{1,0:T(8,128)S(1)} %get-tuple-element.27.refs_0_), channel_id=1, source_target_pairs={{0,3},{1,0},{2,1},{3,2},{4,7},{5,4},{6,5},{7,6},{8,11},{9,8},{10,9... | collective-permute-start | bytes 208904 | tf_op jit(solution)/shard_map/ppermute | solution.py:459
  34.4 7.3 %collective-permute-start.9 = (f32[136,128]{1,0:T(8,128)S(1)}, f32[136,128]{1,0:T(8,128)S(1)}, u32[]{:S(2)}, u32[]{:S(2)}) collective-permute-start(f32[136,128]{1,0:T(8,128)S(1)} %get-tuple-element.27.refs_0_), channel_id=1, source_target_pairs={{0,2},{1,3},{2,0},{3,1},{4,6},{5,7},{6,4},{7,5},{8,10},{9,11},{10,... | collective-permute-start | bytes 208904 | tf_op jit(solution)/shard_map/ppermute | solution.py:459
  35.4 6.3 %collective-permute-start.8 = (f32[136,128]{1,0:T(8,128)S(1)}, f32[136,128]{1,0:T(8,128)S(1)}, u32[]{:S(2)}, u32[]{:S(2)}) collective-permute-start(f32[136,128]{1,0:T(8,128)S(1)} %get-tuple-element.27.refs_0_), channel_id=1, source_target_pairs={{0,1},{1,2},{2,3},{3,0},{4,5},{5,6},{6,7},{7,4},{8,9},{9,10},{10,1... | collective-permute-start | bytes 208904 | tf_op jit(solution)/shard_map/ppermute | solution.py:459

commit v2 on v1

v2 whole, which is shorter than its diff:
```python
import functools

import jax
import jax.numpy as jnp
from jax import lax
from jax.experimental import pallas as pl
from jax.experimental.pallas import tpu as pltpu
from jax.sharding import PartitionSpec as P


WIDE = 3
FIRST_COUNT = 11
LAST_COUNT = 5
SECOND_COUNT = 6
PACK_LIMIT = 24


def moved(values, amount, axis):
    size = values.shape[axis]
    amount = amount % size
    if amount == 0:
        return values
    return pltpu.roll(values, amount, axis)


def flag(condition):
    return condition.astype(jnp.float32)


def iotas(rows, lanes):
    return tuple(lax.broadcasted_iota(jnp.int32, (rows, lanes), d) for d in (0, 1))


def choose(condition, first, second):
    return [jnp.where(condition, a, b) for a, b in zip(first, second)]


def bit_of(stage):
    return (lax.axis_index("gz") >> stage) % 2 == 1


def pack_kernel(stages, facies_in, table_in, breaks_in, facies_ref, table_ref, cut_ref, strip_ref, *refs):
    row_refs, (table, breaks, sems) = refs[:-3], refs[-3:]
    nz, nx, ny = facies_ref.shape
    copies = [
        pltpu.make_async_copy(facies_in, facies_ref, sems.at[0]),
        pltpu.make_async_copy(table_in, table, sems.at[1]),
        pltpu.make_async_copy(breaks_in, breaks, sems.at[2]),
    ]
    for copy in copies:
        copy.start()
    copies[0].wait()
    lane = lax.broadcasted_iota(jnp.int32, (nx, ny), 1)
    strip = jnp.zeros((nx, ny), jnp.int32)
    for z in range(nz):
        strip = jnp.where(lane // 8 == z, moved(facies_ref[z], 8 * z + WIDE, 1), strip)
    strip_ref[...] = strip
    for z in range(nz):
        leading = facies_ref[z, 0:WIDE, :]
        last = facies_ref[z, nx - WIDE : nx, :]
        spot = slice(z * WIDE, (z + 1) * WIDE)
        if len(row_refs) == 1:
            row_refs[0][spot, :] = jnp.where(lax.axis_index("gx") == 0, last, leading)
        else:
            row_refs[0][spot, :] = leading
            row_refs[1][spot, :] = last
    copies[1].wait()
    copies[2].wait()
    lane = iotas(8, ny)[1]
    for q in range(3):
        values = jnp.zeros((8, ny), jnp.float32)
        for label in range(table.shape[1]):
            values = jnp.where(lane == label, table[q, label], values)
        table_ref[q] = values
    at_z = lax.axis_index("gz")
    layers = [at_z * nz + r - 1 for r in range(nz + 1)]
    for s in range(stages):
        base, size = (at_z >> (s + 1)) << (s + 1), 2**s
        layers.append((base + size) * nz - 1)
        layers.append(jnp.where(bit_of(s), base, base + 2 * size) * nz - 1)
    for r, layer in enumerate(layers):
        cut = breaks[jnp.clip(layer, 0, breaks.shape[0] - 1)].astype(jnp.float32)
        cut_ref[r : r + 1, :] = jnp.full((1, ny), cut, jnp.float32)


def face(a, b):
    product = a * b
    total = a + b
    harmonic = 2.0 * product / total
    inside = product > 0.0
    link = jnp.where(inside, harmonic, 0.0)
    flow = jnp.where(inside, harmonic, total)
    tau = jnp.where(inside, harmonic, 2.0 * total)
    return link, flow, tau


class Message:
    def __init__(self, count, halo, nx, ny):
        self.count, self.halo, self.nx, self.ny = count, halo, nx, ny
        self.one_sided = lax.axis_size("gx") == 2
        self.rows_each = halo if self.one_sided else 2 * halo
        self.per_tile = 8 // self.rows_each
        self.tiles = -(-count // self.per_tile)
        self.strip = slice(count * nx, count * nx + nx + 8)
        self.rows = self.strip.stop + 8 * self.tiles

    def tile(self, q):
        start = self.strip.stop + 8 * (q // self.per_tile)
        return slice(start, start + 8)

    def side_moved(self, tile, q, sign):
        part = q % self.per_tile
        if not self.one_sided:
            return moved(tile, sign * (self.rows_each * part + self.halo), 0)
        first = lax.axis_index("gx") == 0
        out = jnp.where(
            first,
            moved(tile, sign * self.halo * part, 0),
            moved(tile, sign * self.halo * (part + 1), 0),
        )
        if sign > 0:
            return out
        row = iotas(8, self.ny)[0]
        return jnp.where(jnp.where(first, row, 7 - row) < self.halo, out, 1.0)

    def write(self, ref, slabs):
        nx, ny, halo = self.nx, self.ny, self.halo
        lane = iotas(nx + 8, ny)[1]
        strip = moved(slabs[0][:, ny:], halo, 1)
        for q in range(1, self.count):
            turned = moved(slabs[q][:, ny:], 2 * halo * q + halo, 1)
            strip = jnp.where(lane < 2 * halo * q, strip, turned)
        ref[self.strip, :] = strip
        row = iotas(8, ny)[0]
        for q, slab in enumerate(slabs):
            ref[q * nx : (q + 1) * nx, :] = slab[:nx, :ny]
            turned = self.side_moved(slab[nx:, :ny], q, 1)
            part = q % self.per_tile
            tile = turned if part == 0 else jnp.where(row < self.rows_each * part, tile, turned)
            if part == self.per_tile - 1 or q == self.count - 1:
                ref[self.tile(q), :] = tile

    def read(self, ref):
        nx, halo = self.nx, self.halo
        strip = ref[self.strip, :]
        slabs = []
        for q in range(self.count):
            side = self.side_moved(ref[self.tile(q), :], q, -1)
            body = jnp.concatenate([ref[q * nx : (q + 1) * nx, :], side], axis=0)
            beside = moved(strip, -(2 * halo * q + halo), 1)
            slabs.append(jnp.concatenate([body, beside], axis=1))
        return slabs


def eliminate_kernel(
    table_ref, cut_ref, facies_ref, row_low, row_high, y_low, y_high,
    low_low, low_high, high_low, high_high,
    message_ref, own_ref, lx_ref, ly_ref, lz_ref, source_ref, centre_ref,
    d_ref, e_ref, inverse_ref, side_ref,
):
    nz, nx, ny = facies_ref.shape
    outside = ny - 1
    at_x, at_y = lax.axis_index("gx"), lax.axis_index("gy")
    has_x_low, has_x_high = at_x > 0, at_x < lax.axis_size("gx") - 1
    has_y_low, has_y_high = at_y > 0, at_y < lax.axis_size("gy") - 1
    tables = [table_ref[q] for q in range(3)]

    side_ref[...] = jnp.full(side_ref.shape, outside, jnp.int32)
    for z in range(nz):
        spot = slice(z * WIDE, (z + 1) * WIDE)
        side_ref[z, 0:WIDE, :] = jnp.where(has_x_high, row_high[spot, :], outside)
        side_ref[z, 8 - WIDE : 8, :] = jnp.where(has_x_low, row_low[spot, :], outside)

    def corner(high_ref, low_ref):
        row = iotas(8, ny)[0]
        high = jnp.where(has_x_high, high_ref[0:8, :], outside)
        low = jnp.where(has_x_low, low_ref[nx - 8 : nx, :], outside)
        middle = jnp.where(row >= 8 - WIDE, low, outside)
        return jnp.where(row < WIDE, high, middle)

    before = jnp.concatenate([y_low[...], corner(low_high, low_low)], axis=0)
    after = jnp.concatenate([y_high[...], corner(high_high, high_low)], axis=0)
    lane = iotas(nx + 8, ny)[1]
    strip = jnp.where(
        lane % 8 < WIDE,
        jnp.where(has_y_low, before, outside),
        jnp.where(has_y_high, after, outside),
    )
    near = (lane < WIDE) | (lane >= ny - WIDE)

    def labels(z):
        beside = jnp.where(near, moved(strip, -(8 * z + WIDE), 1), outside)
        return jnp.concatenate(
            [jnp.concatenate([facies_ref[z], side_ref[z]], axis=0), beside], axis=1
        )

    def lookup(table, index):
        rows = []
        for r in range(0, nx + 8, 8):
            parts = [
                jnp.take_along_axis(table, index[r : r + 8, c : c + ny], axis=1)
                for c in (0, ny)
            ]
            rows.append(jnp.concatenate(parts, axis=1))
        return jnp.concatenate(rows, axis=0)

    def coefficients(label):
        return [lookup(table, label) for table in tables]

    label = labels(0)
    valid = flag(label != outside)
    cell = valid > 0.0
    in_x, in_xp = valid * moved(valid, -1, 0), valid * moved(valid, 1, 0)
    in_y, in_yp = valid * moved(valid, -1, 1), valid * moved(valid, 1, 1)

    def side_faces(here, axis, inside, inside_back):
        there = moved(here, -1, axis)
        total = here + there
        flow = jnp.where(inside > 0.0, 2.0 * (here * there) / total, total)
        flow_back = moved(flow, 1, axis)
        tau = flow * (2.0 - inside) + flow_back * (2.0 - inside_back)
        return flow * inside, tau, flow - flow_back

    next_k = coefficients(label)
    link_below = None
    for z in range(nz):
        kx, ky, kz = next_k
        link_x, tau_x, source_x = side_faces(kx, 0, in_x, in_xp)
        link_y, tau_y, source_y = side_faces(ky, 1, in_y, in_yp)
        lx_ref[z] = link_x
        ly_ref[z] = link_y
        centre = tau_x + tau_y
        if z == 0:
            kz_first = kz
        if z < nz - 1:
            next_k = coefficients(labels(z + 1))
            above = next_k[2]
            link_z = jnp.where(cell, 2.0 * (kz * above) / (kz + above), 0.0)
            lz_ref[z] = link_z
        if z == 0:
            centre = centre + link_z
            source_z = link_z
        elif z == nz - 1:
            centre = centre + link_below
            source_z = -link_below
        else:
            centre = centre + (link_below + link_z)
            source_z = link_z - link_below
        centre = jnp.where(cell, centre, 1.0)
        sources = [source_x, source_y, source_z]
        for f in range(3):
            source_ref[f, z] = sources[f]
        centre_ref[z] = centre
        if z == 0:
            s_uu = centre
            g_u = list(sources)
        elif z < nz - 1:
            if z == 1:
                pivot = centre
                forward = list(sources)
                numerator = coupling
            else:
                pivot = centre - coupling * ratio
                forward = [sources[f] + coupling * value[f] for f in range(3)]
                numerator = coupling * spike
            inverse = 1.0 / pivot
            value = [forward[f] * inverse for f in range(3)]
            spike = numerator * inverse
            s_uu = s_uu - numerator * spike
            g_u = [g_u[f] + spike * forward[f] for f in range(3)]
            inverse_ref[z] = inverse
            e_ref[z] = spike
            for f in range(3):
                d_ref[f, z] = value[f]
        else:
            s_vv = centre - coupling * ratio
            s_uv = -coupling * spike
            g_v = [sources[f] + coupling * value[f] for f in range(3)]
        if z < nz - 1:
            coupling = link_z * open_after(cut_ref, z + 1)
            if z > 0:
                ratio = coupling * inverse
        link_below = link_z
    slabs = [s_uu, s_uv, s_vv, kz_first, kz] + g_u + g_v
    for q, slab in enumerate(slabs):
        own_ref[q] = slab
    Message(FIRST_COUNT, 2, nx, ny).write(message_ref, slabs)


def open_after(cut_ref, r):
    cut = 1.0 - cut_ref[r : r + 1, :]
    return jnp.concatenate([cut, cut], axis=1)


def slab_size(ref):
    return ref.shape[-2] - 8, ref.shape[-1] // 2


def join_kernel(stage, last, nz, cut_ref, own_ref, message_ref, sibling_ref, factor_ref, next_ref, *joined):
    nx, ny = slab_size(own_ref)
    own = [own_ref[q] for q in range(FIRST_COUNT)]
    sibling = Message(FIRST_COUNT, 2, nx, ny).read(message_ref)
    for q, slab in enumerate(sibling):
        sibling_ref[q] = slab
    above = bit_of(stage)
    low, high = choose(above, sibling, own), choose(above, own, sibling)
    link, flow, tau = face(low[4], high[3])
    coupling = link * open_after(cut_ref, nz + 1 + 2 * stage)
    inverse = 1.0 / (low[2] + tau)
    step = coupling * inverse
    last_inverse = 1.0 / (high[0] + tau - coupling * step)
    outer = low[1] * inverse
    weight = step * low[1]
    weight_low, weight_high = weight * last_inverse, high[1] * last_inverse
    right_low = low[8:10] + [low[10] + flow]
    right_high = high[5:7] + [high[7] - flow]
    middle = [b + step * a for a, b in zip(right_low, right_high)]
    s_uu = low[0] - outer * low[1] - weight * weight_low
    s_uv = -weight * weight_high
    s_vv = high[2] - high[1] * weight_high
    g_u = [g - outer * a - weight_low * m for g, a, m in zip(low[5:8], right_low, middle)]
    g_v = [g - weight_high * m for g, m in zip(high[8:11], middle)]
    for n, values in enumerate((outer, step, weight_low, weight_high)):
        factor_ref[n] = values
    if not last:
        slabs = [s_uu, s_uv, s_vv, low[3], high[4]] + g_u + g_v
        for q, slab in enumerate(slabs):
            joined[0][q] = slab
        Message(FIRST_COUNT, 2, nx, ny).write(next_ref, slabs)
        return
    top = bit_of(stage + 1)
    far_s, near_s = choose(top, [s_vv, s_uu], [s_uu, s_vv])
    far_k, near_k = choose(top, [high[4], low[3]], [low[3], high[4]])
    far_g, near_g = choose(top, g_v, g_u), choose(top, g_u, g_v)
    far_g[2] = far_g[2] + far_k * jnp.where(top, 1.0, -1.0)
    factor = s_uv / (far_s + 2.0 * far_k)
    factor_ref[4] = factor
    slabs = [near_s - s_uv * factor, near_k] + [n - factor * g for n, g in zip(near_g, far_g)]
    Message(LAST_COUNT, 2, nx, ny).write(next_ref, slabs)


def join_again_kernel(stage, last, own_ref, message_ref, factor_ref, sibling_ref, next_ref, *joined):
    nx, ny = slab_size(own_ref)
    own = [own_ref[q] for q in range(SECOND_COUNT)]
    sibling = Message(SECOND_COUNT, 1, nx, ny).read(message_ref)
    for q, slab in enumerate(sibling):
        sibling_ref[q] = slab
    above = bit_of(stage)
    low, high = choose(above, sibling, own), choose(above, own, sibling)
    outer, step, weight_low, weight_high = [factor_ref[n] for n in range(4)]
    middle = [b + step * a for a, b in zip(low[3:], high[:3])]
    g_u = [g - outer * a - weight_low * m for g, a, m in zip(low[:3], low[3:], middle)]
    g_v = [g - weight_high * m for g, m in zip(high[3:], middle)]
    if not last:
        for q, slab in enumerate(g_u + g_v):
            joined[0][q] = slab
        Message(SECOND_COUNT, 1, nx, ny).write(next_ref, g_u + g_v)
        return
    top = bit_of(stage + 1)
    factor = factor_ref[4]
    far_g, near_g = choose(top, g_v, g_u), choose(top, g_u, g_v)
    Message(3, 1, nx, ny).write(next_ref, [n - factor * g for n, g in zip(near_g, far_g)])


def stencil(slab, link_x, link_y):
    return (
        link_x * moved(slab, -1, 0)
        + moved(link_x * slab, 1, 0)
        + (link_y * moved(slab, -1, 1) + moved(link_y * slab, 1, 1))
    )


def middle_kernel(stages, cut_ref, *refs):
    own_ref, siblings, message_ref = refs[0], refs[1:stages], refs[stages]
    refs = refs[stages + 1 :]
    lx_ref, ly_ref, lz_ref, source_ref, d_ref, e_ref, inverse_ref = refs[:7]
    next_ref, own2_ref, d2_ref, factor_ref, end_ref, first_ref = refs[7:]
    nz = lx_ref.shape[0]
    nx, ny = slab_size(lx_ref)
    own = [own_ref[q] for q in range(FIRST_COUNT)]
    slots = []

    def keep(values):
        factor_ref[len(slots)] = values
        slots.append(None)

    def attach(state, sign, row, pivot, right, k):
        beside, k_beside, rights, exists = state[0], state[1], state[2:5], state[5]
        link, flow, tau = face(k_beside * exists, k)
        coupling = link * open_after(cut_ref, row)
        rights = rights[:2] + [rights[2] + sign * flow]
        inverse = 1.0 / (beside + tau)
        step = coupling * inverse
        right = [a + step * b for a, b in zip(right, rights)]
        right[2] = right[2] - sign * flow
        return pivot + tau - coupling * step, right, step, inverse, rights, (link, flow, tau)

    far = Message(LAST_COUNT, 2, nx, ny).read(message_ref)
    top = bit_of(stages - 1)
    below, above = far + [flag(top)], far + [flag(jnp.logical_not(top))]
    for s in range(stages - 2, -1, -1):
        up = bit_of(s)
        block = [siblings[s][q] for q in range(FIRST_COUNT)]
        sign = jnp.where(up, 1.0, -1.0)
        state = choose(up, below, above)
        far_s, far_k, near_s, near_k = choose(
            up, [block[0], block[3], block[2], block[4]], [block[2], block[4], block[0], block[3]]
        )
        far_g = choose(up, block[5:8], block[8:11])
        near_g = choose(up, block[8:11], block[5:8])
        pivot, right, step, _, _, _ = attach(state, sign, nz + 2 + 2 * s, far_s, far_g, far_k)
        factor = block[1] / pivot
        keep(step)
        keep(factor)
        state = [near_s - block[1] * factor, near_k]
        state += [n - factor * r for n, r in zip(near_g, right)] + [jnp.float32(1.0)]
        below, above = choose(up, state, below), choose(up, above, state)

    pivot_u, right_u, step_b, inverse_b, rights_b, ends_b = attach(
        below, 1.0, 0, own[0], own[5:8], own[3]
    )
    pivot_v, right_v, step_a, inverse_a, rights_a, ends_a = attach(
        above, -1.0, nz, own[2], own[8:11], own[4]
    )
    held_b, held_a = inverse_b * below[5], inverse_a * above[5]
    inverse_u = 1.0 / pivot_u
    factor = own[1] * inverse_u
    inverse_v = 1.0 / (pivot_v - own[1] * factor)
    for values in (step_b, held_b, step_a, held_a, inverse_u, factor, inverse_v):
        keep(values)
    (link_b, flow_b, tau_b), (link_a, flow_a, tau_a) = ends_b, ends_a
    for n, values in enumerate((link_b, link_a, tau_b, tau_a, flow_b, flow_a)):
        end_ref[n] = values

    for f in range(3):
        last = (right_v[f] - factor * right_u[f]) * inverse_v
        first_u = right_u[f] * inverse_u - factor * last
        first_ref[f, 0] = rights_b[f] * held_b + step_b * first_u
        first_ref[f, nz + 1] = rights_a[f] * held_a + step_a * last
        first_ref[f, 1] = first_u
        first_ref[f, nz] = last
    for z in range(nz - 2, 0, -1):
        ratio = lz_ref[z] * open_after(cut_ref, z + 1) * inverse_ref[z]
        spike = e_ref[z]
        for f in range(3):
            first_ref[f, z + 1] = (
                d_ref[f, z] + spike * first_ref[f, 1] + ratio * first_ref[f, z + 2]
            )

    for z in range(nz):
        link_low = link_b if z == 0 else lz_ref[z - 1]
        link_high = link_a if z == nz - 1 else lz_ref[z]
        cut_low = link_low * (1.0 - open_after(cut_ref, z))
        cut_high = link_high * (1.0 - open_after(cut_ref, z + 1))
        right = []
        for f in range(3):
            origin = source_ref[f, z]
            if f == 2 and z == 0:
                origin = origin - flow_b
            if f == 2 and z == nz - 1:
                origin = origin + flow_a
            right.append(
                origin
                + stencil(first_ref[f, z + 1], lx_ref[z], ly_ref[z])
                + (cut_low * first_ref[f, z] + cut_high * first_ref[f, z + 2])
            )
        if z == 0:
            g_u = list(right)
        else:
            if z == 1:
                forward = right
            else:
                forward = [right[f] + coupling * value[f] for f in range(3)]
            if z < nz - 1:
                inverse, spike = inverse_ref[z], e_ref[z]
                value = [forward[f] * inverse for f in range(3)]
                g_u = [g_u[f] + spike * forward[f] for f in range(3)]
                for f in range(3):
                    d2_ref[f, z] = value[f]
                coupling = lz_ref[z] * open_after(cut_ref, z + 1)
    slabs = g_u + forward
    for q, slab in enumerate(slabs):
        own2_ref[q] = slab
    Message(SECOND_COUNT, 1, nx, ny).write(next_ref, slabs)


def final_kernel(stages, cut_ref, *refs):
    own_ref, siblings, message_ref = refs[0], refs[1:stages], refs[stages]
    refs = refs[stages + 1 :]
    lx_ref, ly_ref, lz_ref, source_ref, centre_ref, d2_ref, e_ref, inverse_ref = refs[:8]
    factor_ref, end_ref, pressure_ref, residual_ref, second_ref = refs[8:]
    nz = lx_ref.shape[0]
    nx, ny = slab_size(lx_ref)
    own = [own_ref[q] for q in range(SECOND_COUNT)]
    slots = []

    def kept():
        slots.append(None)
        return factor_ref[len(slots) - 1]

    below = above = Message(3, 1, nx, ny).read(message_ref)
    for s in range(stages - 2, -1, -1):
        up = bit_of(s)
        block = [siblings[s][q] for q in range(SECOND_COUNT)]
        state = choose(up, below, above)
        far_g = choose(up, block[:3], block[3:])
        near_g = choose(up, block[3:], block[:3])
        step, factor = kept(), kept()
        right = [a + step * b for a, b in zip(far_g, state)]
        state = [n - factor * r for n, r in zip(near_g, right)]
        below, above = choose(up, state, below), choose(up, above, state)
    step_b, held_b, step_a, held_a = kept(), kept(), kept(), kept()
    inverse_u, factor, inverse_v = kept(), kept(), kept()
    for f in range(3):
        right_u = own[f] + step_b * below[f]
        right_v = own[3 + f] + step_a * above[f]
        last = (right_v - factor * right_u) * inverse_v
        first_u = right_u * inverse_u - factor * last
        second_ref[f, 0] = below[f] * held_b + step_b * first_u
        second_ref[f, nz + 1] = above[f] * held_a + step_a * last
        second_ref[f, 1] = first_u
        second_ref[f, nz] = last
    for z in range(nz - 2, 0, -1):
        ratio = lz_ref[z] * open_after(cut_ref, z + 1) * inverse_ref[z]
        spike = e_ref[z]
        for f in range(3):
            second_ref[f, z + 1] = (
                d2_ref[f, z] + spike * second_ref[f, 1] + ratio * second_ref[f, z + 2]
            )
    own_part = (slice(0, nx), slice(0, ny))
    for z in range(nz):
        link_low = end_ref[0] if z == 0 else lz_ref[z - 1]
        link_high = end_ref[1] if z == nz - 1 else lz_ref[z]
        centre = centre_ref[z]
        if z == 0:
            centre = centre + end_ref[2]
        if z == nz - 1:
            centre = centre + end_ref[3]
        for f in range(3):
            origin = source_ref[f, z]
            if f == 2 and z == 0:
                origin = origin - end_ref[4]
            if f == 2 and z == nz - 1:
                origin = origin + end_ref[5]
            here = second_ref[f, z + 1]
            total = stencil(here, lx_ref[z], ly_ref[z]) + (
                link_low * second_ref[f, z] + link_high * second_ref[f, z + 2]
            )
            pressure_ref[f, z] = here[own_part]
            residual_ref[f, z] = (origin - centre * here + total)[own_part]


def kernel_call(kernel, outputs, operands, scratch=(), space=pltpu.VMEM, limit=24):
    return pl.pallas_call(
        kernel,
        out_shape=[jax.ShapeDtypeStruct(s, t) for s, t in outputs],
        in_specs=[pl.BlockSpec(memory_space=space)] * len(operands),
        out_specs=[pl.BlockSpec(memory_space=pltpu.VMEM)] * len(outputs),
        scratch_shapes=list(scratch),
        compiler_params=pltpu.CompilerParams(vmem_limit_bytes=limit * 2**20),
    )(*operands)


def swapped(values, stage):
    size = lax.axis_size("gz")
    return lax.ppermute(values, "gz", [(i, i ^ 2**stage) for i in range(size)])


def ring(values, axis, distance):
    size = lax.axis_size(axis)
    return lax.ppermute(values, axis, [(i, (i + distance) % size) for i in range(size)])


def diagonal(values, x_distance, y_distance):
    nx, ny = lax.axis_size("gx"), lax.axis_size("gy")
    route = []
    for i in range(nx):
        for j in range(ny):
            target = ((i + x_distance) % nx) * ny + (j + y_distance) % ny
            route.append((i * ny + j, target))
    return lax.ppermute(values, ("gx", "gy"), route)


def per_device(facies, perm_table, line_breaks):
    nz, nx, ny = facies.shape
    stages = (lax.axis_size("gz") - 1).bit_length()
    i32, f32 = jnp.int32, jnp.float32
    two = lax.axis_size("gx") == 2
    cut_rows = -(-(nz + 1 + 2 * stages) // 8) * 8
    facies, table, cuts, strip, *rows = kernel_call(
        functools.partial(pack_kernel, stages),
        [((nz, nx, ny), i32), ((3, 8, ny), f32), ((cut_rows, ny), f32), ((nx, ny), i32)]
        + [((nz * WIDE, ny), i32)] * (1 if two else 2),
        [facies, perm_table, line_breaks],
        [
            pltpu.SMEM(perm_table.shape, f32),
            pltpu.SMEM(line_breaks.shape, i32),
            pltpu.SemaphoreType.DMA((3,)),
        ],
        pltpu.HBM,
        PACK_LIMIT,
    )
    y_low, y_high = ring(strip, "gy", 1), ring(strip, "gy", -1)
    if two:
        row_low = row_high = ring(rows[0], "gx", 1)
        low_low = low_high = diagonal(strip, 1, 1)
        high_low = high_high = diagonal(strip, 1, -1)
    else:
        row_low, row_high = ring(rows[1], "gx", 1), ring(rows[0], "gx", -1)
        low_low, low_high = diagonal(strip, 1, 1), diagonal(strip, -1, 1)
        high_low, high_high = diagonal(strip, 1, -1), diagonal(strip, -1, -1)

    slab = (nx + 8, 2 * ny)
    one, three = ((nz,) + slab, f32), ((3, nz) + slab, f32)

    def slabs(count):
        return ((count,) + slab, f32)

    def message_of(count, halo):
        return ((Message(count, halo, nx, ny).rows, ny), f32)

    message, own, lx, ly, lz, source, centre, d, e, inverse = kernel_call(
        eliminate_kernel,
        [message_of(FIRST_COUNT, 2), slabs(FIRST_COUNT)]
        + [one] * 3 + [three, one, three, one, one],
        [table, cuts, facies, row_low, row_high, y_low, y_high,
         low_low, low_high, high_low, high_high],
        [pltpu.VMEM((nz, 8, ny), i32)],
    )
    siblings, factors, group = [], [], own
    for s in range(stages - 1):
        last = s == stages - 2
        outputs = [slabs(FIRST_COUNT), slabs(5), message_of(LAST_COUNT if last else FIRST_COUNT, 2)]
        sibling, factor, message, *joined = kernel_call(
            functools.partial(join_kernel, s, last, nz),
            outputs + ([] if last else [slabs(FIRST_COUNT)]),
            [cuts, group, swapped(message, s)],
        )
        siblings.append(sibling)
        factors.append(factor)
        group = None if last else joined[0]
    message, own, d2, kept, ends = kernel_call(
        functools.partial(middle_kernel, stages),
        [message_of(SECOND_COUNT, 1), slabs(SECOND_COUNT), three, slabs(2 * stages + 5), slabs(6)],
        [cuts, own] + siblings + [swapped(message, stages - 1)]
        + [lx, ly, lz, source, d, e, inverse],
        [pltpu.VMEM((3, nz + 2) + slab, f32)],
    )
    siblings, group = [], own
    for s in range(stages - 1):
        last = s == stages - 2
        outputs = [slabs(SECOND_COUNT), message_of(3 if last else SECOND_COUNT, 1)]
        sibling, message, *joined = kernel_call(
            functools.partial(join_again_kernel, s, last),
            outputs + ([] if last else [slabs(SECOND_COUNT)]),
            [group, swapped(message, s), factors[s]],
        )
        siblings.append(sibling)
        group = None if last else joined[0]
    out = ((3, nz, nx, ny), f32)
    pressure, residual = kernel_call(
        functools.partial(final_kernel, stages),
        [out, out],
        [cuts, own] + siblings + [swapped(message, stages - 1)]
        + [lx, ly, lz, source, centre, d2, e, inverse, kept, ends],
        [pltpu.VMEM((3, nz + 2) + slab, f32)],
    )
    return pressure, residual


def solution(mesh):
    return jax.shard_map(
        per_device,
        mesh=mesh,
        in_specs=(P("gz", "gx", "gy"), P(), P()),
        out_specs=(P(None, "gz", "gx", "gy"), P(None, "gz", "gx", "gy")),
        check_vma=False,
    )
```

time: 43.9 us -> 39.3 us (0.90)
  waiting for transfers between devices: 17 us -> 14.6 us
  Pallas kernels: 8.1 us -> 7.06 us
  local copies, waits for them, and re-layouts: 2.89 us -> 2.23 us
  starting transfers between devices: 15.1 us -> 14.5 us
    ppermute x9 -> x3, waiting for transfers between devices: 15.7 us -> 1.78 us  [ring(): lax.ppermute(values, axis, [(i, (i + distance) % size) for i in range(siz...]
    ppermute x0 -> x4, waiting for transfers between devices: none -> 11.5 us  [swapped(): lax.ppermute(values, 'gz', [(i, i ^ 2 ** stage) for i in range(size)])]
    ppermute x9 -> x3, starting transfers between devices: 13.3 us -> 4.58 us  [ring(): lax.ppermute(values, axis, [(i, (i + distance) % size) for i in range(siz...]
    ppermute x0 -> x4, starting transfers between devices: none -> 8.21 us  [swapped(): lax.ppermute(values, 'gz', [(i, i ^ 2 ** stage) for i in range(size)])]
    pallas_call x4 -> x6, Pallas kernels: 8.1 us -> 7.06 us  [kernel_call(): pl.pallas_call(kernel, out_shape=[jax.ShapeDtypeStruct(s, t) for s, t in...]
    unnamed x8 -> x6, local copies, waits for them, and re-layouts: 2.89 us -> 2.23 us
  transfers between devices with their start and end apart: 11 -> 9, of which waited for: 7 -> 7; matrix products, arithmetic and copies ran while one was open for 0% -> 0% of each run, Pallas kernels for 0% -> 0%
where the time goes in v2:
time: 39.3 us; the launch traced here: 39.1 us
  waiting for transfers between devices  14.6 us (37%)
  starting transfers between devices  14.5 us (37%)
  Pallas kernels  7.06 us (18%)
  local copies, waits for them, and re-layouts  2.23 us (6%)
  between operations  0.67 us (2%)
    ppermute x4, waiting for transfers between devices, swapped(): lax.ppermute(values, 'gz', [(i, i ^ 2 ** stage) for i in range(size)])  11.5 us
    ppermute x4, starting transfers between devices, swapped(): lax.ppermute(values, 'gz', [(i, i ^ 2 ** stage) for i in range(size)])  8.21 us
    pallas_call x6, Pallas kernels, kernel_call(): pl.pallas_call(kernel, out_shape=[jax.ShapeDtypeStruct(s, t) for s, t in...  7.06 us
    ppermute x3, starting transfers between devices, ring(): lax.ppermute(values, axis, [(i, (i + distance) % size) for i in range(siz...  4.58 us
    unnamed x6, local copies, waits for them, and re-layouts  2.23 us
    ppermute x3, waiting for transfers between devices, ring(): lax.ppermute(values, axis, [(i, (i + distance) % size) for i in range(siz...  1.78 us
    ppermute x2, starting transfers between devices, diagonal(): return lax.ppermute(values, ('gx', 'gy'), route)  1.75 us
    ppermute x2, waiting for transfers between devices, diagonal(): return lax.ppermute(values, ('gx', 'gy'), route)  1.3 us
  transfers between devices with their start and end apart: 9, of which 7 were waited for; matrix products, arithmetic and copies ran while one was open for 0% of the time, Pallas kernels for 0%

profile of v2, /device:TPU:0, one launch (start us, length us, event | category | flops | bytes accessed | tf_op | source)
XLA Modules:
  0.0 39.1 jit_solution(9795547463255776646)
XLA Ops:
  0.6 0.0 copy-start
  0.6 0.9 %copy-done = s32[16,16,128]{2,1,0:T(8,128)S(1)} copy-done((s32[16,16,128]{2,1,0:T(8,128)S(1)}, s32[16,16,128]{2,1,0:T(8,128)}, u32[]{:S(2)}) %copy-start) | copy-done | bytes 131096
  1.5 0.0 copy-start.1
  1.5 0.7 %copy-done.1 = f32[3,16]{1,0:T(4,128)S(1)} copy-done((f32[3,16]{1,0:T(4,128)S(1)}, f32[3,16]{1,0:T(4,128)}, u32[]{:S(2)}) %copy-start.1) | copy-done | bytes 216
  2.2 0.0 copy-start.2
  2.2 0.7 %copy-done.2 = s32[63]{0:T(128)S(1)} copy-done((s32[63]{0:T(128)S(1)}, s32[63]{0:T(128)}, u32[]{:S(2)}) %copy-start.2) | copy-done | bytes 276
  2.9 0.8 %shard_map.50 = (s32[16,16,128]{2,1,0:T(8,128)S(1)}, f32[3,8,128]{2,1,0:T(8,128)S(1)}, f32[24,128]{1,0:T(8,128)S(1)}, s32[16,128]{1,0:T(8,128)S(1)}, s32[48,128]{1,0:T(8,128)S(1)}) custom-call(s32[16,16,128]{2,1,0:T(8,128)S(1)} %copy-done, f32[3,16]{1,0:T(4,128)S(1)} %copy-done.1, s32[63]{0:T(128)S(1)} %copy-done.2), custom_call_target="tpu_custom_call" | custom-call | tf_op jit(solution)/shard_map/pallas_call | solution.py:554
  3.7 3.0 %collective-permute-start = (s32[48,128]{1,0:T(8,128)S(1)}, s32[48,128]{1,0:T(8,128)S(1)}, u32[]{:S(2)}, u32[]{:S(2)}) collective-permute-start(s32[48,128]{1,0:T(8,128)S(1)} %get-tuple-element.30), channel_id=1, source_target_pairs={{0,16},{16,0},{1,17},{17,1},{2,18},{18,2},{3,19},{19,3},{4,20},{20... | collective-permute-start | bytes 73736 | tf_op jit(solution)/shard_map/ppermute | solution.py:571
  6.7 0.7 %collective-permute-start.4 = (s32[16,128]{1,0:T(8,128)S(1)}, s32[16,128]{1,0:T(8,128)S(1)}, u32[]{:S(2)}, u32[]{:S(2)}) collective-permute-start(s32[16,128]{1,0:T(8,128)S(1)} %get-tuple-element.31), channel_id=1, source_target_pairs={{0,28},{4,16},{8,20},{12,24},{16,12},{20,0},{24,4},{28,8},{1,29},{... | collective-permute-start | bytes 24584 | tf_op jit(solution)/shard_map/ppermute | solution.py:581
  7.3 1.1 %collective-permute-start.3 = (s32[16,128]{1,0:T(8,128)S(1)}, s32[16,128]{1,0:T(8,128)S(1)}, u32[]{:S(2)}, u32[]{:S(2)}) collective-permute-start(s32[16,128]{1,0:T(8,128)S(1)} %get-tuple-element.31), channel_id=1, source_target_pairs={{0,20},{4,24},{8,28},{12,16},{16,4},{20,8},{24,12},{28,0},{1,21},{... | collective-permute-start | bytes 24584 | tf_op jit(solution)/shard_map/ppermute | solution.py:581
  8.4 1.6 %collective-permute-start.2 = (s32[16,128]{1,0:T(8,128)S(1)}, s32[16,128]{1,0:T(8,128)S(1)}, u32[]{:S(2)}, u32[]{:S(2)}) collective-permute-start(s32[16,128]{1,0:T(8,128)S(1)} %get-tuple-element.31), channel_id=1, source_target_pairs={{0,12},{4,0},{8,4},{12,8},{1,13},{5,1},{9,5},{13,9},{2,14},{6,2},{... | collective-permute-start | bytes 24584 | tf_op jit(solution)/shard_map/ppermute | solution.py:571
  10.0 0.0 collective-permute-start.1
  10.0 0.0 collective-permute-done.4.high_low.high_high
  10.0 1.3 %collective-permute-done.3.low_low.low_high = s32[16,128]{1,0:T(8,128)S(1)} collective-permute-done((s32[16,128]{1,0:T(8,128)S(1)}, s32[16,128]{1,0:T(8,128)S(1)}, u32[]{:S(2)}, u32[]{:S(2)}) %collective-permute-start.3) | collective-permute-done | bytes 8224 | tf_op jit(solution)/shard_map/ppermute | solution.py:581
  11.3 0.1 collective-permute-done.2.y_high
  11.4 1.7 %collective-permute-done.1.y_low = s32[16,128]{1,0:T(8,128)S(1)} collective-permute-done((s32[16,128]{1,0:T(8,128)S(1)}, s32[16,128]{1,0:T(8,128)S(1)}, u32[]{:S(2)}, u32[]{:S(2)}) %collective-permute-start.1) | collective-permute-done | bytes 8224 | tf_op jit(solution)/shard_map/ppermute | solution.py:571
  13.1 0.0 collective-permute-done.row_low.row_high
  13.1 3.0 %shard_map.51 = (f32[224,128]{1,0:T(8,128)S(1)}, f32[11,24,256]{2,1,0:T(8,128)S(1)}, f32[16,24,256]{2,1,0:T(8,128)S(1)}, f32[16,24,256]{2,1,0:T(8,128)S(1)}, f32...) custom-call(f32[3,8,128]{2,1,0:T(8,128)S(1)} %get-tuple-element.28.t, ...), custom_call_target="tpu_custom_call" | custom-call | tf_op jit(solution)/shard_map/pallas_call | solution.py:554
  16.1 1.6 %collective-permute-start.5 = (f32[224,128]{1,0:T(8,128)S(1)}, f32[224,128]{1,0:T(8,128)S(1)}, u32[]{:S(2)}, u32[]{:S(2)}) collective-permute-start(f32[224,128]{1,0:T(8,128)S(1)} %get-tuple-element.33), channel_id=1, source_target_pairs={{0,1},{1,0},{2,3},{3,2},{4,5},{5,4},{6,7},{7,6},{8,9},{9,8},{10,11... | collective-permute-start | bytes 344072 | tf_op jit(solution)/shard_map/ppermute | solution.py:566
  17.7 3.2 %collective-permute-done.5.message_ref = f32[224,128]{1,0:T(8,128)S(1)} collective-permute-done((f32[224,128]{1,0:T(8,128)S(1)}, f32[224,128]{1,0:T(8,128)S(1)}, u32[]{:S(2)}, u32[]{:S(2)}) %collective-permute-start.5) | collective-permute-done | bytes 114720 | tf_op jit(solution)/shard_map/ppermute | solution.py:566
  20.9 0.2 shard_map.52
  21.1 2.7 %collective-permute-start.6 = (f32[120,128]{1,0:T(8,128)S(1)}, f32[120,128]{1,0:T(8,128)S(1)}, u32[]{:S(2)}, u32[]{:S(2)}) collective-permute-start(f32[120,128]{1,0:T(8,128)S(1)} %get-tuple-element.35), channel_id=1, source_target_pairs={{0,2},{1,3},{2,0},{3,1},{4,6},{5,7},{6,4},{7,5},{8,10},{9,11},{10,... | collective-permute-start | bytes 184328 | tf_op jit(solution)/shard_map/ppermute | solution.py:566
  23.8 2.5 %collective-permute-done.6.refs_2_ = f32[120,128]{1,0:T(8,128)S(1)} collective-permute-done((f32[120,128]{1,0:T(8,128)S(1)}, f32[120,128]{1,0:T(8,128)S(1)}, u32[]{:S(2)}, u32[]{:S(2)}) %collective-permute-start.6) | collective-permute-done | bytes 61472 | tf_op jit(solution)/shard_map/ppermute | solution.py:566
  26.3 1.5 %shard_map.53 = (f32[128,128]{1,0:T(8,128)S(1)}, f32[6,24,256]{2,1,0:T(8,128)S(1)}, f32[3,16,24,256]{3,2,1,0:T(8,128)S(1)}, f32[9,24,256]{2,1,0:T(8,128)S(1)}, f32[6,24,256]{2,1,0:T(8,128)S(1)}) custom-call(f32[24,128]{1,0:T(8,128)S(1)} %get-tuple-element.27.cut_ref, f32[11,24,256]{2,1,0:T(8,128)S(1)} %get-tuple-element.32.own_ref.refs_0_, ...), custom_call_target="tpu_custom_call" | custom-call | tf_op jit(solution)/shard_map/pallas_call | solution.py:554
  27.8 1.6 %collective-permute-start.7 = (f32[128,128]{1,0:T(8,128)S(1)}, f32[128,128]{1,0:T(8,128)S(1)}, u32[]{:S(2)}, u32[]{:S(2)}) collective-permute-start(f32[128,128]{1,0:T(8,128)S(1)} %get-tuple-element.44), channel_id=1, source_target_pairs={{0,1},{1,0},{2,3},{3,2},{4,5},{5,4},{6,7},{7,6},{8,9},{9,8},{10,11... | collective-permute-start | bytes 196616 | tf_op jit(solution)/shard_map/ppermute | solution.py:566
  29.4 3.1 %collective-permute-done.7.message_ref = f32[128,128]{1,0:T(8,128)S(1)} collective-permute-done((f32[128,128]{1,0:T(8,128)S(1)}, f32[128,128]{1,0:T(8,128)S(1)}, u32[]{:S(2)}, u32[]{:S(2)}) %collective-permute-start.7) | collective-permute-done | bytes 65568 | tf_op jit(solution)/shard_map/ppermute | solution.py:566
  32.6 0.2 shard_map.54
  32.7 2.3 %collective-permute-start.8 = (f32[80,128]{1,0:T(8,128)S(1)}, f32[80,128]{1,0:T(8,128)S(1)}, u32[]{:S(2)}, u32[]{:S(2)}) collective-permute-start(f32[80,128]{1,0:T(8,128)S(1)} %get-tuple-element.47), channel_id=1, source_target_pairs={{0,2},{1,3},{2,0},{3,1},{4,6},{5,7},{6,4},{7,5},{8,10},{9,11},{10,... | collective-permute-start | bytes 122888 | tf_op jit(solution)/shard_map/ppermute | solution.py:566
  35.0 2.6 %collective-permute-done.8.refs_2_ = f32[80,128]{1,0:T(8,128)S(1)} collective-permute-done((f32[80,128]{1,0:T(8,128)S(1)}, f32[80,128]{1,0:T(8,128)S(1)}, u32[]{:S(2)}, u32[]{:S(2)}) %collective-permute-start.8) | collective-permute-done | bytes 40992 | tf_op jit(solution)/shard_map/ppermute | solution.py:566
  37.7 1.4 %shard_map.55 = (f32[3,16,16,128]{3,2,1,0:T(8,128)}, f32[3,16,16,128]{3,2,1,0:T(8,128)}) custom-call(f32[24,128]{1,0:T(8,128)S(1)} %get-tuple-element.27.cut_ref, f32[6,24,256]{2,1,0:T(8,128)S(1)} %get-tuple-element.43.own_ref.refs_0_, f32[6,24,256]{2,1,0:T(8,128)S(1)} %get-tuple-element.46.refs_1_, f32[80,128]{1,0:T(8,128)S(1)} %collective-permute-done.8.refs_2_, ...), custom_call_target="tpu_custom_call" | custom-call | tf_op jit(solution)/shard_map/pallas_call | solution.py:554
Async XLA Ops:
  0.6 0.9 %copy-start = (s32[16,16,128]{2,1,0:T(8,128)S(1)}, s32[16,16,128]{2,1,0:T(8,128)}, u32[]{:S(2)}) copy-start(s32[16,16,128]{2,1,0:T(8,128)} %facies_in.1) | copy-start | bytes 393220
  1.5 0.7 %copy-start.1 = (f32[3,16]{1,0:T(4,128)S(1)}, f32[3,16]{1,0:T(4,128)}, u32[]{:S(2)}) copy-start(f32[3,16]{1,0:T(4,128)} %table_in.1) | copy-start | bytes 580
  2.2 0.7 %copy-start.2 = (s32[63]{0:T(128)S(1)}, s32[63]{0:T(128)}, u32[]{:S(2)}) copy-start(s32[63]{0:T(128)} %breaks_in.1) | copy-start | bytes 760
  3.7 9.4 %collective-permute-start = (s32[48,128]{1,0:T(8,128)S(1)}, s32[48,128]{1,0:T(8,128)S(1)}, u32[]{:S(2)}, u32[]{:S(2)}) collective-permute-start(s32[48,128]{1,0:T(8,128)S(1)} %get-tuple-element.30), channel_id=1, source_target_pairs={{0,16},{16,0},{1,17},{17,1},{2,18},{18,2},{3,19},{19,3},{4,20},{20... | collective-permute-start | bytes 73736 | tf_op jit(solution)/shard_map/ppermute | solution.py:571
  6.7 3.3 %collective-permute-start.4 = (s32[16,128]{1,0:T(8,128)S(1)}, s32[16,128]{1,0:T(8,128)S(1)}, u32[]{:S(2)}, u32[]{:S(2)}) collective-permute-start(s32[16,128]{1,0:T(8,128)S(1)} %get-tuple-element.31), channel_id=1, source_target_pairs={{0,28},{4,16},{8,20},{12,24},{16,12},{20,0},{24,4},{28,8},{1,29},{... | collective-permute-start | bytes 24584 | tf_op jit(solution)/shard_map/ppermute | solution.py:581
  7.3 4.0 %collective-permute-start.3 = (s32[16,128]{1,0:T(8,128)S(1)}, s32[16,128]{1,0:T(8,128)S(1)}, u32[]{:S(2)}, u32[]{:S(2)}) collective-permute-start(s32[16,128]{1,0:T(8,128)S(1)} %get-tuple-element.31), channel_id=1, source_target_pairs={{0,20},{4,24},{8,28},{12,16},{16,4},{20,8},{24,12},{28,0},{1,21},{... | collective-permute-start | bytes 24584 | tf_op jit(solution)/shard_map/ppermute | solution.py:581
  8.4 2.9 %collective-permute-start.2 = (s32[16,128]{1,0:T(8,128)S(1)}, s32[16,128]{1,0:T(8,128)S(1)}, u32[]{:S(2)}, u32[]{:S(2)}) collective-permute-start(s32[16,128]{1,0:T(8,128)S(1)} %get-tuple-element.31), channel_id=1, source_target_pairs={{0,12},{4,0},{8,4},{12,8},{1,13},{5,1},{9,5},{13,9},{2,14},{6,2},{... | collective-permute-start | bytes 24584 | tf_op jit(solution)/shard_map/ppermute | solution.py:571
  10.0 3.1 %collective-permute-start.1 = (s32[16,128]{1,0:T(8,128)S(1)}, s32[16,128]{1,0:T(8,128)S(1)}, u32[]{:S(2)}, u32[]{:S(2)}) collective-permute-start(s32[16,128]{1,0:T(8,128)S(1)} %get-tuple-element.31), channel_id=1, source_target_pairs={{0,4},{4,8},{8,12},{12,0},{1,5},{5,9},{9,13},{13,1},{2,6},{6,10},{... | collective-permute-start | bytes 24584 | tf_op jit(solution)/shard_map/ppermute | solution.py:571
  16.1 4.9 %collective-permute-start.5 = (f32[224,128]{1,0:T(8,128)S(1)}, f32[224,128]{1,0:T(8,128)S(1)}, u32[]{:S(2)}, u32[]{:S(2)}) collective-permute-start(f32[224,128]{1,0:T(8,128)S(1)} %get-tuple-element.33), channel_id=1, source_target_pairs={{0,1},{1,0},{2,3},{3,2},{4,5},{5,4},{6,7},{7,6},{8,9},{9,8},{10,11... | collective-permute-start | bytes 344072 | tf_op jit(solution)/shard_map/ppermute | solution.py:566
  21.1 5.2 %collective-permute-start.6 = (f32[120,128]{1,0:T(8,128)S(1)}, f32[120,128]{1,0:T(8,128)S(1)}, u32[]{:S(2)}, u32[]{:S(2)}) collective-permute-start(f32[120,128]{1,0:T(8,128)S(1)} %get-tuple-element.35), channel_id=1, source_target_pairs={{0,2},{1,3},{2,0},{3,1},{4,6},{5,7},{6,4},{7,5},{8,10},{9,11},{10,... | collective-permute-start | bytes 184328 | tf_op jit(solution)/shard_map/ppermute | solution.py:566
  27.8 4.7 %collective-permute-start.7 = (f32[128,128]{1,0:T(8,128)S(1)}, f32[128,128]{1,0:T(8,128)S(1)}, u32[]{:S(2)}, u32[]{:S(2)}) collective-permute-start(f32[128,128]{1,0:T(8,128)S(1)} %get-tuple-element.44), channel_id=1, source_target_pairs={{0,1},{1,0},{2,3},{3,2},{4,5},{5,4},{6,7},{7,6},{8,9},{9,8},{10,11... | collective-permute-start | bytes 196616 | tf_op jit(solution)/shard_map/ppermute | solution.py:566
  32.7 5.0 %collective-permute-start.8 = (f32[80,128]{1,0:T(8,128)S(1)}, f32[80,128]{1,0:T(8,128)S(1)}, u32[]{:S(2)}, u32[]{:S(2)}) collective-permute-start(f32[80,128]{1,0:T(8,128)S(1)} %get-tuple-element.47), channel_id=1, source_target_pairs={{0,2},{1,3},{2,0},{3,1},{4,6},{5,7},{6,4},{7,5},{8,10},{9,11},{10,... | collective-permute-start | bytes 122888 | tf_op jit(solution)/shard_map/ppermute | solution.py:566

commit v3 on v2

--- a/solution.py
+++ b/solution.py
@@ -12,7 +12,6 @@
 FIRST_COUNT = 11
 LAST_COUNT = 5
 SECOND_COUNT = 6
-PACK_LIMIT = 24
 
 
 def moved(values, amount, axis):
@@ -39,39 +38,45 @@
     return (lax.axis_index("gz") >> stage) % 2 == 1
 
 
-def pack_kernel(stages, facies_in, table_in, breaks_in, facies_ref, table_ref, cut_ref, strip_ref, *refs):
-    row_refs, (table, breaks, sems) = refs[:-3], refs[-3:]
+def pack_kernel(facies_ref, strip_ref, *row_refs):
     nz, nx, ny = facies_ref.shape
-    copies = [
-        pltpu.make_async_copy(facies_in, facies_ref, sems.at[0]),
-        pltpu.make_async_copy(table_in, table, sems.at[1]),
-        pltpu.make_async_copy(breaks_in, breaks, sems.at[2]),
-    ]
-    for copy in copies:
-        copy.start()
-    copies[0].wait()
     lane = lax.broadcasted_iota(jnp.int32, (nx, ny), 1)
     strip = jnp.zeros((nx, ny), jnp.int32)
     for z in range(nz):
         strip = jnp.where(lane // 8 == z, moved(facies_ref[z], 8 * z + WIDE, 1), strip)
     strip_ref[...] = strip
     for z in range(nz):
-        leading = facies_ref[z, 0:WIDE, :]
-        last = facies_ref[z, nx - WIDE : nx, :]
-        spot = slice(z * WIDE, (z + 1) * WIDE)
-        if len(row_refs) == 1:
-            row_refs[0][spot, :] = jnp.where(lax.axis_index("gx") == 0, last, leading)
-        else:
-            row_refs[0][spot, :] = leading
-            row_refs[1][spot, :] = last
-    copies[1].wait()
-    copies[2].wait()
+        for i in range(WIDE):
+            leading = facies_ref[z, i : i + 1, :]
+            last = facies_ref[z, nx - WIDE + i : nx - WIDE + i + 1, :]
+            spot = slice(i * nz + z, i * nz + z + 1)
+            if len(row_refs) == 1:
+                row_refs[0][spot, :] = jnp.where(lax.axis_index("gx") == 0, last, leading)
+            else:
+                row_refs[0][spot, :] = leading
+                row_refs[1][spot, :] = last
+
+
+def lookup(table, index):
+    rows = [
+        jnp.take_along_axis(table, index[r : r + 8], axis=1) for r in range(0, index.shape[0], 8)
+    ]
+    return jnp.concatenate(rows, axis=0)
+
+
+def prepare_kernel(stages, table, breaks, facies_ref, strip_ref, k_ref, table_ref, cut_ref):
+    nz, nx, ny = facies_ref.shape
     lane = iotas(8, ny)[1]
+    tables = []
     for q in range(3):
         values = jnp.zeros((8, ny), jnp.float32)
         for label in range(table.shape[1]):
             values = jnp.where(lane == label, table[q, label], values)
         table_ref[q] = values
+        tables.append(values)
+    for z in range(nz):
+        for q in range(3):
+            k_ref[q, z] = lookup(tables[q], facies_ref[z])
     at_z = lax.axis_index("gz")
     layers = [at_z * nz + r - 1 for r in range(nz + 1)]
     for s in range(stages):
@@ -153,65 +158,54 @@
 
 
 def eliminate_kernel(
-    table_ref, cut_ref, facies_ref, row_low, row_high, y_low, y_high,
+    table_ref, cut_ref, k_ref, row_low, row_high, y_low, y_high,
     low_low, low_high, high_low, high_high,
     message_ref, own_ref, lx_ref, ly_ref, lz_ref, source_ref, centre_ref,
-    d_ref, e_ref, inverse_ref, side_ref,
+    d_ref, e_ref, inverse_ref, low_ref, high_ref,
 ):
-    nz, nx, ny = facies_ref.shape
-    outside = ny - 1
+    nz, nx, ny = k_ref.shape[1:]
     at_x, at_y = lax.axis_index("gx"), lax.axis_index("gy")
     has_x_low, has_x_high = at_x > 0, at_x < lax.axis_size("gx") - 1
     has_y_low, has_y_high = at_y > 0, at_y < lax.axis_size("gy") - 1
     tables = [table_ref[q] for q in range(3)]
 
-    side_ref[...] = jnp.full(side_ref.shape, outside, jnp.int32)
-    for z in range(nz):
-        spot = slice(z * WIDE, (z + 1) * WIDE)
-        side_ref[z, 0:WIDE, :] = jnp.where(has_x_high, row_high[spot, :], outside)
-        side_ref[z, 8 - WIDE : 8, :] = jnp.where(has_x_low, row_low[spot, :], outside)
-
-    def corner(high_ref, low_ref):
-        row = iotas(8, ny)[0]
-        high = jnp.where(has_x_high, high_ref[0:8, :], outside)
-        low = jnp.where(has_x_low, low_ref[nx - 8 : nx, :], outside)
-        middle = jnp.where(row >= 8 - WIDE, low, outside)
-        return jnp.where(row < WIDE, high, middle)
+    row, lane = iotas(nx + 8, 2 * ny)
+    x_in = (row < nx) | ((row < nx + WIDE) & has_x_high) | ((row >= nx + 8 - WIDE) & has_x_low)
+    y_in = (lane < ny) | ((lane < ny + WIDE) & has_y_high)
+    y_in = y_in | ((lane >= 2 * ny - WIDE) & has_y_low)
+    cell = x_in & y_in
+    valid = flag(cell)
+    in_x, in_xp = valid * moved(valid, -1, 0), valid * moved(valid, 1, 0)
+    in_y, in_yp = valid * moved(valid, -1, 1), valid * moved(valid, 1, 1)
+    row_in, strip_in = cell[nx:, :ny], cell[:, ny:]
+
+    row = iotas(8, ny)[0]
+    lane = iotas(nx + 8, ny)[1]
+
+    def corner(high, low):
+        return jnp.where(row < WIDE, high[0:8, :], low[nx - 8 : nx, :])
 
     before = jnp.concatenate([y_low[...], corner(low_high, low_low)], axis=0)
     after = jnp.concatenate([y_high[...], corner(high_high, high_low)], axis=0)
-    lane = iotas(nx + 8, ny)[1]
-    strip = jnp.where(
-        lane % 8 < WIDE,
-        jnp.where(has_y_low, before, outside),
-        jnp.where(has_y_high, after, outside),
-    )
-    near = (lane < WIDE) | (lane >= ny - WIDE)
-
-    def labels(z):
-        beside = jnp.where(near, moved(strip, -(8 * z + WIDE), 1), outside)
-        return jnp.concatenate(
-            [jnp.concatenate([facies_ref[z], side_ref[z]], axis=0), beside], axis=1
-        )
-
-    def lookup(table, index):
-        rows = []
-        for r in range(0, nx + 8, 8):
-            parts = [
-                jnp.take_along_axis(table, index[r : r + 8, c : c + ny], axis=1)
-                for c in (0, ny)
-            ]
-            rows.append(jnp.concatenate(parts, axis=1))
-        return jnp.concatenate(rows, axis=0)
-
-    def coefficients(label):
-        return [lookup(table, label) for table in tables]
-
-    label = labels(0)
-    valid = flag(label != outside)
-    cell = valid > 0.0
-    in_x, in_xp = valid * moved(valid, -1, 0), valid * moved(valid, 1, 0)
-    in_y, in_yp = valid * moved(valid, -1, 1), valid * moved(valid, 1, 1)
+    strip = jnp.where(lane % 8 < WIDE, before, after)
+    strips = [lookup(table, strip) for table in tables]
+    for q in range(3):
+        low_ref[q] = lookup(tables[q], row_low[...])
+        high_ref[q] = lookup(tables[q], row_high[...])
+
+    def coefficients(z):
+        out = []
+        for q in range(3):
+            side = jnp.zeros((8, ny), jnp.float32)
+            for i in range(WIDE):
+                spot = slice(i * nz + z, i * nz + z + 1)
+                side = jnp.where(row == i, high_ref[q, spot, :], side)
+                side = jnp.where(row == 8 - WIDE + i, low_ref[q, spot, :], side)
+            side = jnp.where(row_in, side, 0.0)
+            body = jnp.concatenate([k_ref[q, z], side], axis=0)
+            beside = jnp.where(strip_in, moved(strips[q], -(8 * z + WIDE), 1), 0.0)
+            out.append(jnp.concatenate([body, beside], axis=1))
+        return out
 
     def side_faces(here, axis, inside, inside_back):
         there = moved(here, -1, axis)
@@ -221,7 +215,7 @@
         tau = flow * (2.0 - inside) + flow_back * (2.0 - inside_back)
         return flow * inside, tau, flow - flow_back
 
-    next_k = coefficients(label)
+    next_k = coefficients(0)
     link_below = None
     for z in range(nz):
         kx, ky, kz = next_k
@@ -233,7 +227,7 @@
         if z == 0:
             kz_first = kz
         if z < nz - 1:
-            next_k = coefficients(labels(z + 1))
+            next_k = coefficients(z + 1)
             above = next_k[2]
             link_z = jnp.where(cell, 2.0 * (kz * above) / (kz + above), 0.0)
             lz_ref[z] = link_z
@@ -550,14 +544,17 @@
             residual_ref[f, z] = (origin - centre * here + total)[own_part]
 
 
-def kernel_call(kernel, outputs, operands, scratch=(), space=pltpu.VMEM, limit=24):
+def kernel_call(kernel, outputs, operands, scratch=(), smem=0, cost=None):
+    specs = [pl.BlockSpec(memory_space=pltpu.SMEM)] * smem
+    specs += [pl.BlockSpec(memory_space=pltpu.VMEM)] * (len(operands) - smem)
     return pl.pallas_call(
         kernel,
         out_shape=[jax.ShapeDtypeStruct(s, t) for s, t in outputs],
-        in_specs=[pl.BlockSpec(memory_space=space)] * len(operands),
+        in_specs=specs,
         out_specs=[pl.BlockSpec(memory_space=pltpu.VMEM)] * len(outputs),
         scratch_shapes=list(scratch),
-        compiler_params=pltpu.CompilerParams(vmem_limit_bytes=limit * 2**20),
+        compiler_params=pltpu.CompilerParams(vmem_limit_bytes=24 * 2**20),
+        cost_estimate=cost,
     )(*operands)
 
 
@@ -587,18 +584,17 @@
     i32, f32 = jnp.int32, jnp.float32
     two = lax.axis_size("gx") == 2
     cut_rows = -(-(nz + 1 + 2 * stages) // 8) * 8
-    facies, table, cuts, strip, *rows = kernel_call(
-        functools.partial(pack_kernel, stages),
-        [((nz, nx, ny), i32), ((3, 8, ny), f32), ((cut_rows, ny), f32), ((nx, ny), i32)]
-        + [((nz * WIDE, ny), i32)] * (1 if two else 2),
-        [facies, perm_table, line_breaks],
-        [
-            pltpu.SMEM(perm_table.shape, f32),
-            pltpu.SMEM(line_breaks.shape, i32),
-            pltpu.SemaphoreType.DMA((3,)),
-        ],
-        pltpu.HBM,
-        PACK_LIMIT,
+    strip, *rows = kernel_call(
+        pack_kernel,
+        [((nx, ny), i32)] + [((nz * WIDE, ny), i32)] * (1 if two else 2),
+        [facies],
+    )
+    k, table, cuts = kernel_call(
+        functools.partial(prepare_kernel, stages),
+        [((3, nz, nx, ny), f32), ((3, 8, ny), f32), ((cut_rows, ny), f32)],
+        [perm_table, line_breaks, facies, strip],
+        smem=2,
+        cost=pl.CostEstimate(flops=10**7, bytes_accessed=10**6, transcendentals=0),
     )
     y_low, y_high = ring(strip, "gy", 1), ring(strip, "gy", -1)
     if two:
@@ -623,9 +619,9 @@
         eliminate_kernel,
         [message_of(FIRST_COUNT, 2), slabs(FIRST_COUNT)]
         + [one] * 3 + [three, one, three, one, one],
-        [table, cuts, facies, row_low, row_high, y_low, y_high,
+        [table, cuts, k, row_low, row_high, y_low, y_high,
          low_low, low_high, high_low, high_high],
-        [pltpu.VMEM((nz, 8, ny), i32)],
+        [pltpu.VMEM((3, nz * WIDE, ny), f32)] * 2,
     )
     siblings, factors, group = [], [], own
     for s in range(stages - 1):

time: 39.3 us -> 35.6 us (0.906)
  waiting for transfers between devices: 14.6 us -> 11.3 us
  Pallas kernels: 7.06 us -> 5.7 us
  starting transfers between devices: 14.5 us -> 15.3 us
    pallas_call x6 -> x7, Pallas kernels: 7.06 us -> 5.7 us  [kernel_call(): pl.pallas_call(kernel, out_shape=[jax.ShapeDtypeStruct(s, t) for s, t in...]
    ppermute x2, waiting for transfers between devices: 1.3 us -> 0.01 us  [diagonal(): return lax.ppermute(values, ('gx', 'gy'), route)]
    ppermute x4, waiting for transfers between devices: 11.5 us -> 10.5 us  [swapped(): lax.ppermute(values, 'gz', [(i, i ^ 2 ** stage) for i in range(size)])]
    ppermute x3, waiting for transfers between devices: 1.78 us -> 0.82 us  [ring(): lax.ppermute(values, axis, [(i, (i + distance) % size) for i in range(siz...]
    ppermute x4, starting transfers between devices: 8.21 us -> 8.98 us  [swapped(): lax.ppermute(values, 'gz', [(i, i ^ 2 ** stage) for i in range(size)])]
  transfers between devices with their start and end apart: 9 -> 9, of which waited for: 7 -> 5; matrix products, arithmetic and copies ran while one was open for 0% -> 0% of each run, Pallas kernels for 0% -> 3%
where the time goes in v3:
time: 35.6 us; the launch traced here: 35.2 us
  starting transfers between devices  15.3 us (43%)
  waiting for transfers between devices  11.3 us (32%)
  Pallas kernels  5.7 us (16%)
  local copies, waits for them, and re-layouts  2.23 us (6%)
  between operations  0.68 us (2%)
    ppermute x4, waiting for transfers between devices, swapped(): lax.ppermute(values, 'gz', [(i, i ^ 2 ** stage) for i in range(size)])  10.5 us
    ppermute x4, starting transfers between devices, swapped(): lax.ppermute(values, 'gz', [(i, i ^ 2 ** stage) for i in range(size)])  8.98 us
    pallas_call x7, Pallas kernels, kernel_call(): pl.pallas_call(kernel, out_shape=[jax.ShapeDtypeStruct(s, t) for s, t in...  5.7 us
    ppermute x3, starting transfers between devices, ring(): lax.ppermute(values, axis, [(i, (i + distance) % size) for i in range(siz...  4.58 us
    unnamed x6, local copies, waits for them, and re-layouts  2.23 us
    ppermute x2, starting transfers between devices, diagonal(): return lax.ppermute(values, ('gx', 'gy'), route)  1.75 us
    ppermute x3, waiting for transfers between devices, ring(): lax.ppermute(values, axis, [(i, (i + distance) % size) for i in range(siz...  0.82 us
  transfers between devices with their start and end apart: 9, of which 5 were waited for; matrix products, arithmetic and copies ran while one was open for 0% of the time, Pallas kernels for 3%

profile of v3, /device:TPU:0, one launch (start us, length us, event | category | flops | bytes accessed | tf_op | source)
XLA Modules:
  0.0 35.2 jit_solution(2483367975542317297)
XLA Ops:
  0.6 0.0 copy-start
  0.6 0.9 %copy-done = s32[16,16,128]{2,1,0:T(8,128)S(1)} copy-done((s32[16,16,128]{2,1,0:T(8,128)S(1)}, s32[16,16,128]{2,1,0:T(8,128)}, u32[]{:S(2)}) %copy-start) | copy-done | bytes 131096
  1.5 0.1 shard_map.50
  1.6 3.0 %collective-permute-start = (s32[48,128]{1,0:T(8,128)S(1)}, s32[48,128]{1,0:T(8,128)S(1)}, u32[]{:S(2)}, u32[]{:S(2)}) collective-permute-start(s32[48,128]{1,0:T(8,128)S(1)} %get-tuple-element.31), channel_id=1, source_target_pairs={{0,16},{16,0},{1,17},{17,1},{2,18},{18,2},{3,19},{19,3},{4,20},{20... | collective-permute-start | bytes 73736 | tf_op jit(solution)/shard_map/ppermute | solution.py:568
  4.6 0.7 %collective-permute-start.4 = (s32[16,128]{1,0:T(8,128)S(1)}, s32[16,128]{1,0:T(8,128)S(1)}, u32[]{:S(2)}, u32[]{:S(2)}) collective-permute-start(s32[16,128]{1,0:T(8,128)S(1)} %get-tuple-element.27.strip_ref), channel_id=1, source_target_pairs={{0,28},{4,16},{8,20},{12,24},{16,12},{20,0},{24,4},{28,8},{1,29},{... | collective-permute-start | bytes 24584 | tf_op jit(solution)/shard_map/ppermute | solution.py:578
  5.3 1.1 %collective-permute-start.3 = (s32[16,128]{1,0:T(8,128)S(1)}, s32[16,128]{1,0:T(8,128)S(1)}, u32[]{:S(2)}, u32[]{:S(2)}) collective-permute-start(s32[16,128]{1,0:T(8,128)S(1)} %get-tuple-element.27.strip_ref), channel_id=1, source_target_pairs={{0,20},{4,24},{8,28},{12,16},{16,4},{20,8},{24,12},{28,0},{1,21},{... | collective-permute-start | bytes 24584 | tf_op jit(solution)/shard_map/ppermute | solution.py:578
  6.4 1.6 %collective-permute-start.2 = (s32[16,128]{1,0:T(8,128)S(1)}, s32[16,128]{1,0:T(8,128)S(1)}, u32[]{:S(2)}, u32[]{:S(2)}) collective-permute-start(s32[16,128]{1,0:T(8,128)S(1)} %get-tuple-element.27.strip_ref), channel_id=1, source_target_pairs={{0,12},{4,0},{8,4},{12,8},{1,13},{5,1},{9,5},{13,9},{2,14},{6,2},{... | collective-permute-start | bytes 24584 | tf_op jit(solution)/shard_map/ppermute | solution.py:568
  8.0 0.0 collective-permute-start.1
  8.0 0.0 copy-start.1
  8.0 0.7 %copy-done.1 = f32[3,16]{1,0:T(4,128)S(1)} copy-done((f32[3,16]{1,0:T(4,128)S(1)}, f32[3,16]{1,0:T(4,128)}, u32[]{:S(2)}) %copy-start.1) | copy-done | bytes 216
  8.6 0.0 copy-start.2
  8.6 0.7 %copy-done.2 = s32[63]{0:T(128)S(1)} copy-done((s32[63]{0:T(128)S(1)}, s32[63]{0:T(128)}, u32[]{:S(2)}) %copy-start.2) | copy-done | bytes 276
  9.3 0.9 %shard_map.51 = (f32[3,16,16,128]{3,2,1,0:T(8,128)S(1)}, f32[3,8,128]{2,1,0:T(8,128)S(1)}, f32[24,128]{1,0:T(8,128)S(1)}) custom-call(f32[3,16]{1,0:T(4,128)S(1)} %copy-done.1, s32[63]{0:T(128)S(1)} %copy-done.2, s32[16,16,128]{2,1,0:T(8,128)S(1)} %copy-done, s32[16,128]{1,0:T(8,128)S(1)} %get-tuple-element.27.strip_ref), custom_call_target="tpu_custom_call" | custom-call | flops 10000000 | bytes 1000000 | tf_op jit(solution)/shard_map/pallas_call | solution.py:550
  10.2 0.0 collective-permute-done.4.high_low.high_high
  10.2 0.0 collective-permute-done.3.low_low.low_high
  10.2 0.0 collective-permute-done.2.y_high
  10.2 0.8 %collective-permute-done.1.y_low = s32[16,128]{1,0:T(8,128)S(1)} collective-permute-done((s32[16,128]{1,0:T(8,128)S(1)}, s32[16,128]{1,0:T(8,128)S(1)}, u32[]{:S(2)}, u32[]{:S(2)}) %collective-permute-start.1) | collective-permute-done | bytes 8224 | tf_op jit(solution)/shard_map/ppermute | solution.py:568
  11.0 0.0 collective-permute-done.row_low.row_high
  11.0 1.4 %shard_map.52 = (f32[224,128]{1,0:T(8,128)S(1)}, f32[11,24,256]{2,1,0:T(8,128)S(1)}, f32[16,24,256]{2,1,0:T(8,128)S(1)}, f32[16,24,256]{2,1,0:T(8,128)S(1)}, f32...) custom-call(f32[3,8,128]{2,1,0:T(8,128)S(1)} %get-tuple-element.29.t, ...), custom_call_target="tpu_custom_call" | custom-call | tf_op jit(solution)/shard_map/pallas_call | solution.py:550
  12.5 1.6 %collective-permute-start.5 = (f32[224,128]{1,0:T(8,128)S(1)}, f32[224,128]{1,0:T(8,128)S(1)}, u32[]{:S(2)}, u32[]{:S(2)}) collective-permute-start(f32[224,128]{1,0:T(8,128)S(1)} %get-tuple-element.33), channel_id=1, source_target_pairs={{0,1},{1,0},{2,3},{3,2},{4,5},{5,4},{6,7},{7,6},{8,9},{9,8},{10,11... | collective-permute-start | bytes 344072 | tf_op jit(solution)/shard_map/ppermute | solution.py:563
  14.1 3.3 %collective-permute-done.5.message_ref = f32[224,128]{1,0:T(8,128)S(1)} collective-permute-done((f32[224,128]{1,0:T(8,128)S(1)}, f32[224,128]{1,0:T(8,128)S(1)}, u32[]{:S(2)}, u32[]{:S(2)}) %collective-permute-start.5) | collective-permute-done | bytes 114720 | tf_op jit(solution)/shard_map/ppermute | solution.py:563
  17.4 0.2 shard_map.53
  17.6 2.7 %collective-permute-start.6 = (f32[120,128]{1,0:T(8,128)S(1)}, f32[120,128]{1,0:T(8,128)S(1)}, u32[]{:S(2)}, u32[]{:S(2)}) collective-permute-start(f32[120,128]{1,0:T(8,128)S(1)} %get-tuple-element.35), channel_id=1, source_target_pairs={{0,2},{1,3},{2,0},{3,1},{4,6},{5,7},{6,4},{7,5},{8,10},{9,11},{10,... | collective-permute-start | bytes 184328 | tf_op jit(solution)/shard_map/ppermute | solution.py:563
  20.3 2.5 %collective-permute-done.6.refs_2_ = f32[120,128]{1,0:T(8,128)S(1)} collective-permute-done((f32[120,128]{1,0:T(8,128)S(1)}, f32[120,128]{1,0:T(8,128)S(1)}, u32[]{:S(2)}, u32[]{:S(2)}) %collective-permute-start.6) | collective-permute-done | bytes 61472 | tf_op jit(solution)/shard_map/ppermute | solution.py:563
  22.8 1.5 %shard_map.54 = (f32[128,128]{1,0:T(8,128)S(1)}, f32[6,24,256]{2,1,0:T(8,128)S(1)}, f32[3,16,24,256]{3,2,1,0:T(8,128)S(1)}, f32[9,24,256]{2,1,0:T(8,128)S(1)}, f32[6,24,256]{2,1,0:T(8,128)S(1)}) custom-call(f32[24,128]{1,0:T(8,128)S(1)} %get-tuple-element.28.cut_ref, f32[11,24,256]{2,1,0:T(8,128)S(1)} %get-tuple-element.32.own_ref.refs_0_, ...), custom_call_target="tpu_custom_call" | custom-call | tf_op jit(solution)/shard_map/pallas_call | solution.py:550
  24.3 1.6 %collective-permute-start.7 = (f32[128,128]{1,0:T(8,128)S(1)}, f32[128,128]{1,0:T(8,128)S(1)}, u32[]{:S(2)}, u32[]{:S(2)}) collective-permute-start(f32[128,128]{1,0:T(8,128)S(1)} %get-tuple-element.44), channel_id=1, source_target_pairs={{0,1},{1,0},{2,3},{3,2},{4,5},{5,4},{6,7},{7,6},{8,9},{9,8},{10,11... | collective-permute-start | bytes 196616 | tf_op jit(solution)/shard_map/ppermute | solution.py:563
  25.9 2.7 %collective-permute-done.7.message_ref = f32[128,128]{1,0:T(8,128)S(1)} collective-permute-done((f32[128,128]{1,0:T(8,128)S(1)}, f32[128,128]{1,0:T(8,128)S(1)}, u32[]{:S(2)}, u32[]{:S(2)}) %collective-permute-start.7) | collective-permute-done | bytes 65568 | tf_op jit(solution)/shard_map/ppermute | solution.py:563
  28.6 0.2 shard_map.55
  28.8 3.1 %collective-permute-start.8 = (f32[80,128]{1,0:T(8,128)S(1)}, f32[80,128]{1,0:T(8,128)S(1)}, u32[]{:S(2)}, u32[]{:S(2)}) collective-permute-start(f32[80,128]{1,0:T(8,128)S(1)} %get-tuple-element.47), channel_id=1, source_target_pairs={{0,2},{1,3},{2,0},{3,1},{4,6},{5,7},{6,4},{7,5},{8,10},{9,11},{10,... | collective-permute-start | bytes 122888 | tf_op jit(solution)/shard_map/ppermute | solution.py:563
  31.8 2.0 %collective-permute-done.8.refs_2_ = f32[80,128]{1,0:T(8,128)S(1)} collective-permute-done((f32[80,128]{1,0:T(8,128)S(1)}, f32[80,128]{1,0:T(8,128)S(1)}, u32[]{:S(2)}, u32[]{:S(2)}) %collective-permute-start.8) | collective-permute-done | bytes 40992 | tf_op jit(solution)/shard_map/ppermute | solution.py:563
  33.8 1.4 %shard_map.56 = (f32[3,16,16,128]{3,2,1,0:T(8,128)}, f32[3,16,16,128]{3,2,1,0:T(8,128)}) custom-call(f32[24,128]{1,0:T(8,128)S(1)} %get-tuple-element.28.cut_ref, f32[6,24,256]{2,1,0:T(8,128)S(1)} %get-tuple-element.43.own_ref.refs_0_, f32[6,24,256]{2,1,0:T(8,128)S(1)} %get-tuple-element.46.refs_1_, f32[80,128]{1,0:T(8,128)S(1)} %collective-permute-done.8.refs_2_, ...), custom_call_target="tpu_custom_call" | custom-call | tf_op jit(solution)/shard_map/pallas_call | solution.py:550
Async XLA Ops:
  0.6 0.9 %copy-start = (s32[16,16,128]{2,1,0:T(8,128)S(1)}, s32[16,16,128]{2,1,0:T(8,128)}, u32[]{:S(2)}) copy-start(s32[16,16,128]{2,1,0:T(8,128)} %facies_ref.3) | copy-start | bytes 393220
  1.6 9.4 %collective-permute-start = (s32[48,128]{1,0:T(8,128)S(1)}, s32[48,128]{1,0:T(8,128)S(1)}, u32[]{:S(2)}, u32[]{:S(2)}) collective-permute-start(s32[48,128]{1,0:T(8,128)S(1)} %get-tuple-element.31), channel_id=1, source_target_pairs={{0,16},{16,0},{1,17},{17,1},{2,18},{18,2},{3,19},{19,3},{4,20},{20... | collective-permute-start | bytes 73736 | tf_op jit(solution)/shard_map/ppermute | solution.py:568
  4.6 5.6 %collective-permute-start.4 = (s32[16,128]{1,0:T(8,128)S(1)}, s32[16,128]{1,0:T(8,128)S(1)}, u32[]{:S(2)}, u32[]{:S(2)}) collective-permute-start(s32[16,128]{1,0:T(8,128)S(1)} %get-tuple-element.27.strip_ref), channel_id=1, source_target_pairs={{0,28},{4,16},{8,20},{12,24},{16,12},{20,0},{24,4},{28,8},{1,29},{... | collective-permute-start | bytes 24584 | tf_op jit(solution)/shard_map/ppermute | solution.py:578
  5.3 4.9 %collective-permute-start.3 = (s32[16,128]{1,0:T(8,128)S(1)}, s32[16,128]{1,0:T(8,128)S(1)}, u32[]{:S(2)}, u32[]{:S(2)}) collective-permute-start(s32[16,128]{1,0:T(8,128)S(1)} %get-tuple-element.27.strip_ref), channel_id=1, source_target_pairs={{0,20},{4,24},{8,28},{12,16},{16,4},{20,8},{24,12},{28,0},{1,21},{... | collective-permute-start | bytes 24584 | tf_op jit(solution)/shard_map/ppermute | solution.py:578
  6.4 3.8 %collective-permute-start.2 = (s32[16,128]{1,0:T(8,128)S(1)}, s32[16,128]{1,0:T(8,128)S(1)}, u32[]{:S(2)}, u32[]{:S(2)}) collective-permute-start(s32[16,128]{1,0:T(8,128)S(1)} %get-tuple-element.27.strip_ref), channel_id=1, source_target_pairs={{0,12},{4,0},{8,4},{12,8},{1,13},{5,1},{9,5},{13,9},{2,14},{6,2},{... | collective-permute-start | bytes 24584 | tf_op jit(solution)/shard_map/ppermute | solution.py:568
  8.0 3.1 %collective-permute-start.1 = (s32[16,128]{1,0:T(8,128)S(1)}, s32[16,128]{1,0:T(8,128)S(1)}, u32[]{:S(2)}, u32[]{:S(2)}) collective-permute-start(s32[16,128]{1,0:T(8,128)S(1)} %get-tuple-element.27.strip_ref), channel_id=1, source_target_pairs={{0,4},{4,8},{8,12},{12,0},{1,5},{5,9},{9,13},{13,1},{2,6},{6,10},{... | collective-permute-start | bytes 24584 | tf_op jit(solution)/shard_map/ppermute | solution.py:568
  8.0 0.7 %copy-start.1 = (f32[3,16]{1,0:T(4,128)S(1)}, f32[3,16]{1,0:T(4,128)}, u32[]{:S(2)}) copy-start(f32[3,16]{1,0:T(4,128)} %table.1) | copy-start | bytes 580
  8.6 0.7 %copy-start.2 = (s32[63]{0:T(128)S(1)}, s32[63]{0:T(128)}, u32[]{:S(2)}) copy-start(s32[63]{0:T(128)} %breaks.1) | copy-start | bytes 760
  12.5 4.9 %collective-permute-start.5 = (f32[224,128]{1,0:T(8,128)S(1)}, f32[224,128]{1,0:T(8,128)S(1)}, u32[]{:S(2)}, u32[]{:S(2)}) collective-permute-start(f32[224,128]{1,0:T(8,128)S(1)} %get-tuple-element.33), channel_id=1, source_target_pairs={{0,1},{1,0},{2,3},{3,2},{4,5},{5,4},{6,7},{7,6},{8,9},{9,8},{10,11... | collective-permute-start | bytes 344072 | tf_op jit(solution)/shard_map/ppermute | solution.py:563
  17.6 5.2 %collective-permute-start.6 = (f32[120,128]{1,0:T(8,128)S(1)}, f32[120,128]{1,0:T(8,128)S(1)}, u32[]{:S(2)}, u32[]{:S(2)}) collective-permute-start(f32[120,128]{1,0:T(8,128)S(1)} %get-tuple-element.35), channel_id=1, source_target_pairs={{0,2},{1,3},{2,0},{3,1},{4,6},{5,7},{6,4},{7,5},{8,10},{9,11},{10,... | collective-permute-start | bytes 184328 | tf_op jit(solution)/shard_map/ppermute | solution.py:563
  24.3 4.3 %collective-permute-start.7 = (f32[128,128]{1,0:T(8,128)S(1)}, f32[128,128]{1,0:T(8,128)S(1)}, u32[]{:S(2)}, u32[]{:S(2)}) collective-permute-start(f32[128,128]{1,0:T(8,128)S(1)} %get-tuple-element.44), channel_id=1, source_target_pairs={{0,1},{1,0},{2,3},{3,2},{4,5},{5,4},{6,7},{7,6},{8,9},{9,8},{10,11... | collective-permute-start | bytes 196616 | tf_op jit(solution)/shard_map/ppermute | solution.py:563
  28.8 5.1 %collective-permute-start.8 = (f32[80,128]{1,0:T(8,128)S(1)}, f32[80,128]{1,0:T(8,128)S(1)}, u32[]{:S(2)}, u32[]{:S(2)}) collective-permute-start(f32[80,128]{1,0:T(8,128)S(1)} %get-tuple-element.47), channel_id=1, source_target_pairs={{0,2},{1,3},{2,0},{3,1},{4,6},{5,7},{6,4},{7,5},{8,10},{9,11},{10,... | collective-permute-start | bytes 122888 | tf_op jit(solution)/shard_map/ppermute | solution.py:563

commit v4 on v3

v4 whole, which is shorter than its diff:
```python
import functools

import jax
import jax.numpy as jnp
from jax import lax
from jax.experimental import pallas as pl
from jax.experimental.pallas import tpu as pltpu
from jax.sharding import PartitionSpec as P


WIDE = 3
FIRST_COUNT = 11
LAST_COUNT = 5
SECOND_COUNT = 6
PAIR_COUNT = 16
CHUNK = 4


def moved(values, amount, axis):
    size = values.shape[axis]
    amount = amount % size
    if amount == 0:
        return values
    return pltpu.roll(values, amount, axis)


def flag(condition):
    return condition.astype(jnp.float32)


def iotas(rows, lanes):
    return tuple(lax.broadcasted_iota(jnp.int32, (rows, lanes), d) for d in (0, 1))


def choose(condition, first, second):
    return [jnp.where(condition, a, b) for a, b in zip(first, second)]


def is_high(stage):
    return (lax.axis_index("gz") >> (stage + 1)) % 2 == 1


def own_start(nz):
    return (lax.axis_index("gz") % 2) * nz


def pack_kernel(own_ref, other_ref, table_ref, strip_ref, *row_refs):
    nz, nx, ny = own_ref.shape
    lane = lax.broadcasted_iota(jnp.int32, (nx, ny), 1)
    row = iotas(8, ny)[0]
    swap = own_start(nz) > 0
    for b in range(2):
        strip = jnp.zeros((nx, ny), jnp.int32)
        for z in range(0, nz, 2):
            pair = []
            for at in (z, z + 1):
                layer = jnp.where(swap == (b == 1), own_ref[at], other_ref[at])
                pair.append(layer)
                strip = jnp.where(lane // 8 == at, moved(layer, 8 * at + WIDE, 1), strip)
            first = jnp.where(row < 4, pair[0][:8], moved(pair[1][:8], 4, 0))
            last = jnp.where(row < 4, moved(pair[0][nx - 8 :], 4, 0), pair[1][nx - 8 :])
            start = (b * nz + z) * 4
            spot = slice(start, start + 8)
            if len(row_refs) == 1:
                row_refs[0][spot, :] = jnp.where(lax.axis_index("gx") == 0, last, first)
            else:
                row_refs[0][spot, :] = first
                row_refs[1][spot, :] = last
        strip_ref[b * nx : (b + 1) * nx, :] = strip


def lookup(table, index):
    rows = [
        jnp.take_along_axis(table, index[r : r + 8], axis=1) for r in range(0, index.shape[0], 8)
    ]
    return jnp.concatenate(rows, axis=0)


def prepare_kernel(stages, table, breaks, facies_ref, k_ref, table_ref, cut_ref):
    nz, nx, ny = facies_ref.shape
    lane = iotas(8, ny)[1]
    tables = []
    for q in range(3):
        values = jnp.zeros((8, ny), jnp.float32)
        for label in range(table.shape[1]):
            values = jnp.where(lane == label, table[q, label], values)
        table_ref[q] = values
        tables.append(values)
    for z in range(nz):
        for q in range(3):
            k_ref[q, z] = lookup(tables[q], facies_ref[z])
    pair = lax.axis_index("gz") // 2
    layers = [pair * 2 * nz + r - 1 for r in range(2 * nz + 1)]
    for s in range(stages):
        base, size = (pair >> (s + 1)) << (s + 1), 2**s
        layers.append((base + size) * 2 * nz - 1)
        layers.append(jnp.where(is_high(s), base, base + 2 * size) * 2 * nz - 1)
    for r, layer in enumerate(layers):
        cut = breaks[jnp.clip(layer, 0, breaks.shape[0] - 1)].astype(jnp.float32)
        cut_ref[r : r + 1, :] = jnp.full((1, ny), cut, jnp.float32)


def prepare_other_kernel(table_ref, own_ref, other_ref, strip_ref, k_ref):
    nz = other_ref.shape[0]
    start = own_start(nz)
    for q in range(3):
        k_ref[q, pl.ds(start, nz)] = own_ref[q]
        for z in range(nz):
            k_ref[q, nz - start + z] = lookup(table_ref[q], other_ref[z])


def face(a, b):
    product = a * b
    total = a + b
    harmonic = 2.0 * product / total
    inside = product > 0.0
    link = jnp.where(inside, harmonic, 0.0)
    flow = jnp.where(inside, harmonic, total)
    tau = jnp.where(inside, harmonic, 2.0 * total)
    return link, flow, tau


class Message:
    def __init__(self, count, halo, nx, ny):
        self.count, self.halo, self.nx, self.ny = count, halo, nx, ny
        self.one_sided = lax.axis_size("gx") == 2
        self.rows_each = halo if self.one_sided else 2 * halo
        self.per_tile = 8 // self.rows_each
        self.tiles = -(-count // self.per_tile)
        self.strip = slice(count * nx, count * nx + nx + 8)
        self.rows = self.strip.stop + 8 * self.tiles

    def tile(self, q):
        start = self.strip.stop + 8 * (q // self.per_tile)
        return slice(start, start + 8)

    def side_moved(self, tile, q, sign):
        part = q % self.per_tile
        if not self.one_sided:
            return moved(tile, sign * (self.rows_each * part + self.halo), 0)
        first = lax.axis_index("gx") == 0
        out = jnp.where(
            first,
            moved(tile, sign * self.halo * part, 0),
            moved(tile, sign * self.halo * (part + 1), 0),
        )
        if sign > 0:
            return out
        row = iotas(8, self.ny)[0]
        return jnp.where(jnp.where(first, row, 7 - row) < self.halo, out, 1.0)

    def write(self, ref, slabs):
        nx, ny, halo = self.nx, self.ny, self.halo
        lane = iotas(nx + 8, ny)[1]
        strip = moved(slabs[0][:, ny:], halo, 1)
        for q in range(1, self.count):
            turned = moved(slabs[q][:, ny:], 2 * halo * q + halo, 1)
            strip = jnp.where(lane < 2 * halo * q, strip, turned)
        ref[self.strip, :] = strip
        row = iotas(8, ny)[0]
        for q, slab in enumerate(slabs):
            ref[q * nx : (q + 1) * nx, :] = slab[:nx, :ny]
            turned = self.side_moved(slab[nx:, :ny], q, 1)
            part = q % self.per_tile
            tile = turned if part == 0 else jnp.where(row < self.rows_each * part, tile, turned)
            if part == self.per_tile - 1 or q == self.count - 1:
                ref[self.tile(q), :] = tile

    def read(self, ref):
        nx, halo = self.nx, self.halo
        strip = ref[self.strip, :]
        slabs = []
        for q in range(self.count):
            side = self.side_moved(ref[self.tile(q), :], q, -1)
            body = jnp.concatenate([ref[q * nx : (q + 1) * nx, :], side], axis=0)
            beside = moved(strip, -(2 * halo * q + halo), 1)
            slabs.append(jnp.concatenate([body, beside], axis=1))
        return slabs


def open_after(cut_ref, r):
    cut = 1.0 - cut_ref[r : r + 1, :]
    return jnp.concatenate([cut, cut], axis=1)


def slab_size(ref):
    return ref.shape[-2] - 8, ref.shape[-1] // 2


def join(low, high, opened):
    ends = link, flow, tau = face(low[4], high[3])
    coupling = link * opened
    inverse = 1.0 / (low[2] + tau)
    step = coupling * inverse
    last_inverse = 1.0 / (high[0] + tau - coupling * step)
    outer = low[1] * inverse
    weight = step * low[1]
    weight_low, weight_high = weight * last_inverse, high[1] * last_inverse
    right_low = low[8:10] + [low[10] + flow]
    right_high = high[5:7] + [high[7] - flow]
    s_uu = low[0] - outer * low[1] - weight * weight_low
    s_uv = -weight * weight_high
    s_vv = high[2] - high[1] * weight_high
    factors = [outer, step, weight_low, weight_high, inverse, last_inverse]
    g_u, g_v, middle = join_right(factors, low[5:8], right_low, right_high, high[8:11])
    return [s_uu, s_uv, s_vv, low[3], high[4]] + g_u + g_v, factors, right_low + middle, ends


def join_right(factors, low_u, low_v, high_u, high_v):
    outer, step, weight_low, weight_high = factors[:4]
    middle = [b + step * a for a, b in zip(low_v, high_u)]
    g_u = [g - outer * a - weight_low * m for g, a, m in zip(low_u, low_v, middle)]
    g_v = [g - weight_high * m for g, m in zip(high_v, middle)]
    return g_u, g_v, middle


def join_inner(factors, right_low, middle, first, last):
    outer, step, weight_low, weight_high, inverse, last_inverse = factors
    high = last_inverse * middle - weight_low * first - weight_high * last
    return inverse * right_low - outer * first + step * high, high


def reduce_end(slabs, top):
    s_uu, s_uv, s_vv, k_u, k_v = slabs[:5]
    far_s, near_s = choose(top, [s_vv, s_uu], [s_uu, s_vv])
    far_k, near_k = choose(top, [k_v, k_u], [k_u, k_v])
    sign = jnp.where(top, 1.0, -1.0)
    factor = s_uv / (far_s + 2.0 * far_k)
    g_u, g_v = slabs[5:8], slabs[8:11]
    far_g, near_g = choose(top, g_v, g_u), choose(top, g_u, g_v)
    far_g[2] = far_g[2] + far_k * sign
    return [near_s - s_uv * factor, near_k] + [n - factor * g for n, g in zip(near_g, far_g)], factor


def reduce_end_right(factor, g_u, g_v, top):
    far_g, near_g = choose(top, g_v, g_u), choose(top, g_u, g_v)
    return [n - factor * g for n, g in zip(near_g, far_g)]


def eliminate_kernel(
    stages, table_ref, cut_ref, k_ref, row_low, row_high, y_low, y_high,
    low_low, low_high, high_low, high_high,
    message_ref, own_ref, pair_ref, lx_ref, ly_ref, lz_ref, d_ref, e_ref, inverse_ref,
    all_ref, flow_ref, source_ref, centre_ref, low_ref, high_ref=None,
):
    high_ref = low_ref if high_ref is None else high_ref
    layers, nx, ny = k_ref.shape[1:]
    nz = layers // 2
    at_x, at_y = lax.axis_index("gx"), lax.axis_index("gy")
    has_x_low, has_x_high = at_x > 0, at_x < lax.axis_size("gx") - 1
    has_y_low, has_y_high = at_y > 0, at_y < lax.axis_size("gy") - 1
    tables = [table_ref[q] for q in range(3)]

    row, lane = iotas(nx + 8, 2 * ny)
    x_in = (row < nx) | ((row < nx + WIDE) & has_x_high) | ((row >= nx + 8 - WIDE) & has_x_low)
    y_in = (lane < ny) | ((lane < ny + WIDE) & has_y_high)
    y_in = y_in | ((lane >= 2 * ny - WIDE) & has_y_low)
    cell = x_in & y_in
    valid = flag(cell)
    in_x, in_xp = valid * moved(valid, -1, 0), valid * moved(valid, 1, 0)
    in_y, in_yp = valid * moved(valid, -1, 1), valid * moved(valid, 1, 1)
    row_in, strip_in = cell[nx:, :ny], cell[:, ny:]

    row = iotas(8, ny)[0]
    lane = iotas(nx + 8, ny)[1]
    strips = []
    for b in range(2):
        part = slice(b * nx, (b + 1) * nx)

        def whole(own, high, low):
            side = jnp.where(row < WIDE, high[part, :][0:8], low[part, :][nx - 8 :])
            return jnp.concatenate([own[part, :], side], axis=0)

        before, after = whole(y_low, low_high, low_low), whole(y_high, high_high, high_low)
        strip = jnp.where(lane % 8 < WIDE, before, after)
        strips.append([lookup(table, strip) for table in tables])
    for q in range(3):
        low_ref[q] = lookup(tables[q], row_low[...])
        if high_ref is not low_ref:
            high_ref[q] = lookup(tables[q], row_high[...])

    for b in range(2):
        for z in range(nz):
            at = b * nz + z
            start = at // 2 * 8
            for q in range(3):
                low, high = low_ref[q, start : start + 8, :], high_ref[q, start : start + 8, :]
                if z % 2 == 0:
                    low = moved(low, 4, 0)
                else:
                    high = moved(high, 4, 0)
                side = jnp.where(row_in, jnp.where(row < 4, high, low), 0.0)
                beside = jnp.where(strip_in, moved(strips[b][q], -(8 * z + WIDE), 1), 0.0)
                all_ref[q, at, :nx, :ny] = k_ref[q, at]
                all_ref[q, at, nx:, :ny] = side
                all_ref[q, at, :, ny:] = beside

    def flow_after(here, axis, inside):
        there = moved(here, -1, axis)
        total = here + there
        return jnp.where(inside > 0.0, 2.0 * (here * there) / total, total)

    def tau_and_source(flow, axis, inside, inside_back):
        back = moved(flow, 1, axis)
        return flow * (2.0 - inside) + back * (2.0 - inside_back), flow - back

    for at in range(layers):
        flow_x = flow_after(all_ref[0, at], 0, in_x)
        flow_ref[at] = flow_after(all_ref[1, at], 1, in_y)
        lx_ref[at] = flow_x * in_x
        centre_ref[at], source_ref[0, at] = tau_and_source(flow_x, 0, in_x, in_xp)
        if at % nz < nz - 1:
            kz, above = all_ref[2, at], all_ref[2, at + 1]
            lz_ref[at] = jnp.where(cell, 2.0 * (kz * above) / (kz + above), 0.0)
    for at in range(layers):
        flow_y = flow_ref[at]
        ly_ref[at] = flow_y * in_y
        tau_y, source_ref[1, at] = tau_and_source(flow_y, 1, in_y, in_yp)
        centre = centre_ref[at] + tau_y
        if at % nz > 0:
            centre = centre + lz_ref[at - 1]
        if at % nz < nz - 1:
            centre = centre + lz_ref[at]
        centre_ref[at] = jnp.where(cell, centre, 1.0)

    states = [{}, {}]
    for z in range(nz):
        for b in range(2):
            at, v = b * nz + z, states[b]
            centre = centre_ref[at]
            sources = [source_ref[0, at], source_ref[1, at]]
            if z == 0:
                v["source"] = sources + [lz_ref[at]]
                v["s_uu"], v["g_u"] = centre, v["source"]
            elif z == nz - 1:
                sources = sources + [-lz_ref[at - 1]]
                v["s_vv"] = centre - v["coupling"] * v["ratio"]
                v["s_uv"] = -v["coupling"] * v["spike"]
                v["g_v"] = [a + v["coupling"] * d for a, d in zip(sources, v["value"])]
            else:
                forward = sources + [lz_ref[at] - lz_ref[at - 1]]
                if z == 1:
                    pivot, numerator = centre, v["coupling"]
                else:
                    pivot = centre - v["coupling"] * v["ratio"]
                    forward = [a + v["coupling"] * d for a, d in zip(forward, v["value"])]
                    numerator = v["coupling"] * v["spike"]
                inverse = 1.0 / pivot
                v["value"] = [a * inverse for a in forward]
                v["spike"] = numerator * inverse
                v["s_uu"] = v["s_uu"] - numerator * v["spike"]
                v["g_u"] = [g + v["spike"] * a for g, a in zip(v["g_u"], forward)]
                inverse_ref[at] = inverse
                e_ref[at] = v["spike"]
                for f in range(3):
                    d_ref[f, at] = v["value"][f]
            if z < nz - 1:
                v["coupling"] = lz_ref[at] * open_after(cut_ref, at + 1)
                if z > 0:
                    v["ratio"] = v["coupling"] * inverse

    def block(b):
        v = states[b]
        k_ends = [all_ref[2, b * nz], all_ref[2, b * nz + nz - 1]]
        return [v["s_uu"], v["s_uv"], v["s_vv"]] + k_ends + v["g_u"] + v["g_v"]

    slabs, factors, rights, ends = join(block(0), block(1), open_after(cut_ref, nz))
    for q, slab in enumerate(slabs):
        own_ref[q] = slab
    for n, slab in enumerate(factors + rights + list(ends)):
        pair_ref[n] = slab
    if stages == 1:
        slabs, pair_ref[PAIR_COUNT - 1] = reduce_end(slabs, is_high(0))
    Message(len(slabs), 2, nx, ny).write(message_ref, slabs)


def join_kernel(stage, last, base, cut_ref, own_ref, message_ref, sibling_ref, factor_ref, next_ref, *joined):
    nx, ny = slab_size(own_ref)
    own = [own_ref[q] for q in range(FIRST_COUNT)]
    sibling = Message(FIRST_COUNT, 2, nx, ny).read(message_ref)
    for q, slab in enumerate(sibling):
        sibling_ref[q] = slab
    high = is_high(stage)
    slabs, factors, _, _ = join(
        choose(high, sibling, own),
        choose(high, own, sibling),
        open_after(cut_ref, base + 2 * stage),
    )
    for n, values in enumerate(factors):
        factor_ref[n] = values
    if last:
        slabs, factor_ref[6] = reduce_end(slabs, is_high(stage + 1))
    else:
        for q, slab in enumerate(slabs):
            joined[0][q] = slab
    Message(len(slabs), 2, nx, ny).write(next_ref, slabs)


def join_again_kernel(stage, last, own_ref, message_ref, factor_ref, sibling_ref, next_ref, *joined):
    nx, ny = slab_size(own_ref)
    own = [own_ref[q] for q in range(SECOND_COUNT)]
    sibling = Message(SECOND_COUNT, 1, nx, ny).read(message_ref)
    for q, slab in enumerate(sibling):
        sibling_ref[q] = slab
    above = is_high(stage)
    low, high = choose(above, sibling, own), choose(above, own, sibling)
    factors = [factor_ref[n] for n in range(6)]
    g_u, g_v, _ = join_right(factors, low[:3], low[3:], high[:3], high[3:])
    slabs = g_u + g_v
    if last:
        slabs = reduce_end_right(factor_ref[6], g_u, g_v, is_high(stage + 1))
    else:
        for q, slab in enumerate(slabs):
            joined[0][q] = slab
    Message(len(slabs), 1, nx, ny).write(next_ref, slabs)


def stencil(slab, link_x, link_y):
    return (
        link_x * moved(slab, -1, 0)
        + moved(link_x * slab, 1, 0)
        + (link_y * moved(slab, -1, 1) + moved(link_y * slab, 1, 1))
    )


def beyond_cuts(cut_ref, at, link_low, link_high):
    low, high = cut_ref[pl.ds(at, 1), :], cut_ref[pl.ds(at + 1, 1), :]
    return (
        link_low * jnp.concatenate([low, low], axis=1),
        link_high * jnp.concatenate([high, high], axis=1),
    )


def left_out(field_ref, f, at, link_x, link_y, cuts):
    return stencil(field_ref[f, at + 1], link_x, link_y) + (
        cuts[0] * field_ref[f, at] + cuts[1] * field_ref[f, at + 2]
    )


def middle_kernel(stages, cut_ref, *refs):
    own_ref, pair_ref, siblings, message_ref = refs[0], refs[1], refs[2 : stages + 1], refs[stages + 1]
    refs = refs[stages + 2 :]
    lx_ref, ly_ref, lz_ref, d_ref, e_ref, inverse_ref = refs[:6]
    next_ref, own2_ref, right_ref, d2_ref, factor_ref, end_ref, first_ref = refs[6:]
    layers = lx_ref.shape[0]
    nz = layers // 2
    nx, ny = slab_size(lx_ref)
    own = [own_ref[q] for q in range(FIRST_COUNT)]
    slots = []

    def keep(values):
        factor_ref[len(slots)] = values
        slots.append(None)

    def attach(state, sign, row, pivot, right, k):
        beside, k_beside, rights, exists = state[0], state[1], state[2:5], state[5]
        link, flow, tau = face(k_beside * exists, k)
        coupling = link * open_after(cut_ref, row)
        rights = rights[:2] + [rights[2] + sign * flow]
        inverse = 1.0 / (beside + tau)
        step = coupling * inverse
        right = [a + step * b for a, b in zip(right, rights)]
        right[2] = right[2] - sign * flow
        return pivot + tau - coupling * step, right, step, inverse, rights, (link, flow, tau)

    far = Message(LAST_COUNT, 2, nx, ny).read(message_ref)
    top = is_high(stages - 1)
    below, above = far + [flag(top)], far + [flag(jnp.logical_not(top))]
    for s in range(stages - 2, -1, -1):
        up = is_high(s)
        block = [siblings[s][q] for q in range(FIRST_COUNT)]
        sign = jnp.where(up, 1.0, -1.0)
        state = choose(up, below, above)
        far_s, far_k, near_s, near_k = choose(
            up, [block[0], block[3], block[2], block[4]], [block[2], block[4], block[0], block[3]]
        )
        far_g = choose(up, block[5:8], block[8:11])
        near_g = choose(up, block[8:11], block[5:8])
        row = layers + 2 + 2 * s
        pivot, right, step, _, _, _ = attach(state, sign, row, far_s, far_g, far_k)
        factor = block[1] / pivot
        keep(step)
        keep(factor)
        state = [near_s - block[1] * factor, near_k]
        state += [n - factor * r for n, r in zip(near_g, right)] + [jnp.float32(1.0)]
        below, above = choose(up, state, below), choose(up, above, state)

    pivot_u, right_u, step_b, inverse_b, rights_b, ends_b = attach(
        below, 1.0, 0, own[0], own[5:8], own[3]
    )
    pivot_v, right_v, step_a, inverse_a, rights_a, ends_a = attach(
        above, -1.0, layers, own[2], own[8:11], own[4]
    )
    held_b, held_a = inverse_b * below[5], inverse_a * above[5]
    inverse_u = 1.0 / pivot_u
    factor = own[1] * inverse_u
    inverse_v = 1.0 / (pivot_v - own[1] * factor)
    for values in (step_b, held_b, step_a, held_a, inverse_u, factor, inverse_v):
        keep(values)
    pair = [pair_ref[n] for n in range(PAIR_COUNT)]
    inner = pair[:6]
    ends = [ends_b[0], pair[12], ends_a[0]]
    for n, values in enumerate(ends):
        end_ref[n] = values

    for f in range(3):
        last = (right_v[f] - factor * right_u[f]) * inverse_v
        first_u = right_u[f] * inverse_u - factor * last
        low_v, high_u = join_inner(inner, pair[6 + f], pair[9 + f], first_u, last)
        first_ref[f, 0] = rights_b[f] * held_b + step_b * first_u
        first_ref[f, layers + 1] = rights_a[f] * held_a + step_a * last
        first_ref[f, 1] = first_u
        first_ref[f, nz] = low_v
        first_ref[f, nz + 1] = high_u
        first_ref[f, layers] = last
    for z in range(nz - 2, 0, -1):
        for at in (z, nz + z):
            ratio = lz_ref[at] * open_after(cut_ref, at + 1) * inverse_ref[at]
            spike = e_ref[at]
            for f in range(3):
                first_ref[f, at + 1] = (
                    d_ref[f, at]
                    + spike * first_ref[f, 1 + at - z]
                    + ratio * first_ref[f, at + 2]
                )

    def block(b):
        for z in range(nz):
            at = b * nz + z
            cuts = beyond_cuts(
                cut_ref, at,
                ends[b] if z == 0 else lz_ref[at - 1],
                ends[b + 1] if z == nz - 1 else lz_ref[at],
            )
            right = [left_out(first_ref, f, at, lx_ref[at], ly_ref[at], cuts) for f in range(3)]
            if z == 0:
                g_u = list(right)
            else:
                if z == 1:
                    forward = right
                else:
                    forward = [right[f] + coupling * value[f] for f in range(3)]
                if z < nz - 1:
                    inverse, spike = inverse_ref[at], e_ref[at]
                    value = [forward[f] * inverse for f in range(3)]
                    g_u = [g_u[f] + spike * forward[f] for f in range(3)]
                    for f in range(3):
                        d2_ref[f, at] = value[f]
                    coupling = lz_ref[at] * open_after(cut_ref, at + 1)
        return g_u, forward

    (low_u, low_v), (high_u, high_v) = block(0), block(1)
    g_u, g_v, middle = join_right(inner, low_u, low_v, high_u, high_v)
    for n, slab in enumerate(low_v + middle):
        right_ref[n] = slab
    for q, slab in enumerate(g_u + g_v):
        own2_ref[q] = slab
    slabs = g_u + g_v
    if stages == 1:
        slabs = reduce_end_right(pair[PAIR_COUNT - 1], g_u, g_v, is_high(0))
    Message(len(slabs), 1, nx, ny).write(next_ref, slabs)


def final_kernel(stages, cut_ref, *refs):
    own_ref, pair_ref, siblings, message_ref = refs[0], refs[1], refs[2 : stages + 1], refs[stages + 1]
    refs = refs[stages + 2 :]
    lx_ref, ly_ref, lz_ref, first_ref, right_ref, d2_ref, e_ref, inverse_ref = refs[:8]
    factor_ref, end_ref, pressure_out, residual_out = refs[8:12]
    change_ref, pressure_ref, residual_ref, sems = refs[12:]
    nz = lx_ref.shape[0] // 2
    nx, ny = slab_size(lx_ref)
    own = [own_ref[q] for q in range(SECOND_COUNT)]
    slots = []

    def kept():
        slots.append(None)
        return factor_ref[len(slots) - 1]

    below = above = Message(3, 1, nx, ny).read(message_ref)
    for s in range(stages - 2, -1, -1):
        up = is_high(s)
        block = [siblings[s][q] for q in range(SECOND_COUNT)]
        state = choose(up, below, above)
        far_g = choose(up, block[:3], block[3:])
        near_g = choose(up, block[3:], block[:3])
        step, factor = kept(), kept()
        right = [a + step * b for a, b in zip(far_g, state)]
        state = [n - factor * r for n, r in zip(near_g, right)]
        below, above = choose(up, state, below), choose(up, above, state)
    step_b, held_b, step_a, held_a = kept(), kept(), kept(), kept()
    inverse_u, factor, inverse_v = kept(), kept(), kept()
    inner = [pair_ref[n] for n in range(6)]
    start = own_start(nz)
    high = start > 0
    for f in range(3):
        right_u = own[f] + step_b * below[f]
        right_v = own[3 + f] + step_a * above[f]
        last = (right_v - factor * right_u) * inverse_v
        first = right_u * inverse_u - factor * last
        low_v, high_u = join_inner(inner, right_ref[f], right_ref[3 + f], first, last)
        beyond_b = below[f] * held_b + step_b * first
        beyond_a = above[f] * held_a + step_a * last
        values = choose(high, [low_v, high_u, last, beyond_a], [beyond_b, first, low_v, high_u])
        for at, slab in zip((0, 1, nz, nz + 1), values):
            change_ref[f, at] = slab
    ends = choose(high, [end_ref[1], end_ref[2]], [end_ref[0], end_ref[1]])
    for z in range(nz - 2, 0, -1):
        at = start + z
        opened = 1.0 - cut_ref[pl.ds(at + 1, 1), :]
        opened = jnp.concatenate([opened, opened], axis=1)
        ratio = lz_ref[at] * opened * inverse_ref[at]
        spike = e_ref[at]
        for f in range(3):
            change_ref[f, z + 1] = (
                d2_ref[f, at] + spike * change_ref[f, 1] + ratio * change_ref[f, z + 2]
            )
    own_part = (slice(0, nx), slice(0, ny))
    copies = []
    for z in range(nz):
        at = start + z
        cuts = beyond_cuts(
            cut_ref, at,
            ends[0] if z == 0 else lz_ref[at - 1],
            ends[1] if z == nz - 1 else lz_ref[at],
        )
        link_x, link_y = lx_ref[at], ly_ref[at]
        for f in range(3):
            pressure_ref[f, z] = (first_ref[f, at + 1] + change_ref[f, z + 1])[own_part]
            residual_ref[f, z] = left_out(change_ref, f, z, link_x, link_y, cuts)[own_part]
        if (z + 1) % CHUNK == 0:
            part = (slice(None), slice(z + 1 - CHUNK, z + 1))
            for n, (buffer, out) in enumerate(
                ((pressure_ref, pressure_out), (residual_ref, residual_out))
            ):
                copy = pltpu.make_async_copy(
                    buffer.at[part], out.at[part], sems.at[n, z // CHUNK]
                )
                copy.start()
                copies.append(copy)
    for copy in copies:
        copy.wait()


def kernel_call(kernel, outputs, operands, scratch=(), smem=0, cost=None, space=pltpu.VMEM):
    specs = [pl.BlockSpec(memory_space=pltpu.SMEM)] * smem
    specs += [pl.BlockSpec(memory_space=pltpu.VMEM)] * (len(operands) - smem)
    return pl.pallas_call(
        kernel,
        out_shape=[jax.ShapeDtypeStruct(s, t) for s, t in outputs],
        in_specs=specs,
        out_specs=[pl.BlockSpec(memory_space=space)] * len(outputs),
        scratch_shapes=list(scratch),
        compiler_params=pltpu.CompilerParams(vmem_limit_bytes=24 * 2**20),
        cost_estimate=cost,
    )(*operands)


def swapped(values, stage):
    size = lax.axis_size("gz")
    return lax.ppermute(values, "gz", [(i, i ^ 2**stage) for i in range(size)])


def ring(values, axis, distance):
    size = lax.axis_size(axis)
    return lax.ppermute(values, axis, [(i, (i + distance) % size) for i in range(size)])


def diagonal(values, x_distance, y_distance):
    nx, ny = lax.axis_size("gx"), lax.axis_size("gy")
    route = []
    for i in range(nx):
        for j in range(ny):
            target = ((i + x_distance) % nx) * ny + (j + y_distance) % ny
            route.append((i * ny + j, target))
    return lax.ppermute(values, ("gx", "gy"), route)


def per_device(facies, perm_table, line_breaks):
    nz, nx, ny = facies.shape
    stages = (lax.axis_size("gz") - 1).bit_length() - 1
    i32, f32 = jnp.int32, jnp.float32
    two = lax.axis_size("gx") == 2
    layers = 2 * nz
    cut_rows = -(-(layers + 1 + 2 * stages) // 8) * 8
    other = swapped(facies, 0)
    k, table, cuts = kernel_call(
        functools.partial(prepare_kernel, stages),
        [((3, nz, nx, ny), f32), ((3, 8, ny), f32), ((cut_rows, ny), f32)],
        [perm_table, line_breaks, facies],
        smem=2,
        cost=pl.CostEstimate(flops=10**7, bytes_accessed=10**6, transcendentals=0),
    )
    strip, *rows = kernel_call(
        pack_kernel,
        [((2 * nx, ny), i32)] + [((layers * 4, ny), i32)] * (1 if two else 2),
        [facies, other, table],
    )
    k, = kernel_call(
        prepare_other_kernel,
        [((3, layers, nx, ny), f32)],
        [table, k, other, strip],
        cost=pl.CostEstimate(flops=10**7, bytes_accessed=10**6, transcendentals=0),
    )
    y_low, y_high = ring(strip, "gy", 1), ring(strip, "gy", -1)
    if two:
        row_low = row_high = ring(rows[0], "gx", 1)
        low_low = low_high = diagonal(strip, 1, 1)
        high_low = high_high = diagonal(strip, 1, -1)
    else:
        row_low, row_high = ring(rows[1], "gx", 1), ring(rows[0], "gx", -1)
        low_low, low_high = diagonal(strip, 1, 1), diagonal(strip, -1, 1)
        high_low, high_high = diagonal(strip, 1, -1), diagonal(strip, -1, -1)

    slab = (nx + 8, 2 * ny)
    one, three = ((layers,) + slab, f32), ((3, layers) + slab, f32)

    def slabs(count):
        return ((count,) + slab, f32)

    def message_of(count, halo):
        return ((Message(count, halo, nx, ny).rows, ny), f32)

    message, own, pair, lx, ly, lz, d, e, inverse = kernel_call(
        functools.partial(eliminate_kernel, stages),
        [message_of(LAST_COUNT if stages == 1 else FIRST_COUNT, 2)]
        + [slabs(FIRST_COUNT), slabs(PAIR_COUNT)]
        + [one] * 3 + [three, one, one],
        [table, cuts, k, row_low, row_high, y_low, y_high,
         low_low, low_high, high_low, high_high],
        [pltpu.VMEM(s, f32) for s in (three[0], one[0], (2,) + one[0], one[0])]
        + [pltpu.VMEM((3, layers * 4, ny), f32)] * (1 if two else 2),
    )
    siblings, factors, group = [], [], own
    for s in range(stages - 1):
        last = s == stages - 2
        outputs = [slabs(FIRST_COUNT), slabs(7), message_of(LAST_COUNT if last else FIRST_COUNT, 2)]
        sibling, factor, message, *joined = kernel_call(
            functools.partial(join_kernel, s, last, layers + 1),
            outputs + ([] if last else [slabs(FIRST_COUNT)]),
            [cuts, group, swapped(message, s + 1)],
        )
        siblings.append(sibling)
        factors.append(factor)
        group = None if last else joined[0]
    fields = ((3, layers + 2) + slab, f32)
    message, own, rights, d2, kept, ends, first = kernel_call(
        functools.partial(middle_kernel, stages),
        [message_of(3 if stages == 1 else SECOND_COUNT, 1), slabs(SECOND_COUNT), slabs(6), three,
         slabs(2 * stages + 5), slabs(3), fields],
        [cuts, own, pair] + siblings + [swapped(message, stages)]
        + [lx, ly, lz, d, e, inverse],
    )
    siblings, group = [], own
    for s in range(stages - 1):
        last = s == stages - 2
        outputs = [slabs(SECOND_COUNT), message_of(3 if last else SECOND_COUNT, 1)]
        sibling, message, *joined = kernel_call(
            functools.partial(join_again_kernel, s, last),
            outputs + ([] if last else [slabs(SECOND_COUNT)]),
            [group, swapped(message, s + 1), factors[s]],
        )
        siblings.append(sibling)
        group = None if last else joined[0]
    out = ((3, nz, nx, ny), f32)
    pressure, residual = kernel_call(
        functools.partial(final_kernel, stages),
        [out, out],
        [cuts, own, pair] + siblings + [swapped(message, stages)]
        + [lx, ly, lz, first, rights, d2, e, inverse, kept, ends],
        [pltpu.VMEM((3, nz + 2) + slab, f32)]
        + [pltpu.VMEM((3, nz, nx, ny), f32)] * 2
        + [pltpu.SemaphoreType.DMA((2, nz // CHUNK))],
        space=pl.ANY,
    )
    return pressure, residual


def solution(mesh):
    return jax.shard_map(
        per_device,
        mesh=mesh,
        in_specs=(P("gz", "gx", "gy"), P(), P()),
        out_specs=(P(None, "gz", "gx", "gy"), P(None, "gz", "gx", "gy")),
        check_vma=False,
    )
```

time: 35.6 us -> 32.4 us (0.910)
  waiting for transfers between devices: 11.3 us -> 8.15 us
  starting transfers between devices: 15.3 us -> 12.5 us
  Pallas kernels: 5.7 us -> 7.74 us
  local copies, waits for them, and re-layouts: 2.23 us -> 3.18 us
    ppermute x4 -> x3, waiting for transfers between devices: 10.5 us -> 5.32 us  [swapped(): lax.ppermute(values, 'gz', [(i, i ^ 2 ** stage) for i in range(size)])]
    ppermute x3, starting transfers between devices: 4.58 us -> 2.43 us  [ring(): lax.ppermute(values, axis, [(i, (i + distance) % size) for i in range(siz...]
    pallas_call x7 -> x6, Pallas kernels: 5.7 us -> 7.74 us  [kernel_call(): pl.pallas_call(kernel, out_shape=[jax.ShapeDtypeStruct(s, t) for s, t in...]
    ppermute x2, waiting for transfers between devices: 0.01 us -> 1.51 us  [diagonal(): return lax.ppermute(values, ('gx', 'gy'), route)]
    unnamed x6 -> x8, local copies, waits for them, and re-layouts: 2.23 us -> 3.18 us
    ppermute x4 -> x3, starting transfers between devices: 8.98 us -> 8.37 us  [swapped(): lax.ppermute(values, 'gz', [(i, i ^ 2 ** stage) for i in range(size)])]
    ppermute x3, waiting for transfers between devices: 0.82 us -> 1.32 us  [ring(): lax.ppermute(values, axis, [(i, (i + distance) % size) for i in range(siz...]
  transfers between devices with their start and end apart: 9 -> 8, of which waited for: 5 -> 6; matrix products, arithmetic and copies ran while one was open for 0% -> 0% of each run, Pallas kernels for 3% -> 4%
where the time goes in v4:
time: 32.4 us; the launch traced here: 32.3 us
  starting transfers between devices  12.5 us (39%)
  waiting for transfers between devices  8.15 us (25%)
  Pallas kernels  7.74 us (24%)
  local copies, waits for them, and re-layouts  3.18 us (10%)
  between operations  0.65 us (2%)
    ppermute x3, starting transfers between devices, swapped(): lax.ppermute(values, 'gz', [(i, i ^ 2 ** stage) for i in range(size)])  8.37 us
    pallas_call x6, Pallas kernels, kernel_call(): pl.pallas_call(kernel, out_shape=[jax.ShapeDtypeStruct(s, t) for s, t in...  7.74 us
    ppermute x3, waiting for transfers between devices, swapped(): lax.ppermute(values, 'gz', [(i, i ^ 2 ** stage) for i in range(size)])  5.32 us
    unnamed x8, local copies, waits for them, and re-layouts  3.18 us
    ppermute x3, starting transfers between devices, ring(): lax.ppermute(values, axis, [(i, (i + distance) % size) for i in range(siz...  2.43 us
    ppermute x2, starting transfers between devices, diagonal(): return lax.ppermute(values, ('gx', 'gy'), route)  1.75 us
    ppermute x2, waiting for transfers between devices, diagonal(): return lax.ppermute(values, ('gx', 'gy'), route)  1.51 us
    ppermute x3, waiting for transfers between devices, ring(): lax.ppermute(values, axis, [(i, (i + distance) % size) for i in range(siz...  1.32 us
  transfers between devices with their start and end apart: 8, of which 6 were waited for; matrix products, arithmetic and copies ran while one was open for 0% of the time, Pallas kernels for 4%

profile of v4, /device:TPU:0, one launch (start us, length us, event | category | flops | bytes accessed | tf_op | source)
XLA Modules:
  0.0 32.3 jit_solution(5743496977590219754)
XLA Ops:
  0.6 3.1 %collective-permute-start = (s32[16,16,128]{2,1,0:T(8,128)}, s32[16,16,128]{2,1,0:T(8,128)S(1)}, u32[]{:S(2)}, u32[]{:S(2)}) collective-permute-start(s32[16,16,128]{2,1,0:T(8,128)} %own_ref.1), channel_id=1, source_target_pairs={{0,1},{1,0},{2,3},{3,2},{4,5},{5,4},{6,7},{7,6},{8,9},{9,8},{10,11... | collective-permute-start | bytes 393224 | tf_op jit(solution)/shard_map/ppermute | solution.py:660
  3.7 0.0 copy-start
  3.7 0.9 %copy-done = s32[16,16,128]{2,1,0:T(8,128)S(1)} copy-done((s32[16,16,128]{2,1,0:T(8,128)S(1)}, s32[16,16,128]{2,1,0:T(8,128)}, u32[]{:S(2)}) %copy-start) | copy-done | bytes 131096
  4.7 0.0 copy-start.2
  4.7 0.7 %copy-done.2 = f32[3,16]{1,0:T(4,128)S(1)} copy-done((f32[3,16]{1,0:T(4,128)S(1)}, f32[3,16]{1,0:T(4,128)}, u32[]{:S(2)}) %copy-start.2) | copy-done | bytes 216
  5.3 0.0 copy-start.3
  5.3 0.7 %copy-done.3 = s32[63]{0:T(128)S(1)} copy-done((s32[63]{0:T(128)S(1)}, s32[63]{0:T(128)}, u32[]{:S(2)}) %copy-start.3) | copy-done | bytes 276
  6.0 0.9 %shard_map.50 = (f32[3,16,16,128]{3,2,1,0:T(8,128)S(1)}, f32[3,8,128]{2,1,0:T(8,128)S(1)}, f32[40,128]{1,0:T(8,128)S(1)}) custom-call(f32[3,16]{1,0:T(4,128)S(1)} %copy-done.2, s32[63]{0:T(128)S(1)} %copy-done.3, s32[16,16,128]{2,1,0:T(8,128)S(1)} %copy-done), custom_call_target="tpu_custom_call" | custom-call | flops 10000000 | bytes 1000000 | tf_op jit(solution)/shard_map/pallas_call | solution.py:647
  6.9 0.5 %collective-permute-done.other_ref = s32[16,16,128]{2,1,0:T(8,128)S(1)} collective-permute-done((s32[16,16,128]{2,1,0:T(8,128)}, s32[16,16,128]{2,1,0:T(8,128)S(1)}, u32[]{:S(2)}, u32[]{:S(2)}) %collective-permute-start) | collective-permute-done | bytes 131104 | tf_op jit(solution)/shard_map/ppermute | solution.py:660
  7.4 0.0 copy-start.1
  7.4 0.9 %copy-done.1 = s32[16,16,128]{2,1,0:T(8,128)S(1)} copy-done((s32[16,16,128]{2,1,0:T(8,128)S(1)}, s32[16,16,128]{2,1,0:T(8,128)}, u32[]{:S(2)}) %copy-start.1) | copy-done | bytes 131096
  8.3 0.1 shard_map.51
  8.5 1.7 %collective-permute-start.1 = (s32[128,128]{1,0:T(8,128)S(1)}, s32[128,128]{1,0:T(8,128)S(1)}, u32[]{:S(2)}, u32[]{:S(2)}) collective-permute-start(s32[128,128]{1,0:T(8,128)S(1)} %get-tuple-element.27), channel_id=1, source_target_pairs={{0,16},{16,0},{1,17},{17,1},{2,18},{18,2},{3,19},{19,3},{4,20},{20... | collective-permute-start | bytes 196616 | tf_op jit(solution)/shard_map/ppermute | solution.py:665
  10.2 0.0 collective-permute-start.5
  10.2 1.7 %collective-permute-start.4 = (s32[32,128]{1,0:T(8,128)S(1)}, s32[32,128]{1,0:T(8,128)S(1)}, u32[]{:S(2)}, u32[]{:S(2)}) collective-permute-start(s32[32,128]{1,0:T(8,128)S(1)} %get-tuple-element.26.strip_ref), channel_id=1, source_target_pairs={{0,20},{4,24},{8,28},{12,16},{16,4},{20,8},{24,12},{28,0},{1,21},{... | collective-permute-start | bytes 49160 | tf_op jit(solution)/shard_map/ppermute | solution.py:675
  11.9 0.7 %collective-permute-start.3 = (s32[32,128]{1,0:T(8,128)S(1)}, s32[32,128]{1,0:T(8,128)S(1)}, u32[]{:S(2)}, u32[]{:S(2)}) collective-permute-start(s32[32,128]{1,0:T(8,128)S(1)} %get-tuple-element.26.strip_ref), channel_id=1, source_target_pairs={{0,12},{4,0},{8,4},{12,8},{1,13},{5,1},{9,5},{13,9},{2,14},{6,2},{... | collective-permute-start | bytes 49160 | tf_op jit(solution)/shard_map/ppermute | solution.py:665
  12.7 0.0 collective-permute-start.2
  12.7 0.3 %shard_map.52.k_ref = f32[3,32,16,128]{3,2,1,0:T(8,128)S(1)} custom-call(f32[3,8,128]{2,1,0:T(8,128)S(1)} %get-tuple-element.24.table_ref, f32[3,16,16,128]{3,2,1,0:T(8,128)S(1)} %get-tuple-element.25.own_ref, s32[16,16,128]{2,1,0:T(8,128)S(1)} %collective-permute-done.other_ref, s32[32,128]{1,0:T(8,128)S(1)} %get-tuple-element.26.strip_ref), custom_call_target="tpu_custom_call" | custom-call | flops 10000000 | bytes 1000000 | tf_op jit(solution)/shard_map/pallas_call | solution.py:647
  13.0 0.4 %collective-permute-done.5.high_low.high_high = s32[32,128]{1,0:T(8,128)S(1)} collective-permute-done((s32[32,128]{1,0:T(8,128)S(1)}, s32[32,128]{1,0:T(8,128)S(1)}, u32[]{:S(2)}, u32[]{:S(2)}) %collective-permute-start.5) | collective-permute-done | bytes 16416 | tf_op jit(solution)/shard_map/ppermute | solution.py:675
  13.4 1.1 %collective-permute-done.4.low_low.low_high = s32[32,128]{1,0:T(8,128)S(1)} collective-permute-done((s32[32,128]{1,0:T(8,128)S(1)}, s32[32,128]{1,0:T(8,128)S(1)}, u32[]{:S(2)}, u32[]{:S(2)}) %collective-permute-start.4) | collective-permute-done | bytes 16416 | tf_op jit(solution)/shard_map/ppermute | solution.py:675
  14.5 0.0 collective-permute-done.3.y_high
  14.5 1.3 %collective-permute-done.2.y_low = s32[32,128]{1,0:T(8,128)S(1)} collective-permute-done((s32[32,128]{1,0:T(8,128)S(1)}, s32[32,128]{1,0:T(8,128)S(1)}, u32[]{:S(2)}, u32[]{:S(2)}) %collective-permute-start.2) | collective-permute-done | bytes 16416 | tf_op jit(solution)/shard_map/ppermute | solution.py:665
  15.8 0.0 collective-permute-done.1.row_low.row_high
  15.8 2.2 %shard_map.53 = (f32[120,128]{1,0:T(8,128)S(1)}, f32[11,24,256]{2,1,0:T(8,128)S(1)}, f32[16,24,256]{2,1,0:T(8,128)S(1)}, f32[32,24,256]{2,1,0:T(8,128)S(1)}, f32...) custom-call(f32[3,8,128]{2,1,0:T(8,128)S(1)} %get-tuple-element.24.t, ...), custom_call_target="tpu_custom_call" | custom-call | tf_op jit(solution)/shard_map/pallas_call | solution.py:647
  18.0 2.6 %collective-permute-start.6 = (f32[120,128]{1,0:T(8,128)S(1)}, f32[120,128]{1,0:T(8,128)S(1)}, u32[]{:S(2)}, u32[]{:S(2)}) collective-permute-start(f32[120,128]{1,0:T(8,128)S(1)} %get-tuple-element.30), channel_id=1, source_target_pairs={{0,2},{1,3},{2,0},{3,1},{4,6},{5,7},{6,4},{7,5},{8,10},{9,11},{10,... | collective-permute-start | bytes 184328 | tf_op jit(solution)/shard_map/ppermute | solution.py:660
  20.6 2.5 %collective-permute-done.6.refs_2_ = f32[120,128]{1,0:T(8,128)S(1)} collective-permute-done((f32[120,128]{1,0:T(8,128)S(1)}, f32[120,128]{1,0:T(8,128)S(1)}, u32[]{:S(2)}, u32[]{:S(2)}) %collective-permute-start.6) | collective-permute-done | bytes 61472 | tf_op jit(solution)/shard_map/ppermute | solution.py:660
  23.1 2.8 %shard_map.54 = (f32[80,128]{1,0:T(8,128)S(1)}, f32[6,24,256]{2,1,0:T(8,128)S(1)}, f32[6,24,256]{2,1,0:T(8,128)S(1)}, f32[3,32,24,256]{3,2,1,0:T(8,128)S(1)}, f3...) custom-call(f32[40,128]{1,0:T(8,128)S(1)} %get-tuple-element.23.cut_ref, ...), custom_call_target="tpu_custom_call" | custom-call | tf_op jit(solution)/shard_map/pallas_call | solution.py:647
  26.0 2.7 %collective-permute-start.7 = (f32[80,128]{1,0:T(8,128)S(1)}, f32[80,128]{1,0:T(8,128)S(1)}, u32[]{:S(2)}, u32[]{:S(2)}) collective-permute-start(f32[80,128]{1,0:T(8,128)S(1)} %get-tuple-element.38), channel_id=1, source_target_pairs={{0,2},{1,3},{2,0},{3,1},{4,6},{5,7},{6,4},{7,5},{8,10},{9,11},{10,... | collective-permute-start | bytes 122888 | tf_op jit(solution)/shard_map/ppermute | solution.py:660
  28.7 2.3 %collective-permute-done.7.refs_2_ = f32[80,128]{1,0:T(8,128)S(1)} collective-permute-done((f32[80,128]{1,0:T(8,128)S(1)}, f32[80,128]{1,0:T(8,128)S(1)}, u32[]{:S(2)}, u32[]{:S(2)}) %collective-permute-start.7) | collective-permute-done | bytes 40992 | tf_op jit(solution)/shard_map/ppermute | solution.py:660
  30.9 1.3 %shard_map.55 = (f32[3,16,16,128]{3,2,1,0:T(8,128)}, f32[3,16,16,128]{3,2,1,0:T(8,128)}) custom-call(f32[40,128]{1,0:T(8,128)S(1)} %get-tuple-element.23.cut_ref, f32[6,24,256]{2,1,0:T(8,128)S(1)} %get-tuple-element.37.refs_0_, f32[16,24,256]{2,1,0:T(8,128)S(1)} %get-tuple-element.29.refs_1_, f32[80,128]{1,0:T(8,128)S(1)} %collective-permute-done.7.refs_2_, ...), custom_call_target="tpu_custom_call" | custom-call | tf_op jit(solution)/shard_map/pallas_call | solution.py:647
Async XLA Ops:
  0.6 6.8 %collective-permute-start = (s32[16,16,128]{2,1,0:T(8,128)}, s32[16,16,128]{2,1,0:T(8,128)S(1)}, u32[]{:S(2)}, u32[]{:S(2)}) collective-permute-start(s32[16,16,128]{2,1,0:T(8,128)} %own_ref.1), channel_id=1, source_target_pairs={{0,1},{1,0},{2,3},{3,2},{4,5},{5,4},{6,7},{7,6},{8,9},{9,8},{10,11... | collective-permute-start | bytes 393224 | tf_op jit(solution)/shard_map/ppermute | solution.py:660
  3.7 0.9 %copy-start = (s32[16,16,128]{2,1,0:T(8,128)S(1)}, s32[16,16,128]{2,1,0:T(8,128)}, u32[]{:S(2)}) copy-start(s32[16,16,128]{2,1,0:T(8,128)} %own_ref.1) | copy-start | bytes 393220
  4.7 0.7 %copy-start.2 = (f32[3,16]{1,0:T(4,128)S(1)}, f32[3,16]{1,0:T(4,128)}, u32[]{:S(2)}) copy-start(f32[3,16]{1,0:T(4,128)} %table.1) | copy-start | bytes 580
  5.3 0.7 %copy-start.3 = (s32[63]{0:T(128)S(1)}, s32[63]{0:T(128)}, u32[]{:S(2)}) copy-start(s32[63]{0:T(128)} %breaks.1) | copy-start | bytes 760
  7.4 0.9 %copy-start.1 = (s32[16,16,128]{2,1,0:T(8,128)S(1)}, s32[16,16,128]{2,1,0:T(8,128)}, u32[]{:S(2)}) copy-start(s32[16,16,128]{2,1,0:T(8,128)} %own_ref.1) | copy-start | bytes 393220
  8.5 7.3 %collective-permute-start.1 = (s32[128,128]{1,0:T(8,128)S(1)}, s32[128,128]{1,0:T(8,128)S(1)}, u32[]{:S(2)}, u32[]{:S(2)}) collective-permute-start(s32[128,128]{1,0:T(8,128)S(1)} %get-tuple-element.27), channel_id=1, source_target_pairs={{0,16},{16,0},{1,17},{17,1},{2,18},{18,2},{3,19},{19,3},{4,20},{20... | collective-permute-start | bytes 196616 | tf_op jit(solution)/shard_map/ppermute | solution.py:665
  10.2 3.2 %collective-permute-start.5 = (s32[32,128]{1,0:T(8,128)S(1)}, s32[32,128]{1,0:T(8,128)S(1)}, u32[]{:S(2)}, u32[]{:S(2)}) collective-permute-start(s32[32,128]{1,0:T(8,128)S(1)} %get-tuple-element.26.strip_ref), channel_id=1, source_target_pairs={{0,28},{4,16},{8,20},{12,24},{16,12},{20,0},{24,4},{28,8},{1,29},{... | collective-permute-start | bytes 49160 | tf_op jit(solution)/shard_map/ppermute | solution.py:675
  10.2 4.3 %collective-permute-start.4 = (s32[32,128]{1,0:T(8,128)S(1)}, s32[32,128]{1,0:T(8,128)S(1)}, u32[]{:S(2)}, u32[]{:S(2)}) collective-permute-start(s32[32,128]{1,0:T(8,128)S(1)} %get-tuple-element.26.strip_ref), channel_id=1, source_target_pairs={{0,20},{4,24},{8,28},{12,16},{16,4},{20,8},{24,12},{28,0},{1,21},{... | collective-permute-start | bytes 49160 | tf_op jit(solution)/shard_map/ppermute | solution.py:675
  11.9 2.6 %collective-permute-start.3 = (s32[32,128]{1,0:T(8,128)S(1)}, s32[32,128]{1,0:T(8,128)S(1)}, u32[]{:S(2)}, u32[]{:S(2)}) collective-permute-start(s32[32,128]{1,0:T(8,128)S(1)} %get-tuple-element.26.strip_ref), channel_id=1, source_target_pairs={{0,12},{4,0},{8,4},{12,8},{1,13},{5,1},{9,5},{13,9},{2,14},{6,2},{... | collective-permute-start | bytes 49160 | tf_op jit(solution)/shard_map/ppermute | solution.py:665
  12.7 3.2 %collective-permute-start.2 = (s32[32,128]{1,0:T(8,128)S(1)}, s32[32,128]{1,0:T(8,128)S(1)}, u32[]{:S(2)}, u32[]{:S(2)}) collective-permute-start(s32[32,128]{1,0:T(8,128)S(1)} %get-tuple-element.26.strip_ref), channel_id=1, source_target_pairs={{0,4},{4,8},{8,12},{12,0},{1,5},{5,9},{9,13},{13,1},{2,6},{6,10},{... | collective-permute-start | bytes 49160 | tf_op jit(solution)/shard_map/ppermute | solution.py:665
  18.0 5.1 %collective-permute-start.6 = (f32[120,128]{1,0:T(8,128)S(1)}, f32[120,128]{1,0:T(8,128)S(1)}, u32[]{:S(2)}, u32[]{:S(2)}) collective-permute-start(f32[120,128]{1,0:T(8,128)S(1)} %get-tuple-element.30), channel_id=1, source_target_pairs={{0,2},{1,3},{2,0},{3,1},{4,6},{5,7},{6,4},{7,5},{8,10},{9,11},{10,... | collective-permute-start | bytes 184328 | tf_op jit(solution)/shard_map/ppermute | solution.py:660
  26.0 4.9 %collective-permute-start.7 = (f32[80,128]{1,0:T(8,128)S(1)}, f32[80,128]{1,0:T(8,128)S(1)}, u32[]{:S(2)}, u32[]{:S(2)}) collective-permute-start(f32[80,128]{1,0:T(8,128)S(1)} %get-tuple-element.38), channel_id=1, source_target_pairs={{0,2},{1,3},{2,0},{3,1},{4,6},{5,7},{6,4},{7,5},{8,10},{9,11},{10,... | collective-permute-start | bytes 122888 | tf_op jit(solution)/shard_map/ppermute | solution.py:660

commit v5 on v4

--- a/solution.py
+++ b/solution.py
@@ -44,29 +44,39 @@
     return (lax.axis_index("gz") % 2) * nz
 
 
-def pack_kernel(own_ref, other_ref, table_ref, strip_ref, *row_refs):
-    nz, nx, ny = own_ref.shape
+def pack_kernel(facies_ref, copy_ref, rims_ref):
+    nz, nx, ny = facies_ref.shape
+    copy_ref[...] = facies_ref[...]
     lane = lax.broadcasted_iota(jnp.int32, (nx, ny), 1)
     row = iotas(8, ny)[0]
+    strip = jnp.zeros((nx, ny), jnp.int32)
+    for z in range(0, nz, 2):
+        pair = [facies_ref[z], facies_ref[z + 1]]
+        for at in (z, z + 1):
+            strip = jnp.where(lane // 8 == at, moved(pair[at - z], 8 * at + WIDE, 1), strip)
+        first = jnp.where(row < 4, pair[0][:8], moved(pair[1][:8], 4, 0))
+        last = jnp.where(row < 4, moved(pair[0][nx - 8 :], 4, 0), pair[1][nx - 8 :])
+        start = nx + 4 * z
+        if rims_ref.shape[0] == nx + 4 * nz:
+            rims_ref[start : start + 8, :] = jnp.where(lax.axis_index("gx") == 0, last, first)
+        else:
+            rims_ref[start : start + 8, :] = first
+            rims_ref[start + 4 * nz : start + 4 * nz + 8, :] = last
+    rims_ref[0:nx, :] = strip
+
+
+def merge_kernel(facies_ref, own_ref, other_ref, table_ref, copy_ref, strip_ref, *row_refs):
+    nz = facies_ref.shape[0]
+    size, ny = own_ref.shape
+    copy_ref[...] = facies_ref[...]
+    nx = size - 4 * nz * len(row_refs)
     swap = own_start(nz) > 0
     for b in range(2):
-        strip = jnp.zeros((nx, ny), jnp.int32)
-        for z in range(0, nz, 2):
-            pair = []
-            for at in (z, z + 1):
-                layer = jnp.where(swap == (b == 1), own_ref[at], other_ref[at])
-                pair.append(layer)
-                strip = jnp.where(lane // 8 == at, moved(layer, 8 * at + WIDE, 1), strip)
-            first = jnp.where(row < 4, pair[0][:8], moved(pair[1][:8], 4, 0))
-            last = jnp.where(row < 4, moved(pair[0][nx - 8 :], 4, 0), pair[1][nx - 8 :])
-            start = (b * nz + z) * 4
-            spot = slice(start, start + 8)
-            if len(row_refs) == 1:
-                row_refs[0][spot, :] = jnp.where(lax.axis_index("gx") == 0, last, first)
-            else:
-                row_refs[0][spot, :] = first
-                row_refs[1][spot, :] = last
-        strip_ref[b * nx : (b + 1) * nx, :] = strip
+        rims = jnp.where(swap == (b == 1), own_ref[...], other_ref[...])
+        strip_ref[b * nx : (b + 1) * nx, :] = rims[:nx]
+        for n, ref in enumerate(row_refs):
+            start = nx + 4 * nz * n
+            ref[4 * nz * b : 4 * nz * (b + 1), :] = rims[start : start + 4 * nz]
 
 
 def lookup(table, index):
@@ -91,7 +101,12 @@
             k_ref[q, z] = lookup(tables[q], facies_ref[z])
     pair = lax.axis_index("gz") // 2
     layers = [pair * 2 * nz + r - 1 for r in range(2 * nz + 1)]
-    for s in range(stages):
+    if stages == 1:
+        high = is_high(0)
+        layers = [
+            pair * 2 * nz + jnp.where(high, 2 * nz - 1 - r, r - 1) for r in range(2 * nz + 1)
+        ]
+    for s in range(stages if stages > 1 else 0):
         base, size = (pair >> (s + 1)) << (s + 1), 2**s
         layers.append((base + size) * 2 * nz - 1)
         layers.append(jnp.where(is_high(s), base, base + 2 * size) * 2 * nz - 1)
@@ -127,11 +142,18 @@
         self.rows_each = halo if self.one_sided else 2 * halo
         self.per_tile = 8 // self.rows_each
         self.tiles = -(-count // self.per_tile)
-        self.strip = slice(count * nx, count * nx + nx + 8)
-        self.rows = self.strip.stop + 8 * self.tiles
+        self.abreast = ny // (2 * halo * count)
+        strips = -(-(nx // 8 + 1) // self.abreast)
+        self.sides = count * nx + 8 * strips
+        self.rows = self.sides + 8 * self.tiles
+
+    def strip(self, t, q):
+        start = self.count * self.nx + 8 * (t // self.abreast)
+        shift = 2 * self.halo * (self.count * (t % self.abreast) + q) + self.halo
+        return slice(start, start + 8), shift
 
     def tile(self, q):
-        start = self.strip.stop + 8 * (q // self.per_tile)
+        start = self.sides + 8 * (q // self.per_tile)
         return slice(start, start + 8)
 
     def side_moved(self, tile, q, sign):
@@ -151,13 +173,16 @@
 
     def write(self, ref, slabs):
         nx, ny, halo = self.nx, self.ny, self.halo
-        lane = iotas(nx + 8, ny)[1]
-        strip = moved(slabs[0][:, ny:], halo, 1)
-        for q in range(1, self.count):
-            turned = moved(slabs[q][:, ny:], 2 * halo * q + halo, 1)
-            strip = jnp.where(lane < 2 * halo * q, strip, turned)
-        ref[self.strip, :] = strip
-        row = iotas(8, ny)[0]
+        row, lane = iotas(8, ny)
+        strips = {}
+        for t in range(nx // 8 + 1):
+            for q, slab in enumerate(slabs):
+                spot, shift = self.strip(t, q)
+                turned = moved(slab[8 * t : 8 * t + 8, ny:], shift, 1)
+                held = strips.get(spot.start, turned)
+                strips[spot.start] = jnp.where(lane < shift - halo, held, turned)
+        for start, strip in strips.items():
+            ref[start : start + 8, :] = strip
         for q, slab in enumerate(slabs):
             ref[q * nx : (q + 1) * nx, :] = slab[:nx, :ny]
             turned = self.side_moved(slab[nx:, :ny], q, 1)
@@ -167,14 +192,16 @@
                 ref[self.tile(q), :] = tile
 
     def read(self, ref):
-        nx, halo = self.nx, self.halo
-        strip = ref[self.strip, :]
+        nx = self.nx
         slabs = []
         for q in range(self.count):
             side = self.side_moved(ref[self.tile(q), :], q, -1)
             body = jnp.concatenate([ref[q * nx : (q + 1) * nx, :], side], axis=0)
-            beside = moved(strip, -(2 * halo * q + halo), 1)
-            slabs.append(jnp.concatenate([body, beside], axis=1))
+            beside = []
+            for t in range(nx // 8 + 1):
+                spot, shift = self.strip(t, q)
+                beside.append(moved(ref[spot, :], -shift, 1))
+            slabs.append(jnp.concatenate([body, jnp.concatenate(beside, axis=0)], axis=1))
         return slabs
 
 
@@ -237,19 +264,13 @@
     return [n - factor * g for n, g in zip(near_g, far_g)]
 
 
-def eliminate_kernel(
-    stages, table_ref, cut_ref, k_ref, row_low, row_high, y_low, y_high,
-    low_low, low_high, high_low, high_high,
-    message_ref, own_ref, pair_ref, lx_ref, ly_ref, lz_ref, d_ref, e_ref, inverse_ref,
-    all_ref, flow_ref, source_ref, centre_ref, low_ref, high_ref=None,
-):
-    high_ref = low_ref if high_ref is None else high_ref
+def assemble_slabs(k_ref, tables, rims, low_ref, high_ref, store):
+    row_low, row_high, y_low, y_high, low_low, low_high, high_low, high_high = rims
     layers, nx, ny = k_ref.shape[1:]
     nz = layers // 2
     at_x, at_y = lax.axis_index("gx"), lax.axis_index("gy")
     has_x_low, has_x_high = at_x > 0, at_x < lax.axis_size("gx") - 1
     has_y_low, has_y_high = at_y > 0, at_y < lax.axis_size("gy") - 1
-    tables = [table_ref[q] for q in range(3)]
 
     row, lane = iotas(nx + 8, 2 * ny)
     x_in = (row < nx) | ((row < nx + WIDE) & has_x_high) | ((row >= nx + 8 - WIDE) & has_x_low)
@@ -291,31 +312,55 @@
                     high = moved(high, 4, 0)
                 side = jnp.where(row_in, jnp.where(row < 4, high, low), 0.0)
                 beside = jnp.where(strip_in, moved(strips[b][q], -(8 * z + WIDE), 1), 0.0)
-                all_ref[q, at, :nx, :ny] = k_ref[q, at]
-                all_ref[q, at, nx:, :ny] = side
-                all_ref[q, at, :, ny:] = beside
-
-    def flow_after(here, axis, inside):
-        there = moved(here, -1, axis)
-        total = here + there
-        return jnp.where(inside > 0.0, 2.0 * (here * there) / total, total)
-
-    def tau_and_source(flow, axis, inside, inside_back):
-        back = moved(flow, 1, axis)
-        return flow * (2.0 - inside) + back * (2.0 - inside_back), flow - back
-
+                body = jnp.concatenate([k_ref[q, at], side], axis=0)
+                store(q, at, jnp.concatenate([body, beside], axis=1))
+
+    return cell, in_x, in_xp, in_y, in_yp
+
+
+def flow_after(here, there, inside):
+    total = here + there
+    return jnp.where(inside > 0.0, 2.0 * (here * there) / total, total)
+
+
+def tau_and_source(flow, back, inside, inside_back):
+    return flow * (2.0 - inside) + back * (2.0 - inside_back), flow - back
+
+
+def eliminate_kernel(
+    stages, table_ref, cut_ref, k_ref, row_low, row_high, y_low, y_high,
+    low_low, low_high, high_low, high_high,
+    message_ref, own_ref, pair_ref, lx_ref, ly_ref, lz_ref, d_ref, e_ref, inverse_ref,
+    all_ref, flow_ref, source_ref, centre_ref, low_ref, high_ref=None,
+):
+    layers, nx, ny = k_ref.shape[1:]
+    nz = layers // 2
+    rims = row_low, row_high, y_low, y_high, low_low, low_high, high_low, high_high
+
+    def store(q, at, slab):
+        all_ref[q, at] = slab
+
+    cell, in_x, in_xp, in_y, in_yp = assemble_slabs(
+        k_ref, [table_ref[q] for q in range(3)], rims, low_ref,
+        low_ref if high_ref is None else high_ref, store,
+    )
     for at in range(layers):
-        flow_x = flow_after(all_ref[0, at], 0, in_x)
-        flow_ref[at] = flow_after(all_ref[1, at], 1, in_y)
+        kx, ky = all_ref[0, at], all_ref[1, at]
+        flow_x = flow_after(kx, moved(kx, -1, 0), in_x)
+        flow_ref[at] = flow_after(ky, moved(ky, -1, 1), in_y)
         lx_ref[at] = flow_x * in_x
-        centre_ref[at], source_ref[0, at] = tau_and_source(flow_x, 0, in_x, in_xp)
+        centre_ref[at], source_ref[0, at] = tau_and_source(
+            flow_x, moved(flow_x, 1, 0), in_x, in_xp
+        )
         if at % nz < nz - 1:
             kz, above = all_ref[2, at], all_ref[2, at + 1]
             lz_ref[at] = jnp.where(cell, 2.0 * (kz * above) / (kz + above), 0.0)
     for at in range(layers):
         flow_y = flow_ref[at]
         ly_ref[at] = flow_y * in_y
-        tau_y, source_ref[1, at] = tau_and_source(flow_y, 1, in_y, in_yp)
+        tau_y, source_ref[1, at] = tau_and_source(
+            flow_y, moved(flow_y, 1, 1), in_y, in_yp
+        )
         centre = centre_ref[at] + tau_y
         if at % nz > 0:
             centre = centre + lz_ref[at - 1]
@@ -641,6 +686,257 @@
         copy.wait()
 
 
+def put(ref, index, slab):
+    rows, ny = slab.shape[0], slab.shape[1] // 2
+    for h in range(2):
+        half = slab[:, h * ny : (h + 1) * ny]
+        ref[index + (h, slice(8, 8 + rows))] = half
+        ref[index + (h, slice(0, 8))] = half[rows - 8 :]
+        ref[index + (h, slice(8 + rows, 16 + rows))] = half[:8]
+
+
+def get(ref, index, shift=0):
+    rows = ref.shape[-2] - 16
+    halves = [ref[index + (h, slice(8 + shift, 8 + shift + rows))] for h in range(2)]
+    return jnp.concatenate(halves, axis=1)
+
+
+def signed():
+    return jnp.where(is_high(0), -1.0, 1.0)
+
+
+def both_halves(ref, r):
+    values = ref[pl.ds(r, 1), :]
+    return jnp.concatenate([values, values], axis=1)
+
+
+def beside_sum(field_ref, index, lx_ref, ly_ref, j):
+    here, link_y = get(field_ref, index), ly_ref[j]
+    return (
+        get(lx_ref, (j,)) * get(field_ref, index, 1)
+        + get(lx_ref, (j,), -1) * get(field_ref, index, -1)
+        + (link_y * moved(here, -1, 1) + moved(link_y * here, 1, 1))
+    )
+
+
+def end_eliminate_kernel(
+    table_ref, cut_ref, k_ref, row_low, row_high, y_low, y_high,
+    low_low, low_high, high_low, high_high,
+    message_ref, own_ref, lx_ref, ly_ref, lz_ref, d_ref, ratio_ref, inverse_ref,
+    kx_ref, fx_ref, ky_ref, kz_ref, source_ref, centre_ref, low_ref, high_ref=None,
+):
+    layers, nx, ny = k_ref.shape[1:]
+    rims = row_low, row_high, y_low, y_high, low_low, low_high, high_low, high_high
+    high, sign = is_high(0), signed()
+
+    def store(q, at, slab):
+        j = jnp.where(high, layers - 1 - at, at)
+        if q == 0:
+            put(kx_ref, (j,), slab)
+        else:
+            (ky_ref, kz_ref)[q - 1][j] = slab
+
+    cell, in_x, in_xp, in_y, in_yp = assemble_slabs(
+        k_ref, [table_ref[q] for q in range(3)], rims, low_ref,
+        low_ref if high_ref is None else high_ref, store,
+    )
+    zero = jnp.zeros((nx + 8, 2 * ny), jnp.float32)
+    lz_ref[0] = zero
+    lz_ref[layers] = zero
+    for j in range(layers):
+        flow_x = flow_after(get(kx_ref, (j,)), get(kx_ref, (j,), 1), in_x)
+        put(fx_ref, (j,), flow_x)
+        put(lx_ref, (j,), flow_x * in_x)
+        ky = ky_ref[j]
+        ky_ref[j] = flow_after(ky, moved(ky, -1, 1), in_y)
+        if j < layers - 1:
+            kz, above = kz_ref[j], kz_ref[j + 1]
+            lz_ref[j + 1] = jnp.where(cell, 2.0 * (kz * above) / (kz + above), 0.0)
+    for j in range(layers):
+        flow_y = ky_ref[j]
+        ly_ref[j] = flow_y * in_y
+        tau_x, source_ref[0, j] = tau_and_source(
+            get(fx_ref, (j,)), get(fx_ref, (j,), -1), in_x, in_xp
+        )
+        tau_y, source_ref[1, j] = tau_and_source(flow_y, moved(flow_y, 1, 1), in_y, in_yp)
+        centre = tau_x + tau_y + (2.0 * kz_ref[0] if j == 0 else lz_ref[j])
+        if j < layers - 1:
+            centre = centre + lz_ref[j + 1]
+        centre_ref[j] = jnp.where(cell, centre, 1.0)
+    for j in range(layers):
+        flow_z = -kz_ref[0] if j == 0 else -lz_ref[j]
+        if j < layers - 1:
+            flow_z = flow_z + lz_ref[j + 1]
+        forward = [source_ref[0, j], source_ref[1, j], sign * flow_z]
+        pivot = centre_ref[j]
+        if j > 0:
+            pivot = pivot - coupling * ratio
+            forward = [a + coupling * d for a, d in zip(forward, value)]
+        if j < layers - 1:
+            inverse = 1.0 / pivot
+            coupling = lz_ref[j + 1] * (1.0 - both_halves(cut_ref, j + 1))
+            ratio = coupling * inverse
+            value = [a * inverse for a in forward]
+            inverse_ref[j] = inverse
+            ratio_ref[j] = ratio
+            for f in range(3):
+                d_ref[f, j] = value[f]
+    slabs = [pivot, kz_ref[layers - 1]] + forward
+    for q, slab in enumerate(slabs):
+        own_ref[q] = slab
+    Message(LAST_COUNT, 2, nx, ny).write(message_ref, slabs)
+
+
+def expand_kernel(
+    cut_ref, lx_ref, ly_ref, lz_ref, d_ref, ratio_ref, base_ref, phi_ref, part_ref
+):
+    layers = ly_ref.shape[0]
+    zero = jnp.zeros(ly_ref.shape[1:], jnp.float32)
+    phi, base = zero + 1.0, [zero] * 3
+    put(phi_ref, (layers - 1,), phi)
+    for f in range(3):
+        put(base_ref, (f, layers - 1), zero)
+    for j in range(layers - 2, -1, -1):
+        ratio = ratio_ref[j]
+        phi = ratio * phi
+        put(phi_ref, (j,), phi)
+        for f in range(3):
+            base[f] = d_ref[f, j] + ratio * base[f]
+            put(base_ref, (f, j), base[f])
+    along_x = along_y = along_z = zero
+    parts = [zero] * 3
+    for j in range(layers):
+        phi = get(phi_ref, (j,))
+        along_x = along_x + (get(lx_ref, (j,)) * phi) * get(phi_ref, (j,), 1)
+        along_y = along_y + (ly_ref[j] * phi) * moved(phi, -1, 1)
+        cut_low = lz_ref[j] * both_halves(cut_ref, j)
+        if j < layers - 1:
+            cut_high = lz_ref[j + 1] * both_halves(cut_ref, j + 1)
+            along_z = along_z + (cut_high * phi) * get(phi_ref, (j + 1,))
+        for f in range(3):
+            right = beside_sum(base_ref, (f, j), lx_ref, ly_ref, j)
+            if j > 0:
+                right = right + cut_low * get(base_ref, (f, j - 1))
+            if j < layers - 1:
+                right = right + cut_high * get(base_ref, (f, j + 1))
+            parts[f] = parts[f] + phi * right
+    for n, slab in enumerate(parts + [along_x, along_y, 2.0 * along_z]):
+        part_ref[n] = slab
+
+
+def end_join_kernel(layers, cut_ref, own_ref, message_ref, part_ref, next_ref, near_ref):
+    nx, ny = slab_size(own_ref)
+    own = [own_ref[q] for q in range(LAST_COUNT)]
+    other = Message(LAST_COUNT, 2, nx, ny).read(message_ref)
+    sign = signed()
+    cut = both_halves(cut_ref, layers)
+    link, flow, tau = face(own[1], other[1])
+    coupling = link * (1.0 - cut)
+    inverse_other = 1.0 / (other[0] + tau)
+    step = coupling * inverse_other
+    inverse = 1.0 / (own[0] + tau - coupling * step)
+    right_own = own[2:4] + [own[4] + sign * flow]
+    right_other = other[2:4] + [other[4] - sign * flow]
+    cut_near = link * cut
+    along_x, along_y, along_z = [part_ref[3 + n] for n in range(3)]
+    slabs = []
+    for f in range(3):
+        near = (right_own[f] + step * right_other[f]) * inverse
+        beyond = right_other[f] * inverse_other + step * near
+        near_ref[f], near_ref[3 + f] = near, beyond
+        right = part_ref[f] + stencil(near, along_x, along_y)
+        slabs.append(right + (along_z * near + cut_near * beyond))
+        near_ref[6 + f] = slabs[f]
+    near_ref[9], near_ref[10], near_ref[11], near_ref[12] = step, inverse, inverse_other, link
+    Message(3, 1, nx, ny).write(next_ref, slabs)
+
+
+def correct_kernel(
+    cut_ref, near_ref, lx_ref, ly_ref, lz_ref, ratio_ref, inverse_ref, base_ref, phi_ref,
+    first_ref, change_ref, d_ref,
+):
+    layers = ly_ref.shape[0]
+    for j in range(layers):
+        phi = get(phi_ref, (j,))
+        for f in range(3):
+            put(first_ref, (f, j), get(base_ref, (f, j)) + phi * near_ref[f])
+    for j in range(layers - 1):
+        cut_low = lz_ref[j] * both_halves(cut_ref, j)
+        cut_high = lz_ref[j + 1] * both_halves(cut_ref, j + 1)
+        inverse = inverse_ref[j]
+        if j > 0:
+            coupling = lz_ref[j] * (1.0 - both_halves(cut_ref, j))
+        for f in range(3):
+            right = beside_sum(first_ref, (f, j), lx_ref, ly_ref, j)
+            right = right + cut_high * get(first_ref, (f, j + 1))
+            if j > 0:
+                right = right + cut_low * get(first_ref, (f, j - 1)) + coupling * d_ref[f, j - 1]
+            d_ref[f, j] = right * inverse
+    change = [jnp.zeros(ly_ref.shape[1:], jnp.float32)] * 3
+    for f in range(3):
+        change_ref[f, layers - 1] = change[f]
+    for j in range(layers - 2, -1, -1):
+        ratio = ratio_ref[j]
+        for f in range(3):
+            change[f] = d_ref[f, j] + ratio * change[f]
+            change_ref[f, j] = change[f]
+
+
+def end_final_kernel(
+    cut_ref, message_ref, near_ref, lx_ref, ly_ref, lz_ref, phi_ref, first_ref, base_ref,
+    pressure_out, residual_out, change_ref, pressure_ref, residual_ref, sems,
+):
+    layers = ly_ref.shape[0]
+    nz = layers // 2
+    nx, ny = slab_size(ly_ref)
+    high = is_high(0)
+    start = jnp.where(high, nz - own_start(nz), own_start(nz))
+    beside_other = start > 0
+    other = Message(3, 1, nx, ny).read(message_ref)
+    step, inverse, inverse_other, link_near = [near_ref[9 + n] for n in range(4)]
+    near = [(near_ref[6 + f] + step * other[f]) * inverse for f in range(3)]
+    for i in range(-1, nz + 1):
+        j = jnp.clip(start + i, 0, layers - 1)
+        phi = get(phi_ref, (j,))
+        for f in range(3):
+            change = base_ref[f, j] + phi * near[f]
+            if i == -1:
+                change = jnp.where(beside_other, change, 0.0)
+            if i == nz:
+                beyond = other[f] * inverse_other + step * near[f]
+                change = jnp.where(beside_other, beyond, change)
+            put(change_ref, (f, i + 1), change)
+    own_part = (slice(0, nx), slice(0, ny))
+    copies = []
+    for i in range(nz):
+        j = start + i
+        z = jnp.where(high, nz - 1 - i, i)
+        link_high = lz_ref[j + 1]
+        if i == nz - 1:
+            link_high = jnp.where(beside_other, link_near, link_high)
+        cut_low = lz_ref[j] * both_halves(cut_ref, j)
+        cut_high = link_high * both_halves(cut_ref, j + 1)
+        for f in range(3):
+            left_out = beside_sum(change_ref, (f, i + 1), lx_ref, ly_ref, j) + (
+                cut_low * get(change_ref, (f, i)) + cut_high * get(change_ref, (f, i + 2))
+            )
+            pressure = get(first_ref, (f, j)) + get(change_ref, (f, i + 1))
+            pressure_ref[f, z] = pressure[own_part]
+            residual_ref[f, z] = left_out[own_part]
+        if (i + 1) % CHUNK == 0:
+            part = (slice(None), pl.ds(jnp.where(high, nz - 1 - i, i + 1 - CHUNK), CHUNK))
+            for n, (buffer, out) in enumerate(
+                ((pressure_ref, pressure_out), (residual_ref, residual_out))
+            ):
+                copy = pltpu.make_async_copy(
+                    buffer.at[part], out.at[part], sems.at[n, i // CHUNK]
+                )
+                copy.start()
+                copies.append(copy)
+    for copy in copies:
+        copy.wait()
+
+
 def kernel_call(kernel, outputs, operands, scratch=(), smem=0, cost=None, space=pltpu.VMEM):
     specs = [pl.BlockSpec(memory_space=pltpu.SMEM)] * smem
     specs += [pl.BlockSpec(memory_space=pltpu.VMEM)] * (len(operands) - smem)
@@ -650,7 +946,7 @@
         in_specs=specs,
         out_specs=[pl.BlockSpec(memory_space=space)] * len(outputs),
         scratch_shapes=list(scratch),
-        compiler_params=pltpu.CompilerParams(vmem_limit_bytes=24 * 2**20),
+        compiler_params=pltpu.CompilerParams(vmem_limit_bytes=32 * 2**20),
         cost_estimate=cost,
     )(*operands)
 
@@ -682,7 +978,13 @@
     two = lax.axis_size("gx") == 2
     layers = 2 * nz
     cut_rows = -(-(layers + 1 + 2 * stages) // 8) * 8
-    other = swapped(facies, 0)
+    sides = 1 if two else 2
+    facies, rims = kernel_call(
+        pack_kernel,
+        [((nz, nx, ny), i32), ((nx + 4 * nz * sides, ny), i32)],
+        [facies],
+    )
+    other_rims = swapped(rims, 0)
     k, table, cuts = kernel_call(
         functools.partial(prepare_kernel, stages),
         [((3, nz, nx, ny), f32), ((3, 8, ny), f32), ((cut_rows, ny), f32)],
@@ -690,11 +992,12 @@
         smem=2,
         cost=pl.CostEstimate(flops=10**7, bytes_accessed=10**6, transcendentals=0),
     )
-    strip, *rows = kernel_call(
-        pack_kernel,
-        [((2 * nx, ny), i32)] + [((layers * 4, ny), i32)] * (1 if two else 2),
-        [facies, other, table],
-    )
+    facies, strip, *rows = kernel_call(
+        merge_kernel,
+        [((nz, nx, ny), i32), ((2 * nx, ny), i32)] + [((layers * 4, ny), i32)] * sides,
+        [facies, rims, other_rims, table],
+    )
+    other = swapped(facies, 0)
     k, = kernel_call(
         prepare_other_kernel,
         [((3, layers, nx, ny), f32)],
@@ -711,6 +1014,74 @@
         low_low, low_high = diagonal(strip, 1, 1), diagonal(strip, -1, 1)
         high_low, high_high = diagonal(strip, 1, -1), diagonal(strip, -1, -1)
 
+    sizes = nz, nx, ny
+    operands = [table, cuts, k, row_low, row_high, y_low, y_high,
+                low_low, low_high, high_low, high_high]
+    scratch = [pltpu.VMEM((3, layers * 4, ny), f32)] * sides
+    return (sweep_ends if stages == 1 else sweep_tree)(sizes, stages, operands, scratch)
+
+
+def sweep_ends(sizes, stages, operands, scratch):
+    nz, nx, ny = sizes
+    layers, f32 = 2 * nz, jnp.float32
+    cuts = operands[1]
+    slab, tall = (nx + 8, 2 * ny), (2, nx + 24, ny)
+
+    def slabs(*count):
+        return (count + slab, f32)
+
+    def talls(*count):
+        return (count + tall, f32)
+
+    def message_of(count, halo):
+        return ((Message(count, halo, nx, ny).rows, ny), f32)
+
+    def filler(flops):
+        return pl.CostEstimate(flops=flops, bytes_accessed=10**6, transcendentals=0)
+
+    message, own, lx, ly, lz, d, ratio, inverse = kernel_call(
+        end_eliminate_kernel,
+        [message_of(LAST_COUNT, 2), slabs(LAST_COUNT), talls(layers), slabs(layers),
+         slabs(layers + 1), slabs(3, layers), slabs(layers), slabs(layers)],
+        operands,
+        [pltpu.VMEM(*s) for s in (talls(layers), talls(layers), slabs(layers), slabs(layers),
+                                  slabs(2, layers), slabs(layers))] + scratch,
+    )
+    other = swapped(message, stages)
+    base, phi, parts = kernel_call(
+        expand_kernel,
+        [talls(3, layers), talls(layers), slabs(6)],
+        [cuts, lx, ly, lz, d, ratio],
+        cost=filler(10**7),
+    )
+    message, near = kernel_call(
+        functools.partial(end_join_kernel, layers),
+        [message_of(3, 1), slabs(13)],
+        [cuts, own, other, parts],
+    )
+    other = swapped(message, stages)
+    first, change = kernel_call(
+        correct_kernel,
+        [talls(3, layers), slabs(3, layers)],
+        [cuts, near, lx, ly, lz, ratio, inverse, base, phi],
+        [pltpu.VMEM(*slabs(3, layers))],
+        cost=filler(10**7),
+    )
+    out = ((3, nz, nx, ny), f32)
+    return tuple(kernel_call(
+        end_final_kernel,
+        [out, out],
+        [cuts, other, near, lx, ly, lz, phi, first, change],
+        [pltpu.VMEM(*talls(3, nz + 2)), pltpu.VMEM(*out), pltpu.VMEM(*out),
+         pltpu.SemaphoreType.DMA((2, nz // CHUNK))],
+        space=pl.ANY,
+    ))
+
+
+def sweep_tree(sizes, stages, operands, scratch):
+    nz, nx, ny = sizes
+    layers, f32 = 2 * nz, jnp.float32
+    cuts = operands[1]
     slab = (nx + 8, 2 * ny)
     one, three = ((layers,) + slab, f32), ((3, layers) + slab, f32)
 
@@ -725,10 +1096,9 @@
         [message_of(LAST_COUNT if stages == 1 else FIRST_COUNT, 2)]
         + [slabs(FIRST_COUNT), slabs(PAIR_COUNT)]
         + [one] * 3 + [three, one, one],
-        [table, cuts, k, row_low, row_high, y_low, y_high,
-         low_low, low_high, high_low, high_high],
+        operands,
         [pltpu.VMEM(s, f32) for s in (three[0], one[0], (2,) + one[0], one[0])]
-        + [pltpu.VMEM((3, layers * 4, ny), f32)] * (1 if two else 2),
+        + scratch,
     )
     siblings, factors, group = [], [], own
     for s in range(stages - 1):

time: 32.4 us -> 29.5 us (0.910)
  waiting for transfers between devices: 8.15 us -> 2.58 us
  Pallas kernels: 7.74 us -> 10 us
  starting transfers between devices: 12.5 us -> 13.8 us
  local copies, waits for them, and re-layouts: 3.18 us -> 2.23 us
    ppermute x3 -> x4, waiting for transfers between devices: 5.32 us -> 0.01 us  [swapped(): lax.ppermute(values, 'gz', [(i, i ^ 2 ** stage) for i in range(size)])]
    pallas_call x6 -> x9, Pallas kernels: 7.74 us -> 10 us  [kernel_call(): pl.pallas_call(kernel, out_shape=[jax.ShapeDtypeStruct(s, t) for s, t in...]
    ppermute x3 -> x4, starting transfers between devices: 8.37 us -> 10.1 us  [swapped(): lax.ppermute(values, 'gz', [(i, i ^ 2 ** stage) for i in range(size)])]
    unnamed x8 -> x6, local copies, waits for them, and re-layouts: 3.18 us -> 2.23 us
    ppermute x3, waiting for transfers between devices: 1.32 us -> 0.86 us  [ring(): lax.ppermute(values, axis, [(i, (i + distance) % size) for i in range(siz...]
    ppermute x3, starting transfers between devices: 2.43 us -> 2 us  [ring(): lax.ppermute(values, axis, [(i, (i + distance) % size) for i in range(siz...]
  transfers between devices with their start and end apart: 8 -> 9, of which waited for: 6 -> 3; matrix products, arithmetic and copies ran while one was open for 0% -> 0% of each run, Pallas kernels for 4% -> 22%
where the time goes in v5:
time: 29.5 us; the launch traced here: 29.4 us
  starting transfers between devices  13.8 us (47%)
  Pallas kernels  10 us (34%)
  waiting for transfers between devices  2.58 us (9%)
  local copies, waits for them, and re-layouts  2.23 us (8%)
  between operations  0.69 us (2%)
    ppermute x4, starting transfers between devices, swapped(): lax.ppermute(values, 'gz', [(i, i ^ 2 ** stage) for i in range(size)])  10.1 us
    pallas_call x9, Pallas kernels, kernel_call(): pl.pallas_call(kernel, out_shape=[jax.ShapeDtypeStruct(s, t) for s, t in...  10 us
    unnamed x6, local copies, waits for them, and re-layouts  2.23 us
    ppermute x3, starting transfers between devices, ring(): lax.ppermute(values, axis, [(i, (i + distance) % size) for i in range(siz...  2 us
    ppermute x2, starting transfers between devices, diagonal(): return lax.ppermute(values, ('gx', 'gy'), route)  1.75 us
    ppermute x2, waiting for transfers between devices, diagonal(): return lax.ppermute(values, ('gx', 'gy'), route)  1.7 us
    ppermute x3, waiting for transfers between devices, ring(): lax.ppermute(values, axis, [(i, (i + distance) % size) for i in range(siz...  0.86 us
  transfers between devices with their start and end apart: 9, of which 3 were waited for; matrix products, arithmetic and copies ran while one was open for 0% of the time, Pallas kernels for 22%

profile of v5, /device:TPU:0, one launch (start us, length us, event | category | flops | bytes accessed | tf_op | source)
XLA Modules:
  0.0 29.4 jit_solution(5088894037725575496)
XLA Ops:
  0.6 0.0 copy-start
  0.6 0.9 %copy-done = s32[16,16,128]{2,1,0:T(8,128)S(1)} copy-done((s32[16,16,128]{2,1,0:T(8,128)S(1)}, s32[16,16,128]{2,1,0:T(8,128)}, u32[]{:S(2)}) %copy-start) | copy-done | bytes 131096
  1.5 0.1 shard_map.50
  1.6 3.1 %collective-permute-start = (s32[80,128]{1,0:T(8,128)S(1)}, s32[80,128]{1,0:T(8,128)S(1)}, u32[]{:S(2)}, u32[]{:S(2)}) collective-permute-start(s32[80,128]{1,0:T(8,128)S(1)} %get-tuple-element.29.own_ref), channel_id=1, source_target_pairs={{0,1},{1,0},{2,3},{3,2},{4,5},{5,4},{6,7},{7,6},{8,9},{9,8},{10,11... | collective-permute-start | bytes 122888 | tf_op jit(solution)/shard_map/ppermute | solution.py:956
  4.7 0.0 copy-start.1
  4.7 0.7 %copy-done.1 = f32[3,16]{1,0:T(4,128)S(1)} copy-done((f32[3,16]{1,0:T(4,128)S(1)}, f32[3,16]{1,0:T(4,128)}, u32[]{:S(2)}) %copy-start.1) | copy-done | bytes 216
  5.4 0.0 copy-start.2
  5.4 0.7 %copy-done.2 = s32[63]{0:T(128)S(1)} copy-done((s32[63]{0:T(128)S(1)}, s32[63]{0:T(128)}, u32[]{:S(2)}) %copy-start.2) | copy-done | bytes 276
  6.1 0.9 %shard_map.51 = (f32[3,16,16,128]{3,2,1,0:T(8,128)S(1)}, f32[3,8,128]{2,1,0:T(8,128)S(1)}, f32[40,128]{1,0:T(8,128)S(1)}) custom-call(f32[3,16]{1,0:T(4,128)S(1)} %copy-done.1, s32[63]{0:T(128)S(1)} %copy-done.2, s32[16,16,128]{2,1,0:T(8,128)S(1)} %get-tuple-element.25.facies_ref), custom_call_target="tpu_custom_call" | custom-call | flops 10000000 | bytes 1000000 | tf_op jit(solution)/shard_map/pallas_call | solution.py:943
  7.0 0.0 collective-permute-done.other_ref
  7.0 1.8 %collective-permute-start.1 = (s32[16,16,128]{2,1,0:T(8,128)S(1)}, s32[16,16,128]{2,1,0:T(8,128)S(1)}, u32[]{:S(2)}, u32[]{:S(2)}) collective-permute-start(s32[16,16,128]{2,1,0:T(8,128)S(1)} %get-tuple-element.30), channel_id=1, source_target_pairs={{0,1},{1,0},{2,3},{3,2},{4,5},{5,4},{6,7},{7,6},{8,9},{9,8},{10,11... | collective-permute-start | bytes 393224 | tf_op jit(solution)/shard_map/ppermute | solution.py:956
  8.8 1.5 %collective-permute-start.2 = (s32[128,128]{1,0:T(8,128)S(1)}, s32[128,128]{1,0:T(8,128)S(1)}, u32[]{:S(2)}, u32[]{:S(2)}) collective-permute-start(s32[128,128]{1,0:T(8,128)S(1)} %get-tuple-element.32), channel_id=1, source_target_pairs={{0,16},{16,0},{1,17},{17,1},{2,18},{18,2},{3,19},{19,3},{4,20},{20... | collective-permute-start | bytes 196616 | tf_op jit(solution)/shard_map/ppermute | solution.py:961
  10.3 0.0 collective-permute-start.6
  10.3 1.7 %collective-permute-start.5 = (s32[32,128]{1,0:T(8,128)S(1)}, s32[32,128]{1,0:T(8,128)S(1)}, u32[]{:S(2)}, u32[]{:S(2)}) collective-permute-start(s32[32,128]{1,0:T(8,128)S(1)} %get-tuple-element.31.strip_ref), channel_id=1, source_target_pairs={{0,20},{4,24},{8,28},{12,16},{16,4},{20,8},{24,12},{28,0},{1,21},{... | collective-permute-start | bytes 49160 | tf_op jit(solution)/shard_map/ppermute | solution.py:971
  12.1 0.1 collective-permute-start.4
  12.2 0.0 collective-permute-done.1.other_ref
  12.2 0.4 %collective-permute-start.3 = (s32[32,128]{1,0:T(8,128)S(1)}, s32[32,128]{1,0:T(8,128)S(1)}, u32[]{:S(2)}, u32[]{:S(2)}) collective-permute-start(s32[32,128]{1,0:T(8,128)S(1)} %get-tuple-element.31.strip_ref), channel_id=1, source_target_pairs={{0,4},{4,8},{8,12},{12,0},{1,5},{5,9},{9,13},{13,1},{2,6},{6,10},{... | collective-permute-start | bytes 49160 | tf_op jit(solution)/shard_map/ppermute | solution.py:961
  12.6 0.3 %shard_map.53.k_ref = f32[3,32,16,128]{3,2,1,0:T(8,128)S(1)} custom-call(f32[3,8,128]{2,1,0:T(8,128)S(1)} %get-tuple-element.27.table_ref, f32[3,16,16,128]{3,2,1,0:T(8,128)S(1)} %get-tuple-element.28.own_ref, s32[16,16,128]{2,1,0:T(8,128)S(1)} %collective-permute-done.1.other_ref, s32[32,128]{1,0:T(8,128)S(1)} %get-tuple-element.31.strip_ref), custom_call_target="tpu_custom_call" | custom-call | flops 10000000 | bytes 1000000 | tf_op jit(solution)/shard_map/pallas_call | solution.py:943
  12.9 0.6 %collective-permute-done.6.high_low.high_high = s32[32,128]{1,0:T(8,128)S(1)} collective-permute-done((s32[32,128]{1,0:T(8,128)S(1)}, s32[32,128]{1,0:T(8,128)S(1)}, u32[]{:S(2)}, u32[]{:S(2)}) %collective-permute-start.6) | collective-permute-done | bytes 16416 | tf_op jit(solution)/shard_map/ppermute | solution.py:971
  13.5 1.1 %collective-permute-done.5.low_low.low_high = s32[32,128]{1,0:T(8,128)S(1)} collective-permute-done((s32[32,128]{1,0:T(8,128)S(1)}, s32[32,128]{1,0:T(8,128)S(1)}, u32[]{:S(2)}, u32[]{:S(2)}) %collective-permute-start.5) | collective-permute-done | bytes 16416 | tf_op jit(solution)/shard_map/ppermute | solution.py:971
  14.6 0.0 collective-permute-done.4.y_high
  14.6 0.9 %collective-permute-done.3.y_low = s32[32,128]{1,0:T(8,128)S(1)} collective-permute-done((s32[32,128]{1,0:T(8,128)S(1)}, s32[32,128]{1,0:T(8,128)S(1)}, u32[]{:S(2)}, u32[]{:S(2)}) %collective-permute-start.3) | collective-permute-done | bytes 16416 | tf_op jit(solution)/shard_map/ppermute | solution.py:961
  15.5 0.0 collective-permute-done.2.row_low.row_high
  15.5 2.0 %shard_map.54 = (f32[104,128]{1,0:T(8,128)S(1)}, f32[5,24,256]{2,1,0:T(8,128)S(1)}, f32[32,2,40,128]{3,2,1,0:T(8,128)S(1)}, f32[32,24,256]{2,1,0:T(8,128)S(1)}, ...) custom-call(f32[3,8,128]{2,1,0:T(8,128)S(1)} %get-tuple-element.27.t, ...), custom_call_target="tpu_custom_call" | custom-call | tf_op jit(solution)/shard_map/pallas_call | solution.py:943
  17.4 2.7 %collective-permute-start.7 = (f32[104,128]{1,0:T(8,128)S(1)}, f32[104,128]{1,0:T(8,128)S(1)}, u32[]{:S(2)}, u32[]{:S(2)}) collective-permute-start(f32[104,128]{1,0:T(8,128)S(1)} %get-tuple-element.34), channel_id=1, source_target_pairs={{0,2},{1,3},{2,0},{3,1},{4,6},{5,7},{6,4},{7,5},{8,10},{9,11},{10,... | collective-permute-start | bytes 159752 | tf_op jit(solution)/shard_map/ppermute | solution.py:956
  20.1 2.6 %shard_map.55 = (f32[3,32,2,40,128]{4,3,2,1,0:T(8,128)S(1)}, f32[32,2,40,128]{3,2,1,0:T(8,128)S(1)}, f32[6,24,256]{2,1,0:T(8,128)S(1)}) custom-call(f32[40,128]{1,0:T(8,128)S(1)} %get-tuple-element.26.cut_ref, f32[32,2,40,128]{3,2,1,0:T(8,128)S(1)} %get-tuple-element.35.lx_ref, f32[32,24,256]{2,1,0:T(8,128)S(1)} %get-tuple-element.36.ly_ref, ...), custom_call_target="tpu_custom_call" | custom-call | flops 10000000 | bytes 1000000 | tf_op jit(solution)/shard_map/pallas_call | solution.py:943
  22.7 0.0 collective-permute-done.7.message_ref
  22.7 0.3 shard_map.56
  23.0 2.5 %collective-permute-start.8 = (f32[64,128]{1,0:T(8,128)S(1)}, f32[64,128]{1,0:T(8,128)S(1)}, u32[]{:S(2)}, u32[]{:S(2)}) collective-permute-start(f32[64,128]{1,0:T(8,128)S(1)} %get-tuple-element.41), channel_id=1, source_target_pairs={{0,2},{1,3},{2,0},{3,1},{4,6},{5,7},{6,4},{7,5},{8,10},{9,11},{10,... | collective-permute-start | bytes 98312 | tf_op jit(solution)/shard_map/ppermute | solution.py:956
  25.5 2.5 %shard_map.57 = (f32[3,32,2,40,128]{4,3,2,1,0:T(8,128)S(1)}, f32[3,32,24,256]{3,2,1,0:T(8,128)S(1)}) custom-call(f32[40,128]{1,0:T(8,128)S(1)} %get-tuple-element.26.cut_ref, f32[13,24,256]{2,1,0:T(8,128)S(1)} %get-tuple-element.42.near_ref, f32[32,2,40,128]{3,2,1,0:T(8,128)S(1)} %get-tuple-element.35.lx_ref, f32[32,24,256]{2,1,0:T(8,128)S(1)} %get-tuple-element.36.ly_ref, ...), custom_call_target="tpu_custom_call" | custom-call | flops 10000000 | bytes 1000000 | tf_op jit(solution)/shard_map/pallas_call | solution.py:943
  28.0 0.0 collective-permute-done.8.message_ref
  28.1 1.3 %shard_map.58 = (f32[3,16,16,128]{3,2,1,0:T(8,128)}, f32[3,16,16,128]{3,2,1,0:T(8,128)}) custom-call(f32[40,128]{1,0:T(8,128)S(1)} %get-tuple-element.26.cut_ref, f32[64,128]{1,0:T(8,128)S(1)} %collective-permute-done.8.message_ref, f32[13,24,256]{2,1,0:T(8,128)S(1)} %get-tuple-element.42.near_ref, f32[32,2,40,128]{3,2,1,0:T(8,128)S(1)} %get-tuple-element.35.lx_ref, ...), custom_call_target="tpu_custom_call" | custom-call | tf_op jit(solution)/shard_map/pallas_call | solution.py:943
  (1 shorter events, 0.0 us)
Async XLA Ops:
  0.6 0.9 %copy-start = (s32[16,16,128]{2,1,0:T(8,128)S(1)}, s32[16,16,128]{2,1,0:T(8,128)}, u32[]{:S(2)}) copy-start(s32[16,16,128]{2,1,0:T(8,128)} %facies_ref.1) | copy-start | bytes 393220
  1.6 5.3 %collective-permute-start = (s32[80,128]{1,0:T(8,128)S(1)}, s32[80,128]{1,0:T(8,128)S(1)}, u32[]{:S(2)}, u32[]{:S(2)}) collective-permute-start(s32[80,128]{1,0:T(8,128)S(1)} %get-tuple-element.29.own_ref), channel_id=1, source_target_pairs={{0,1},{1,0},{2,3},{3,2},{4,5},{5,4},{6,7},{7,6},{8,9},{9,8},{10,11... | collective-permute-start | bytes 122888 | tf_op jit(solution)/shard_map/ppermute | solution.py:956
  4.7 0.7 %copy-start.1 = (f32[3,16]{1,0:T(4,128)S(1)}, f32[3,16]{1,0:T(4,128)}, u32[]{:S(2)}) copy-start(f32[3,16]{1,0:T(4,128)} %table.1) | copy-start | bytes 580
  5.4 0.7 %copy-start.2 = (s32[63]{0:T(128)S(1)}, s32[63]{0:T(128)}, u32[]{:S(2)}) copy-start(s32[63]{0:T(128)} %breaks.1) | copy-start | bytes 760
  7.0 5.2 %collective-permute-start.1 = (s32[16,16,128]{2,1,0:T(8,128)S(1)}, s32[16,16,128]{2,1,0:T(8,128)S(1)}, u32[]{:S(2)}, u32[]{:S(2)}) collective-permute-start(s32[16,16,128]{2,1,0:T(8,128)S(1)} %get-tuple-element.30), channel_id=1, source_target_pairs={{0,1},{1,0},{2,3},{3,2},{4,5},{5,4},{6,7},{7,6},{8,9},{9,8},{10,11... | collective-permute-start | bytes 393224 | tf_op jit(solution)/shard_map/ppermute | solution.py:956
  8.8 6.7 %collective-permute-start.2 = (s32[128,128]{1,0:T(8,128)S(1)}, s32[128,128]{1,0:T(8,128)S(1)}, u32[]{:S(2)}, u32[]{:S(2)}) collective-permute-start(s32[128,128]{1,0:T(8,128)S(1)} %get-tuple-element.32), channel_id=1, source_target_pairs={{0,16},{16,0},{1,17},{17,1},{2,18},{18,2},{3,19},{19,3},{4,20},{20... | collective-permute-start | bytes 196616 | tf_op jit(solution)/shard_map/ppermute | solution.py:961
  10.3 3.2 %collective-permute-start.6 = (s32[32,128]{1,0:T(8,128)S(1)}, s32[32,128]{1,0:T(8,128)S(1)}, u32[]{:S(2)}, u32[]{:S(2)}) collective-permute-start(s32[32,128]{1,0:T(8,128)S(1)} %get-tuple-element.31.strip_ref), channel_id=1, source_target_pairs={{0,28},{4,16},{8,20},{12,24},{16,12},{20,0},{24,4},{28,8},{1,29},{... | collective-permute-start | bytes 49160 | tf_op jit(solution)/shard_map/ppermute | solution.py:971
  10.3 4.3 %collective-permute-start.5 = (s32[32,128]{1,0:T(8,128)S(1)}, s32[32,128]{1,0:T(8,128)S(1)}, u32[]{:S(2)}, u32[]{:S(2)}) collective-permute-start(s32[32,128]{1,0:T(8,128)S(1)} %get-tuple-element.31.strip_ref), channel_id=1, source_target_pairs={{0,20},{4,24},{8,28},{12,16},{16,4},{20,8},{24,12},{28,0},{1,21},{... | collective-permute-start | bytes 49160 | tf_op jit(solution)/shard_map/ppermute | solution.py:971
  12.1 2.6 %collective-permute-start.4 = (s32[32,128]{1,0:T(8,128)S(1)}, s32[32,128]{1,0:T(8,128)S(1)}, u32[]{:S(2)}, u32[]{:S(2)}) collective-permute-start(s32[32,128]{1,0:T(8,128)S(1)} %get-tuple-element.31.strip_ref), channel_id=1, source_target_pairs={{0,12},{4,0},{8,4},{12,8},{1,13},{5,1},{9,5},{13,9},{2,14},{6,2},{... | collective-permute-start | bytes 49160 | tf_op jit(solution)/shard_map/ppermute | solution.py:961
  12.2 3.3 %collective-permute-start.3 = (s32[32,128]{1,0:T(8,128)S(1)}, s32[32,128]{1,0:T(8,128)S(1)}, u32[]{:S(2)}, u32[]{:S(2)}) collective-permute-start(s32[32,128]{1,0:T(8,128)S(1)} %get-tuple-element.31.strip_ref), channel_id=1, source_target_pairs={{0,4},{4,8},{8,12},{12,0},{1,5},{5,9},{9,13},{13,1},{2,6},{6,10},{... | collective-permute-start | bytes 49160 | tf_op jit(solution)/shard_map/ppermute | solution.py:961
  17.4 5.3 %collective-permute-start.7 = (f32[104,128]{1,0:T(8,128)S(1)}, f32[104,128]{1,0:T(8,128)S(1)}, u32[]{:S(2)}, u32[]{:S(2)}) collective-permute-start(f32[104,128]{1,0:T(8,128)S(1)} %get-tuple-element.34), channel_id=1, source_target_pairs={{0,2},{1,3},{2,0},{3,1},{4,6},{5,7},{6,4},{7,5},{8,10},{9,11},{10,... | collective-permute-start | bytes 159752 | tf_op jit(solution)/shard_map/ppermute | solution.py:956
  23.0 5.0 %collective-permute-start.8 = (f32[64,128]{1,0:T(8,128)S(1)}, f32[64,128]{1,0:T(8,128)S(1)}, u32[]{:S(2)}, u32[]{:S(2)}) collective-permute-start(f32[64,128]{1,0:T(8,128)S(1)} %get-tuple-element.41), channel_id=1, source_target_pairs={{0,2},{1,3},{2,0},{3,1},{4,6},{5,7},{6,4},{7,5},{8,10},{9,11},{10,... | collective-permute-start | bytes 98312 | tf_op jit(solution)/shard_map/ppermute | solution.py:956

commit v6 on v5

--- a/solution.py
+++ b/solution.py
@@ -44,39 +44,47 @@
     return (lax.axis_index("gz") % 2) * nz
 
 
-def pack_kernel(facies_ref, copy_ref, rims_ref):
+def pack_kernel(facies_ref, copy_ref, *row_refs):
     nz, nx, ny = facies_ref.shape
     copy_ref[...] = facies_ref[...]
-    lane = lax.broadcasted_iota(jnp.int32, (nx, ny), 1)
     row = iotas(8, ny)[0]
-    strip = jnp.zeros((nx, ny), jnp.int32)
     for z in range(0, nz, 2):
         pair = [facies_ref[z], facies_ref[z + 1]]
-        for at in (z, z + 1):
-            strip = jnp.where(lane // 8 == at, moved(pair[at - z], 8 * at + WIDE, 1), strip)
         first = jnp.where(row < 4, pair[0][:8], moved(pair[1][:8], 4, 0))
         last = jnp.where(row < 4, moved(pair[0][nx - 8 :], 4, 0), pair[1][nx - 8 :])
-        start = nx + 4 * z
-        if rims_ref.shape[0] == nx + 4 * nz:
-            rims_ref[start : start + 8, :] = jnp.where(lax.axis_index("gx") == 0, last, first)
+        spot = slice(4 * z, 4 * z + 8)
+        if len(row_refs) == 1:
+            row_refs[0][spot, :] = jnp.where(lax.axis_index("gx") == 0, last, first)
         else:
-            rims_ref[start : start + 8, :] = first
-            rims_ref[start + 4 * nz : start + 4 * nz + 8, :] = last
-    rims_ref[0:nx, :] = strip
-
-
-def merge_kernel(facies_ref, own_ref, other_ref, table_ref, copy_ref, strip_ref, *row_refs):
-    nz = facies_ref.shape[0]
-    size, ny = own_ref.shape
-    copy_ref[...] = facies_ref[...]
-    nx = size - 4 * nz * len(row_refs)
+            row_refs[0][spot, :] = first
+            row_refs[1][spot, :] = last
+
+
+def rim_tile(low, high, layer):
+    row = iotas(8, low.shape[1])[0]
+    if layer % 2 == 0:
+        return jnp.where(row < 4, high, moved(low, 4, 0))
+    return jnp.where(row < 4, moved(high, 4, 0), low)
+
+
+def merge_kernel(own_ref, other_ref, table_ref, *refs):
+    sides = (len(refs) - 1) // 3
+    ins, strip_ref, row_refs = refs[: 2 * sides], refs[2 * sides], refs[2 * sides + 1 :]
+    nz, nx, ny = own_ref.shape
     swap = own_start(nz) > 0
+    lane = lax.broadcasted_iota(jnp.int32, (nx + 8, ny), 1)
     for b in range(2):
-        rims = jnp.where(swap == (b == 1), own_ref[...], other_ref[...])
-        strip_ref[b * nx : (b + 1) * nx, :] = rims[:nx]
+        own = swap == (b == 1)
         for n, ref in enumerate(row_refs):
-            start = nx + 4 * nz * n
-            ref[4 * nz * b : 4 * nz * (b + 1), :] = rims[start : start + 4 * nz]
+            ref[4 * nz * b : 4 * nz * (b + 1), :] = jnp.where(own, ins[n][...], ins[sides + n][...])
+        strip = jnp.zeros((nx + 8, ny), jnp.int32)
+        for z in range(nz):
+            start = 4 * nz * b + z // 2 * 8
+            low, high = [ref[start : start + 8, :] for ref in (row_refs[0], row_refs[-1])]
+            layer = jnp.where(own, own_ref[z], other_ref[z])
+            layer = jnp.concatenate([layer, rim_tile(low, high, z)], axis=0)
+            strip = jnp.where(lane // 8 == z, moved(layer, 8 * z + WIDE, 1), strip)
+        strip_ref[b * (nx + 8) : (b + 1) * (nx + 8), :] = strip
 
 
 def lookup(table, index):
@@ -265,7 +273,7 @@
 
 
 def assemble_slabs(k_ref, tables, rims, low_ref, high_ref, store):
-    row_low, row_high, y_low, y_high, low_low, low_high, high_low, high_high = rims
+    row_low, row_high, y_low, y_high = rims
     layers, nx, ny = k_ref.shape[1:]
     nz = layers // 2
     at_x, at_y = lax.axis_index("gx"), lax.axis_index("gy")
@@ -282,18 +290,11 @@
     in_y, in_yp = valid * moved(valid, -1, 1), valid * moved(valid, 1, 1)
     row_in, strip_in = cell[nx:, :ny], cell[:, ny:]
 
-    row = iotas(8, ny)[0]
     lane = iotas(nx + 8, ny)[1]
     strips = []
     for b in range(2):
-        part = slice(b * nx, (b + 1) * nx)
-
-        def whole(own, high, low):
-            side = jnp.where(row < WIDE, high[part, :][0:8], low[part, :][nx - 8 :])
-            return jnp.concatenate([own[part, :], side], axis=0)
-
-        before, after = whole(y_low, low_high, low_low), whole(y_high, high_high, high_low)
-        strip = jnp.where(lane % 8 < WIDE, before, after)
+        part = slice(b * (nx + 8), (b + 1) * (nx + 8))
+        strip = jnp.where(lane % 8 < WIDE, y_low[part, :], y_high[part, :])
         strips.append([lookup(table, strip) for table in tables])
     for q in range(3):
         low_ref[q] = lookup(tables[q], row_low[...])
@@ -306,11 +307,7 @@
             start = at // 2 * 8
             for q in range(3):
                 low, high = low_ref[q, start : start + 8, :], high_ref[q, start : start + 8, :]
-                if z % 2 == 0:
-                    low = moved(low, 4, 0)
-                else:
-                    high = moved(high, 4, 0)
-                side = jnp.where(row_in, jnp.where(row < 4, high, low), 0.0)
+                side = jnp.where(row_in, rim_tile(low, high, z), 0.0)
                 beside = jnp.where(strip_in, moved(strips[b][q], -(8 * z + WIDE), 1), 0.0)
                 body = jnp.concatenate([k_ref[q, at], side], axis=0)
                 store(q, at, jnp.concatenate([body, beside], axis=1))
@@ -329,13 +326,12 @@
 
 def eliminate_kernel(
     stages, table_ref, cut_ref, k_ref, row_low, row_high, y_low, y_high,
-    low_low, low_high, high_low, high_high,
     message_ref, own_ref, pair_ref, lx_ref, ly_ref, lz_ref, d_ref, e_ref, inverse_ref,
     all_ref, flow_ref, source_ref, centre_ref, low_ref, high_ref=None,
 ):
     layers, nx, ny = k_ref.shape[1:]
     nz = layers // 2
-    rims = row_low, row_high, y_low, y_high, low_low, low_high, high_low, high_high
+    rims = row_low, row_high, y_low, y_high
 
     def store(q, at, slab):
         all_ref[q, at] = slab
@@ -721,12 +717,11 @@
 
 def end_eliminate_kernel(
     table_ref, cut_ref, k_ref, row_low, row_high, y_low, y_high,
-    low_low, low_high, high_low, high_high,
     message_ref, own_ref, lx_ref, ly_ref, lz_ref, d_ref, ratio_ref, inverse_ref,
     kx_ref, fx_ref, ky_ref, kz_ref, source_ref, centre_ref, low_ref, high_ref=None,
 ):
     layers, nx, ny = k_ref.shape[1:]
-    rims = row_low, row_high, y_low, y_high, low_low, low_high, high_low, high_high
+    rims = row_low, row_high, y_low, y_high
     high, sign = is_high(0), signed()
 
     def store(q, at, slab):
@@ -961,14 +956,13 @@
     return lax.ppermute(values, axis, [(i, (i + distance) % size) for i in range(size)])
 
 
-def diagonal(values, x_distance, y_distance):
-    nx, ny = lax.axis_size("gx"), lax.axis_size("gy")
+def slanted(values, x_distance):
+    nx, nz = lax.axis_size("gx"), lax.axis_size("gz")
     route = []
     for i in range(nx):
-        for j in range(ny):
-            target = ((i + x_distance) % nx) * ny + (j + y_distance) % ny
-            route.append((i * ny + j, target))
-    return lax.ppermute(values, ("gx", "gy"), route)
+        for k in range(nz):
+            route.append((i * nz + k, (i + x_distance) % nx * nz + (k ^ 1)))
+    return lax.ppermute(values, ("gx", "gz"), route)
 
 
 def per_device(facies, perm_table, line_breaks):
@@ -979,12 +973,17 @@
     layers = 2 * nz
     cut_rows = -(-(layers + 1 + 2 * stages) // 8) * 8
     sides = 1 if two else 2
-    facies, rims = kernel_call(
+    facies, *rows = kernel_call(
         pack_kernel,
-        [((nz, nx, ny), i32), ((nx + 4 * nz * sides, ny), i32)],
+        [((nz, nx, ny), i32)] + [((nz * 4, ny), i32)] * sides,
         [facies],
     )
-    other_rims = swapped(rims, 0)
+    other = swapped(facies, 0)
+    if two:
+        rims = [ring(rows[0], "gx", 1), slanted(rows[0], 1)]
+    else:
+        rims = [ring(rows[1], "gx", 1), ring(rows[0], "gx", -1)]
+        rims += [slanted(rows[1], 1), slanted(rows[0], -1)]
     k, table, cuts = kernel_call(
         functools.partial(prepare_kernel, stages),
         [((3, nz, nx, ny), f32), ((3, 8, ny), f32), ((cut_rows, ny), f32)],
@@ -992,12 +991,11 @@
         smem=2,
         cost=pl.CostEstimate(flops=10**7, bytes_accessed=10**6, transcendentals=0),
     )
-    facies, strip, *rows = kernel_call(
+    strip, *rows = kernel_call(
         merge_kernel,
-        [((nz, nx, ny), i32), ((2 * nx, ny), i32)] + [((layers * 4, ny), i32)] * sides,
-        [facies, rims, other_rims, table],
-    )
-    other = swapped(facies, 0)
+        [((2 * nx + 16, ny), i32)] + [((layers * 4, ny), i32)] * sides,
+        [facies, other, table] + rims,
+    )
     k, = kernel_call(
         prepare_other_kernel,
         [((3, layers, nx, ny), f32)],
@@ -1005,18 +1003,8 @@
         cost=pl.CostEstimate(flops=10**7, bytes_accessed=10**6, transcendentals=0),
     )
     y_low, y_high = ring(strip, "gy", 1), ring(strip, "gy", -1)
-    if two:
-        row_low = row_high = ring(rows[0], "gx", 1)
-        low_low = low_high = diagonal(strip, 1, 1)
-        high_low = high_high = diagonal(strip, 1, -1)
-    else:
-        row_low, row_high = ring(rows[1], "gx", 1), ring(rows[0], "gx", -1)
-        low_low, low_high = diagonal(strip, 1, 1), diagonal(strip, -1, 1)
-        high_low, high_high = diagonal(strip, 1, -1), diagonal(strip, -1, -1)
-
     sizes = nz, nx, ny
-    operands = [table, cuts, k, row_low, row_high, y_low, y_high,
-                low_low, low_high, high_low, high_high]
+    operands = [table, cuts, k, rows[0], rows[-1], y_low, y_high]
     scratch = [pltpu.VMEM((3, layers * 4, ny), f32)] * sides
     return (sweep_ends if stages == 1 else sweep_tree)(sizes, stages, operands, scratch)
 

time: 29.5 us -> 28.9 us (0.980)
  starting transfers between devices: 13.8 us -> 9.38 us
  waiting for transfers between devices: 2.58 us -> 6.36 us
    ppermute x4 -> x3, starting transfers between devices: 10.1 us -> 7.28 us  [swapped(): lax.ppermute(values, 'gz', [(i, i ^ 2 ** stage) for i in range(size)])]
    ppermute x3, waiting for transfers between devices: 0.86 us -> 3.05 us  [ring(): lax.ppermute(values, axis, [(i, (i + distance) % size) for i in range(siz...]
    ppermute x4 -> x3, waiting for transfers between devices: 0.01 us -> 1.77 us  [swapped(): lax.ppermute(values, 'gz', [(i, i ^ 2 ** stage) for i in range(size)])]
    ppermute x3, starting transfers between devices: 2 us -> 0.72 us  [ring(): lax.ppermute(values, axis, [(i, (i + distance) % size) for i in range(siz...]
    ppermute x2 -> x1, starting transfers between devices: 1.75 us -> 1.38 us  [slanted(): return lax.ppermute(values, ('gx', 'gz'), route)]
    ppermute x2 -> x1, waiting for transfers between devices: 1.7 us -> 1.54 us  [slanted(): return lax.ppermute(values, ('gx', 'gz'), route)]
  transfers between devices with their start and end apart: 9 -> 7, of which waited for: 3 -> 6; matrix products, arithmetic and copies ran while one was open for 0% -> 0% of each run, Pallas kernels for 22% -> 22%
where the time goes in v6:
time: 28.9 us; the launch traced here: 28.7 us
  Pallas kernels  10.1 us (35%)
  starting transfers between devices  9.38 us (32%)
  waiting for transfers between devices  6.36 us (22%)
  local copies, waits for them, and re-layouts  2.23 us (8%)
  between operations  0.68 us (2%)
    pallas_call x9, Pallas kernels, kernel_call(): pl.pallas_call(kernel, out_shape=[jax.ShapeDtypeStruct(s, t) for s, t in...  10.1 us
    ppermute x3, starting transfers between devices, swapped(): lax.ppermute(values, 'gz', [(i, i ^ 2 ** stage) for i in range(size)])  7.28 us
    ppermute x3, waiting for transfers between devices, ring(): lax.ppermute(values, axis, [(i, (i + distance) % size) for i in range(siz...  3.05 us
    unnamed x6, local copies, waits for them, and re-layouts  2.23 us
    ppermute x3, waiting for transfers between devices, swapped(): lax.ppermute(values, 'gz', [(i, i ^ 2 ** stage) for i in range(size)])  1.77 us
    ppermute x1, waiting for transfers between devices, slanted(): return lax.ppermute(values, ('gx', 'gz'), route)  1.54 us
    ppermute x1, starting transfers between devices, slanted(): return lax.ppermute(values, ('gx', 'gz'), route)  1.38 us
    ppermute x3, starting transfers between devices, ring(): lax.ppermute(values, axis, [(i, (i + distance) % size) for i in range(siz...  0.72 us
  transfers between devices with their start and end apart: 7, of which 6 were waited for; matrix products, arithmetic and copies ran while one was open for 0% of the time, Pallas kernels for 22%

profile of v6, /device:TPU:0, one launch (start us, length us, event | category | flops | bytes accessed | tf_op | source)
XLA Modules:
  0.0 28.7 jit_solution(8979060994722066306)
XLA Ops:
  0.6 0.0 copy-start
  0.6 0.9 %copy-done = s32[16,16,128]{2,1,0:T(8,128)S(1)} copy-done((s32[16,16,128]{2,1,0:T(8,128)S(1)}, s32[16,16,128]{2,1,0:T(8,128)}, u32[]{:S(2)}) %copy-start) | copy-done | bytes 131096
  1.6 3.1 %collective-permute-start = (s32[16,16,128]{2,1,0:T(8,128)S(1)}, s32[16,16,128]{2,1,0:T(8,128)S(1)}, u32[]{:S(2)}, u32[]{:S(2)}) collective-permute-start(s32[16,16,128]{2,1,0:T(8,128)S(1)} %get-tuple-element.24.facies_ref.own_ref), channel_id=1, source_target_pairs={{0,1},{1,0},{2,3},{3,2},{4,5},{5,4},{6,7},{7,6},{8,9},{9,8},{10,11... | collective-permute-start | bytes 393224 | tf_op jit(solution)/shard_map/ppermute | solution.py:951
  4.6 1.4 %collective-permute-start.2 = (s32[64,128]{1,0:T(8,128)S(1)}, s32[64,128]{1,0:T(8,128)S(1)}, u32[]{:S(2)}, u32[]{:S(2)}) collective-permute-start(s32[64,128]{1,0:T(8,128)S(1)} %get-tuple-element.28), channel_id=1, source_target_pairs={{0,17},{1,16},{2,19},{3,18},{16,1},{17,0},{18,3},{19,2},{4,21},{5,... | collective-permute-start | bytes 98312 | tf_op jit(solution)/shard_map/ppermute | solution.py:965
  6.0 0.2 collective-permute-start.1
  6.2 0.0 copy-start.1
  6.2 0.7 %copy-done.1 = f32[3,16]{1,0:T(4,128)S(1)} copy-done((f32[3,16]{1,0:T(4,128)S(1)}, f32[3,16]{1,0:T(4,128)}, u32[]{:S(2)}) %copy-start.1) | copy-done | bytes 216
  6.9 0.0 copy-start.2
  6.9 0.7 %copy-done.2 = s32[63]{0:T(128)S(1)} copy-done((s32[63]{0:T(128)S(1)}, s32[63]{0:T(128)}, u32[]{:S(2)}) %copy-start.2) | copy-done | bytes 276
  7.5 0.9 %shard_map.51 = (f32[3,16,16,128]{3,2,1,0:T(8,128)S(1)}, f32[3,8,128]{2,1,0:T(8,128)S(1)}, f32[40,128]{1,0:T(8,128)S(1)}) custom-call(f32[3,16]{1,0:T(4,128)S(1)} %copy-done.1, s32[63]{0:T(128)S(1)} %copy-done.2, s32[16,16,128]{2,1,0:T(8,128)S(1)} %get-tuple-element.24.facies_ref.own_ref), custom_call_target="tpu_custom_call" | custom-call | flops 10000000 | bytes 1000000 | tf_op jit(solution)/shard_map/pallas_call | solution.py:938
  8.4 1.5 %collective-permute-done.2.refs_1_ = s32[64,128]{1,0:T(8,128)S(1)} collective-permute-done((s32[64,128]{1,0:T(8,128)S(1)}, s32[64,128]{1,0:T(8,128)S(1)}, u32[]{:S(2)}, u32[]{:S(2)}) %collective-permute-start.2) | collective-permute-done | bytes 32800 | tf_op jit(solution)/shard_map/ppermute | solution.py:965
  10.0 0.3 %collective-permute-done.1.refs_0_ = s32[64,128]{1,0:T(8,128)S(1)} collective-permute-done((s32[64,128]{1,0:T(8,128)S(1)}, s32[64,128]{1,0:T(8,128)S(1)}, u32[]{:S(2)}, u32[]{:S(2)}) %collective-permute-start.1) | collective-permute-done | bytes 32800 | tf_op jit(solution)/shard_map/ppermute | solution.py:956
  10.3 0.0 collective-permute-done.other_ref
  10.3 0.2 shard_map.52
  10.5 0.1 collective-permute-start.4
  10.5 0.5 %collective-permute-start.3 = (s32[48,128]{1,0:T(8,128)S(1)}, s32[48,128]{1,0:T(8,128)S(1)}, u32[]{:S(2)}, u32[]{:S(2)}) collective-permute-start(s32[48,128]{1,0:T(8,128)S(1)} %get-tuple-element.29.strip_ref), channel_id=1, source_target_pairs={{0,4},{4,8},{8,12},{12,0},{1,5},{5,9},{9,13},{13,1},{2,6},{6,10},{... | collective-permute-start | bytes 73736 | tf_op jit(solution)/shard_map/ppermute | solution.py:956
  11.0 0.3 %shard_map.53.k_ref = f32[3,32,16,128]{3,2,1,0:T(8,128)S(1)} custom-call(f32[3,8,128]{2,1,0:T(8,128)S(1)} %get-tuple-element.26.table_ref, f32[3,16,16,128]{3,2,1,0:T(8,128)S(1)} %get-tuple-element.27.own_ref, s32[16,16,128]{2,1,0:T(8,128)S(1)} %collective-permute-done.other_ref, s32[48,128]{1,0:T(8,128)S(1)} %get-tuple-element.29.strip_ref), custom_call_target="tpu_custom_call" | custom-call | flops 10000000 | bytes 1000000 | tf_op jit(solution)/shard_map/pallas_call | solution.py:938
  11.4 0.7 %collective-permute-done.4.y_high = s32[48,128]{1,0:T(8,128)S(1)} collective-permute-done((s32[48,128]{1,0:T(8,128)S(1)}, s32[48,128]{1,0:T(8,128)S(1)}, u32[]{:S(2)}, u32[]{:S(2)}) %collective-permute-start.4) | collective-permute-done | bytes 24608 | tf_op jit(solution)/shard_map/ppermute | solution.py:956
  12.0 2.0 %collective-permute-done.3.y_low = s32[48,128]{1,0:T(8,128)S(1)} collective-permute-done((s32[48,128]{1,0:T(8,128)S(1)}, s32[48,128]{1,0:T(8,128)S(1)}, u32[]{:S(2)}, u32[]{:S(2)}) %collective-permute-start.3) | collective-permute-done | bytes 24608 | tf_op jit(solution)/shard_map/ppermute | solution.py:956
  14.1 1.9 %shard_map.54 = (f32[104,128]{1,0:T(8,128)S(1)}, f32[5,24,256]{2,1,0:T(8,128)S(1)}, f32[32,2,40,128]{3,2,1,0:T(8,128)S(1)}, f32[32,24,256]{2,1,0:T(8,128)S(1)}, ...) custom-call(f32[3,8,128]{2,1,0:T(8,128)S(1)} %get-tuple-element.26.t, ...), custom_call_target="tpu_custom_call" | custom-call | tf_op jit(solution)/shard_map/pallas_call | solution.py:938
  16.0 2.7 %collective-permute-start.5 = (f32[104,128]{1,0:T(8,128)S(1)}, f32[104,128]{1,0:T(8,128)S(1)}, u32[]{:S(2)}, u32[]{:S(2)}) collective-permute-start(f32[104,128]{1,0:T(8,128)S(1)} %get-tuple-element.32), channel_id=1, source_target_pairs={{0,2},{1,3},{2,0},{3,1},{4,6},{5,7},{6,4},{7,5},{8,10},{9,11},{10,... | collective-permute-start | bytes 159752 | tf_op jit(solution)/shard_map/ppermute | solution.py:951
  18.7 2.6 %shard_map.55 = (f32[3,32,2,40,128]{4,3,2,1,0:T(8,128)S(1)}, f32[32,2,40,128]{3,2,1,0:T(8,128)S(1)}, f32[6,24,256]{2,1,0:T(8,128)S(1)}) custom-call(f32[40,128]{1,0:T(8,128)S(1)} %get-tuple-element.25.cut_ref, f32[32,2,40,128]{3,2,1,0:T(8,128)S(1)} %get-tuple-element.33.lx_ref, f32[32,24,256]{2,1,0:T(8,128)S(1)} %get-tuple-element.34.ly_ref, ...), custom_call_target="tpu_custom_call" | custom-call | flops 10000000 | bytes 1000000 | tf_op jit(solution)/shard_map/pallas_call | solution.py:938
  21.3 0.9 %collective-permute-done.5.message_ref = f32[104,128]{1,0:T(8,128)S(1)} collective-permute-done((f32[104,128]{1,0:T(8,128)S(1)}, f32[104,128]{1,0:T(8,128)S(1)}, u32[]{:S(2)}, u32[]{:S(2)}) %collective-permute-start.5) | collective-permute-done | bytes 53280 | tf_op jit(solution)/shard_map/ppermute | solution.py:951
  22.3 0.3 shard_map.56
  22.6 1.5 %collective-permute-start.6 = (f32[64,128]{1,0:T(8,128)S(1)}, f32[64,128]{1,0:T(8,128)S(1)}, u32[]{:S(2)}, u32[]{:S(2)}) collective-permute-start(f32[64,128]{1,0:T(8,128)S(1)} %get-tuple-element.39), channel_id=1, source_target_pairs={{0,2},{1,3},{2,0},{3,1},{4,6},{5,7},{6,4},{7,5},{8,10},{9,11},{10,... | collective-permute-start | bytes 98312 | tf_op jit(solution)/shard_map/ppermute | solution.py:951
  24.1 2.5 %shard_map.57 = (f32[3,32,2,40,128]{4,3,2,1,0:T(8,128)S(1)}, f32[3,32,24,256]{3,2,1,0:T(8,128)S(1)}) custom-call(f32[40,128]{1,0:T(8,128)S(1)} %get-tuple-element.25.cut_ref, f32[13,24,256]{2,1,0:T(8,128)S(1)} %get-tuple-element.40.near_ref, f32[32,2,40,128]{3,2,1,0:T(8,128)S(1)} %get-tuple-element.33.lx_ref, f32[32,24,256]{2,1,0:T(8,128)S(1)} %get-tuple-element.34.ly_ref, ...), custom_call_target="tpu_custom_call" | custom-call | flops 10000000 | bytes 1000000 | tf_op jit(solution)/shard_map/pallas_call | solution.py:938
  26.6 0.8 %collective-permute-done.6.message_ref = f32[64,128]{1,0:T(8,128)S(1)} collective-permute-done((f32[64,128]{1,0:T(8,128)S(1)}, f32[64,128]{1,0:T(8,128)S(1)}, u32[]{:S(2)}, u32[]{:S(2)}) %collective-permute-start.6) | collective-permute-done | bytes 32800 | tf_op jit(solution)/shard_map/ppermute | solution.py:951
  27.4 1.3 %shard_map.58 = (f32[3,16,16,128]{3,2,1,0:T(8,128)}, f32[3,16,16,128]{3,2,1,0:T(8,128)}) custom-call(f32[40,128]{1,0:T(8,128)S(1)} %get-tuple-element.25.cut_ref, f32[64,128]{1,0:T(8,128)S(1)} %collective-permute-done.6.message_ref, f32[13,24,256]{2,1,0:T(8,128)S(1)} %get-tuple-element.40.near_ref, f32[32,2,40,128]{3,2,1,0:T(8,128)S(1)} %get-tuple-element.33.lx_ref, ...), custom_call_target="tpu_custom_call" | custom-call | tf_op jit(solution)/shard_map/pallas_call | solution.py:938
  (1 shorter events, 0.0 us)
Async XLA Ops:
  0.6 0.9 %copy-start = (s32[16,16,128]{2,1,0:T(8,128)S(1)}, s32[16,16,128]{2,1,0:T(8,128)}, u32[]{:S(2)}) copy-start(s32[16,16,128]{2,1,0:T(8,128)} %facies_ref.1) | copy-start | bytes 393220
  1.6 8.7 %collective-permute-start = (s32[16,16,128]{2,1,0:T(8,128)S(1)}, s32[16,16,128]{2,1,0:T(8,128)S(1)}, u32[]{:S(2)}, u32[]{:S(2)}) collective-permute-start(s32[16,16,128]{2,1,0:T(8,128)S(1)} %get-tuple-element.24.facies_ref.own_ref), channel_id=1, source_target_pairs={{0,1},{1,0},{2,3},{3,2},{4,5},{5,4},{6,7},{7,6},{8,9},{9,8},{10,11... | collective-permute-start | bytes 393224 | tf_op jit(solution)/shard_map/ppermute | solution.py:951
  4.6 5.3 %collective-permute-start.2 = (s32[64,128]{1,0:T(8,128)S(1)}, s32[64,128]{1,0:T(8,128)S(1)}, u32[]{:S(2)}, u32[]{:S(2)}) collective-permute-start(s32[64,128]{1,0:T(8,128)S(1)} %get-tuple-element.28), channel_id=1, source_target_pairs={{0,17},{1,16},{2,19},{3,18},{16,1},{17,0},{18,3},{19,2},{4,21},{5,... | collective-permute-start | bytes 98312 | tf_op jit(solution)/shard_map/ppermute | solution.py:965
  6.0 4.3 %collective-permute-start.1 = (s32[64,128]{1,0:T(8,128)S(1)}, s32[64,128]{1,0:T(8,128)S(1)}, u32[]{:S(2)}, u32[]{:S(2)}) collective-permute-start(s32[64,128]{1,0:T(8,128)S(1)} %get-tuple-element.28), channel_id=1, source_target_pairs={{0,16},{16,0},{1,17},{17,1},{2,18},{18,2},{3,19},{19,3},{4,20},{20... | collective-permute-start | bytes 98312 | tf_op jit(solution)/shard_map/ppermute | solution.py:956
  6.2 0.7 %copy-start.1 = (f32[3,16]{1,0:T(4,128)S(1)}, f32[3,16]{1,0:T(4,128)}, u32[]{:S(2)}) copy-start(f32[3,16]{1,0:T(4,128)} %table.1) | copy-start | bytes 580
  6.9 0.7 %copy-start.2 = (s32[63]{0:T(128)S(1)}, s32[63]{0:T(128)}, u32[]{:S(2)}) copy-start(s32[63]{0:T(128)} %breaks.1) | copy-start | bytes 760
  10.5 1.6 %collective-permute-start.4 = (s32[48,128]{1,0:T(8,128)S(1)}, s32[48,128]{1,0:T(8,128)S(1)}, u32[]{:S(2)}, u32[]{:S(2)}) collective-permute-start(s32[48,128]{1,0:T(8,128)S(1)} %get-tuple-element.29.strip_ref), channel_id=1, source_target_pairs={{0,12},{4,0},{8,4},{12,8},{1,13},{5,1},{9,5},{13,9},{2,14},{6,2},{... | collective-permute-start | bytes 73736 | tf_op jit(solution)/shard_map/ppermute | solution.py:956
  10.5 3.6 %collective-permute-start.3 = (s32[48,128]{1,0:T(8,128)S(1)}, s32[48,128]{1,0:T(8,128)S(1)}, u32[]{:S(2)}, u32[]{:S(2)}) collective-permute-start(s32[48,128]{1,0:T(8,128)S(1)} %get-tuple-element.29.strip_ref), channel_id=1, source_target_pairs={{0,4},{4,8},{8,12},{12,0},{1,5},{5,9},{9,13},{13,1},{2,6},{6,10},{... | collective-permute-start | bytes 73736 | tf_op jit(solution)/shard_map/ppermute | solution.py:956
  16.0 6.2 %collective-permute-start.5 = (f32[104,128]{1,0:T(8,128)S(1)}, f32[104,128]{1,0:T(8,128)S(1)}, u32[]{:S(2)}, u32[]{:S(2)}) collective-permute-start(f32[104,128]{1,0:T(8,128)S(1)} %get-tuple-element.32), channel_id=1, source_target_pairs={{0,2},{1,3},{2,0},{3,1},{4,6},{5,7},{6,4},{7,5},{8,10},{9,11},{10,... | collective-permute-start | bytes 159752 | tf_op jit(solution)/shard_map/ppermute | solution.py:951
  22.6 4.9 %collective-permute-start.6 = (f32[64,128]{1,0:T(8,128)S(1)}, f32[64,128]{1,0:T(8,128)S(1)}, u32[]{:S(2)}, u32[]{:S(2)}) collective-permute-start(f32[64,128]{1,0:T(8,128)S(1)} %get-tuple-element.39), channel_id=1, source_target_pairs={{0,2},{1,3},{2,0},{3,1},{4,6},{5,7},{6,4},{7,5},{8,10},{9,11},{10,... | collective-permute-start | bytes 98312 | tf_op jit(solution)/shard_map/ppermute | solution.py:951

commit v7 on v6

--- a/solution.py
+++ b/solution.py
@@ -34,6 +34,10 @@
 
 def choose(condition, first, second):
     return [jnp.where(condition, a, b) for a, b in zip(first, second)]
+
+
+def flipped(flips):
+    return is_high(0) if flips else False
 
 
 def is_high(stage):
@@ -102,6 +106,8 @@
         values = jnp.zeros((8, ny), jnp.float32)
         for label in range(table.shape[1]):
             values = jnp.where(lane == label, table[q, label], values)
+        if stages == 1:
+            values = 2.0 * values
         table_ref[q] = values
         tables.append(values)
     for z in range(nz):
@@ -123,13 +129,23 @@
         cut_ref[r : r + 1, :] = jnp.full((1, ny), cut, jnp.float32)
 
 
-def prepare_other_kernel(table_ref, own_ref, other_ref, strip_ref, k_ref):
-    nz = other_ref.shape[0]
-    start = own_start(nz)
+def prepare_other_kernel(sides, flips, table_ref, own_ref, other_ref, *refs):
+    rows, k_ref, row_refs = refs[:sides], refs[sides], refs[sides + 1 :]
+    nz, _, ny = other_ref.shape
+    start, flip = own_start(nz), flipped(flips)
+
+    def spot(at, count):
+        return jnp.where(flip, count - 1 - at, at)
+
     for q in range(3):
-        k_ref[q, pl.ds(start, nz)] = own_ref[q]
         for z in range(nz):
-            k_ref[q, nz - start + z] = lookup(table_ref[q], other_ref[z])
+            k_ref[q, spot(start + z, 2 * nz)] = own_ref[q, z]
+            k_ref[q, spot(nz - start + z, 2 * nz)] = lookup(table_ref[q], other_ref[z])
+        for n in range(sides):
+            for t in range(nz):
+                tile = lookup(table_ref[q], rows[n][8 * t : 8 * t + 8, :])
+                tile = jnp.where(flip, moved(tile, 4, 0), tile)
+                row_refs[n][q, pl.ds(pl.multiple_of(8 * spot(t, nz), 8), 8), :] = tile
 
 
 def face(a, b):
@@ -272,14 +288,10 @@
     return [n - factor * g for n, g in zip(near_g, far_g)]
 
 
-def assemble_slabs(k_ref, tables, rims, low_ref, high_ref, store):
-    row_low, row_high, y_low, y_high = rims
-    layers, nx, ny = k_ref.shape[1:]
-    nz = layers // 2
+def grid_masks(nx, ny):
     at_x, at_y = lax.axis_index("gx"), lax.axis_index("gy")
     has_x_low, has_x_high = at_x > 0, at_x < lax.axis_size("gx") - 1
     has_y_low, has_y_high = at_y > 0, at_y < lax.axis_size("gy") - 1
-
     row, lane = iotas(nx + 8, 2 * ny)
     x_in = (row < nx) | ((row < nx + WIDE) & has_x_high) | ((row >= nx + 8 - WIDE) & has_x_low)
     y_in = (lane < ny) | ((lane < ny + WIDE) & has_y_high)
@@ -288,31 +300,38 @@
     valid = flag(cell)
     in_x, in_xp = valid * moved(valid, -1, 0), valid * moved(valid, 1, 0)
     in_y, in_yp = valid * moved(valid, -1, 1), valid * moved(valid, 1, 1)
-    row_in, strip_in = cell[nx:, :ny], cell[:, ny:]
-
-    lane = iotas(nx + 8, ny)[1]
+    return cell, in_x, in_xp, in_y, in_yp
+
+
+def rim_columns(flips, tables, y_low, y_high, cell):
+    ny = cell.shape[1] // 2
+    size = cell.shape[0]
+    strip_in = cell[:, ny:]
+    lane = iotas(size, ny)[1]
     strips = []
     for b in range(2):
-        part = slice(b * (nx + 8), (b + 1) * (nx + 8))
-        strip = jnp.where(lane % 8 < WIDE, y_low[part, :], y_high[part, :])
-        strips.append([lookup(table, strip) for table in tables])
-    for q in range(3):
-        low_ref[q] = lookup(tables[q], row_low[...])
-        if high_ref is not low_ref:
-            high_ref[q] = lookup(tables[q], row_high[...])
-
-    for b in range(2):
-        for z in range(nz):
-            at = b * nz + z
-            start = at // 2 * 8
-            for q in range(3):
-                low, high = low_ref[q, start : start + 8, :], high_ref[q, start : start + 8, :]
-                side = jnp.where(row_in, rim_tile(low, high, z), 0.0)
-                beside = jnp.where(strip_in, moved(strips[b][q], -(8 * z + WIDE), 1), 0.0)
-                body = jnp.concatenate([k_ref[q, at], side], axis=0)
-                store(q, at, jnp.concatenate([body, beside], axis=1))
-
-    return cell, in_x, in_xp, in_y, in_yp
+        part = slice(b * size, (b + 1) * size)
+        strips.append(jnp.where(lane % 8 < WIDE, y_low[part, :], y_high[part, :]))
+    flip, nz = flipped(flips), ny // 8
+    if flips:
+        strips = choose(flip, strips[::-1], strips)
+    strips = [[lookup(table, strip) for table in tables] for strip in strips]
+
+    def beside(q, at):
+        z, strip = at % nz, strips[at // nz][q]
+        if flips:
+            turned = pltpu.roll(strip, ny - WIDE - 8 * jnp.where(flip, nz - 1 - z, z), 1)
+        else:
+            turned = moved(strip, -(8 * z + WIDE), 1)
+        return jnp.where(strip_in, turned, 0.0)
+
+    return beside
+
+
+def body_rows(k_ref, low_ref, high_ref, q, at, row_in):
+    spot = slice(at // 2 * 8, at // 2 * 8 + 8)
+    side = rim_tile(low_ref[q, spot, :], high_ref[q, spot, :], at)
+    return jnp.concatenate([k_ref[q, at], jnp.where(row_in, side, 0.0)], axis=0)
 
 
 def flow_after(here, there, inside):
@@ -327,19 +346,16 @@
 def eliminate_kernel(
     stages, table_ref, cut_ref, k_ref, row_low, row_high, y_low, y_high,
     message_ref, own_ref, pair_ref, lx_ref, ly_ref, lz_ref, d_ref, e_ref, inverse_ref,
-    all_ref, flow_ref, source_ref, centre_ref, low_ref, high_ref=None,
+    all_ref, flow_ref, source_ref, centre_ref,
 ):
     layers, nx, ny = k_ref.shape[1:]
     nz = layers // 2
-    rims = row_low, row_high, y_low, y_high
-
-    def store(q, at, slab):
-        all_ref[q, at] = slab
-
-    cell, in_x, in_xp, in_y, in_yp = assemble_slabs(
-        k_ref, [table_ref[q] for q in range(3)], rims, low_ref,
-        low_ref if high_ref is None else high_ref, store,
-    )
+    cell, in_x, in_xp, in_y, in_yp = grid_masks(nx, ny)
+    beside = rim_columns(False, [table_ref[q] for q in range(3)], y_low, y_high, cell)
+    for at in range(layers):
+        for q in range(3):
+            body = body_rows(k_ref, row_low, row_high, q, at, cell[nx:, :ny])
+            all_ref[q, at] = jnp.concatenate([body, beside(q, at)], axis=1)
     for at in range(layers):
         kx, ky = all_ref[0, at], all_ref[1, at]
         flow_x = flow_after(kx, moved(kx, -1, 0), in_x)
@@ -715,51 +731,91 @@
     )
 
 
-def end_eliminate_kernel(
-    table_ref, cut_ref, k_ref, row_low, row_high, y_low, y_high,
-    message_ref, own_ref, lx_ref, ly_ref, lz_ref, d_ref, ratio_ref, inverse_ref,
-    kx_ref, fx_ref, ky_ref, kz_ref, source_ref, centre_ref, low_ref, high_ref=None,
-):
+def put_half(ref, index, half):
+    rows = half.shape[0]
+    ref[index + (slice(8, 8 + rows),)] = half
+    ref[index + (slice(0, 8),)] = half[rows - 8 :]
+    ref[index + (slice(8 + rows, 16 + rows),)] = half[:8]
+
+
+def harmonic(here, there):
+    return here * there / (here + there)
+
+
+def tau_after(here, there, inside):
+    return jnp.where(inside > 0.0, harmonic(here, there), here + there)
+
+
+def body_kernel(k_ref, row_low, row_high, lx_ref, tau_ref, source_ref, ky_ref, kz_ref, lz_ref):
     layers, nx, ny = k_ref.shape[1:]
-    rims = row_low, row_high, y_low, y_high
-    high, sign = is_high(0), signed()
-
-    def store(q, at, slab):
-        j = jnp.where(high, layers - 1 - at, at)
-        if q == 0:
-            put(kx_ref, (j,), slab)
-        else:
-            (ky_ref, kz_ref)[q - 1][j] = slab
-
-    cell, in_x, in_xp, in_y, in_yp = assemble_slabs(
-        k_ref, [table_ref[q] for q in range(3)], rims, low_ref,
-        low_ref if high_ref is None else high_ref, store,
-    )
-    zero = jnp.zeros((nx + 8, 2 * ny), jnp.float32)
+    cell, in_x, in_xp = [mask[:, :ny] for mask in grid_masks(nx, ny)[:3]]
+    share, share_back = 0.5 + 0.5 * in_x, 0.5 + 0.5 * in_xp
+    zero = jnp.zeros((nx + 8, ny), jnp.float32)
     lz_ref[0] = zero
     lz_ref[layers] = zero
     for j in range(layers):
-        flow_x = flow_after(get(kx_ref, (j,)), get(kx_ref, (j,), 1), in_x)
-        put(fx_ref, (j,), flow_x)
-        put(lx_ref, (j,), flow_x * in_x)
+        kx, ky, kz = [body_rows(k_ref, row_low, row_high, q, j, cell[nx:]) for q in range(3)]
+        tau = tau_after(kx, moved(kx, -1, 0), in_x)
+        back = moved(tau, 1, 0)
+        put_half(lx_ref, (j,), tau * in_x)
+        tau_ref[j] = tau + back
+        source_ref[j] = tau * share - back * share_back
+        ky_ref[j] = ky
+        kz_ref[j] = kz
+        if j > 0:
+            lz_ref[j] = jnp.where(cell, harmonic(below, kz), 0.0)
+        below = kz
+
+
+def end_eliminate_kernel(
+    table_ref, cut_ref, y_low, y_high, lx_body, tau_body, source_body, ky_body, kz_body, lz_body,
+    message_ref, own_ref, lx_ref, ly_ref, lz_ref, d_ref, ratio_ref, inverse_ref,
+    kx_ref, tx_ref, ky_ref, kz_ref, source_ref, centre_ref,
+):
+    layers, size, ny = ky_body.shape
+    nx = size - 8
+    sign = signed()
+    cell, in_x, in_xp, in_y, in_yp = grid_masks(nx, ny)
+    share_x, share_xp = 0.5 + 0.5 * in_x[:, ny:], 0.5 + 0.5 * in_xp[:, ny:]
+    share_y, share_yp = 0.5 + 0.5 * in_y, 0.5 + 0.5 * in_yp
+    side_x, side_in = in_x[:, ny:], cell[:, ny:]
+    rows = slice(8, 8 + size)
+
+    def whole(body, side):
+        return jnp.concatenate([body, side], axis=1)
+
+    beside = rim_columns(True, [table_ref[q] for q in range(3)], y_low, y_high, cell)
+    for j in range(layers):
+        put_half(kx_ref, (j,), beside(0, j))
+        ky_ref[j] = whole(ky_body[j], beside(1, j))
+        kz_ref[j] = beside(2, j)
+    lz_ref[0] = jnp.zeros((size, 2 * ny), jnp.float32)
+    lz_ref[layers] = jnp.zeros((size, 2 * ny), jnp.float32)
+    for j in range(layers):
+        tau = tau_after(kx_ref[j, rows, :], kx_ref[j, slice(9, 9 + size), :], side_x)
+        put_half(tx_ref, (j,), tau)
+        put_half(lx_ref, (j, 1), tau * side_x)
+        lx_ref[j, 0] = lx_body[j]
         ky = ky_ref[j]
-        ky_ref[j] = flow_after(ky, moved(ky, -1, 1), in_y)
+        ky_ref[j] = tau_after(ky, moved(ky, -1, 1), in_y)
         if j < layers - 1:
-            kz, above = kz_ref[j], kz_ref[j + 1]
-            lz_ref[j + 1] = jnp.where(cell, 2.0 * (kz * above) / (kz + above), 0.0)
+            side = jnp.where(side_in, harmonic(kz_ref[j], kz_ref[j + 1]), 0.0)
+            lz_ref[j + 1] = whole(lz_body[j + 1], side)
     for j in range(layers):
-        flow_y = ky_ref[j]
-        ly_ref[j] = flow_y * in_y
-        tau_x, source_ref[0, j] = tau_and_source(
-            get(fx_ref, (j,)), get(fx_ref, (j,), -1), in_x, in_xp
-        )
-        tau_y, source_ref[1, j] = tau_and_source(flow_y, moved(flow_y, 1, 1), in_y, in_yp)
-        centre = tau_x + tau_y + (2.0 * kz_ref[0] if j == 0 else lz_ref[j])
+        tau, back = tx_ref[j, rows, :], tx_ref[j, slice(7, 7 + size), :]
+        source_ref[0, j] = whole(source_body[j], tau * share_x - back * share_xp)
+        centre = whole(tau_body[j], tau + back)
+        tau = ky_ref[j]
+        back = moved(tau, 1, 1)
+        ly_ref[j] = tau * in_y
+        source_ref[1, j] = tau * share_y - back * share_yp
+        centre = centre + (tau + back)
+        centre = centre + (whole(kz_body[0], kz_ref[0]) if j == 0 else lz_ref[j])
         if j < layers - 1:
             centre = centre + lz_ref[j + 1]
         centre_ref[j] = jnp.where(cell, centre, 1.0)
     for j in range(layers):
-        flow_z = -kz_ref[0] if j == 0 else -lz_ref[j]
+        flow_z = -0.5 * whole(kz_body[0], kz_ref[0]) if j == 0 else -lz_ref[j]
         if j < layers - 1:
             flow_z = flow_z + lz_ref[j + 1]
         forward = [source_ref[0, j], source_ref[1, j], sign * flow_z]
@@ -776,7 +832,7 @@
             ratio_ref[j] = ratio
             for f in range(3):
                 d_ref[f, j] = value[f]
-    slabs = [pivot, kz_ref[layers - 1]] + forward
+    slabs = [pivot, 0.5 * whole(kz_body[layers - 1], kz_ref[layers - 1])] + forward
     for q, slab in enumerate(slabs):
         own_ref[q] = slab
     Message(LAST_COUNT, 2, nx, ny).write(message_ref, slabs)
@@ -901,23 +957,39 @@
                 beyond = other[f] * inverse_other + step * near[f]
                 change = jnp.where(beside_other, beyond, change)
             put(change_ref, (f, i + 1), change)
-    own_part = (slice(0, nx), slice(0, ny))
+    lane = iotas(nx, ny)[1]
+    first_lane, last_lane = lane == 0, lane == ny - 1
+
+    def body(ref, index, shift=0):
+        return ref[index + (0, slice(8 + shift, 8 + shift + nx))]
+
+    def edge(ref, index):
+        return ref[index + (1, slice(8, 8 + nx))]
+
     copies = []
     for i in range(nz):
         j = start + i
         z = jnp.where(high, nz - 1 - i, i)
-        link_high = lz_ref[j + 1]
+        link_high = lz_ref[j + 1][:nx, :ny]
         if i == nz - 1:
-            link_high = jnp.where(beside_other, link_near, link_high)
-        cut_low = lz_ref[j] * both_halves(cut_ref, j)
-        cut_high = link_high * both_halves(cut_ref, j + 1)
+            link_high = jnp.where(beside_other, link_near[:nx, :ny], link_high)
+        cut_low = lz_ref[j][:nx, :ny] * cut_ref[pl.ds(j, 1), :]
+        cut_high = link_high * cut_ref[pl.ds(j + 1, 1), :]
+        link_x, link_xp = body(lx_ref, (j,)), body(lx_ref, (j,), -1)
+        link_y = ly_ref[j][:nx]
+        link_yp = moved(jnp.where(last_lane, link_y[:, ny:], link_y[:, :ny]), 1, 1)
         for f in range(3):
-            left_out = beside_sum(change_ref, (f, i + 1), lx_ref, ly_ref, j) + (
-                cut_low * get(change_ref, (f, i)) + cut_high * get(change_ref, (f, i + 2))
+            at = (f, i + 1)
+            here, side = body(change_ref, at), edge(change_ref, at)
+            left_out = (
+                link_x * body(change_ref, at, 1)
+                + link_xp * body(change_ref, at, -1)
+                + link_y[:, :ny] * moved(jnp.where(first_lane, side, here), -1, 1)
+                + link_yp * moved(jnp.where(last_lane, side, here), 1, 1)
             )
-            pressure = get(first_ref, (f, j)) + get(change_ref, (f, i + 1))
-            pressure_ref[f, z] = pressure[own_part]
-            residual_ref[f, z] = left_out[own_part]
+            beyond = cut_low * body(change_ref, (f, i)) + cut_high * body(change_ref, (f, i + 2))
+            pressure_ref[f, z] = body(first_ref, (f, j)) + here
+            residual_ref[f, z] = left_out + beyond
         if (i + 1) % CHUNK == 0:
             part = (slice(None), pl.ds(jnp.where(high, nz - 1 - i, i + 1 - CHUNK), CHUNK))
             for n, (buffer, out) in enumerate(
@@ -996,23 +1068,21 @@
         [((2 * nx + 16, ny), i32)] + [((layers * 4, ny), i32)] * sides,
         [facies, other, table] + rims,
     )
-    k, = kernel_call(
-        prepare_other_kernel,
-        [((3, layers, nx, ny), f32)],
-        [table, k, other, strip],
+    k, *rows = kernel_call(
+        functools.partial(prepare_other_kernel, sides, stages == 1),
+        [((3, layers, nx, ny), f32)] + [((3, layers * 4, ny), f32)] * sides,
+        [table, k, other] + rows,
         cost=pl.CostEstimate(flops=10**7, bytes_accessed=10**6, transcendentals=0),
     )
     y_low, y_high = ring(strip, "gy", 1), ring(strip, "gy", -1)
     sizes = nz, nx, ny
     operands = [table, cuts, k, rows[0], rows[-1], y_low, y_high]
-    scratch = [pltpu.VMEM((3, layers * 4, ny), f32)] * sides
-    return (sweep_ends if stages == 1 else sweep_tree)(sizes, stages, operands, scratch)
-
-
-def sweep_ends(sizes, stages, operands, scratch):
+    return (sweep_ends if stages == 1 else sweep_tree)(sizes, stages, operands)
+
+
+def sweep_ends(sizes, stages, operands):
     nz, nx, ny = sizes
     layers, f32 = 2 * nz, jnp.float32
-    cuts = operands[1]
     slab, tall = (nx + 8, 2 * ny), (2, nx + 24, ny)
 
     def slabs(*count):
@@ -1027,13 +1097,23 @@
     def filler(flops):
         return pl.CostEstimate(flops=flops, bytes_accessed=10**6, transcendentals=0)
 
+    half, tall_half = (nx + 8, ny), (nx + 24, ny)
+    table, cuts, k, row_low, row_high, y_low, y_high = operands
+    body = kernel_call(
+        body_kernel,
+        [((layers,) + tall_half, f32)] + [((layers,) + half, f32)] * 4
+        + [((layers + 1,) + half, f32)],
+        [k, row_low, row_high],
+        cost=filler(10**7),
+    )
     message, own, lx, ly, lz, d, ratio, inverse = kernel_call(
         end_eliminate_kernel,
         [message_of(LAST_COUNT, 2), slabs(LAST_COUNT), talls(layers), slabs(layers),
          slabs(layers + 1), slabs(3, layers), slabs(layers), slabs(layers)],
-        operands,
-        [pltpu.VMEM(*s) for s in (talls(layers), talls(layers), slabs(layers), slabs(layers),
-                                  slabs(2, layers), slabs(layers))] + scratch,
+        [table, cuts, y_low, y_high] + list(body),
+        [pltpu.VMEM((layers,) + tall_half, f32), pltpu.VMEM((layers,) + tall_half, f32),
+         pltpu.VMEM(*slabs(layers)), pltpu.VMEM((layers,) + half, f32),
+         pltpu.VMEM(*slabs(2, layers)), pltpu.VMEM(*slabs(layers))],
     )
     other = swapped(message, stages)
     base, phi, parts = kernel_call(
@@ -1066,7 +1146,7 @@
     ))
 
 
-def sweep_tree(sizes, stages, operands, scratch):
+def sweep_tree(sizes, stages, operands):
     nz, nx, ny = sizes
     layers, f32 = 2 * nz, jnp.float32
     cuts = operands[1]
@@ -1085,8 +1165,7 @@
         + [slabs(FIRST_COUNT), slabs(PAIR_COUNT)]
         + [one] * 3 + [three, one, one],
         operands,
-        [pltpu.VMEM(s, f32) for s in (three[0], one[0], (2,) + one[0], one[0])]
-        + scratch,
+        [pltpu.VMEM(s, f32) for s in (three[0], one[0], (2,) + one[0], one[0])],
     )
     siblings, factors, group = [], [], own
     for s in range(stages - 1):

time: 28.9 us -> 28.5 us (0.986)
  waiting for transfers between devices: 6.36 us -> 5.91 us
    ppermute x3, waiting for transfers between devices: 3.05 us -> 2.61 us  [ring(): lax.ppermute(values, axis, [(i, (i + distance) % size) for i in range(siz...]
    pallas_call x9 -> x10, Pallas kernels: 10.1 us -> 10.1 us  [kernel_call(): pl.pallas_call(kernel, out_shape=[jax.ShapeDtypeStruct(s, t) for s, t in...]
  transfers between devices with their start and end apart: 7 -> 7, of which waited for: 6 -> 6; matrix products, arithmetic and copies ran while one was open for 0% -> 0% of each run, Pallas kernels for 22% -> 24%
where the time goes in v7:
time: 28.5 us; the launch traced here: 28.3 us
  Pallas kernels  10.1 us (35%)
  starting transfers between devices  9.35 us (33%)
  waiting for transfers between devices  5.91 us (21%)
  local copies, waits for them, and re-layouts  2.23 us (8%)
  between operations  0.69 us (2%)
    pallas_call x10, Pallas kernels, kernel_call(): pl.pallas_call(kernel, out_shape=[jax.ShapeDtypeStruct(s, t) for s, t in...  10.1 us
    ppermute x3, starting transfers between devices, swapped(): lax.ppermute(values, 'gz', [(i, i ^ 2 ** stage) for i in range(size)])  7.26 us
    ppermute x3, waiting for transfers between devices, ring(): lax.ppermute(values, axis, [(i, (i + distance) % size) for i in range(siz...  2.61 us
    unnamed x6, local copies, waits for them, and re-layouts  2.23 us
    ppermute x3, waiting for transfers between devices, swapped(): lax.ppermute(values, 'gz', [(i, i ^ 2 ** stage) for i in range(size)])  1.77 us
    ppermute x1, waiting for transfers between devices, slanted(): return lax.ppermute(values, ('gx', 'gz'), route)  1.53 us
    ppermute x1, starting transfers between devices, slanted(): return lax.ppermute(values, ('gx', 'gz'), route)  1.38 us
    ppermute x3, starting transfers between devices, ring(): lax.ppermute(values, axis, [(i, (i + distance) % size) for i in range(siz...  0.72 us
  transfers between devices with their start and end apart: 7, of which 6 were waited for; matrix products, arithmetic and copies ran while one was open for 0% of the time, Pallas kernels for 24%

profile of v7, /device:TPU:0, one launch (start us, length us, event | category | flops | bytes accessed | tf_op | source)
XLA Modules:
  0.0 28.3 jit_solution(3437372698633506549)
XLA Ops:
  0.6 0.0 copy-start
  0.6 0.9 %copy-done = s32[16,16,128]{2,1,0:T(8,128)S(1)} copy-done((s32[16,16,128]{2,1,0:T(8,128)S(1)}, s32[16,16,128]{2,1,0:T(8,128)}, u32[]{:S(2)}) %copy-start) | copy-done | bytes 131096
  1.6 3.1 %collective-permute-start = (s32[16,16,128]{2,1,0:T(8,128)S(1)}, s32[16,16,128]{2,1,0:T(8,128)S(1)}, u32[]{:S(2)}, u32[]{:S(2)}) collective-permute-start(s32[16,16,128]{2,1,0:T(8,128)S(1)} %get-tuple-element.32.facies_ref.own_ref), channel_id=1, source_target_pairs={{0,1},{1,0},{2,3},{3,2},{4,5},{5,4},{6,7},{7,6},{8,9},{9,8},{10,11... | collective-permute-start | bytes 393224 | tf_op jit(solution)/shard_map/ppermute | solution.py:1023
  4.6 1.4 %collective-permute-start.2 = (s32[64,128]{1,0:T(8,128)S(1)}, s32[64,128]{1,0:T(8,128)S(1)}, u32[]{:S(2)}, u32[]{:S(2)}) collective-permute-start(s32[64,128]{1,0:T(8,128)S(1)} %get-tuple-element.35), channel_id=1, source_target_pairs={{0,17},{1,16},{2,19},{3,18},{16,1},{17,0},{18,3},{19,2},{4,21},{5,... | collective-permute-start | bytes 98312 | tf_op jit(solution)/shard_map/ppermute | solution.py:1037
  6.0 0.2 collective-permute-start.1
  6.2 0.0 copy-start.1
  6.2 0.7 %copy-done.1 = f32[3,16]{1,0:T(4,128)S(1)} copy-done((f32[3,16]{1,0:T(4,128)S(1)}, f32[3,16]{1,0:T(4,128)}, u32[]{:S(2)}) %copy-start.1) | copy-done | bytes 216
  6.9 0.0 copy-start.2
  6.9 0.7 %copy-done.2 = s32[63]{0:T(128)S(1)} copy-done((s32[63]{0:T(128)S(1)}, s32[63]{0:T(128)}, u32[]{:S(2)}) %copy-start.2) | copy-done | bytes 276
  7.5 0.9 %shard_map.51 = (f32[3,16,16,128]{3,2,1,0:T(8,128)S(1)}, f32[3,8,128]{2,1,0:T(8,128)S(1)}, f32[40,128]{1,0:T(8,128)S(1)}) custom-call(f32[3,16]{1,0:T(4,128)S(1)} %copy-done.1, s32[63]{0:T(128)S(1)} %copy-done.2, s32[16,16,128]{2,1,0:T(8,128)S(1)} %get-tuple-element.32.facies_ref.own_ref), custom_call_target="tpu_custom_call" | custom-call | flops 10000000 | bytes 1000000 | tf_op jit(solution)/shard_map/pallas_call | solution.py:1010
  8.4 1.5 %collective-permute-done.2.refs_1_ = s32[64,128]{1,0:T(8,128)S(1)} collective-permute-done((s32[64,128]{1,0:T(8,128)S(1)}, s32[64,128]{1,0:T(8,128)S(1)}, u32[]{:S(2)}, u32[]{:S(2)}) %collective-permute-start.2) | collective-permute-done | bytes 32800 | tf_op jit(solution)/shard_map/ppermute | solution.py:1037
  10.0 0.3 %collective-permute-done.1.refs_0_ = s32[64,128]{1,0:T(8,128)S(1)} collective-permute-done((s32[64,128]{1,0:T(8,128)S(1)}, s32[64,128]{1,0:T(8,128)S(1)}, u32[]{:S(2)}, u32[]{:S(2)}) %collective-permute-start.1) | collective-permute-done | bytes 32800 | tf_op jit(solution)/shard_map/ppermute | solution.py:1028
  10.3 0.0 collective-permute-done.other_ref
  10.3 0.2 shard_map.52
  10.5 0.1 collective-permute-start.4
  10.5 0.5 %collective-permute-start.3 = (s32[48,128]{1,0:T(8,128)S(1)}, s32[48,128]{1,0:T(8,128)S(1)}, u32[]{:S(2)}, u32[]{:S(2)}) collective-permute-start(s32[48,128]{1,0:T(8,128)S(1)} %get-tuple-element.36), channel_id=1, source_target_pairs={{0,4},{4,8},{8,12},{12,0},{1,5},{5,9},{9,13},{13,1},{2,6},{6,10},{... | collective-permute-start | bytes 73736 | tf_op jit(solution)/shard_map/ppermute | solution.py:1028
  11.0 0.5 %shard_map.53 = (f32[3,32,16,128]{3,2,1,0:T(8,128)S(1)}, f32[3,128,128]{2,1,0:T(8,128)S(1)}) custom-call(f32[3,8,128]{2,1,0:T(8,128)S(1)} %get-tuple-element.34.table_ref, f32[3,16,16,128]{3,2,1,0:T(8,128)S(1)} %get-tuple-element.37.own_ref, s32[16,16,128]{2,1,0:T(8,128)S(1)} %collective-permute-done.other_ref, s32[128,128]{1,0:T(8,128)S(1)} %get-tuple-element.38.refs_0_), custom_call_target="tpu_custom_call" | custom-call | flops 10000000 | bytes 1000000 | tf_op jit(solution)/shard_map/pallas_call | solution.py:1010
  11.5 0.3 %shard_map.54 = (f32[32,40,128]{2,1,0:T(8,128)S(1)}, f32[32,24,128]{2,1,0:T(8,128)S(1)}, f32[32,24,128]{2,1,0:T(8,128)S(1)}, f32[32,24,128]{2,1,0:T(8,128)S(1)},...) custom-call(f32[3,32,16,128]{3,2,1,0:T(8,128)S(1)} %get-tuple-element.39.k_ref, ...), custom_call_target="tpu_custom_call" | custom-call | flops 10000000 | bytes 1000000 | tf_op jit(solution)/shard_map/pallas_call | solution.py:1010
  11.8 0.2 collective-permute-done.4.y_high
  12.0 2.0 %collective-permute-done.3.y_low = s32[48,128]{1,0:T(8,128)S(1)} collective-permute-done((s32[48,128]{1,0:T(8,128)S(1)}, s32[48,128]{1,0:T(8,128)S(1)}, u32[]{:S(2)}, u32[]{:S(2)}) %collective-permute-start.3) | collective-permute-done | bytes 24608 | tf_op jit(solution)/shard_map/ppermute | solution.py:1028
  14.1 1.6 %shard_map.55 = (f32[104,128]{1,0:T(8,128)S(1)}, f32[5,24,256]{2,1,0:T(8,128)S(1)}, f32[32,2,40,128]{3,2,1,0:T(8,128)S(1)}, f32[32,24,256]{2,1,0:T(8,128)S(1)}, ...) custom-call(f32[3,8,128]{2,1,0:T(8,128)S(1)} %get-tuple-element.34.t, ...), custom_call_target="tpu_custom_call" | custom-call | tf_op jit(solution)/shard_map/pallas_call | solution.py:1010
  15.7 2.7 %collective-permute-start.5 = (f32[104,128]{1,0:T(8,128)S(1)}, f32[104,128]{1,0:T(8,128)S(1)}, u32[]{:S(2)}, u32[]{:S(2)}) collective-permute-start(f32[104,128]{1,0:T(8,128)S(1)} %get-tuple-element.48), channel_id=1, source_target_pairs={{0,2},{1,3},{2,0},{3,1},{4,6},{5,7},{6,4},{7,5},{8,10},{9,11},{10,... | collective-permute-start | bytes 159752 | tf_op jit(solution)/shard_map/ppermute | solution.py:1023
  18.3 2.6 %shard_map.56 = (f32[3,32,2,40,128]{4,3,2,1,0:T(8,128)S(1)}, f32[32,2,40,128]{3,2,1,0:T(8,128)S(1)}, f32[6,24,256]{2,1,0:T(8,128)S(1)}) custom-call(f32[40,128]{1,0:T(8,128)S(1)} %get-tuple-element.33.cut_ref, f32[32,2,40,128]{3,2,1,0:T(8,128)S(1)} %get-tuple-element.49.lx_ref, f32[32,24,256]{2,1,0:T(8,128)S(1)} %get-tuple-element.50.ly_ref, ...), custom_call_target="tpu_custom_call" | custom-call | flops 10000000 | bytes 1000000 | tf_op jit(solution)/shard_map/pallas_call | solution.py:1010
  21.0 0.9 %collective-permute-done.5.message_ref = f32[104,128]{1,0:T(8,128)S(1)} collective-permute-done((f32[104,128]{1,0:T(8,128)S(1)}, f32[104,128]{1,0:T(8,128)S(1)}, u32[]{:S(2)}, u32[]{:S(2)}) %collective-permute-start.5) | collective-permute-done | bytes 53280 | tf_op jit(solution)/shard_map/ppermute | solution.py:1023
  21.9 0.3 shard_map.57
  22.2 1.5 %collective-permute-start.6 = (f32[64,128]{1,0:T(8,128)S(1)}, f32[64,128]{1,0:T(8,128)S(1)}, u32[]{:S(2)}, u32[]{:S(2)}) collective-permute-start(f32[64,128]{1,0:T(8,128)S(1)} %get-tuple-element.55), channel_id=1, source_target_pairs={{0,2},{1,3},{2,0},{3,1},{4,6},{5,7},{6,4},{7,5},{8,10},{9,11},{10,... | collective-permute-start | bytes 98312 | tf_op jit(solution)/shard_map/ppermute | solution.py:1023
  23.7 2.5 %shard_map.58 = (f32[3,32,2,40,128]{4,3,2,1,0:T(8,128)S(1)}, f32[3,32,24,256]{3,2,1,0:T(8,128)S(1)}) custom-call(f32[40,128]{1,0:T(8,128)S(1)} %get-tuple-element.33.cut_ref, f32[13,24,256]{2,1,0:T(8,128)S(1)} %get-tuple-element.56.near_ref, f32[32,2,40,128]{3,2,1,0:T(8,128)S(1)} %get-tuple-element.49.lx_ref, f32[32,24,256]{2,1,0:T(8,128)S(1)} %get-tuple-element.50.ly_ref, ...), custom_call_target="tpu_custom_call" | custom-call | flops 10000000 | bytes 1000000 | tf_op jit(solution)/shard_map/pallas_call | solution.py:1010
  26.3 0.8 %collective-permute-done.6.message_ref = f32[64,128]{1,0:T(8,128)S(1)} collective-permute-done((f32[64,128]{1,0:T(8,128)S(1)}, f32[64,128]{1,0:T(8,128)S(1)}, u32[]{:S(2)}, u32[]{:S(2)}) %collective-permute-start.6) | collective-permute-done | bytes 32800 | tf_op jit(solution)/shard_map/ppermute | solution.py:1023
  27.1 1.2 %shard_map.59 = (f32[3,16,16,128]{3,2,1,0:T(8,128)}, f32[3,16,16,128]{3,2,1,0:T(8,128)}) custom-call(f32[40,128]{1,0:T(8,128)S(1)} %get-tuple-element.33.cut_ref, f32[64,128]{1,0:T(8,128)S(1)} %collective-permute-done.6.message_ref, f32[13,24,256]{2,1,0:T(8,128)S(1)} %get-tuple-element.56.near_ref, f32[32,2,40,128]{3,2,1,0:T(8,128)S(1)} %get-tuple-element.49.lx_ref, ...), custom_call_target="tpu_custom_call" | custom-call | tf_op jit(solution)/shard_map/pallas_call | solution.py:1010
  (1 shorter events, 0.0 us)
Async XLA Ops:
  0.6 0.9 %copy-start = (s32[16,16,128]{2,1,0:T(8,128)S(1)}, s32[16,16,128]{2,1,0:T(8,128)}, u32[]{:S(2)}) copy-start(s32[16,16,128]{2,1,0:T(8,128)} %facies_ref.1) | copy-start | bytes 393220
  1.6 8.7 %collective-permute-start = (s32[16,16,128]{2,1,0:T(8,128)S(1)}, s32[16,16,128]{2,1,0:T(8,128)S(1)}, u32[]{:S(2)}, u32[]{:S(2)}) collective-permute-start(s32[16,16,128]{2,1,0:T(8,128)S(1)} %get-tuple-element.32.facies_ref.own_ref), channel_id=1, source_target_pairs={{0,1},{1,0},{2,3},{3,2},{4,5},{5,4},{6,7},{7,6},{8,9},{9,8},{10,11... | collective-permute-start | bytes 393224 | tf_op jit(solution)/shard_map/ppermute | solution.py:1023
  4.6 5.3 %collective-permute-start.2 = (s32[64,128]{1,0:T(8,128)S(1)}, s32[64,128]{1,0:T(8,128)S(1)}, u32[]{:S(2)}, u32[]{:S(2)}) collective-permute-start(s32[64,128]{1,0:T(8,128)S(1)} %get-tuple-element.35), channel_id=1, source_target_pairs={{0,17},{1,16},{2,19},{3,18},{16,1},{17,0},{18,3},{19,2},{4,21},{5,... | collective-permute-start | bytes 98312 | tf_op jit(solution)/shard_map/ppermute | solution.py:1037
  6.0 4.3 %collective-permute-start.1 = (s32[64,128]{1,0:T(8,128)S(1)}, s32[64,128]{1,0:T(8,128)S(1)}, u32[]{:S(2)}, u32[]{:S(2)}) collective-permute-start(s32[64,128]{1,0:T(8,128)S(1)} %get-tuple-element.35), channel_id=1, source_target_pairs={{0,16},{16,0},{1,17},{17,1},{2,18},{18,2},{3,19},{19,3},{4,20},{20... | collective-permute-start | bytes 98312 | tf_op jit(solution)/shard_map/ppermute | solution.py:1028
  6.2 0.7 %copy-start.1 = (f32[3,16]{1,0:T(4,128)S(1)}, f32[3,16]{1,0:T(4,128)}, u32[]{:S(2)}) copy-start(f32[3,16]{1,0:T(4,128)} %table.1) | copy-start | bytes 580
  6.9 0.7 %copy-start.2 = (s32[63]{0:T(128)S(1)}, s32[63]{0:T(128)}, u32[]{:S(2)}) copy-start(s32[63]{0:T(128)} %breaks.1) | copy-start | bytes 760
  10.5 1.6 %collective-permute-start.4 = (s32[48,128]{1,0:T(8,128)S(1)}, s32[48,128]{1,0:T(8,128)S(1)}, u32[]{:S(2)}, u32[]{:S(2)}) collective-permute-start(s32[48,128]{1,0:T(8,128)S(1)} %get-tuple-element.36), channel_id=1, source_target_pairs={{0,12},{4,0},{8,4},{12,8},{1,13},{5,1},{9,5},{13,9},{2,14},{6,2},{... | collective-permute-start | bytes 73736 | tf_op jit(solution)/shard_map/ppermute | solution.py:1028
  10.5 3.6 %collective-permute-start.3 = (s32[48,128]{1,0:T(8,128)S(1)}, s32[48,128]{1,0:T(8,128)S(1)}, u32[]{:S(2)}, u32[]{:S(2)}) collective-permute-start(s32[48,128]{1,0:T(8,128)S(1)} %get-tuple-element.36), channel_id=1, source_target_pairs={{0,4},{4,8},{8,12},{12,0},{1,5},{5,9},{9,13},{13,1},{2,6},{6,10},{... | collective-permute-start | bytes 73736 | tf_op jit(solution)/shard_map/ppermute | solution.py:1028
  15.7 6.2 %collective-permute-start.5 = (f32[104,128]{1,0:T(8,128)S(1)}, f32[104,128]{1,0:T(8,128)S(1)}, u32[]{:S(2)}, u32[]{:S(2)}) collective-permute-start(f32[104,128]{1,0:T(8,128)S(1)} %get-tuple-element.48), channel_id=1, source_target_pairs={{0,2},{1,3},{2,0},{3,1},{4,6},{5,7},{6,4},{7,5},{8,10},{9,11},{10,... | collective-permute-start | bytes 159752 | tf_op jit(solution)/shard_map/ppermute | solution.py:1023
  22.2 4.9 %collective-permute-start.6 = (f32[64,128]{1,0:T(8,128)S(1)}, f32[64,128]{1,0:T(8,128)S(1)}, u32[]{:S(2)}, u32[]{:S(2)}) collective-permute-start(f32[64,128]{1,0:T(8,128)S(1)} %get-tuple-element.55), channel_id=1, source_target_pairs={{0,2},{1,3},{2,0},{3,1},{4,6},{5,7},{6,4},{7,5},{8,10},{9,11},{10,... | collective-permute-start | bytes 98312 | tf_op jit(solution)/shard_map/ppermute | solution.py:1023

commit v8 on v7

--- a/solution.py
+++ b/solution.py
@@ -71,7 +71,7 @@
     return jnp.where(row < 4, moved(high, 4, 0), low)
 
 
-def merge_kernel(own_ref, other_ref, table_ref, *refs):
+def merge_kernel(own_ref, other_ref, *refs):
     sides = (len(refs) - 1) // 3
     ins, strip_ref, row_refs = refs[: 2 * sides], refs[2 * sides], refs[2 * sides + 1 :]
     nz, nx, ny = own_ref.shape
@@ -1045,12 +1045,12 @@
     layers = 2 * nz
     cut_rows = -(-(layers + 1 + 2 * stages) // 8) * 8
     sides = 1 if two else 2
+    other = swapped(facies, 0)
     facies, *rows = kernel_call(
         pack_kernel,
         [((nz, nx, ny), i32)] + [((nz * 4, ny), i32)] * sides,
         [facies],
     )
-    other = swapped(facies, 0)
     if two:
         rims = [ring(rows[0], "gx", 1), slanted(rows[0], 1)]
     else:
@@ -1066,7 +1066,7 @@
     strip, *rows = kernel_call(
         merge_kernel,
         [((2 * nx + 16, ny), i32)] + [((layers * 4, ny), i32)] * sides,
-        [facies, other, table] + rims,
+        [facies, other] + rims,
     )
     k, *rows = kernel_call(
         functools.partial(prepare_other_kernel, sides, stages == 1),

time: 28.5 us -> 27.9 us (0.979)
  waiting for transfers between devices: 5.91 us -> 3.93 us
  starting transfers between devices: 9.35 us -> 10.7 us
    ppermute x3, waiting for transfers between devices: 2.61 us -> 0.51 us  [ring(): lax.ppermute(values, axis, [(i, (i + distance) % size) for i in range(siz...]
    ppermute x1, waiting for transfers between devices: 1.53 us -> 3.24 us  [slanted(): return lax.ppermute(values, ('gx', 'gz'), route)]
    ppermute x3, waiting for transfers between devices: 1.77 us -> 0.17 us  [swapped(): lax.ppermute(values, 'gz', [(i, i ^ 2 ** stage) for i in range(size)])]
    ppermute x3, starting transfers between devices: 7.26 us -> 8.47 us  [swapped(): lax.ppermute(values, 'gz', [(i, i ^ 2 ** stage) for i in range(size)])]
  transfers between devices with their start and end apart: 7 -> 7, of which waited for: 6 -> 3; matrix products, arithmetic and copies ran while one was open for 0% -> 0% of each run, Pallas kernels for 24% -> 25%
where the time goes in v8:
time: 27.9 us; the launch traced here: 27.7 us
  starting transfers between devices  10.7 us (38%)
  Pallas kernels  10.1 us (36%)
  waiting for transfers between devices  3.93 us (14%)
  local copies, waits for them, and re-layouts  2.27 us (8%)
  between operations  0.7 us (3%)
    pallas_call x10, Pallas kernels, kernel_call(): pl.pallas_call(kernel, out_shape=[jax.ShapeDtypeStruct(s, t) for s, t in...  10.1 us
    ppermute x3, starting transfers between devices, swapped(): lax.ppermute(values, 'gz', [(i, i ^ 2 ** stage) for i in range(size)])  8.47 us
    ppermute x1, waiting for transfers between devices, slanted(): return lax.ppermute(values, ('gx', 'gz'), route)  3.24 us
    unnamed x6, local copies, waits for them, and re-layouts  2.27 us
    ppermute x1, starting transfers between devices, slanted(): return lax.ppermute(values, ('gx', 'gz'), route)  1.44 us
    ppermute x3, starting transfers between devices, ring(): lax.ppermute(values, axis, [(i, (i + distance) % size) for i in range(siz...  0.75 us
  transfers between devices with their start and end apart: 7, of which 3 were waited for; matrix products, arithmetic and copies ran while one was open for 0% of the time, Pallas kernels for 25%

profile of v8, /device:TPU:0, one launch (start us, length us, event | category | flops | bytes accessed | tf_op | source)
XLA Modules:
  0.0 27.7 jit_solution(7376974378326833485)
XLA Ops:
  0.6 3.1 %collective-permute-start = (s32[16,16,128]{2,1,0:T(8,128)}, s32[16,16,128]{2,1,0:T(8,128)S(1)}, u32[]{:S(2)}, u32[]{:S(2)}) collective-permute-start(s32[16,16,128]{2,1,0:T(8,128)} %facies_ref.1), channel_id=1, source_target_pairs={{0,1},{1,0},{2,3},{3,2},{4,5},{5,4},{6,7},{7,6},{8,9},{9,8},{10,11... | collective-permute-start | bytes 393224 | tf_op jit(solution)/shard_map/ppermute | solution.py:1023
  3.7 0.0 copy-start
  3.7 0.9 %copy-done = s32[16,16,128]{2,1,0:T(8,128)S(1)} copy-done((s32[16,16,128]{2,1,0:T(8,128)S(1)}, s32[16,16,128]{2,1,0:T(8,128)}, u32[]{:S(2)}) %copy-start) | copy-done | bytes 131096
  4.7 1.4 %collective-permute-start.2 = (s32[64,128]{1,0:T(8,128)S(1)}, s32[64,128]{1,0:T(8,128)S(1)}, u32[]{:S(2)}, u32[]{:S(2)}) collective-permute-start(s32[64,128]{1,0:T(8,128)S(1)} %get-tuple-element.35), channel_id=1, source_target_pairs={{0,17},{1,16},{2,19},{3,18},{16,1},{17,0},{18,3},{19,2},{4,21},{5,... | collective-permute-start | bytes 98312 | tf_op jit(solution)/shard_map/ppermute | solution.py:1037
  6.1 0.2 collective-permute-start.1
  6.3 3.2 %collective-permute-done.2.refs_1_ = s32[64,128]{1,0:T(8,128)S(1)} collective-permute-done((s32[64,128]{1,0:T(8,128)S(1)}, s32[64,128]{1,0:T(8,128)S(1)}, u32[]{:S(2)}, u32[]{:S(2)}) %collective-permute-start.2) | collective-permute-done | bytes 32800 | tf_op jit(solution)/shard_map/ppermute | solution.py:1037
  9.6 0.5 %collective-permute-done.1.refs_0_ = s32[64,128]{1,0:T(8,128)S(1)} collective-permute-done((s32[64,128]{1,0:T(8,128)S(1)}, s32[64,128]{1,0:T(8,128)S(1)}, u32[]{:S(2)}, u32[]{:S(2)}) %collective-permute-start.1) | collective-permute-done | bytes 32800 | tf_op jit(solution)/shard_map/ppermute | solution.py:1028
  10.0 0.0 collective-permute-done.other_ref
  10.0 0.2 shard_map.52
  10.2 0.1 collective-permute-start.4
  10.3 0.5 %collective-permute-start.3 = (s32[48,128]{1,0:T(8,128)S(1)}, s32[48,128]{1,0:T(8,128)S(1)}, u32[]{:S(2)}, u32[]{:S(2)}) collective-permute-start(s32[48,128]{1,0:T(8,128)S(1)} %get-tuple-element.36), channel_id=1, source_target_pairs={{0,4},{4,8},{8,12},{12,0},{1,5},{5,9},{9,13},{13,1},{2,6},{6,10},{... | collective-permute-start | bytes 73736 | tf_op jit(solution)/shard_map/ppermute | solution.py:1028
  10.8 0.0 copy-start.1
  10.8 0.7 %copy-done.1 = f32[3,16]{1,0:T(4,128)S(1)} copy-done((f32[3,16]{1,0:T(4,128)S(1)}, f32[3,16]{1,0:T(4,128)}, u32[]{:S(2)}) %copy-start.1) | copy-done | bytes 216
  11.5 0.0 copy-start.2
  11.5 0.7 %copy-done.2 = s32[63]{0:T(128)S(1)} copy-done((s32[63]{0:T(128)S(1)}, s32[63]{0:T(128)}, u32[]{:S(2)}) %copy-start.2) | copy-done | bytes 276
  12.1 0.9 %shard_map.51 = (f32[3,16,16,128]{3,2,1,0:T(8,128)S(1)}, f32[3,8,128]{2,1,0:T(8,128)S(1)}, f32[40,128]{1,0:T(8,128)S(1)}) custom-call(f32[3,16]{1,0:T(4,128)S(1)} %copy-done.1, s32[63]{0:T(128)S(1)} %copy-done.2, s32[16,16,128]{2,1,0:T(8,128)S(1)} %get-tuple-element.32.facies_ref.own_ref), custom_call_target="tpu_custom_call" | custom-call | flops 10000000 | bytes 1000000 | tf_op jit(solution)/shard_map/pallas_call | solution.py:1010
  13.0 0.5 %shard_map.53 = (f32[3,32,16,128]{3,2,1,0:T(8,128)S(1)}, f32[3,128,128]{2,1,0:T(8,128)S(1)}) custom-call(f32[3,8,128]{2,1,0:T(8,128)S(1)} %get-tuple-element.34.table_ref, f32[3,16,16,128]{3,2,1,0:T(8,128)S(1)} %get-tuple-element.37.own_ref, s32[16,16,128]{2,1,0:T(8,128)S(1)} %collective-permute-done.other_ref, s32[128,128]{1,0:T(8,128)S(1)} %get-tuple-element.38.refs_0_), custom_call_target="tpu_custom_call" | custom-call | flops 10000000 | bytes 1000000 | tf_op jit(solution)/shard_map/pallas_call | solution.py:1010
  13.5 0.3 %shard_map.54 = (f32[32,40,128]{2,1,0:T(8,128)S(1)}, f32[32,24,128]{2,1,0:T(8,128)S(1)}, f32[32,24,128]{2,1,0:T(8,128)S(1)}, f32[32,24,128]{2,1,0:T(8,128)S(1)},...) custom-call(f32[3,32,16,128]{3,2,1,0:T(8,128)S(1)} %get-tuple-element.39.k_ref, ...), custom_call_target="tpu_custom_call" | custom-call | flops 10000000 | bytes 1000000 | tf_op jit(solution)/shard_map/pallas_call | solution.py:1010
  13.8 0.0 collective-permute-done.4.y_high
  13.8 0.0 collective-permute-done.3.y_low
  13.8 1.6 %shard_map.55 = (f32[104,128]{1,0:T(8,128)S(1)}, f32[5,24,256]{2,1,0:T(8,128)S(1)}, f32[32,2,40,128]{3,2,1,0:T(8,128)S(1)}, f32[32,24,256]{2,1,0:T(8,128)S(1)}, ...) custom-call(f32[3,8,128]{2,1,0:T(8,128)S(1)} %get-tuple-element.34.t, ...), custom_call_target="tpu_custom_call" | custom-call | tf_op jit(solution)/shard_map/pallas_call | solution.py:1010
  15.4 2.7 %collective-permute-start.5 = (f32[104,128]{1,0:T(8,128)S(1)}, f32[104,128]{1,0:T(8,128)S(1)}, u32[]{:S(2)}, u32[]{:S(2)}) collective-permute-start(f32[104,128]{1,0:T(8,128)S(1)} %get-tuple-element.48), channel_id=1, source_target_pairs={{0,2},{1,3},{2,0},{3,1},{4,6},{5,7},{6,4},{7,5},{8,10},{9,11},{10,... | collective-permute-start | bytes 159752 | tf_op jit(solution)/shard_map/ppermute | solution.py:1023
  18.1 2.6 %shard_map.56 = (f32[3,32,2,40,128]{4,3,2,1,0:T(8,128)S(1)}, f32[32,2,40,128]{3,2,1,0:T(8,128)S(1)}, f32[6,24,256]{2,1,0:T(8,128)S(1)}) custom-call(f32[40,128]{1,0:T(8,128)S(1)} %get-tuple-element.33.cut_ref, f32[32,2,40,128]{3,2,1,0:T(8,128)S(1)} %get-tuple-element.49.lx_ref, f32[32,24,256]{2,1,0:T(8,128)S(1)} %get-tuple-element.50.ly_ref, ...), custom_call_target="tpu_custom_call" | custom-call | flops 10000000 | bytes 1000000 | tf_op jit(solution)/shard_map/pallas_call | solution.py:1010
  20.7 0.2 collective-permute-done.5.message_ref
  20.9 0.3 shard_map.57
  21.2 2.7 %collective-permute-start.6 = (f32[64,128]{1,0:T(8,128)S(1)}, f32[64,128]{1,0:T(8,128)S(1)}, u32[]{:S(2)}, u32[]{:S(2)}) collective-permute-start(f32[64,128]{1,0:T(8,128)S(1)} %get-tuple-element.55), channel_id=1, source_target_pairs={{0,2},{1,3},{2,0},{3,1},{4,6},{5,7},{6,4},{7,5},{8,10},{9,11},{10,... | collective-permute-start | bytes 98312 | tf_op jit(solution)/shard_map/ppermute | solution.py:1023
  23.9 2.5 %shard_map.58 = (f32[3,32,2,40,128]{4,3,2,1,0:T(8,128)S(1)}, f32[3,32,24,256]{3,2,1,0:T(8,128)S(1)}) custom-call(f32[40,128]{1,0:T(8,128)S(1)} %get-tuple-element.33.cut_ref, f32[13,24,256]{2,1,0:T(8,128)S(1)} %get-tuple-element.56.near_ref, f32[32,2,40,128]{3,2,1,0:T(8,128)S(1)} %get-tuple-element.49.lx_ref, f32[32,24,256]{2,1,0:T(8,128)S(1)} %get-tuple-element.50.ly_ref, ...), custom_call_target="tpu_custom_call" | custom-call | flops 10000000 | bytes 1000000 | tf_op jit(solution)/shard_map/pallas_call | solution.py:1010
  26.4 0.0 collective-permute-done.6.message_ref
  26.5 1.2 %shard_map.59 = (f32[3,16,16,128]{3,2,1,0:T(8,128)}, f32[3,16,16,128]{3,2,1,0:T(8,128)}) custom-call(f32[40,128]{1,0:T(8,128)S(1)} %get-tuple-element.33.cut_ref, f32[64,128]{1,0:T(8,128)S(1)} %collective-permute-done.6.message_ref, f32[13,24,256]{2,1,0:T(8,128)S(1)} %get-tuple-element.56.near_ref, f32[32,2,40,128]{3,2,1,0:T(8,128)S(1)} %get-tuple-element.49.lx_ref, ...), custom_call_target="tpu_custom_call" | custom-call | tf_op jit(solution)/shard_map/pallas_call | solution.py:1010
  (1 shorter events, 0.0 us)
Async XLA Ops:
  0.6 9.4 %collective-permute-start = (s32[16,16,128]{2,1,0:T(8,128)}, s32[16,16,128]{2,1,0:T(8,128)S(1)}, u32[]{:S(2)}, u32[]{:S(2)}) collective-permute-start(s32[16,16,128]{2,1,0:T(8,128)} %facies_ref.1), channel_id=1, source_target_pairs={{0,1},{1,0},{2,3},{3,2},{4,5},{5,4},{6,7},{7,6},{8,9},{9,8},{10,11... | collective-permute-start | bytes 393224 | tf_op jit(solution)/shard_map/ppermute | solution.py:1023
  3.7 0.9 %copy-start = (s32[16,16,128]{2,1,0:T(8,128)S(1)}, s32[16,16,128]{2,1,0:T(8,128)}, u32[]{:S(2)}) copy-start(s32[16,16,128]{2,1,0:T(8,128)} %facies_ref.1) | copy-start | bytes 393220
  4.7 4.9 %collective-permute-start.2 = (s32[64,128]{1,0:T(8,128)S(1)}, s32[64,128]{1,0:T(8,128)S(1)}, u32[]{:S(2)}, u32[]{:S(2)}) collective-permute-start(s32[64,128]{1,0:T(8,128)S(1)} %get-tuple-element.35), channel_id=1, source_target_pairs={{0,17},{1,16},{2,19},{3,18},{16,1},{17,0},{18,3},{19,2},{4,21},{5,... | collective-permute-start | bytes 98312 | tf_op jit(solution)/shard_map/ppermute | solution.py:1037
  6.1 3.9 %collective-permute-start.1 = (s32[64,128]{1,0:T(8,128)S(1)}, s32[64,128]{1,0:T(8,128)S(1)}, u32[]{:S(2)}, u32[]{:S(2)}) collective-permute-start(s32[64,128]{1,0:T(8,128)S(1)} %get-tuple-element.35), channel_id=1, source_target_pairs={{0,16},{16,0},{1,17},{17,1},{2,18},{18,2},{3,19},{19,3},{4,20},{20... | collective-permute-start | bytes 98312 | tf_op jit(solution)/shard_map/ppermute | solution.py:1028
  10.2 3.6 %collective-permute-start.4 = (s32[48,128]{1,0:T(8,128)S(1)}, s32[48,128]{1,0:T(8,128)S(1)}, u32[]{:S(2)}, u32[]{:S(2)}) collective-permute-start(s32[48,128]{1,0:T(8,128)S(1)} %get-tuple-element.36), channel_id=1, source_target_pairs={{0,12},{4,0},{8,4},{12,8},{1,13},{5,1},{9,5},{13,9},{2,14},{6,2},{... | collective-permute-start | bytes 73736 | tf_op jit(solution)/shard_map/ppermute | solution.py:1028
  10.3 3.6 %collective-permute-start.3 = (s32[48,128]{1,0:T(8,128)S(1)}, s32[48,128]{1,0:T(8,128)S(1)}, u32[]{:S(2)}, u32[]{:S(2)}) collective-permute-start(s32[48,128]{1,0:T(8,128)S(1)} %get-tuple-element.36), channel_id=1, source_target_pairs={{0,4},{4,8},{8,12},{12,0},{1,5},{5,9},{9,13},{13,1},{2,6},{6,10},{... | collective-permute-start | bytes 73736 | tf_op jit(solution)/shard_map/ppermute | solution.py:1028
  10.8 0.7 %copy-start.1 = (f32[3,16]{1,0:T(4,128)S(1)}, f32[3,16]{1,0:T(4,128)}, u32[]{:S(2)}) copy-start(f32[3,16]{1,0:T(4,128)} %table.1) | copy-start | bytes 580
  11.5 0.7 %copy-start.2 = (s32[63]{0:T(128)S(1)}, s32[63]{0:T(128)}, u32[]{:S(2)}) copy-start(s32[63]{0:T(128)} %breaks.1) | copy-start | bytes 760
  15.4 5.5 %collective-permute-start.5 = (f32[104,128]{1,0:T(8,128)S(1)}, f32[104,128]{1,0:T(8,128)S(1)}, u32[]{:S(2)}, u32[]{:S(2)}) collective-permute-start(f32[104,128]{1,0:T(8,128)S(1)} %get-tuple-element.48), channel_id=1, source_target_pairs={{0,2},{1,3},{2,0},{3,1},{4,6},{5,7},{6,4},{7,5},{8,10},{9,11},{10,... | collective-permute-start | bytes 159752 | tf_op jit(solution)/shard_map/ppermute | solution.py:1023
  21.2 5.3 %collective-permute-start.6 = (f32[64,128]{1,0:T(8,128)S(1)}, f32[64,128]{1,0:T(8,128)S(1)}, u32[]{:S(2)}, u32[]{:S(2)}) collective-permute-start(f32[64,128]{1,0:T(8,128)S(1)} %get-tuple-element.55), channel_id=1, source_target_pairs={{0,2},{1,3},{2,0},{3,1},{4,6},{5,7},{6,4},{7,5},{8,10},{9,11},{10,... | collective-permute-start | bytes 98312 | tf_op jit(solution)/shard_map/ppermute | solution.py:1023

commit v9 on v8

--- a/solution.py
+++ b/solution.py
@@ -713,6 +713,12 @@
     return jnp.concatenate(halves, axis=1)
 
 
+def blank(slab):
+    rows, ny = slab.shape[0] - 8, slab.shape[1] // 2
+    side = jnp.concatenate([slab[:rows, ny:], jnp.zeros((8, ny), jnp.float32)], axis=0)
+    return jnp.concatenate([slab[:, :ny], side], axis=1)
+
+
 def signed():
     return jnp.where(is_high(0), -1.0, 1.0)
 
@@ -725,8 +731,8 @@
 def beside_sum(field_ref, index, lx_ref, ly_ref, j):
     here, link_y = get(field_ref, index), ly_ref[j]
     return (
-        get(lx_ref, (j,)) * get(field_ref, index, 1)
-        + get(lx_ref, (j,), -1) * get(field_ref, index, -1)
+        get(lx_ref, (j,)) * moved(here, -1, 0)
+        + get(lx_ref, (j,), -1) * moved(here, 1, 0)
         + (link_y * moved(here, -1, 1) + moved(link_y * here, 1, 1))
     )
 
@@ -870,7 +876,7 @@
                 right = right + cut_low * get(base_ref, (f, j - 1))
             if j < layers - 1:
                 right = right + cut_high * get(base_ref, (f, j + 1))
-            parts[f] = parts[f] + phi * right
+            parts[f] = blank(parts[f] + phi * right)
     for n, slab in enumerate(parts + [along_x, along_y, 2.0 * along_z]):
         part_ref[n] = slab
 
@@ -922,14 +928,14 @@
             right = right + cut_high * get(first_ref, (f, j + 1))
             if j > 0:
                 right = right + cut_low * get(first_ref, (f, j - 1)) + coupling * d_ref[f, j - 1]
-            d_ref[f, j] = right * inverse
+            d_ref[f, j] = blank(right * inverse)
     change = [jnp.zeros(ly_ref.shape[1:], jnp.float32)] * 3
     for f in range(3):
         change_ref[f, layers - 1] = change[f]
     for j in range(layers - 2, -1, -1):
         ratio = ratio_ref[j]
         for f in range(3):
-            change[f] = d_ref[f, j] + ratio * change[f]
+            change[f] = blank(d_ref[f, j] + ratio * change[f])
             change_ref[f, j] = change[f]
 
 
@@ -956,7 +962,7 @@
             if i == nz:
                 beyond = other[f] * inverse_other + step * near[f]
                 change = jnp.where(beside_other, beyond, change)
-            put(change_ref, (f, i + 1), change)
+            put(change_ref, (f, i + 1), blank(change))
     lane = iotas(nx, ny)[1]
     first_lane, last_lane = lane == 0, lane == ny - 1
 
@@ -998,7 +1004,7 @@
                 copy = pltpu.make_async_copy(
                     buffer.at[part], out.at[part], sems.at[n, i // CHUNK]
                 )
-                copy.start()
+                copy.start(priority=n)
                 copies.append(copy)
     for copy in copies:
         copy.wait()

time: 27.9 us -> 27.8 us (level)
  transfers between devices with their start and end apart: 7 -> 7, of which waited for: 3 -> 3; matrix products, arithmetic and copies ran while one was open for 0% -> 0% of each run, Pallas kernels for 25% -> 24%
where the time goes in v9:
time: 27.8 us; the launch traced here: 27.6 us
  starting transfers between devices  10.7 us (38%)
  Pallas kernels  9.94 us (36%)
  waiting for transfers between devices  4 us (14%)
  local copies, waits for them, and re-layouts  2.27 us (8%)
  between operations  0.7 us (3%)
    pallas_call x10, Pallas kernels, kernel_call(): pl.pallas_call(kernel, out_shape=[jax.ShapeDtypeStruct(s, t) for s, t in...  9.94 us
    ppermute x3, starting transfers between devices, swapped(): lax.ppermute(values, 'gz', [(i, i ^ 2 ** stage) for i in range(size)])  8.47 us
    ppermute x1, waiting for transfers between devices, slanted(): return lax.ppermute(values, ('gx', 'gz'), route)  3.24 us
    unnamed x6, local copies, waits for them, and re-layouts  2.27 us
    ppermute x1, starting transfers between devices, slanted(): return lax.ppermute(values, ('gx', 'gz'), route)  1.44 us
    ppermute x3, starting transfers between devices, ring(): lax.ppermute(values, axis, [(i, (i + distance) % size) for i in range(siz...  0.75 us
  transfers between devices with their start and end apart: 7, of which 3 were waited for; matrix products, arithmetic and copies ran while one was open for 0% of the time, Pallas kernels for 24%

profile of v9, /device:TPU:0, one launch (start us, length us, event | category | flops | bytes accessed | tf_op | source)
XLA Modules:
  0.0 27.6 jit_solution(15541946959073733538)
XLA Ops:
  0.6 3.1 %collective-permute-start = (s32[16,16,128]{2,1,0:T(8,128)}, s32[16,16,128]{2,1,0:T(8,128)S(1)}, u32[]{:S(2)}, u32[]{:S(2)}) collective-permute-start(s32[16,16,128]{2,1,0:T(8,128)} %facies_ref.1), channel_id=1, source_target_pairs={{0,1},{1,0},{2,3},{3,2},{4,5},{5,4},{6,7},{7,6},{8,9},{9,8},{10,11... | collective-permute-start | bytes 393224 | tf_op jit(solution)/shard_map/ppermute | solution.py:1029
  3.7 0.0 copy-start
  3.7 0.9 %copy-done = s32[16,16,128]{2,1,0:T(8,128)S(1)} copy-done((s32[16,16,128]{2,1,0:T(8,128)S(1)}, s32[16,16,128]{2,1,0:T(8,128)}, u32[]{:S(2)}) %copy-start) | copy-done | bytes 131096
  4.7 1.4 %collective-permute-start.2 = (s32[64,128]{1,0:T(8,128)S(1)}, s32[64,128]{1,0:T(8,128)S(1)}, u32[]{:S(2)}, u32[]{:S(2)}) collective-permute-start(s32[64,128]{1,0:T(8,128)S(1)} %get-tuple-element.35), channel_id=1, source_target_pairs={{0,17},{1,16},{2,19},{3,18},{16,1},{17,0},{18,3},{19,2},{4,21},{5,... | collective-permute-start | bytes 98312 | tf_op jit(solution)/shard_map/ppermute | solution.py:1043
  6.1 0.2 collective-permute-start.1
  6.3 3.2 %collective-permute-done.2.refs_1_ = s32[64,128]{1,0:T(8,128)S(1)} collective-permute-done((s32[64,128]{1,0:T(8,128)S(1)}, s32[64,128]{1,0:T(8,128)S(1)}, u32[]{:S(2)}, u32[]{:S(2)}) %collective-permute-start.2) | collective-permute-done | bytes 32800 | tf_op jit(solution)/shard_map/ppermute | solution.py:1043
  9.6 0.5 %collective-permute-done.1.refs_0_ = s32[64,128]{1,0:T(8,128)S(1)} collective-permute-done((s32[64,128]{1,0:T(8,128)S(1)}, s32[64,128]{1,0:T(8,128)S(1)}, u32[]{:S(2)}, u32[]{:S(2)}) %collective-permute-start.1) | collective-permute-done | bytes 32800 | tf_op jit(solution)/shard_map/ppermute | solution.py:1034
  10.0 0.0 collective-permute-done.other_ref
  10.0 0.2 shard_map.52
  10.2 0.1 collective-permute-start.4
  10.3 0.5 %collective-permute-start.3 = (s32[48,128]{1,0:T(8,128)S(1)}, s32[48,128]{1,0:T(8,128)S(1)}, u32[]{:S(2)}, u32[]{:S(2)}) collective-permute-start(s32[48,128]{1,0:T(8,128)S(1)} %get-tuple-element.36), channel_id=1, source_target_pairs={{0,4},{4,8},{8,12},{12,0},{1,5},{5,9},{9,13},{13,1},{2,6},{6,10},{... | collective-permute-start | bytes 73736 | tf_op jit(solution)/shard_map/ppermute | solution.py:1034
  10.8 0.0 copy-start.1
  10.8 0.7 %copy-done.1 = f32[3,16]{1,0:T(4,128)S(1)} copy-done((f32[3,16]{1,0:T(4,128)S(1)}, f32[3,16]{1,0:T(4,128)}, u32[]{:S(2)}) %copy-start.1) | copy-done | bytes 216
  11.5 0.0 copy-start.2
  11.5 0.7 %copy-done.2 = s32[63]{0:T(128)S(1)} copy-done((s32[63]{0:T(128)S(1)}, s32[63]{0:T(128)}, u32[]{:S(2)}) %copy-start.2) | copy-done | bytes 276
  12.1 0.9 %shard_map.51 = (f32[3,16,16,128]{3,2,1,0:T(8,128)S(1)}, f32[3,8,128]{2,1,0:T(8,128)S(1)}, f32[40,128]{1,0:T(8,128)S(1)}) custom-call(f32[3,16]{1,0:T(4,128)S(1)} %copy-done.1, s32[63]{0:T(128)S(1)} %copy-done.2, s32[16,16,128]{2,1,0:T(8,128)S(1)} %get-tuple-element.32.facies_ref.own_ref), custom_call_target="tpu_custom_call" | custom-call | flops 10000000 | bytes 1000000 | tf_op jit(solution)/shard_map/pallas_call | solution.py:1016
  13.0 0.5 %shard_map.53 = (f32[3,32,16,128]{3,2,1,0:T(8,128)S(1)}, f32[3,128,128]{2,1,0:T(8,128)S(1)}) custom-call(f32[3,8,128]{2,1,0:T(8,128)S(1)} %get-tuple-element.34.table_ref, f32[3,16,16,128]{3,2,1,0:T(8,128)S(1)} %get-tuple-element.37.own_ref, s32[16,16,128]{2,1,0:T(8,128)S(1)} %collective-permute-done.other_ref, s32[128,128]{1,0:T(8,128)S(1)} %get-tuple-element.38.refs_0_), custom_call_target="tpu_custom_call" | custom-call | flops 10000000 | bytes 1000000 | tf_op jit(solution)/shard_map/pallas_call | solution.py:1016
  13.5 0.3 %shard_map.54 = (f32[32,40,128]{2,1,0:T(8,128)S(1)}, f32[32,24,128]{2,1,0:T(8,128)S(1)}, f32[32,24,128]{2,1,0:T(8,128)S(1)}, f32[32,24,128]{2,1,0:T(8,128)S(1)},...) custom-call(f32[3,32,16,128]{3,2,1,0:T(8,128)S(1)} %get-tuple-element.39.k_ref, ...), custom_call_target="tpu_custom_call" | custom-call | flops 10000000 | bytes 1000000 | tf_op jit(solution)/shard_map/pallas_call | solution.py:1016
  13.8 0.0 collective-permute-done.4.y_high
  13.8 0.0 collective-permute-done.3.y_low
  13.8 1.6 %shard_map.55 = (f32[104,128]{1,0:T(8,128)S(1)}, f32[5,24,256]{2,1,0:T(8,128)S(1)}, f32[32,2,40,128]{3,2,1,0:T(8,128)S(1)}, f32[32,24,256]{2,1,0:T(8,128)S(1)}, ...) custom-call(f32[3,8,128]{2,1,0:T(8,128)S(1)} %get-tuple-element.34.t, ...), custom_call_target="tpu_custom_call" | custom-call | tf_op jit(solution)/shard_map/pallas_call | solution.py:1016
  15.4 2.7 %collective-permute-start.5 = (f32[104,128]{1,0:T(8,128)S(1)}, f32[104,128]{1,0:T(8,128)S(1)}, u32[]{:S(2)}, u32[]{:S(2)}) collective-permute-start(f32[104,128]{1,0:T(8,128)S(1)} %get-tuple-element.48), channel_id=1, source_target_pairs={{0,2},{1,3},{2,0},{3,1},{4,6},{5,7},{6,4},{7,5},{8,10},{9,11},{10,... | collective-permute-start | bytes 159752 | tf_op jit(solution)/shard_map/ppermute | solution.py:1029
  18.1 2.6 %shard_map.56 = (f32[3,32,2,40,128]{4,3,2,1,0:T(8,128)S(1)}, f32[32,2,40,128]{3,2,1,0:T(8,128)S(1)}, f32[6,24,256]{2,1,0:T(8,128)S(1)}) custom-call(f32[40,128]{1,0:T(8,128)S(1)} %get-tuple-element.33.cut_ref, f32[32,2,40,128]{3,2,1,0:T(8,128)S(1)} %get-tuple-element.49.lx_ref, f32[32,24,256]{2,1,0:T(8,128)S(1)} %get-tuple-element.50.ly_ref, ...), custom_call_target="tpu_custom_call" | custom-call | flops 10000000 | bytes 1000000 | tf_op jit(solution)/shard_map/pallas_call | solution.py:1016
  20.7 0.2 collective-permute-done.5.message_ref
  20.9 0.3 shard_map.57
  21.2 2.7 %collective-permute-start.6 = (f32[64,128]{1,0:T(8,128)S(1)}, f32[64,128]{1,0:T(8,128)S(1)}, u32[]{:S(2)}, u32[]{:S(2)}) collective-permute-start(f32[64,128]{1,0:T(8,128)S(1)} %get-tuple-element.55), channel_id=1, source_target_pairs={{0,2},{1,3},{2,0},{3,1},{4,6},{5,7},{6,4},{7,5},{8,10},{9,11},{10,... | collective-permute-start | bytes 98312 | tf_op jit(solution)/shard_map/ppermute | solution.py:1029
  23.9 2.4 %shard_map.58 = (f32[3,32,2,40,128]{4,3,2,1,0:T(8,128)S(1)}, f32[3,32,24,256]{3,2,1,0:T(8,128)S(1)}) custom-call(f32[40,128]{1,0:T(8,128)S(1)} %get-tuple-element.33.cut_ref, f32[13,24,256]{2,1,0:T(8,128)S(1)} %get-tuple-element.56.near_ref, f32[32,2,40,128]{3,2,1,0:T(8,128)S(1)} %get-tuple-element.49.lx_ref, f32[32,24,256]{2,1,0:T(8,128)S(1)} %get-tuple-element.50.ly_ref, ...), custom_call_target="tpu_custom_call" | custom-call | flops 10000000 | bytes 1000000 | tf_op jit(solution)/shard_map/pallas_call | solution.py:1016
  26.4 0.0 collective-permute-done.6.message_ref
  26.4 1.2 %shard_map.59 = (f32[3,16,16,128]{3,2,1,0:T(8,128)}, f32[3,16,16,128]{3,2,1,0:T(8,128)}) custom-call(f32[40,128]{1,0:T(8,128)S(1)} %get-tuple-element.33.cut_ref, f32[64,128]{1,0:T(8,128)S(1)} %collective-permute-done.6.message_ref, f32[13,24,256]{2,1,0:T(8,128)S(1)} %get-tuple-element.56.near_ref, f32[32,2,40,128]{3,2,1,0:T(8,128)S(1)} %get-tuple-element.49.lx_ref, ...), custom_call_target="tpu_custom_call" | custom-call | tf_op jit(solution)/shard_map/pallas_call | solution.py:1016
  (1 shorter events, 0.0 us)
Async XLA Ops:
  0.6 9.4 %collective-permute-start = (s32[16,16,128]{2,1,0:T(8,128)}, s32[16,16,128]{2,1,0:T(8,128)S(1)}, u32[]{:S(2)}, u32[]{:S(2)}) collective-permute-start(s32[16,16,128]{2,1,0:T(8,128)} %facies_ref.1), channel_id=1, source_target_pairs={{0,1},{1,0},{2,3},{3,2},{4,5},{5,4},{6,7},{7,6},{8,9},{9,8},{10,11... | collective-permute-start | bytes 393224 | tf_op jit(solution)/shard_map/ppermute | solution.py:1029
  3.7 0.9 %copy-start = (s32[16,16,128]{2,1,0:T(8,128)S(1)}, s32[16,16,128]{2,1,0:T(8,128)}, u32[]{:S(2)}) copy-start(s32[16,16,128]{2,1,0:T(8,128)} %facies_ref.1) | copy-start | bytes 393220
  4.7 4.9 %collective-permute-start.2 = (s32[64,128]{1,0:T(8,128)S(1)}, s32[64,128]{1,0:T(8,128)S(1)}, u32[]{:S(2)}, u32[]{:S(2)}) collective-permute-start(s32[64,128]{1,0:T(8,128)S(1)} %get-tuple-element.35), channel_id=1, source_target_pairs={{0,17},{1,16},{2,19},{3,18},{16,1},{17,0},{18,3},{19,2},{4,21},{5,... | collective-permute-start | bytes 98312 | tf_op jit(solution)/shard_map/ppermute | solution.py:1043
  6.1 3.9 %collective-permute-start.1 = (s32[64,128]{1,0:T(8,128)S(1)}, s32[64,128]{1,0:T(8,128)S(1)}, u32[]{:S(2)}, u32[]{:S(2)}) collective-permute-start(s32[64,128]{1,0:T(8,128)S(1)} %get-tuple-element.35), channel_id=1, source_target_pairs={{0,16},{16,0},{1,17},{17,1},{2,18},{18,2},{3,19},{19,3},{4,20},{20... | collective-permute-start | bytes 98312 | tf_op jit(solution)/shard_map/ppermute | solution.py:1034
  10.2 3.6 %collective-permute-start.4 = (s32[48,128]{1,0:T(8,128)S(1)}, s32[48,128]{1,0:T(8,128)S(1)}, u32[]{:S(2)}, u32[]{:S(2)}) collective-permute-start(s32[48,128]{1,0:T(8,128)S(1)} %get-tuple-element.36), channel_id=1, source_target_pairs={{0,12},{4,0},{8,4},{12,8},{1,13},{5,1},{9,5},{13,9},{2,14},{6,2},{... | collective-permute-start | bytes 73736 | tf_op jit(solution)/shard_map/ppermute | solution.py:1034
  10.3 3.6 %collective-permute-start.3 = (s32[48,128]{1,0:T(8,128)S(1)}, s32[48,128]{1,0:T(8,128)S(1)}, u32[]{:S(2)}, u32[]{:S(2)}) collective-permute-start(s32[48,128]{1,0:T(8,128)S(1)} %get-tuple-element.36), channel_id=1, source_target_pairs={{0,4},{4,8},{8,12},{12,0},{1,5},{5,9},{9,13},{13,1},{2,6},{6,10},{... | collective-permute-start | bytes 73736 | tf_op jit(solution)/shard_map/ppermute | solution.py:1034
  10.8 0.7 %copy-start.1 = (f32[3,16]{1,0:T(4,128)S(1)}, f32[3,16]{1,0:T(4,128)}, u32[]{:S(2)}) copy-start(f32[3,16]{1,0:T(4,128)} %table.1) | copy-start | bytes 580
  11.5 0.7 %copy-start.2 = (s32[63]{0:T(128)S(1)}, s32[63]{0:T(128)}, u32[]{:S(2)}) copy-start(s32[63]{0:T(128)} %breaks.1) | copy-start | bytes 760
  15.4 5.5 %collective-permute-start.5 = (f32[104,128]{1,0:T(8,128)S(1)}, f32[104,128]{1,0:T(8,128)S(1)}, u32[]{:S(2)}, u32[]{:S(2)}) collective-permute-start(f32[104,128]{1,0:T(8,128)S(1)} %get-tuple-element.48), channel_id=1, source_target_pairs={{0,2},{1,3},{2,0},{3,1},{4,6},{5,7},{6,4},{7,5},{8,10},{9,11},{10,... | collective-permute-start | bytes 159752 | tf_op jit(solution)/shard_map/ppermute | solution.py:1029
  21.2 5.2 %collective-permute-start.6 = (f32[64,128]{1,0:T(8,128)S(1)}, f32[64,128]{1,0:T(8,128)S(1)}, u32[]{:S(2)}, u32[]{:S(2)}) collective-permute-start(f32[64,128]{1,0:T(8,128)S(1)} %get-tuple-element.55), channel_id=1, source_target_pairs={{0,2},{1,3},{2,0},{3,1},{4,6},{5,7},{6,4},{7,5},{8,10},{9,11},{10,... | collective-permute-start | bytes 98312 | tf_op jit(solution)/shard_map/ppermute | solution.py:1029

commit v10 on v8

--- a/solution.py
+++ b/solution.py
@@ -98,14 +98,14 @@
     return jnp.concatenate(rows, axis=0)
 
 
-def prepare_kernel(stages, table, breaks, facies_ref, k_ref, table_ref, cut_ref):
+def prepare_kernel(stages, labels, scalars, facies_ref, k_ref, table_ref, cut_ref):
     nz, nx, ny = facies_ref.shape
     lane = iotas(8, ny)[1]
     tables = []
     for q in range(3):
         values = jnp.zeros((8, ny), jnp.float32)
-        for label in range(table.shape[1]):
-            values = jnp.where(lane == label, table[q, label], values)
+        for label in range(labels):
+            values = jnp.where(lane == label, scalars[q * labels + label], values)
         if stages == 1:
             values = 2.0 * values
         table_ref[q] = values
@@ -125,7 +125,8 @@
         layers.append((base + size) * 2 * nz - 1)
         layers.append(jnp.where(is_high(s), base, base + 2 * size) * 2 * nz - 1)
     for r, layer in enumerate(layers):
-        cut = breaks[jnp.clip(layer, 0, breaks.shape[0] - 1)].astype(jnp.float32)
+        last = scalars.shape[0] - 1 - 3 * labels
+        cut = scalars[3 * labels + jnp.clip(layer, 0, last)]
         cut_ref[r : r + 1, :] = jnp.full((1, ny), cut, jnp.float32)
 
 
@@ -1056,11 +1057,12 @@
     else:
         rims = [ring(rows[1], "gx", 1), ring(rows[0], "gx", -1)]
         rims += [slanted(rows[1], 1), slanted(rows[0], -1)]
+    scalars = jnp.concatenate([perm_table.reshape(-1), line_breaks.astype(f32)])
     k, table, cuts = kernel_call(
-        functools.partial(prepare_kernel, stages),
+        functools.partial(prepare_kernel, stages, perm_table.shape[1]),
         [((3, nz, nx, ny), f32), ((3, 8, ny), f32), ((cut_rows, ny), f32)],
-        [perm_table, line_breaks, facies],
-        smem=2,
+        [scalars, facies],
+        smem=1,
         cost=pl.CostEstimate(flops=10**7, bytes_accessed=10**6, transcendentals=0),
     )
     strip, *rows = kernel_call(

time: 27.9 us -> 28.2 us (1.011)
  waiting for transfers between devices: 3.93 us -> 5.39 us
  starting transfers between devices: 10.7 us -> 9.45 us
  other arithmetic: 0 us -> 0.73 us
  local copies, waits for them, and re-layouts: 2.27 us -> 1.7 us
    ppermute x3, waiting for transfers between devices: 0.17 us -> 1.77 us  [swapped(): lax.ppermute(values, 'gz', [(i, i ^ 2 ** stage) for i in range(size)])]
    ppermute x1, waiting for transfers between devices: 3.24 us -> 1.82 us  [slanted(): return lax.ppermute(values, ('gx', 'gz'), route)]
    unnamed x6 -> x2, local copies, waits for them, and re-layouts: 2.27 us -> 0.94 us
    ppermute x3, waiting for transfers between devices: 0.51 us -> 1.8 us  [ring(): lax.ppermute(values, axis, [(i, (i + distance) % size) for i in range(siz...]
    ppermute x3, starting transfers between devices: 8.47 us -> 7.26 us  [swapped(): lax.ppermute(values, 'gz', [(i, i ^ 2 ** stage) for i in range(size)])]
    reshape x0 -> x1, local copies, waits for them, and re-layouts: none -> 0.76 us  [per_device(): scalars = jnp.concatenate([perm_table.reshape(-1), line_breaks.astype(f32)])]
    convert_element_type x0 -> x1, other arithmetic: none -> 0.66 us  [per_device(): scalars = jnp.concatenate([perm_table.reshape(-1), line_breaks.astype(f32)])]
  transfers between devices with their start and end apart: 7 -> 7, of which waited for: 3 -> 5; matrix products, arithmetic and copies ran while one was open for 0% -> 5% of each run, Pallas kernels for 25% -> 24%
where the time goes in v10:
time: 28.2 us; the launch traced here: 28 us
  Pallas kernels  10.1 us (36%)
  starting transfers between devices  9.45 us (34%)
  waiting for transfers between devices  5.39 us (19%)
  local copies, waits for them, and re-layouts  1.7 us (6%)
  other arithmetic  0.73 us (3%)
  between operations  0.69 us (2%)
    pallas_call x10, Pallas kernels, kernel_call(): pl.pallas_call(kernel, out_shape=[jax.ShapeDtypeStruct(s, t) for s, t in...  10.1 us
    ppermute x3, starting transfers between devices, swapped(): lax.ppermute(values, 'gz', [(i, i ^ 2 ** stage) for i in range(size)])  7.26 us
    ppermute x1, waiting for transfers between devices, slanted(): return lax.ppermute(values, ('gx', 'gz'), route)  1.82 us
    ppermute x3, waiting for transfers between devices, ring(): lax.ppermute(values, axis, [(i, (i + distance) % size) for i in range(siz...  1.8 us
    ppermute x3, waiting for transfers between devices, swapped(): lax.ppermute(values, 'gz', [(i, i ^ 2 ** stage) for i in range(size)])  1.77 us
    ppermute x1, starting transfers between devices, slanted(): return lax.ppermute(values, ('gx', 'gz'), route)  1.44 us
    unnamed x2, local copies, waits for them, and re-layouts  0.94 us
    reshape x1, local copies, waits for them, and re-layouts, per_device(): scalars = jnp.concatenate([perm_table.reshape(-1), line_breaks.astype(f32)])  0.76 us
  transfers between devices with their start and end apart: 7, of which 5 were waited for; matrix products, arithmetic and copies ran while one was open for 5% of the time, Pallas kernels for 24%

profile of v10, /device:TPU:0, one launch (start us, length us, event | category | flops | bytes accessed | tf_op | source)
XLA Modules:
  0.0 28.0 jit_solution(1910669687985091891)
XLA Ops:
  0.6 3.1 %collective-permute-start = (s32[16,16,128]{2,1,0:T(8,128)}, s32[16,16,128]{2,1,0:T(8,128)S(1)}, u32[]{:S(2)}, u32[]{:S(2)}) collective-permute-start(s32[16,16,128]{2,1,0:T(8,128)} %facies_ref.1), channel_id=1, source_target_pairs={{0,1},{1,0},{2,3},{3,2},{4,5},{5,4},{6,7},{7,6},{8,9},{9,8},{10,11... | collective-permute-start | bytes 393224 | tf_op jit(solution)/shard_map/ppermute | solution.py:1024
  3.7 0.0 copy-start
  3.7 0.9 %copy-done = s32[16,16,128]{2,1,0:T(8,128)S(1)} copy-done((s32[16,16,128]{2,1,0:T(8,128)S(1)}, s32[16,16,128]{2,1,0:T(8,128)}, u32[]{:S(2)}) %copy-start) | copy-done | bytes 131096
  4.7 1.4 %collective-permute-start.2 = (s32[64,128]{1,0:T(8,128)S(1)}, s32[64,128]{1,0:T(8,128)S(1)}, u32[]{:S(2)}, u32[]{:S(2)}) collective-permute-start(s32[64,128]{1,0:T(8,128)S(1)} %get-tuple-element.35), channel_id=1, source_target_pairs={{0,17},{1,16},{2,19},{3,18},{16,1},{17,0},{18,3},{19,2},{4,21},{5,... | collective-permute-start | bytes 98312 | tf_op jit(solution)/shard_map/ppermute | solution.py:1038
  6.1 0.2 collective-permute-start.1
  6.3 0.8 %reshape.7 = f32[48]{0:T(128)S(1)} reshape(f32[3,16]{1,0:T(4,128)} %param.4) | data formatting | bytes 384 | tf_op jit(solution)/shard_map/reshape | solution.py:1060
  7.1 0.7 %convert_element_type.3 = f32[63]{0:T(128)S(1)} convert(s32[63]{0:T(128)} %param.5) | non-fusion elementwise | flops 63 | bytes 504 | tf_op jit(solution)/shard_map/convert_element_type | solution.py:1060
  7.7 1.8 %collective-permute-done.2.refs_1_ = s32[64,128]{1,0:T(8,128)S(1)} collective-permute-done((s32[64,128]{1,0:T(8,128)S(1)}, s32[64,128]{1,0:T(8,128)S(1)}, u32[]{:S(2)}, u32[]{:S(2)}) %collective-permute-start.2) | collective-permute-done | bytes 32800 | tf_op jit(solution)/shard_map/ppermute | solution.py:1038
  9.6 0.5 %collective-permute-done.1.refs_0_ = s32[64,128]{1,0:T(8,128)S(1)} collective-permute-done((s32[64,128]{1,0:T(8,128)S(1)}, s32[64,128]{1,0:T(8,128)S(1)}, u32[]{:S(2)}, u32[]{:S(2)}) %collective-permute-start.1) | collective-permute-done | bytes 32800 | tf_op jit(solution)/shard_map/ppermute | solution.py:1029
  10.0 0.0 collective-permute-done.other_ref
  10.0 0.2 shard_map.52
  10.2 0.1 collective-permute-start.4
  10.3 0.5 %collective-permute-start.3 = (s32[48,128]{1,0:T(8,128)S(1)}, s32[48,128]{1,0:T(8,128)S(1)}, u32[]{:S(2)}, u32[]{:S(2)}) collective-permute-start(s32[48,128]{1,0:T(8,128)S(1)} %get-tuple-element.36), channel_id=1, source_target_pairs={{0,4},{4,8},{8,12},{12,0},{1,5},{5,9},{9,13},{13,1},{2,6},{6,10},{... | collective-permute-start | bytes 73736 | tf_op jit(solution)/shard_map/ppermute | solution.py:1029
  10.8 0.1 pad_maximum_fusion.scalars
  10.9 0.9 %shard_map.51 = (f32[3,16,16,128]{3,2,1,0:T(8,128)S(1)}, f32[3,8,128]{2,1,0:T(8,128)S(1)}, f32[40,128]{1,0:T(8,128)S(1)}) custom-call(f32[111]{0:T(128)S(1)} %pad_maximum_fusion.scalars, s32[16,16,128]{2,1,0:T(8,128)S(1)} %get-tuple-element.32.facies_ref.own_ref), custom_call_target="tpu_custom_call" | custom-call | flops 10000000 | bytes 1000000 | tf_op jit(solution)/shard_map/pallas_call | solution.py:1011
  11.7 0.5 %shard_map.53 = (f32[3,32,16,128]{3,2,1,0:T(8,128)S(1)}, f32[3,128,128]{2,1,0:T(8,128)S(1)}) custom-call(f32[3,8,128]{2,1,0:T(8,128)S(1)} %get-tuple-element.34.table_ref, f32[3,16,16,128]{3,2,1,0:T(8,128)S(1)} %get-tuple-element.37.own_ref, s32[16,16,128]{2,1,0:T(8,128)S(1)} %collective-permute-done.other_ref, s32[128,128]{1,0:T(8,128)S(1)} %get-tuple-element.38.refs_0_), custom_call_target="tpu_custom_call" | custom-call | flops 10000000 | bytes 1000000 | tf_op jit(solution)/shard_map/pallas_call | solution.py:1011
  12.2 0.3 %shard_map.54 = (f32[32,40,128]{2,1,0:T(8,128)S(1)}, f32[32,24,128]{2,1,0:T(8,128)S(1)}, f32[32,24,128]{2,1,0:T(8,128)S(1)}, f32[32,24,128]{2,1,0:T(8,128)S(1)},...) custom-call(f32[3,32,16,128]{3,2,1,0:T(8,128)S(1)} %get-tuple-element.39.k_ref, ...), custom_call_target="tpu_custom_call" | custom-call | flops 10000000 | bytes 1000000 | tf_op jit(solution)/shard_map/pallas_call | solution.py:1011
  12.5 0.0 collective-permute-done.4.y_high
  12.5 1.3 %collective-permute-done.3.y_low = s32[48,128]{1,0:T(8,128)S(1)} collective-permute-done((s32[48,128]{1,0:T(8,128)S(1)}, s32[48,128]{1,0:T(8,128)S(1)}, u32[]{:S(2)}, u32[]{:S(2)}) %collective-permute-start.3) | collective-permute-done | bytes 24608 | tf_op jit(solution)/shard_map/ppermute | solution.py:1029
  13.8 1.6 %shard_map.55 = (f32[104,128]{1,0:T(8,128)S(1)}, f32[5,24,256]{2,1,0:T(8,128)S(1)}, f32[32,2,40,128]{3,2,1,0:T(8,128)S(1)}, f32[32,24,256]{2,1,0:T(8,128)S(1)}, ...) custom-call(f32[3,8,128]{2,1,0:T(8,128)S(1)} %get-tuple-element.34.t, ...), custom_call_target="tpu_custom_call" | custom-call | tf_op jit(solution)/shard_map/pallas_call | solution.py:1011
  15.4 2.7 %collective-permute-start.5 = (f32[104,128]{1,0:T(8,128)S(1)}, f32[104,128]{1,0:T(8,128)S(1)}, u32[]{:S(2)}, u32[]{:S(2)}) collective-permute-start(f32[104,128]{1,0:T(8,128)S(1)} %get-tuple-element.48), channel_id=1, source_target_pairs={{0,2},{1,3},{2,0},{3,1},{4,6},{5,7},{6,4},{7,5},{8,10},{9,11},{10,... | collective-permute-start | bytes 159752 | tf_op jit(solution)/shard_map/ppermute | solution.py:1024
  18.1 2.6 %shard_map.56 = (f32[3,32,2,40,128]{4,3,2,1,0:T(8,128)S(1)}, f32[32,2,40,128]{3,2,1,0:T(8,128)S(1)}, f32[6,24,256]{2,1,0:T(8,128)S(1)}) custom-call(f32[40,128]{1,0:T(8,128)S(1)} %get-tuple-element.33.cut_ref, f32[32,2,40,128]{3,2,1,0:T(8,128)S(1)} %get-tuple-element.49.lx_ref, f32[32,24,256]{2,1,0:T(8,128)S(1)} %get-tuple-element.50.ly_ref, ...), custom_call_target="tpu_custom_call" | custom-call | flops 10000000 | bytes 1000000 | tf_op jit(solution)/shard_map/pallas_call | solution.py:1011
  20.7 0.9 %collective-permute-done.5.message_ref = f32[104,128]{1,0:T(8,128)S(1)} collective-permute-done((f32[104,128]{1,0:T(8,128)S(1)}, f32[104,128]{1,0:T(8,128)S(1)}, u32[]{:S(2)}, u32[]{:S(2)}) %collective-permute-start.5) | collective-permute-done | bytes 53280 | tf_op jit(solution)/shard_map/ppermute | solution.py:1024
  21.7 0.3 shard_map.57
  21.9 1.5 %collective-permute-start.6 = (f32[64,128]{1,0:T(8,128)S(1)}, f32[64,128]{1,0:T(8,128)S(1)}, u32[]{:S(2)}, u32[]{:S(2)}) collective-permute-start(f32[64,128]{1,0:T(8,128)S(1)} %get-tuple-element.55), channel_id=1, source_target_pairs={{0,2},{1,3},{2,0},{3,1},{4,6},{5,7},{6,4},{7,5},{8,10},{9,11},{10,... | collective-permute-start | bytes 98312 | tf_op jit(solution)/shard_map/ppermute | solution.py:1024
  23.5 2.5 %shard_map.58 = (f32[3,32,2,40,128]{4,3,2,1,0:T(8,128)S(1)}, f32[3,32,24,256]{3,2,1,0:T(8,128)S(1)}) custom-call(f32[40,128]{1,0:T(8,128)S(1)} %get-tuple-element.33.cut_ref, f32[13,24,256]{2,1,0:T(8,128)S(1)} %get-tuple-element.56.near_ref, f32[32,2,40,128]{3,2,1,0:T(8,128)S(1)} %get-tuple-element.49.lx_ref, f32[32,24,256]{2,1,0:T(8,128)S(1)} %get-tuple-element.50.ly_ref, ...), custom_call_target="tpu_custom_call" | custom-call | flops 10000000 | bytes 1000000 | tf_op jit(solution)/shard_map/pallas_call | solution.py:1011
  26.0 0.8 %collective-permute-done.6.message_ref = f32[64,128]{1,0:T(8,128)S(1)} collective-permute-done((f32[64,128]{1,0:T(8,128)S(1)}, f32[64,128]{1,0:T(8,128)S(1)}, u32[]{:S(2)}, u32[]{:S(2)}) %collective-permute-start.6) | collective-permute-done | bytes 32800 | tf_op jit(solution)/shard_map/ppermute | solution.py:1024
  26.8 1.2 %shard_map.59 = (f32[3,16,16,128]{3,2,1,0:T(8,128)}, f32[3,16,16,128]{3,2,1,0:T(8,128)}) custom-call(f32[40,128]{1,0:T(8,128)S(1)} %get-tuple-element.33.cut_ref, f32[64,128]{1,0:T(8,128)S(1)} %collective-permute-done.6.message_ref, f32[13,24,256]{2,1,0:T(8,128)S(1)} %get-tuple-element.56.near_ref, f32[32,2,40,128]{3,2,1,0:T(8,128)S(1)} %get-tuple-element.49.lx_ref, ...), custom_call_target="tpu_custom_call" | custom-call | tf_op jit(solution)/shard_map/pallas_call | solution.py:1011
  (1 shorter events, 0.0 us)
Async XLA Ops:
  0.6 9.4 %collective-permute-start = (s32[16,16,128]{2,1,0:T(8,128)}, s32[16,16,128]{2,1,0:T(8,128)S(1)}, u32[]{:S(2)}, u32[]{:S(2)}) collective-permute-start(s32[16,16,128]{2,1,0:T(8,128)} %facies_ref.1), channel_id=1, source_target_pairs={{0,1},{1,0},{2,3},{3,2},{4,5},{5,4},{6,7},{7,6},{8,9},{9,8},{10,11... | collective-permute-start | bytes 393224 | tf_op jit(solution)/shard_map/ppermute | solution.py:1024
  3.7 0.9 %copy-start = (s32[16,16,128]{2,1,0:T(8,128)S(1)}, s32[16,16,128]{2,1,0:T(8,128)}, u32[]{:S(2)}) copy-start(s32[16,16,128]{2,1,0:T(8,128)} %facies_ref.1) | copy-start | bytes 393220
  4.7 4.9 %collective-permute-start.2 = (s32[64,128]{1,0:T(8,128)S(1)}, s32[64,128]{1,0:T(8,128)S(1)}, u32[]{:S(2)}, u32[]{:S(2)}) collective-permute-start(s32[64,128]{1,0:T(8,128)S(1)} %get-tuple-element.35), channel_id=1, source_target_pairs={{0,17},{1,16},{2,19},{3,18},{16,1},{17,0},{18,3},{19,2},{4,21},{5,... | collective-permute-start | bytes 98312 | tf_op jit(solution)/shard_map/ppermute | solution.py:1038
  6.1 3.9 %collective-permute-start.1 = (s32[64,128]{1,0:T(8,128)S(1)}, s32[64,128]{1,0:T(8,128)S(1)}, u32[]{:S(2)}, u32[]{:S(2)}) collective-permute-start(s32[64,128]{1,0:T(8,128)S(1)} %get-tuple-element.35), channel_id=1, source_target_pairs={{0,16},{16,0},{1,17},{17,1},{2,18},{18,2},{3,19},{19,3},{4,20},{20... | collective-permute-start | bytes 98312 | tf_op jit(solution)/shard_map/ppermute | solution.py:1029
  10.2 2.3 %collective-permute-start.4 = (s32[48,128]{1,0:T(8,128)S(1)}, s32[48,128]{1,0:T(8,128)S(1)}, u32[]{:S(2)}, u32[]{:S(2)}) collective-permute-start(s32[48,128]{1,0:T(8,128)S(1)} %get-tuple-element.36), channel_id=1, source_target_pairs={{0,12},{4,0},{8,4},{12,8},{1,13},{5,1},{9,5},{13,9},{2,14},{6,2},{... | collective-permute-start | bytes 73736 | tf_op jit(solution)/shard_map/ppermute | solution.py:1029
  10.3 3.6 %collective-permute-start.3 = (s32[48,128]{1,0:T(8,128)S(1)}, s32[48,128]{1,0:T(8,128)S(1)}, u32[]{:S(2)}, u32[]{:S(2)}) collective-permute-start(s32[48,128]{1,0:T(8,128)S(1)} %get-tuple-element.36), channel_id=1, source_target_pairs={{0,4},{4,8},{8,12},{12,0},{1,5},{5,9},{9,13},{13,1},{2,6},{6,10},{... | collective-permute-start | bytes 73736 | tf_op jit(solution)/shard_map/ppermute | solution.py:1029
  15.4 6.2 %collective-permute-start.5 = (f32[104,128]{1,0:T(8,128)S(1)}, f32[104,128]{1,0:T(8,128)S(1)}, u32[]{:S(2)}, u32[]{:S(2)}) collective-permute-start(f32[104,128]{1,0:T(8,128)S(1)} %get-tuple-element.48), channel_id=1, source_target_pairs={{0,2},{1,3},{2,0},{3,1},{4,6},{5,7},{6,4},{7,5},{8,10},{9,11},{10,... | collective-permute-start | bytes 159752 | tf_op jit(solution)/shard_map/ppermute | solution.py:1024
  21.9 4.9 %collective-permute-start.6 = (f32[64,128]{1,0:T(8,128)S(1)}, f32[64,128]{1,0:T(8,128)S(1)}, u32[]{:S(2)}, u32[]{:S(2)}) collective-permute-start(f32[64,128]{1,0:T(8,128)S(1)} %get-tuple-element.55), channel_id=1, source_target_pairs={{0,2},{1,3},{2,0},{3,1},{4,6},{5,7},{6,4},{7,5},{8,10},{9,11},{10,... | collective-permute-start | bytes 98312 | tf_op jit(solution)/shard_map/ppermute | solution.py:1024
